TPU v7x, 32 devices: a whole 2x2x4 slice. The times are simulated.
32 devices in a mesh: fsdp: 4 (over z), ctx: 4 (over x, core), tp: 2 (over y).
Axes of the slice: x: 2, y: 2, z: 4, core: 2. Of those that a mesh axis runs over, the one named last changes fastest.
Arguments:
- tokens: bfloat16 [8192, 768], P(('fsdp', 'ctx')), may hold values from -6 to 6
- segments: int32 [4, 2048], P('fsdp'), may hold values from 0 to 23, never falling along the last dimension, each value on 1 to 1538 neighbouring positions
- experts: int32 [8192, 2], P(('fsdp', 'ctx')), may hold values from 0 to 15, all different within a row; in each aligned block of 512 rows (0 to 511, 512 to 1023, ...) at most 128 rows name the same one
- attn_gain: bfloat16 [768], P(('fsdp', 'ctx')), may hold values from 0.5 to 1.5
- qkv_proj: bfloat16 [3, 768, 768], P(None, ('fsdp', 'ctx'), 'tp'), may hold values from -0.3125 to 0.3125
- out_proj: bfloat16 [768, 768], P('tp', ('fsdp', 'ctx')), may hold values from -0.875 to 0.875
- ffn_gain: bfloat16 [768], P(('fsdp', 'ctx')), may hold values from 0.5 to 1.5
- router_proj: bfloat16 [768, 16], P(('fsdp', 'ctx')), may hold values from -0.15625 to 0.15625
- expert_gate_up: bfloat16 [16, 2, 768, 2048], P('ctx', None, 'fsdp', 'tp'), may hold values from -0.21875 to 0.21875
- expert_down: bfloat16 [16, 2048, 768], P('ctx', 'tp', 'fsdp'), may hold values from -2 to 2
- shared_gate_up: bfloat16 [2, 768, 2048], P(None, ('fsdp', 'ctx'), 'tp'), may hold values from -0.21875 to 0.21875
- shared_down: bfloat16 [2048, 768], P('tp', ('fsdp', 'ctx')), may hold values from -0.125 to 0.125
- cotangent: bfloat16 [8192, 768], P(('fsdp', 'ctx')), may hold values from -6 to 6
Outputs:
- layer_out: bfloat16 [8192, 768], P(('fsdp', 'ctx'))
- tokens_grad: float32 [8192, 768], P(('fsdp', 'ctx'))
- attn_gain_grad: float32 [768], P(('fsdp', 'ctx'))
- qkv_grad: float32 [3, 768, 768], P(None, ('fsdp', 'ctx'), 'tp')
- out_grad: float32 [768, 768], P('tp', ('fsdp', 'ctx'))
- ffn_gain_grad: float32 [768], P(('fsdp', 'ctx'))
- router_grad: float32 [768, 16], P(('fsdp', 'ctx'))
- expert_gate_up_grad: float32 [16, 2, 768, 2048], P('ctx', None, 'fsdp', 'tp')
- expert_down_grad: float32 [16, 2048, 768], P('ctx', 'tp', 'fsdp')
- shared_gate_up_grad: float32 [2, 768, 2048], P(None, ('fsdp', 'ctx'), 'tp')
- shared_down_grad: float32 [2048, 768], P('tp', ('fsdp', 'ctx'))
Inputs may be any that keep to these rules, and one draw needn't show every extreme that they name: In each aligned block of 512 tokens (the tokens of one device) no expert is named by more than 128 tokens, and some expert reaches 128 in every draw; a token's two experts differ. `segments`: document numbers never fall along a sequence; one document of each sequence has exactly 1538 tokens.
All inputs are finite; a program needn't handle non-finite values.
Results may differ from a plain program's by a relative error of at most 0.015.
The roundings to bfloat16 on the way count: a program that leaves them out, or rounds other values in their place, can miss the bound.
Values may be sent and summed in bfloat16 or wider, within the bound.
No kernel may reach another device: no remote copies, remote signals or barrier semaphores. Data moves between devices by JAX's collectives and lax.ppermute only.
A program may use at most 192 MiB of HBM per device.

v0:
```python
import jax
import jax.numpy as jnp
from jax import lax
from jax.sharding import PartitionSpec as P

D = 768
HD = 64
E = 16
ROWS = 512
CAP = 128


eps = 1e-06


def rotary(values, positions, direction):
    half_dim = values.shape[-1] // 2
    frequency = 10000.0 ** (-jnp.arange(half_dim, dtype=jnp.float32) / half_dim)
    angles = direction * positions.astype(jnp.float32)[:, None] * frequency[None, :]
    cosine = jnp.cos(angles)[:, None, :]
    sine_part = jnp.sin(angles)[:, None, :]
    first = values[..., :half_dim]
    second = values[..., half_dim:]
    return jnp.concatenate(
        [first * cosine - second * sine_part, second * cosine + first * sine_part], axis=-1
    )


def silu_slope(values):
    logistic = jax.nn.sigmoid(values)
    return logistic * (1.0 + values * (1.0 - logistic))


def norm_back(grad_normed, residual, scale, gain):
    normalized = residual * scale
    scaled_grad = grad_normed * gain
    grad_resid = scale * (
        scaled_grad - normalized * jnp.mean(scaled_grad * normalized, axis=-1, keepdims=True)
    )
    return (grad_resid, jnp.sum(grad_normed * normalized, axis=0))


def per_device(
    tokens,
    segments,
    experts,
    attn_gain,
    qkv_proj,
    out_proj,
    ffn_gain,
    router_proj,
    expert_gate_up,
    expert_down,
    shared_gate_up,
    shared_down,
    cotangent,
):
    ctx_count = lax.axis_size("ctx")
    ctx_index = lax.axis_index("ctx")
    seq_len = ROWS * ctx_count
    score_scale = HD ** (-0.5)

    def dense_fetch():
        return (
            lax.all_gather(qkv_proj, ("fsdp", "ctx"), axis=1, tiled=True),
            lax.all_gather(out_proj, ("fsdp", "ctx"), axis=1, tiled=True),
            lax.all_gather(shared_gate_up, ("fsdp", "ctx"), axis=1, tiled=True),
            lax.all_gather(shared_down, ("fsdp", "ctx"), axis=1, tiled=True),
            lax.all_gather(attn_gain, ("fsdp", "ctx"), axis=0, tiled=True),
            lax.all_gather(ffn_gain, ("fsdp", "ctx"), axis=0, tiled=True),
            lax.all_gather(router_proj, ("fsdp", "ctx"), axis=0, tiled=True),
        )

    def expert_fetch():
        return (
            lax.all_gather(expert_gate_up, "fsdp", axis=2, tiled=True),
            lax.all_gather(expert_down, "fsdp", axis=2, tiled=True),
        )

    qkv_full, out_full, shared_gu_full, shared_down_full, gain_one, gain_two, router_full = (
        dense_fetch()
    )
    gain_one = gain_one.astype(jnp.float32)
    gain_two = gain_two.astype(jnp.float32)
    residual = tokens.astype(jnp.float32)
    scale_one = lax.rsqrt(jnp.mean(residual * residual, axis=-1, keepdims=True) + eps)
    normed_one = (residual * scale_one * gain_one).astype(jnp.bfloat16)
    projected = jnp.einsum("rd,jdc->rjc", normed_one, qkv_full, preferred_element_type=jnp.float32)
    local_heads = projected.shape[2] // HD
    positions = ctx_index * ROWS + jnp.arange(ROWS, dtype=jnp.int32)
    queries = rotary(projected[:, 0].reshape(ROWS, local_heads, HD), positions, 1.0).astype(
        jnp.bfloat16
    )
    key_rows = (
        rotary(projected[:, 1].reshape(ROWS, local_heads, HD), positions, 1.0)
        .reshape(ROWS, -1)
        .astype(jnp.bfloat16)
    )
    value_rows = projected[:, 2].astype(jnp.bfloat16)
    key_all, value_all = (
        lax.all_gather(key_rows, "ctx", axis=0, tiled=True),
        lax.all_gather(value_rows, "ctx", axis=0, tiled=True),
    )
    key_block = key_all.reshape(seq_len, local_heads, HD)
    value_block = value_all.reshape(seq_len, local_heads, HD)
    seq_ids = segments[0]
    query_ids = lax.dynamic_slice_in_dim(seq_ids, ctx_index * ROWS, ROWS, 0)
    key_pos = jnp.arange(seq_len, dtype=jnp.int32)
    allowed = (positions[:, None] >= key_pos[None, :]) & (query_ids[:, None] == seq_ids[None, :])
    raw_scores = (
        jnp.einsum("qhc,khc->hqk", queries, key_block, preferred_element_type=jnp.float32)
        * score_scale
    )
    masked = jnp.where(allowed[None], raw_scores, -jnp.inf)
    highest = jnp.max(masked, axis=-1, keepdims=True)
    log_total = highest + jnp.log(jnp.sum(jnp.exp(masked - highest), axis=-1, keepdims=True))
    attn_probs = jnp.exp(masked - log_total)
    attended = (
        jnp.einsum(
            "hqk,khc->qhc",
            attn_probs.astype(jnp.bfloat16),
            value_block,
            preferred_element_type=jnp.float32,
        )
        .reshape(ROWS, -1)
        .astype(jnp.bfloat16)
    )
    attn_part = jnp.dot(attended, out_full, preferred_element_type=jnp.float32)
    middle = residual + lax.psum(attn_part, "tp")
    scale_two = lax.rsqrt(jnp.mean(middle * middle, axis=-1, keepdims=True) + eps)
    normed_two = (middle * scale_two * gain_two).astype(jnp.bfloat16)
    router_probs = jax.nn.softmax(
        jnp.dot(normed_two, router_full, preferred_element_type=jnp.float32), axis=-1
    )
    gate_values = jnp.take_along_axis(router_probs, experts, axis=1)
    shared_pair = jnp.einsum(
        "rd,jdf->rjf", normed_two, shared_gu_full, preferred_element_type=jnp.float32
    )
    shared_hidden = (jax.nn.silu(shared_pair[:, 0]) * shared_pair[:, 1]).astype(jnp.bfloat16)
    shared_part = jnp.dot(shared_hidden, shared_down_full, preferred_element_type=jnp.float32)
    expert_ids = experts.reshape(-1)
    onehot = (expert_ids[:, None] == jnp.arange(E, dtype=jnp.int32)[None, :]).astype(jnp.int32)
    slot_index = jnp.sum((jnp.cumsum(onehot, axis=0) - onehot) * onehot, axis=1)
    slot_target = expert_ids * CAP + slot_index
    slot_table = (
        jnp.full((E * CAP,), 2 * ROWS, jnp.int32)
        .at[slot_target]
        .set(jnp.arange(2 * ROWS, dtype=jnp.int32))
    )
    token_index = jnp.where(slot_table < 2 * ROWS, slot_table // 2, ROWS)
    local_experts = expert_gate_up.shape[0]
    padded_in = jnp.concatenate([normed_two, jnp.zeros((1, D), jnp.bfloat16)], axis=0)
    send_rows = padded_in[token_index].reshape(ctx_count, local_experts, CAP, D)
    received = lax.all_to_all(send_rows, "ctx", split_axis=0, concat_axis=0, tiled=True)
    gate_up_full, down_full = expert_fetch()
    expert_gate = jnp.einsum(
        "secd,edf->secf", received, gate_up_full[:, 0], preferred_element_type=jnp.float32
    )
    expert_up = jnp.einsum(
        "secd,edf->secf", received, gate_up_full[:, 1], preferred_element_type=jnp.float32
    )
    expert_hidden = (jax.nn.silu(expert_gate) * expert_up).astype(jnp.bfloat16)
    expert_part = jnp.einsum(
        "secf,efd->secd", expert_hidden, down_full, preferred_element_type=jnp.float32
    )
    returned = lax.all_to_all(expert_part, "ctx", split_axis=0, concat_axis=0, tiled=True).reshape(
        E * CAP, D
    )
    picked_rows = returned[slot_target].reshape(ROWS, 2, D)
    moe_part = shared_part + jnp.sum(gate_values[:, :, None] * picked_rows, axis=1)
    layer_out = (middle + lax.psum(moe_part.astype(jnp.bfloat16), "tp").astype(jnp.float32)).astype(
        jnp.bfloat16
    )
    qkv_full, out_full, shared_gu_full, shared_down_full, gain_again, ffn_again, router_full = (
        dense_fetch()
    )
    gate_up_full, down_full = expert_fetch()
    grad_out = cotangent.astype(jnp.float32)
    shared_down_grad = jnp.einsum(
        "rf,rd->fd", shared_hidden, cotangent, preferred_element_type=jnp.float32
    )
    shared_hidden_grad = jnp.einsum(
        "rd,fd->rf", cotangent, shared_down_full, preferred_element_type=jnp.float32
    )
    shared_gate_grad = (
        shared_hidden_grad * shared_pair[:, 1] * silu_slope(shared_pair[:, 0])
    ).astype(jnp.bfloat16)
    shared_up_grad = (shared_hidden_grad * jax.nn.silu(shared_pair[:, 0])).astype(jnp.bfloat16)
    shared_pair_grad = jnp.stack([shared_gate_grad, shared_up_grad], axis=1)
    shared_gate_up_grad = jnp.einsum(
        "rd,rjf->jdf", normed_two, shared_pair_grad, preferred_element_type=jnp.float32
    )
    shared_back = jnp.einsum(
        "rjf,jdf->rd", shared_pair_grad, shared_gu_full, preferred_element_type=jnp.float32
    )
    assign_grad = (
        (gate_values[:, :, None] * grad_out[:, None, :]).reshape(2 * ROWS, D).astype(jnp.bfloat16)
    )
    padded_grad = jnp.concatenate([assign_grad, jnp.zeros((1, D), jnp.bfloat16)], axis=0)
    grad_send = padded_grad[slot_table].reshape(ctx_count, local_experts, CAP, D)
    grad_received = lax.all_to_all(grad_send, "ctx", split_axis=0, concat_axis=0, tiled=True)
    hidden_grad = jnp.einsum(
        "secd,efd->secf", grad_received, down_full, preferred_element_type=jnp.float32
    )
    expert_down_grad = jnp.einsum(
        "secf,secd->efd", expert_hidden, grad_received, preferred_element_type=jnp.float32
    )
    expert_gate_grad = (hidden_grad * expert_up * silu_slope(expert_gate)).astype(jnp.bfloat16)
    expert_up_grad = (hidden_grad * jax.nn.silu(expert_gate)).astype(jnp.bfloat16)
    expert_gate_up_grad = jnp.stack(
        [
            jnp.einsum(
                "secd,secf->edf", received, expert_gate_grad, preferred_element_type=jnp.float32
            ),
            jnp.einsum(
                "secd,secf->edf", received, expert_up_grad, preferred_element_type=jnp.float32
            ),
        ],
        axis=1,
    )
    back_rows = jnp.einsum(
        "secf,edf->secd", expert_gate_grad, gate_up_full[:, 0], preferred_element_type=jnp.float32
    )
    back_rows = back_rows + jnp.einsum(
        "secf,edf->secd", expert_up_grad, gate_up_full[:, 1], preferred_element_type=jnp.float32
    )
    back_returned = lax.all_to_all(
        back_rows, "ctx", split_axis=0, concat_axis=0, tiled=True
    ).reshape(E * CAP, D)
    back_picked = back_returned[slot_target].reshape(ROWS, 2, D)
    gate_dots = jnp.sum(grad_out[:, None, :] * picked_rows, axis=-1)
    ffn_back, gate_grad = lax.psum((shared_back + jnp.sum(back_picked, axis=1), gate_dots), "tp")
    expert_onehot = (experts[:, :, None] == jnp.arange(E, dtype=jnp.int32)[None, None, :]).astype(
        jnp.float32
    )
    probs_grad = jnp.sum(gate_grad[:, :, None] * expert_onehot, axis=1)
    logits_grad = router_probs * (
        probs_grad - jnp.sum(router_probs * probs_grad, axis=-1, keepdims=True)
    )
    router_f32 = router_full.astype(jnp.float32)
    normed_two_grad = ffn_back + jnp.dot(logits_grad, router_f32.T, precision=lax.Precision.HIGHEST)
    router_grad = jnp.dot(
        normed_two.astype(jnp.float32).T, logits_grad, precision=lax.Precision.HIGHEST
    )
    middle_part, ffn_gain_grad = norm_back(normed_two_grad, middle, scale_two, gain_two)
    middle_grad = grad_out + middle_part
    middle_low = middle_grad.astype(jnp.bfloat16)
    out_grad = jnp.einsum("rc,rd->cd", attended, middle_low, preferred_element_type=jnp.float32)
    attended_grad = (
        jnp.einsum("rd,cd->rc", middle_low, out_full, preferred_element_type=jnp.float32)
        .astype(jnp.bfloat16)
        .reshape(ROWS, local_heads, HD)
    )
    probs_again = jnp.exp(
        jnp.where(
            allowed[None],
            jnp.einsum("qhc,khc->hqk", queries, key_block, preferred_element_type=jnp.float32)
            * score_scale,
            -jnp.inf,
        )
        - log_total
    )
    probs_grad_attn = jnp.einsum(
        "qhc,khc->hqk", attended_grad, value_block, preferred_element_type=jnp.float32
    )
    row_dots = jnp.sum(probs_again * probs_grad_attn, axis=-1, keepdims=True)
    scores_grad = (probs_again * (probs_grad_attn - row_dots)).astype(jnp.bfloat16)
    query_grad = (
        jnp.einsum("hqk,khc->qhc", scores_grad, key_block, preferred_element_type=jnp.float32)
        * score_scale
    )
    key_grad_all = (
        jnp.einsum("hqk,qhc->khc", scores_grad, queries, preferred_element_type=jnp.float32)
        * score_scale
    )
    value_grad_all = jnp.einsum(
        "hqk,qhc->khc",
        probs_again.astype(jnp.bfloat16),
        attended_grad,
        preferred_element_type=jnp.float32,
    )
    key_grad, value_grad = (
        lax.psum_scatter(key_grad_all.reshape(seq_len, -1), "ctx", scatter_dimension=0, tiled=True),
        lax.psum_scatter(
            value_grad_all.reshape(seq_len, -1), "ctx", scatter_dimension=0, tiled=True
        ),
    )
    query_raw = rotary(query_grad, positions, -1.0).reshape(ROWS, -1)
    key_raw = rotary(key_grad.reshape(ROWS, local_heads, HD), positions, -1.0).reshape(ROWS, -1)
    projected_grad = jnp.stack([query_raw, key_raw, value_grad], axis=1).astype(jnp.bfloat16)
    qkv_grad = jnp.einsum(
        "rd,rjc->jdc", normed_one, projected_grad, preferred_element_type=jnp.float32
    )
    normed_one_part = jnp.einsum(
        "rjc,jdc->rd", projected_grad, qkv_full, preferred_element_type=jnp.float32
    )
    normed_one_grad = lax.psum(normed_one_part, "tp")
    tokens_part, attn_gain_grad = norm_back(normed_one_grad, residual, scale_one, gain_one)
    tokens_grad = middle_grad + tokens_part
    (
        qkv_grad,
        out_grad,
        shared_gate_up_grad,
        shared_down_grad,
        attn_gain_grad,
        ffn_gain_grad,
        router_grad,
    ) = (
        lax.psum_scatter(qkv_grad, ("fsdp", "ctx"), scatter_dimension=1, tiled=True),
        lax.psum_scatter(out_grad, ("fsdp", "ctx"), scatter_dimension=1, tiled=True),
        lax.psum_scatter(shared_gate_up_grad, ("fsdp", "ctx"), scatter_dimension=1, tiled=True),
        lax.psum_scatter(shared_down_grad, ("fsdp", "ctx"), scatter_dimension=1, tiled=True),
        lax.psum_scatter(attn_gain_grad, ("fsdp", "ctx"), scatter_dimension=0, tiled=True),
        lax.psum_scatter(ffn_gain_grad, ("fsdp", "ctx"), scatter_dimension=0, tiled=True),
        lax.psum_scatter(router_grad, ("fsdp", "ctx"), scatter_dimension=0, tiled=True),
    )
    expert_gate_up_grad, expert_down_grad = (
        lax.psum_scatter(expert_gate_up_grad, "fsdp", scatter_dimension=2, tiled=True),
        lax.psum_scatter(expert_down_grad, "fsdp", scatter_dimension=2, tiled=True),
    )
    return (
        layer_out,
        tokens_grad,
        attn_gain_grad,
        qkv_grad,
        out_grad,
        ffn_gain_grad,
        router_grad,
        expert_gate_up_grad,
        expert_down_grad,
        shared_gate_up_grad,
        shared_down_grad,
    )


def solution(mesh):
    return jax.shard_map(
        per_device,
        mesh=mesh,
        in_specs=(
            P(("fsdp", "ctx"), None),
            P("fsdp", None),
            P(("fsdp", "ctx"), None),
            P(("fsdp", "ctx")),
            P(None, ("fsdp", "ctx"), "tp"),
            P("tp", ("fsdp", "ctx")),
            P(("fsdp", "ctx")),
            P(("fsdp", "ctx"), None),
            P("ctx", None, "fsdp", "tp"),
            P("ctx", "tp", "fsdp"),
            P(None, ("fsdp", "ctx"), "tp"),
            P("tp", ("fsdp", "ctx")),
            P(("fsdp", "ctx"), None),
        ),
        out_specs=(
            P(("fsdp", "ctx"), None),
            P(("fsdp", "ctx"), None),
            P(("fsdp", "ctx")),
            P(None, ("fsdp", "ctx"), "tp"),
            P("tp", ("fsdp", "ctx")),
            P(("fsdp", "ctx")),
            P(("fsdp", "ctx"), None),
            P("ctx", None, "fsdp", "tp"),
            P("ctx", "tp", "fsdp"),
            P(None, ("fsdp", "ctx"), "tp"),
            P("tp", ("fsdp", "ctx")),
        ),
        check_vma=False,
    )
```

profile of v0, /device:TPU:0, one launch (start us, length us, event | category | flops | bytes accessed | tf_op | source)
XLA Modules:
  0.0 1944.5 jit_solution(11374341808528524450)
XLA Ops:
  12.5 35.2 %all-reduce.10 = (bf16[768]{0:T(1024)(128)(2,1)S(1)}, bf16[768]{0:T(1024)(128)(2,1)S(1)}) all-reduce(bf16[768]{0:T(1024)(128)(2,1)S(1)} %dynamic-update-slice, bf16[768]{0:T(1024)(128)(2,1)S(1)} %dynamic-update-slice.1), channel_id=1, replica_groups=mesh['fsdp'=4,'ctx'=4,'tp'=2] {'fsdp','ctx'}, use_global_device_ids=true, to_apply=%add.2 | all-reduce | flops 1536 | bytes 6144
  50.2 4.1 all-gather.10.cloned.1.call-done
  59.0 21.3 %all_gather.44 = bf16[384,768]{0,1:T(8,128)(2,1)S(1)} all-gather(bf16[384,48]{0,1:T(8,128)(2,1)S(1)} %copy-done.47), channel_id=1, replica_groups=mesh['fsdp'=4,'ctx'=4,'tp'=2] {'fsdp','ctx'}, dimensions={1}, use_global_device_ids=true | all-gather | bytes 626688 | tf_op jit(solution)/shard_map/all_gather | solution.py:66
  83.7 12.3 fusion
  96.0 12.0 exponential_reduce_fusion
  108.0 11.7 convolution_convert_fusion
  122.7 3.9 copy.173
  128.2 4.5 reduce-window.6
  133.2 4.3 scatter_custom_fusion
  137.5 34.2 %all-reduce.17.cloned.1.call-done = f32[512,768]{1,0:T(8,128)} async-done(((f32[512,768]{1,0:T(8,128)}), f32[512,768]{1,0:T(8,128)}) %all-reduce.17.cloned.1.call-update) | async-done | bytes 1572880 | tf_op jit(solution)/shard_map/psum | solution.py:129
  174.9 9.4 gather_fusion
  184.3 4.8 all-to-all-start
  192.2 5.4 mul.455
  197.6 42.6 %all-gather.1 = bf16[16,48,16]{1,2,0:T(8,128)(2,1)S(1)} all-gather(bf16[1,48,16]{1,2,0:T(8,128)(2,1)S(1)} %bitcast.234), channel_id=1, replica_groups=mesh['fsdp'=4,'ctx'=4,'tp'=2] {'fsdp','ctx'}, dimensions={0}, use_global_device_ids=true | all-gather | bytes 26112 | tf_op jit(solution)/shard_map/all_gather | solution.py:71
  241.6 8.6 gather_fusion.4
  251.3 9.4 gather_fusion.2
  260.8 3.9 all-to-all-start.2
  264.7 78.3 %all-gather.18.cloned.1.call-done = bf16[4,2,768,1024]{3,2,0,1:T(8,128)(2,1)} async-done(((bf16[4,2,192,1024]{3,2,0,1:T(8,128)(2,1)}), bf16[4,2,768,1024]{3,2,0,1:T(8,128)(2,1)}) %all-gather.18.cloned.1.call-update) | async-done | bytes 12582928 | tf_op jit(solution)/shard_map/all_gather | solution.py:76
  343.0 11.0 fusion.16
  353.9 7.7 fusion.18
  361.7 96.4 %all-gather.20.cloned.1.call-done = bf16[4,1024,768]{1,2,0:T(8,128)(2,1)} async-done(((bf16[4,1024,192]{1,2,0:T(8,128)(2,1)}), bf16[4,1024,768]{1,2,0:T(8,128)(2,1)}) %all-gather.20.cloned.1.call-update) | async-done | bytes 6291472 | tf_op jit(solution)/shard_map/all_gather | solution.py:77
  458.0 14.5 fusion.4
  472.5 9.7 fusion.15
  482.2 8.2 add_bitcast_fusion
  493.6 5.3 all-to-all-start.3
  499.7 7.2 fusion.26
  510.1 64.8 %all-to-all-done.3 = f32[4,4,128,768]{3,2,1,0:T(8,128)} async-done(((f32[4,4,128,768]{3,2,1,0:T(8,128)}), f32[4,4,128,768]{3,2,1,0:T(8,128)}, u32[]{:S(2)}, u32[]{:S(2)}) %all-to-all-start.3) | async-done | bytes 6291488 | tf_op jit(solution)/shard_map/all_to_all | solution.py:227
  574.9 5.2 all-to-all-start.1
  580.3 5.8 fusion.46
  586.0 6.0 fusion.43
  592.1 8.6 gather_fusion.3
  600.7 3.7 reshape.349
  604.4 5.3 reduce_sum.144
  609.7 6.0 bitcast_add_fusion
  617.3 33.6 %all-to-all-done.1 = f32[4,4,128,768]{3,2,1,0:T(8,128)} async-done(((f32[4,4,128,768]{3,2,1,0:T(8,128)}), f32[4,4,128,768]{3,2,1,0:T(8,128)}, u32[]{:S(2)}, u32[]{:S(2)}) %all-to-all-start.1) | async-done | bytes 6291488 | tf_op jit(solution)/shard_map/all_to_all | solution.py:166
  650.9 8.6 gather_fusion.1
  659.4 3.7 reshape.346
  663.2 9.3 multiply_reduce_fusion.1
  672.5 11.9 psum.38
  684.6 4.2 add_convert_fusion.1
  692.7 27.0 %all-reduce.19.cloned.1.call-done = bf16[512,768]{1,0:T(8,128)(2,1)} async-done(((bf16[512,768]{1,0:T(8,128)(2,1)}), bf16[512,768]{1,0:T(8,128)(2,1)}) %all-reduce.19.cloned.1.call-update) | async-done | bytes 786448 | tf_op jit(solution)/shard_map/psum | solution.py:171
  724.6 20.0 %multiply_reduce_fusion = (f32[6,512]{1,0:T(8,128)S(1)}, f32[6,512,2048]{2,1,0:T(8,128)}) fusion(f32[6,512,2048]{2,1,0:T(8,128)} %get-tuple-element.124, f32[6,512]{1,0:T(8,128)S(1)} %copy-done.43, pred[512,2048]{1,0:T(8,128)(4,1)S(1)} %copy-done.2, bf16[512,6,64]{0,2,1:T(8,128)(2,1)S(1)} %bitcast.217, bf16[2048,6,64]{0,2,1:T(8,128)(2,1)} %bitcast.220), kind=kOutput, calls=%fused_computation.8 | convolution fusion | flops 836760576 | bytes 53370880 | tf_op jit(solution)/shard_map/qhc,khc->hqk/dot_general | solution.py:263
  744.5 17.2 multiply_convert_fusion
  761.8 4.4 convolution_multiply_fusion
  767.3 14.4 fusion.76
  788.6 9.4 fusion.41
  798.0 7.3 reduce-scatter.10.cloned.1.call-done
  807.5 39.0 %reduce-scatter.12.cloned.1.call-done = f32[512,384]{1,0:T(8,128)} async-done(((f32[2048,384]{1,0:T(8,128)}), f32[512,384]{1,0:T(8,128)}) %reduce-scatter.12.cloned.1.call-update) | async-done | bytes 786448 | tf_op jit(solution)/shard_map/reduce_scatter | solution.py:284
  847.6 3.8 convolution_bitcast_fusion.5
  851.5 6.1 convolution_bitcast_fusion.3
  857.6 10.5 copy.192
  871.3 6.2 copy.185
  877.8 6.4 convolution_bitcast_fusion.1
  884.2 8.4 convolution_bitcast_fusion.2
  892.6 14.4 pad_maximum_fusion
  914.2 11.2 convolution_bitcast_fusion
  927.5 31.1 %all-reduce.23.cloned.1.call-done = f32[512,768]{1,0:T(8,128)} async-done(((f32[512,768]{1,0:T(8,128)}), f32[512,768]{1,0:T(8,128)}) %all-reduce.23.cloned.1.call-update) | async-done | bytes 1572880 | tf_op jit(solution)/shard_map/psum | solution.py:297
  960.6 35.5 %all-reduce.8 = (f32[768]{0:T(1024)S(1)}, f32[768]{0:T(1024)S(1)}) all-reduce(f32[768]{0:T(1024)S(1)} %get-tuple-element.81, f32[768]{0:T(1024)S(1)} %get-tuple-element.77), channel_id=5, replica_groups=mesh['fsdp'=4,'ctx'=4,'tp'=2] {'fsdp','ctx'}, use_global_device_ids=true, to_apply=%region_26.27.clone | all-reduce | flops 1536 | bytes 12288
  1000.3 172.6 %all-reduce.25.cloned.1.call-done = (f32[3,768,384]{2,0,1:T(4,128)}, f32[2,768,1024]{2,0,1:T(2,128)}) async-done(((f32[3,768,384]{2,0,1:T(4,128)}, f32[2,768,1024]{2,0,1:T(2,128)}), (f32[3,768,384]{2,0,1:T(4,128)}, f32[2,768,1024]{2,0,1:T(2,128)})) %all-reduce.25.cloned.1.call-update) | async-done | bytes 9830416
  1176.5 413.3 %reduce-scatter.16.cloned.1.call-done = f32[4,2,192,1024]{3,2,0,1:T(8,128)} async-done(((f32[4,2,768,1024]{3,2,0,1:T(8,128)}), f32[4,2,192,1024]{3,2,0,1:T(8,128)}) %reduce-scatter.16.cloned.1.call-update) | async-done | bytes 6291472 | tf_op jit(solution)/shard_map/reduce_scatter | solution.py:318
  1589.8 6.6 copy.194
  1596.4 65.8 %reduce-scatter.20.cloned.1.call-done = f32[1024,48]{0,1:T(8,128)} async-done(((f32[1024,768]{0,1:T(8,128)}), f32[1024,48]{0,1:T(8,128)}) %reduce-scatter.20.cloned.1.call-update) | async-done | bytes 196624 | tf_op jit(solution)/shard_map/reduce_scatter | solution.py:312
  1662.2 61.1 %reduce-scatter.14.cloned.1.call-done = f32[384,48]{0,1:T(8,128)} async-done(((f32[384,768]{0,1:T(8,128)}), f32[384,48]{0,1:T(8,128)}) %reduce-scatter.14.cloned.1.call-update) | async-done | bytes 73744 | tf_op jit(solution)/shard_map/reduce_scatter | solution.py:310
  1723.3 213.7 %reduce-scatter.18.cloned.1.call-done = f32[4,1024,192]{1,2,0:T(8,128)} async-done(((f32[4,1024,768]{1,2,0:T(8,128)}), f32[4,1024,192]{1,2,0:T(8,128)}) %reduce-scatter.18.cloned.1.call-update) | async-done | bytes 3145744 | tf_op jit(solution)/shard_map/reduce_scatter | solution.py:319
  (263 shorter events, 78.2 us)
Async XLA Ops:
  8.0 46.3 %all-gather.10.cloned.1.call-start = ((), (), s32[]{:S(2)}) async-start(), calls=%async_computation.11 | async-start | bytes 1880064 | tf_op jit(solution)/shard_map/all_gather | solution.py:65
  8.7 75.0 %all-gather.12.cloned.1.call-start = ((), (), s32[]{:S(2)}) async-start(), calls=%async_computation.12 | async-start | bytes 1966080 | tf_op jit(solution)/shard_map/all_gather | solution.py:101
  47.6 6.7 copy-start.48
  49.0 5.3 copy-start.54
  57.7 38.3 %copy-start.25 = (bf16[512,6,32]{0,2,1:T(8,128)(2,1)}, bf16[512,6,32]{0,2,1:T(8,128)(2,1)S(1)}, u32[]{:S(2)}) copy-start(bf16[512,6,32]{0,2,1:T(8,128)(2,1)S(1)} %get-tuple-element.105) | copy-start | bytes 589828
  57.7 38.2 %copy-start.27 = (bf16[512,6,32]{0,2,1:T(8,128)(2,1)}, bf16[512,6,32]{0,2,1:T(8,128)(2,1)S(1)}, u32[]{:S(2)}) copy-start(bf16[512,6,32]{0,2,1:T(8,128)(2,1)S(1)} %get-tuple-element.106) | copy-start | bytes 589828
  58.9 49.1 %all-gather.22.cloned.1.call-start = ((), (), s32[]{:S(2)}) async-start(), calls=%async_computation.27 | async-start | bytes 1966080 | tf_op jit(solution)/shard_map/all_gather | solution.py:102
  80.3 39.4 %copy-start.22 = (bf16[384,768]{0,1:T(8,128)(2,1)}, bf16[384,768]{0,1:T(8,128)(2,1)S(1)}, u32[]{:S(2)}) copy-start(bf16[384,768]{0,1:T(8,128)(2,1)S(1)} %all_gather.44) | copy-start | bytes 1769476
  81.3 26.7 %copy-start.1 = (pred[512,2048]{1,0:T(8,128)(4,1)}, pred[512,2048]{1,0:T(8,128)(4,1)S(1)}, u32[]{:S(2)}) copy-start(pred[512,2048]{1,0:T(8,128)(4,1)S(1)} %fusion.21) | copy-start | bytes 3145732
  83.6 88.1 %all-reduce.17.cloned.1.call-start = ((), (), s32[]{:S(2)}) async-start(), calls=%async_computation.13 | async-start | bytes 3145728 | tf_op jit(solution)/shard_map/psum | solution.py:129
  108.0 11.7 copy-start.42
  122.2 220.7 %all-gather.18.cloned.1.call-start = ((), (), s32[]{:S(2)}) async-start(), calls=%async_computation.16 | async-start | bytes 15728640 | tf_op jit(solution)/shard_map/all_gather | solution.py:76
  126.6 45.2 %copy-start.12 = (bf16[512,768]{1,0:T(8,128)(2,1)S(1)}, bf16[512,768]{1,0:T(8,128)(2,1)}, u32[]{:S(2)}) copy-start(bf16[512,768]{1,0:T(8,128)(2,1)} %param.13) | copy-start | bytes 2359300
  126.6 331.4 %all-gather.20.cloned.1.call-start = ((), (), s32[]{:S(2)}) async-start(), calls=%async_computation.17 | async-start | bytes 7864320 | tf_op jit(solution)/shard_map/all_gather | solution.py:77
  127.8 47.0 %copy-start.45 = (f32[768]{0:T(1024)}, f32[768]{0:T(1024)S(1)}, u32[]{:S(2)}) copy-start(f32[768]{0:T(1024)S(1)} %convert_element_type.113) | copy-start | bytes 9220
  133.1 40.3 %copy-start.58 = (s32[1024,1]{0,1:T(1,128)}, s32[1024,1]{0,1:T(1,128)S(1)}, u32[]{:S(2)}) copy-start(s32[1024,1]{0,1:T(1,128)S(1)} %compare_select_fusion) | copy-start | bytes 12292
  174.8 65.9 %copy-start.8 = (bf16[512,768]{1,0:T(8,128)(2,1)}, bf16[512,768]{1,0:T(8,128)(2,1)S(1)}, u32[]{:S(2)}) copy-start(bf16[512,768]{1,0:T(8,128)(2,1)S(1)} %multiply_convert_fusion.5) | copy-start | bytes 2359300
  184.3 5.4 copy-start.14
  184.3 76.5 %all-to-all-start = ((bf16[4,4,128,768]{3,2,1,0:T(8,128)(2,1)}), bf16[4,4,128,768]{3,2,1,0:T(8,128)(2,1)}, u32[]{:S(2)}, u32[]{:S(2)}) async-start(bf16[4,4,128,768]{3,2,1,0:T(8,128)(2,1)} %bitcast.209), calls=%async_computation | async-start | bytes 6291456 | tf_op jit(solution)/shard_map/all_to_all | solution.py:154
  189.1 391.2 %all-gather.14.cloned.1.call-start = ((), (), s32[]{:S(2)}) async-start(), calls=%async_computation.14 | async-start | bytes 3342336 | tf_op jit(solution)/shard_map/all_gather | solution.py:67
  192.2 5.4 copy-start.61
  241.6 8.7 copy-start.56
  241.6 9.3 copy-start.11
  260.8 197.3 %all-to-all-start.2 = ((bf16[4,4,128,768]{3,2,1,0:T(8,128)(2,1)}), bf16[4,4,128,768]{3,2,1,0:T(8,128)(2,1)S(1)}, u32[]{:S(2)}, u32[]{:S(2)}) async-start(bf16[4,4,128,768]{3,2,1,0:T(8,128)(2,1)} %bitcast.211), calls=%async_computation.2 | async-start | bytes 6291456 | tf_op jit(solution)/shard_map/all_to_all | solution.py:201
  343.0 11.0 copy-start.62
  458.0 14.5 copy-start.7
  472.5 9.7 copy-start.19
  472.5 9.7 copy-start.21
  493.6 81.3 %all-to-all-start.3 = ((f32[4,4,128,768]{3,2,1,0:T(8,128)}), f32[4,4,128,768]{3,2,1,0:T(8,128)}, u32[]{:S(2)}, u32[]{:S(2)}) async-start(f32[4,4,128,768]{3,2,1,0:T(8,128)} %copy.179), calls=%async_computation.3 | async-start | bytes 12582912 | tf_op jit(solution)/shard_map/all_to_all | solution.py:227
  498.9 87.1 %all-gather.16.cloned.1.call-start = ((), (), s32[]{:S(2)}) async-start(), calls=%async_computation.15 | async-start | bytes 1671168 | tf_op jit(solution)/shard_map/all_gather | solution.py:68
  510.1 70.1 %copy-start.59 = (s32[1024,1]{0,1:T(1,128)S(1)}, s32[1024,1]{0,1:T(1,128)}, u32[]{:S(2)}) copy-start(s32[1024,1]{0,1:T(1,128)} %copy-done.58) | copy-start | bytes 12292
  510.1 70.2 %copy-start.9 = (bf16[512,768]{1,0:T(8,128)(2,1)S(1)}, bf16[512,768]{1,0:T(8,128)(2,1)}, u32[]{:S(2)}) copy-start(bf16[512,768]{1,0:T(8,128)(2,1)} %copy-done.8) | copy-start | bytes 2359300
  574.9 76.0 %all-to-all-start.1 = ((f32[4,4,128,768]{3,2,1,0:T(8,128)}), f32[4,4,128,768]{3,2,1,0:T(8,128)}, u32[]{:S(2)}, u32[]{:S(2)}) async-start(f32[4,4,128,768]{3,2,1,0:T(8,128)} %copy.176), calls=%async_computation.1 | async-start | bytes 12582912 | tf_op jit(solution)/shard_map/all_to_all | solution.py:166
  580.1 108.8 %all-reduce.21.cloned.1.call-start = ((), (), s32[]{:S(2)}) async-start(), calls=%async_computation.19 | async-start | bytes 3145728 | tf_op jit(solution)/shard_map/psum | solution.py:232
  580.2 5.8 copy-start.15
  609.7 6.3 copy-start.16
  615.7 104.0 %all-reduce.19.cloned.1.call-start = ((), (), s32[]{:S(2)}) async-start(), calls=%async_computation.18 | async-start | bytes 1572864 | tf_op jit(solution)/shard_map/psum | solution.py:171
  684.5 4.5 copy-start.4
  684.5 4.5 copy-start.41
  688.8 30.9 %copy-start.17 = (bf16[512,768]{1,0:T(8,128)(2,1)S(1)}, bf16[512,768]{1,0:T(8,128)(2,1)}, u32[]{:S(2)}) copy-start(bf16[512,768]{1,0:T(8,128)(2,1)} %param.25) | copy-start | bytes 2359300
  688.8 116.5 %reduce-scatter.10.cloned.1.call-start = ((), (), s32[]{:S(2)}) async-start(), calls=%async_computation.20 | async-start | bytes 3932160 | tf_op jit(solution)/shard_map/reduce_scatter | solution.py:283
  719.7 4.8 copy-start.2
  719.7 4.8 copy-start.43
  744.5 17.2 copy-start.26
  744.5 17.2 copy-start.28
  761.8 5.4 copy-start
  767.2 79.2 %reduce-scatter.12.cloned.1.call-start = ((), (), s32[]{:S(2)}) async-start(), calls=%async_computation.21 | async-start | bytes 3932160 | tf_op jit(solution)/shard_map/reduce_scatter | solution.py:284
  785.3 140.8 %reduce-scatter.22.cloned.1.call-start = ((), (), s32[]{:S(2)}) async-start(), calls=%async_computation.28 | async-start | bytes 417792
  788.1 17.2 copy-start.38
  788.2 17.2 copy-start.39
  788.2 170.5 %all-reduce.23.cloned.1.call-start = ((), (), s32[]{:S(2)}) async-start(), calls=%async_computation.22 | async-start | bytes 3145728 | tf_op jit(solution)/shard_map/psum | solution.py:297
  807.2 44.2 %copy-start.34 = (bf16[512,1,384]{2,0,1:T(8,128)(2,1)}, bf16[512,1,384]{2,0,1:T(8,128)(2,1)S(1)}, u32[]{:S(2)}) copy-start(bf16[512,1,384]{2,0,1:T(8,128)(2,1)S(1)} %copy.183) | copy-start | bytes 1179652
  807.4 44.0 %copy-start.36 = (bf16[512,1,384]{2,0,1:T(8,128)(2,1)}, bf16[512,1,384]{2,0,1:T(8,128)(2,1)S(1)}, u32[]{:S(2)}) copy-start(bf16[512,1,384]{2,0,1:T(8,128)(2,1)S(1)} %copy.182) | copy-start | bytes 1179652
  851.5 321.4 %all-reduce.25.cloned.1.call-start = ((), (), s32[]{:S(2)}) async-start(), calls=%async_computation.29 | async-start | bytes 22020096
  857.6 10.6 copy-start.13
  857.6 10.6 copy-start.35
  857.6 10.6 copy-start.37
  857.6 10.6 copy-start.49
  857.6 10.6 copy-start.55
  877.6 712.2 %reduce-scatter.16.cloned.1.call-start = ((), (), s32[]{:S(2)}) async-start(), calls=%async_computation.24 | async-start | bytes 31457280 | tf_op jit(solution)/shard_map/reduce_scatter | solution.py:318
  877.8 6.4 copy-start.20
  907.1 755.1 %reduce-scatter.20.cloned.1.call-start = ((), (), s32[]{:S(2)}) async-start(), calls=%async_computation.26 | async-start | bytes 3342336 | tf_op jit(solution)/shard_map/reduce_scatter | solution.py:312
  911.0 812.3 %reduce-scatter.14.cloned.1.call-start = ((), (), s32[]{:S(2)}) async-start(), calls=%async_computation.23 | async-start | bytes 1253376 | tf_op jit(solution)/shard_map/reduce_scatter | solution.py:310
  914.1 1022.8 %reduce-scatter.18.cloned.1.call-start = ((), (), s32[]{:S(2)}) async-start(), calls=%async_computation.25 | async-start | bytes 15728640 | tf_op jit(solution)/shard_map/reduce_scatter | solution.py:319
  (22 other events, 47.0 us)
Sparse Core Ops, SparseCore 0:
  11.2 43.1 all-gather.9
  59.0 21.9 all-gather.11
  83.7 18.7 all-gather.21
  122.3 49.3 all-reduce.16
  615.8 50.0 all-reduce.20
  688.9 30.7 all-reduce.18
  767.3 37.9 reduce-scatter.9
  808.4 37.9 reduce-scatter.11
  850.3 55.5 reduce-scatter.21
  908.1 50.5 all-reduce.22
  963.4 209.4 all-reduce.24
  1175.2 414.4 reduce-scatter.15
  1594.1 68.0 reduce-scatter.19
  1666.2 56.9 reduce-scatter.13
  1726.0 210.8 reduce-scatter.17
Sparse Core Ops, SparseCore 1:
  126.7 216.2 all-gather.17
  344.5 113.5 all-gather.19
  460.4 43.6 all-gather.13
  506.7 41.7 all-gather.15
where the time goes:
time: 1950 us; the launch traced here: 1940 us
  waiting for transfers between devices  1340 us (69%)
  matrix products  207 us (11%)
  blocking collectives  146 us (7%)
  local copies, waits for them, and re-layouts  125 us (6%)
  other arithmetic  82.3 us (4%)
  starting transfers between devices  21.6 us (1%)
    reduce_scatter x1, waiting for transfers between devices, per_device(): lax.psum_scatter(expert_gate_up_grad, 'fsdp', scatter_dimension=2, tiled=...  413 us
    reduce_scatter x1, waiting for transfers between devices, per_device(): lax.psum_scatter(expert_down_grad, 'fsdp', scatter_dimension=2, tiled=True)  214 us
    unnamed x21, waiting for transfers between devices  175 us
    all_gather x1, waiting for transfers between devices, expert_fetch(): lax.all_gather(expert_down, 'fsdp', axis=2, tiled=True)  96.4 us
    all_gather x1, waiting for transfers between devices, expert_fetch(): lax.all_gather(expert_gate_up, 'fsdp', axis=2, tiled=True)  78.3 us
    unnamed x2, blocking collectives  70.6 us
    reduce_scatter x1, waiting for transfers between devices, per_device(): lax.psum_scatter(shared_down_grad, ('fsdp', 'ctx'), scatter_dimension=1,...  65.8 us
    all_to_all x1, waiting for transfers between devices, per_device(): lax.all_to_all(back_rows, 'ctx', split_axis=0, concat_axis=0, tiled=True)  64.8 us
  transfers between devices with their start and end apart: 23, of which 15 were waited for; matrix products, arithmetic and copies ran while one was open for 18% of the time, Pallas kernels for 0%

commit v1 on v0

v1 whole, which is shorter than its diff:
```python
import functools

import jax
import jax.numpy as jnp
from jax import lax
from jax.experimental import pallas as pl
from jax.experimental.pallas import tpu as pltpu
from jax.sharding import PartitionSpec as P

D = 768
HALF = D // 2
HD = 64
E = 16
ROWS = 512
CAP = 128
NEG = -1e30
eps = 1e-06
bf16 = jnp.bfloat16
f32 = jnp.float32
VMEM_LIMIT = 56 * 1024 * 1024


def mm(a, b):
    return lax.dot_general(a, b, (((1,), (0,)), ((), ())), preferred_element_type=f32)


def mm_t(a, b):
    return lax.dot_general(a, b, (((1,), (1,)), ((), ())), preferred_element_type=f32)


def t_mm(a, b):
    return lax.dot_general(a, b, (((0,), (0,)), ((), ())), preferred_element_type=f32)


def sds(shape, dtype):
    return jax.ShapeDtypeStruct(shape, dtype)


SMEM = pl.BlockSpec(memory_space=pltpu.SMEM)
VM = pl.BlockSpec(memory_space=pltpu.VMEM)


def call(body, outs, scratch=(), flops=0, moved=0, name=None):
    def run(scalars, *args):
        return pl.pallas_call(
            body,
            out_shape=outs,
            in_specs=[SMEM] + [VM] * len(args),
            out_specs=jax.tree.map(lambda _: VM, outs),
            scratch_shapes=list(scratch),
            compiler_params=pltpu.CompilerParams(vmem_limit_bytes=VMEM_LIMIT),
            cost_estimate=pl.CostEstimate(flops=flops, bytes_accessed=moved, transcendentals=0),
            name=name,
        )(scalars, *args)

    return run


def partner(v, lane):
    return jnp.where(lane % 64 < 32, pltpu.roll(v, 96, 1), pltpu.roll(v, 32, 1))


def lane_id(rows):
    return lax.broadcasted_iota(jnp.int32, (rows, 128), 1)


def qkv_body(sc, tok, gain, w, cos, sin, a_o, q_o, kv_o):
    x = tok[...].astype(f32)
    scale = lax.rsqrt(jnp.mean(x * x, axis=1, keepdims=True) + eps)
    a = (x * scale * gain[...]).astype(bf16)
    a_o[...] = a
    n = w.shape[1] // 3
    lane = lane_id(ROWS)
    for g in range(3 * n // 128):
        v = mm(a, w[:, g * 128 : (g + 1) * 128])
        lo = g * 128
        if lo < n:
            r = v * cos[...] + partner(v, lane) * sin[...]
            q_o[:, lo : lo + 128] = (r.astype(bf16).astype(f32) * (HD**-0.5)).astype(bf16)
        elif lo < 2 * n:
            r = v * cos[...] + partner(v, lane) * sin[...]
            kv_o[:, lo - n : lo - n + 128] = r.astype(bf16)
        else:
            kv_o[:, lo - n : lo - n + 128] = v.astype(bf16)


def block_bias(c, kb, segc, segq):
    off = pl.multiple_of(kb * ROWS, ROWS)
    kpos = off + lax.broadcasted_iota(jnp.int32, (ROWS, ROWS), 0)
    qpos = c * ROWS + lax.broadcasted_iota(jnp.int32, (ROWS, ROWS), 1)
    ok = (segc[pl.ds(off, ROWS), :] == segq[...]) & (kpos <= qpos)
    return jnp.where(ok, 0.0, NEG)


def attn_body(sc, q, k0, k1, k2, k3, segc, segq, wo, o_o, zown_o, zoth_o, lse_o, kvs, bias, st, ot):
    c, y = sc[0], sc[1]
    nb = c + 1
    n = q.shape[1]
    for r, ref in enumerate((k0, k1, k2, k3)):
        kvs[pl.ds(pl.multiple_of((c ^ r) * ROWS, ROWS), ROWS), :] = ref[...]

    def bias_step(kb, carry):
        bias[pl.ds(pl.multiple_of(kb * ROWS, ROWS), ROWS), :] = block_bias(c, kb, segc, segq)
        return carry

    lax.fori_loop(0, nb, bias_step, 0)
    for h in range(n // HD):
        lo = h * HD
        qh = q[:, lo : lo + HD]

        def score_step(kb, m, lo=lo, qh=qh):
            rows = pl.ds(pl.multiple_of(kb * ROWS, ROWS), ROWS)
            s = mm_t(kvs[rows, lo : lo + HD], qh) + bias[rows, :]
            st[rows, :] = s
            return jnp.maximum(m, jnp.max(s, axis=0, keepdims=True))

        m = lax.fori_loop(0, nb, score_step, jnp.full((1, ROWS), NEG, f32))

        def value_step(kb, carry, lo=lo, m=m):
            total, acc = carry
            rows = pl.ds(pl.multiple_of(kb * ROWS, ROWS), ROWS)
            p = jnp.exp(st[rows, :] - m)
            total = total + jnp.sum(p, axis=0, keepdims=True)
            return total, acc + t_mm(kvs[rows, n + lo : n + lo + HD], p.astype(bf16))

        total, acc = lax.fori_loop(
            0, nb, value_step, (jnp.zeros((1, ROWS), f32), jnp.zeros((HD, ROWS), f32))
        )
        ot[lo : lo + HD, :] = acc / total
        lse_o[h : h + 1, :] = m + jnp.log(total)
    o = ot[...].T.astype(bf16)
    o_o[...] = o
    own = pl.ds(pl.multiple_of(y * HALF, HALF), HALF)
    oth = pl.ds(pl.multiple_of((1 - y) * HALF, HALF), HALF)
    zoth_o[...] = mm_t(o, wo[oth, :]).astype(bf16)
    zown_o[...] = mm_t(o, wo[own, :])


def attn_back_body(
    sc, q, k0, k1, k2, k3, segc, segq, lse, o, zown, zoth, wo, cos, sin, dq_o, dkv_o,
    kvs, bias, do_s, delta, dqt,
):
    c, y = sc[0], sc[1]
    nb = c + 1
    n = q.shape[1]
    heads = n // HD
    for r, ref in enumerate((k0, k1, k2, k3)):
        kvs[pl.ds(pl.multiple_of((c ^ r) * ROWS, ROWS), ROWS), :] = ref[...]

    def bias_step(kb, carry):
        bias[pl.ds(pl.multiple_of(kb * ROWS, ROWS), ROWS), :] = block_bias(c, kb, segc, segq)
        return carry

    lax.fori_loop(0, nb, bias_step, 0)
    own = pl.ds(pl.multiple_of(y * HALF, HALF), HALF)
    oth = pl.ds(pl.multiple_of((1 - y) * HALF, HALF), HALF)
    do = (mm(zown[...], wo[own, :]) + mm(zoth[...], wo[oth, :])).astype(bf16)
    do_s[...] = do
    pick = (
        lax.broadcasted_iota(jnp.int32, (8, n), 1) // HD
        == lax.broadcasted_iota(jnp.int32, (8, n), 0)
    ).astype(f32)
    delta[...] = lax.dot_general(
        pick,
        do.astype(f32) * o[...].astype(f32),
        (((1,), (1,)), ((), ())),
        precision=lax.Precision.HIGHEST,
        preferred_element_type=f32,
    )

    def zero_step(kb, carry):
        dkv_o[kb ^ c] = jnp.zeros((ROWS, 2 * n), bf16)
        return carry

    lax.fori_loop(nb, 4, zero_step, 0)
    for pair in range(heads // 2):
        at = pair * 128

        def step(kb, carry, at=at, pair=pair):
            rows = pl.ds(pl.multiple_of(kb * ROWS, ROWS), ROWS)
            dks, dvs, dqs = [], [], []
            for i in range(2):
                lo = at + i * HD
                h = 2 * pair + i
                kh = kvs[rows, lo : lo + HD]
                vh = kvs[rows, n + lo : n + lo + HD]
                qh = q[:, lo : lo + HD]
                dh = do_s[:, lo : lo + HD]
                p = jnp.exp(mm_t(kh, qh) + bias[rows, :] - lse[h : h + 1, :])
                ds = (p * (mm_t(vh, dh) - delta[h : h + 1, :])).astype(bf16)
                dvs.append(mm(p.astype(bf16), dh))
                dks.append(mm(ds, qh))
                dqs.append(carry[i] + t_mm(kh, ds))
            at_k = kb ^ c
            dkv_o[at_k, :, at : at + 128] = jnp.concatenate(dks, axis=1).astype(bf16)
            dkv_o[at_k, :, n + at : n + at + 128] = jnp.concatenate(dvs, axis=1).astype(bf16)
            return tuple(dqs)

        zero = jnp.zeros((HD, ROWS), f32)
        dqs = lax.fori_loop(0, nb, step, (zero, zero))
        dqt[at : at + HD, :] = dqs[0]
        dqt[at + HD : at + 128, :] = dqs[1]
    lane = lane_id(ROWS)
    for g in range(n // 128):
        v = dqt[g * 128 : (g + 1) * 128, :].T * (HD**-0.5)
        dq_o[:, g * 128 : (g + 1) * 128] = (v * cos[...] - partner(v, lane) * sin[...]).astype(bf16)


def proj_back_body(sc, dq, keep, recv, w, cos, sin, dp_o, own_o, oth_o):
    y = sc[1]
    n = dq.shape[1]
    lane = lane_id(ROWS)
    dp_o[:, :n] = dq[...]
    for g in range(2 * n // 128):
        cols = slice(g * 128, (g + 1) * 128)
        v = keep[:, cols].astype(f32) + recv[:, cols].astype(f32)
        if g < n // 128:
            v = v * cos[...] - partner(v, lane) * sin[...]
        dp_o[:, n + g * 128 : n + (g + 1) * 128] = v.astype(bf16)
    own = pl.ds(pl.multiple_of(y * HALF, HALF), HALF)
    oth = pl.ds(pl.multiple_of((1 - y) * HALF, HALF), HALF)
    oth_o[...] = mm_t(dp_o[...], w[oth, :]).astype(bf16)
    own_o[...] = mm_t(dp_o[...], w[own, :])


def slots_onehot(ids, r):
    i = lax.broadcasted_iota(jnp.int32, (4 * CAP, ROWS), 0)
    hit = (i == ids[2 * r : 2 * r + 1, :]) | (i == ids[2 * r + 1 : 2 * r + 2, :])
    return jnp.where(hit, 1.0, 0.0).astype(bf16)


def pack_body(sc, ids, b0, b1, b2, b3, p0, p1, p2, p3):
    for r, ref in enumerate((b0, b1, b2, b3)):
        rows = mm(slots_onehot(ids, r), ref[...]).astype(bf16)
        for s, out in enumerate((p0, p1, p2, p3)):
            out[r * CAP : (r + 1) * CAP, :] = rows[s * CAP : (s + 1) * CAP, :]


def unpack_body(sc, ids, p0, p1, p2, p3, keep_o, send_o):
    for r in range(4):
        rows = jnp.concatenate(
            [p[r * CAP : (r + 1) * CAP, :] for p in (p0, p1, p2, p3)], axis=0
        )
        tok = t_mm(slots_onehot(ids, r), rows).astype(bf16)
        if r % 2 == 0:
            keep_o[r // 2] = tok
        else:
            send_o[r // 2] = tok


def halves(y, a, b):
    first = y == 0
    return jnp.concatenate([jnp.where(first, a, b), jnp.where(first, b, a)], axis=1)


def ffn_body(routed, sc, xa, xb, wa, wb, gu, dt, rt, *refs):
    if routed:
        refs = refs[len(refs) - 9 :]
        out_o, db_o, rg_o, dgu_o, y_o, x_o, de_o, acc_o, acc_b = refs
    else:
        out_o, db_o, dgu_o, y_o, acc_o, acc_b = refs
    y, e = sc[1], sc[2]
    x = halves(y, xa[...], xb[...])
    w = halves(y, wa[...], wb[...])
    hidden = dt.shape[1]
    if routed:
        lane = lane_id(ROWS)
        logits = jnp.where(lane < E, mm(x, rt[...]), NEG)
        ex = jnp.exp(logits - jnp.max(logits, axis=1, keepdims=True))
        probs = ex / jnp.sum(ex, axis=1, keepdims=True)
        gate = jnp.sum(jnp.where(lane == e, probs, 0.0), axis=1, keepdims=True)
        x_o[0] = x
        de_o[0] = (w.astype(f32) * gate).astype(bf16)
    acc_o[...] = jnp.zeros_like(acc_o)
    acc_b[...] = jnp.zeros_like(acc_b)
    tile = 256

    def step(j, dots):
        lo = pl.multiple_of(j * tile, tile)
        hi = pl.multiple_of(hidden + j * tile, tile)
        g = mm(x, gu[:, pl.ds(lo, tile)])
        u = mm(x, gu[:, pl.ds(hi, tile)])
        h = mm(w, dt[:, pl.ds(lo, tile)])
        sg = 1.0 / (1.0 + jnp.exp(-g))
        act = g * sg
        yv = (act * u).astype(bf16)
        if routed:
            dots = dots + jnp.sum(yv.astype(f32) * h, axis=1, keepdims=True)
            h = h * gate
        dg = (h * u * (sg + act * (1.0 - sg))).astype(bf16)
        du = (h * act).astype(bf16)
        y_o[0, :, pl.ds(lo, tile)] = yv
        dgu_o[0, :, pl.ds(lo, tile)] = dg
        dgu_o[0, :, pl.ds(hi, tile)] = du
        acc_o[...] += mm_t(yv, dt[:, pl.ds(lo, tile)])
        acc_b[...] += mm_t(dg, gu[:, pl.ds(lo, tile)]) + mm_t(du, gu[:, pl.ds(hi, tile)])
        return dots

    dots = lax.fori_loop(0, hidden // tile, step, jnp.zeros((ROWS, 1), f32))
    if routed:
        coef = (dots * gate) * (jnp.where(lane == e, 1.0, 0.0) - probs)
        coef = jnp.where(lane < E, coef, 0.0).astype(bf16)
        acc_b[...] += mm_t(coef, rt[...])
        rg_o[...] = t_mm(x, coef)
    for i, at in enumerate((y, 1 - y)):
        cols = pl.ds(pl.multiple_of(at * HALF, HALF), HALF)
        out = acc_o[:, cols]
        if routed:
            out = out * gate
        out_o[i] = out.astype(bf16)
        db_o[i] = acc_b[:, cols].astype(bf16)


def ffn(scalars, s, groups, xa, xb, wa, wb, gu, dt, rt, prev):
    routed = rt is not None
    hidden = dt.shape[1]
    full = lambda shape: pl.BlockSpec(shape, lambda i, n=len(shape): (0,) * n)
    part = lambda width: pl.BlockSpec((1, ROWS, width), lambda i: (s, 0, 0))
    two = (2, ROWS, HALF)
    outs = [sds(two, bf16), sds(two, bf16)]
    out_specs = [full(two), full(two)]
    if routed:
        outs.append(sds((D, 128), f32))
        out_specs.append(full((D, 128)))
    widths = [2 * hidden, hidden] + ([D, D] if routed else [])
    base = len(outs)
    for width in widths:
        outs.append(sds((groups, ROWS, width), bf16))
        out_specs.append(part(width))
    args = [xa, xb, wa, wb, gu, dt] + ([rt] if routed else [])
    in_specs = [SMEM] + [full(a.shape) for a in args]
    aliases = {}
    if not routed:
        args.append(dt[:16, :128])
        in_specs.append(full((16, 128)))
    if prev is not None:
        for i, arr in enumerate(prev):
            aliases[1 + len(args)] = base + i
            args.append(arr)
            in_specs.append(pl.BlockSpec(memory_space=pl.ANY))
    return pl.pallas_call(
        functools.partial(ffn_body, routed),
        grid=(1,),
        out_shape=outs,
        in_specs=in_specs,
        out_specs=out_specs,
        scratch_shapes=[pltpu.VMEM((ROWS, D), f32), pltpu.VMEM((ROWS, D), f32)],
        input_output_aliases=aliases,
        compiler_params=pltpu.CompilerParams(vmem_limit_bytes=VMEM_LIMIT),
        cost_estimate=pl.CostEstimate(
            flops=2 * ROWS * D * hidden * 6, bytes_accessed=16 << 20, transcendentals=0
        ),
        name="expert_ffn" if routed else "shared_ffn",
    )(scalars, *args)


def dense_assemble(scalars, offs, st, xs, co, widths):
    rows = st.shape[1]

    def body(sc, st, xs, co, *outs):
        for rc in range(4):
            for s in range(4):
                piece = (st, co.at[0], xs, co.at[1])[rc]
                at = pl.ds(pl.multiple_of(sc[rc * 4 + s], 16), rows)
                lo = 0
                for out, width in zip(outs, widths):
                    out[at, :] = piece[s, :, lo : lo + width]
                    lo += width

    outs = [sds((16 * rows, width), bf16) for width in widths]
    return call(body, outs, moved=4 * 16 * rows * sum(widths), name="dense_assemble")(offs, st, xs, co)


def dense_split(offs, full, rows):
    def body(sc, full, out):
        for k in range(16):
            at = pl.ds(pl.multiple_of(sc[k], 16), rows)
            out[k] = full[at, :]

    n = full.shape[1]
    return call(body, sds((16, rows, n), bf16), moved=64 * rows * n, name="dense_split")(offs, full)


def expert_assemble(offs, gus, dts):
    rows = dts[0].shape[0]
    hidden = dts[0].shape[1]

    def body(sc, g0, g1, g2, g3, d0, d1, d2, d3, gu_o, dt_o):
        for s, (g, d) in enumerate(((g0, d0), (g1, d1), (g2, d2), (g3, d3))):
            at = pl.ds(pl.multiple_of(sc[s], 16), rows)
            gu_o[at, :hidden] = g[0]
            gu_o[at, hidden:] = g[1]
            dt_o[at, :] = d[...]

    outs = [sds((4 * rows, 2 * hidden), bf16), sds((4 * rows, hidden), bf16)]
    return call(body, outs, moved=4 * 4 * rows * 3 * hidden, name="expert_assemble")(offs, *gus, *dts)


def grads_place(order, gus, dts):
    rows, hidden = dts[0].shape

    def body(sc, g0, g1, g2, g3, d0, d1, d2, d3, gu_o, dt_o):
        for s, (g, d) in enumerate(((g0, d0), (g1, d1), (g2, d2), (g3, d3))):
            gu_o[sc[s], 0] = g[:, :hidden].astype(f32)
            gu_o[sc[s], 1] = g[:, hidden:].astype(f32)
            dt_o[sc[s]] = d[...].astype(f32).T

    outs = [sds((4, 2, rows, hidden), f32), sds((4, hidden, rows), f32)]
    return call(body, outs, moved=6 * 4 * rows * 3 * hidden, name="grads_place")(order, *gus, *dts)


def per_device(
    tokens,
    segments,
    experts,
    attn_gain,
    qkv_proj,
    out_proj,
    ffn_gain,
    router_proj,
    expert_gate_up,
    expert_down,
    shared_gate_up,
    shared_down,
    cotangent,
):
    F, C = lax.axis_size("fsdp"), lax.axis_size("ctx")
    f, c, y = lax.axis_index("fsdp"), lax.axis_index("ctx"), lax.axis_index("tp")
    EL = expert_gate_up.shape[0]
    small = F == EL and C == 4
    heads_width = qkv_proj.shape[2]
    hidden = expert_down.shape[1]
    shared_hidden = shared_down.shape[0]
    zi = f % EL
    i32 = jnp.int32

    def yx(v):
        return lax.ppermute(v, "tp", [(0, 1), (1, 0)])

    def cx(v, flip):
        return lax.ppermute(v, "ctx", [(i, i ^ flip) for i in range(C)])

    def zs(v, s):
        return lax.ppermute(
            v, "fsdp", [(i, i // EL * EL + (i % EL + s) % EL) for i in range(F)]
        )

    scalars = jnp.stack([c, y, EL * c + zi]).astype(i32)
    rows_own = D // (F * C)
    rc = jnp.arange(4, dtype=i32)
    if small:
        dense_offs = (
            (((f - rc)[None, :] % 4) * 4 + (c ^ rc)[:, None]).reshape(16) * rows_own
        ).astype(i32)
        back_offs = (
            (((f + rc)[None, :] % 4) * 4 + (c ^ rc)[:, None]).reshape(16) * rows_own
        ).astype(i32)

    def dense_gather(shard, widths):
        if small:
            st = jnp.stack([shard] + [zs(shard, s) for s in (1, 2, 3)])
            xs = cx(st, 2)
            co = cx(jnp.stack([st, xs]), 1)
            return dense_assemble(scalars, dense_offs, st, xs, co, widths)
        full = lax.all_gather(shard, ("fsdp", "ctx"), axis=0, tiled=True)
        cuts, lo = [], 0
        for width in widths:
            cuts.append(full[:, lo : lo + width])
            lo += width
        return cuts

    def reduce_blocks(blocks):
        kind = blocks.dtype
        part = blocks[0::2].astype(f32) + cx(blocks[1::2], 1).astype(f32)
        part = part[0] + cx(part[1].astype(kind), 2).astype(f32)
        total = part[0]
        for s in (1, 2, 3):
            total = total + zs(part[s].astype(kind), s).astype(f32)
        return total

    def dense_reduce(full):
        n = full.shape[1]
        if small:
            blocks = dense_split(back_offs, full.astype(bf16), rows_own)
            return reduce_blocks(blocks.reshape(4, 4, rows_own, n))
        return lax.psum_scatter(
            full.astype(f32), ("fsdp", "ctx"), scatter_dimension=0, tiled=True
        )

    def half(v, which):
        return lax.dynamic_slice_in_dim(v, which * HALF, HALF, v.ndim - 1)

    qkv_shard = jnp.concatenate(
        [
            qkv_proj.transpose(1, 0, 2).reshape(rows_own, 3 * heads_width),
            router_proj,
            attn_gain[:, None],
            ffn_gain[:, None],
            jnp.zeros((rows_own, 128 - E - 2), bf16),
        ],
        axis=1,
    )
    qkv_w, extra = dense_gather(qkv_shard, (3 * heads_width, 128))
    rest_shard = jnp.concatenate(
        [
            out_proj.T,
            shared_gate_up.transpose(1, 0, 2).reshape(rows_own, 2 * shared_hidden),
            shared_down.T,
        ],
        axis=1,
    )
    out_w, shared_gu, shared_dt = dense_gather(
        rest_shard, (heads_width, 2 * shared_hidden, shared_hidden)
    )
    gains = extra[:, E : E + 2].astype(f32)
    gain_one, gain_two = gains[:, 0], gains[:, 1]
    gain_two_h = half(gain_two, y)
    gain_one_h = half(gain_one, y)

    if small:
        gus, dts = [], []
        for s in range(4):
            j = (zi + s) % EL
            gu = lax.dynamic_index_in_dim(expert_gate_up, j, 0, keepdims=False)
            dt = lax.dynamic_index_in_dim(expert_down, j, 0, keepdims=False).T
            gus.append(gu if s == 0 else zs(gu, s))
            dts.append(dt if s == 0 else zs(dt, s))
        expert_offs = (((zi - rc) % 4) * (D // 4)).astype(i32)
        expert_gu, expert_dt = expert_assemble(expert_offs, gus, dts)
    else:
        inner = [[g * EL + i for i in range(EL)] for g in range(F // EL)]
        outer = [[g * EL + i for g in range(F // EL)] for i in range(EL)]
        mine = lax.all_to_all(
            jnp.concatenate(
                [expert_gate_up[:, 0], expert_gate_up[:, 1], expert_down.transpose(0, 2, 1)], axis=2
            ),
            "fsdp", 0, 0, axis_index_groups=inner, tiled=True,
        )
        mine = lax.all_gather(mine, "fsdp", axis=0, axis_index_groups=outer, tiled=True)
        mine = mine.reshape(D, 3 * hidden)
        expert_gu, expert_dt = mine[:, : 2 * hidden], mine[:, 2 * hidden :]

    lanes = jnp.arange(E, dtype=i32)[None, :]
    named = [(experts[:, k : k + 1] == lanes) for k in range(2)]
    both = (named[0] | named[1]).astype(bf16)
    before = (jnp.arange(ROWS)[:, None] > jnp.arange(ROWS)[None, :]).astype(bf16)
    counts = jnp.dot(before, both, preferred_element_type=f32)
    code = jnp.stack(
        [
            experts[:, k] * CAP + jnp.sum(jnp.where(named[k], counts, 0.0), axis=1).astype(i32)
            for k in range(2)
        ]
    )
    code_two = jnp.stack([code, cx(code, 2)])
    code_core = cx(code_two, 1)
    codes = jnp.concatenate([code_two[0], code_core[0], code_two[1], code_core[1]], axis=0)
    which, rank = codes // CAP, codes % CAP
    ids = jnp.where(which // EL == c, ((which - zi) % EL) * CAP + rank, -1).astype(i32)

    def dispatch(own):
        far = cx(own, 2)
        near = cx(own, 1)
        both_far = cx(far, 1)
        packs = call(
            pack_body, [sds((4 * CAP, HALF), bf16)] * 4, flops=8 * ROWS * ROWS * HALF,
            moved=6 << 20, name="pack",
        )(scalars, ids, own, near, far, both_far)
        mine = [packs[0]] + [zs(packs[s], s) for s in (1, 2, 3)]
        return [(m, yx(m)) for m in mine]

    def give_back(parts):
        rows = []
        for s, two in enumerate(parts):
            total = (two[0].astype(f32) + yx(two[1]).astype(f32)).astype(bf16)
            rows.append(total if s == 0 else zs(total, EL - s))
        rows = [rows[0], rows[1], rows[2], rows[3]]
        keep, send = call(
            unpack_body, [sds((2, ROWS, HALF), bf16)] * 2, flops=8 * ROWS * ROWS * HALF,
            moved=6 << 20, name="unpack",
        )(scalars, ids, *rows)
        got = cx(send, 1)
        far = (keep[1].astype(f32) + got[1].astype(f32)).astype(bf16)
        return keep[0].astype(f32) + got[0].astype(f32) + cx(far, 2).astype(f32)

    cot_h, cot_o = half(cotangent, y), half(cotangent, 1 - y)
    cot_chunks = dispatch(cot_h)

    positions = (c * ROWS + jnp.arange(ROWS, dtype=i32)).astype(f32)
    table = jnp.arange(128, dtype=i32)
    frequency = 10000.0 ** (-(table % 32).astype(f32) / 32)
    angles = positions[:, None] * frequency[None, :]
    cos = jnp.cos(angles)
    sin = jnp.sin(angles) * jnp.where(table % 64 < 32, -1.0, 1.0)[None, :]
    normed_one, queries, kv = call(
        qkv_body,
        [sds((ROWS, D), bf16), sds((ROWS, heads_width), bf16), sds((ROWS, 2 * heads_width), bf16)],
        flops=2 * ROWS * D * 3 * heads_width, moved=6 << 20, name="qkv",
    )(scalars, tokens, gain_one[None, :], qkv_w, cos, sin)
    kv_far = cx(kv, 2)
    kv_near = cx(kv, 1)
    kv_both = cx(kv_far, 1)
    kvs = (kv, kv_near, kv_far, kv_both)
    seq_ids = segments[0]
    seg_col = seq_ids[:, None]
    seg_row = lax.dynamic_slice_in_dim(seq_ids, c * ROWS, ROWS, 0)[None, :]
    attended, z_own, z_oth, lse = call(
        attn_body,
        [
            sds((ROWS, heads_width), bf16),
            sds((ROWS, HALF), f32),
            sds((ROWS, HALF), bf16),
            sds((8, ROWS), f32),
        ],
        scratch=[
            pltpu.VMEM((4 * ROWS, 2 * heads_width), bf16),
            pltpu.VMEM((4 * ROWS, ROWS), f32),
            pltpu.VMEM((4 * ROWS, ROWS), f32),
            pltpu.VMEM((heads_width, ROWS), f32),
        ],
        flops=16 * ROWS * ROWS * heads_width * 4, moved=8 << 20, name="attn",
    )(scalars, queries, *kvs, seg_col, seg_row, out_w)
    tok_h = half(tokens, y).astype(f32)
    middle = tok_h + z_own + yx(z_oth).astype(f32)

    def both_halves(sums):
        return sums + yx(sums)

    square = both_halves(jnp.sum(middle * middle, axis=1))
    scale_two = lax.rsqrt(square / D + eps)[:, None]
    normal_two = middle * scale_two
    normed_two = (normal_two * gain_two_h[None, :]).astype(bf16)

    chunks = dispatch(normed_two)
    normed_two_oth = yx(normed_two)
    sh_out, sh_db, sh_dgu, sh_y = ffn(
        scalars, 0, 1, normed_two, normed_two_oth, cot_h, cot_o, shared_gu, shared_dt, None, None
    )
    saved, outs, backs, router_part = None, [], [], 0.0
    for s in range(4):
        res = ffn(
            scalars, s, 4, *chunks[s], *cot_chunks[s], expert_gu, expert_dt, extra, saved
        )
        outs.append(res[0])
        backs.append(res[1])
        router_part = router_part + res[2][:, :E]
        saved = res[3:]
    ex_dgu, ex_y, ex_x, ex_de = [v.reshape(4 * ROWS, -1) for v in saved]
    sh_db_recv = yx(sh_db[1])
    sh_out_recv = yx(sh_out[1])
    back_h = give_back(backs) + sh_db[0].astype(f32) + sh_db_recv.astype(f32)

    scaled = back_h * gain_two_h[None, :]
    mean_two = both_halves(jnp.sum(scaled * normal_two, axis=1))[:, None] / D
    ffn_gain_part = jnp.sum(back_h * normal_two, axis=0)
    middle_grad = cot_h.astype(f32) + scale_two * (scaled - normal_two * mean_two)
    dz_own = middle_grad.astype(bf16)
    dz_oth = yx(dz_own)
    dq, dkv = call(
        attn_back_body,
        [sds((ROWS, heads_width), bf16), sds((4, ROWS, 2 * heads_width), bf16)],
        scratch=[
            pltpu.VMEM((4 * ROWS, 2 * heads_width), bf16),
            pltpu.VMEM((4 * ROWS, ROWS), f32),
            pltpu.VMEM((ROWS, heads_width), bf16),
            pltpu.VMEM((8, ROWS), f32),
            pltpu.VMEM((heads_width, ROWS), f32),
        ],
        flops=40 * ROWS * ROWS * heads_width * 4, moved=10 << 20, name="attn_back",
    )(
        scalars, queries, *kvs, seg_col, seg_row, lse, attended, dz_own, dz_oth, out_w, cos, sin
    )
    kv_part = dkv[0::2].astype(f32) + cx(dkv[1::2], 1).astype(f32)
    kv_recv = cx(kv_part[1].astype(bf16), 2)
    dp, da_own, da_oth = call(
        proj_back_body,
        [sds((ROWS, 3 * heads_width), bf16), sds((ROWS, HALF), f32), sds((ROWS, HALF), bf16)],
        flops=2 * ROWS * D * 3 * heads_width, moved=8 << 20, name="proj_back",
    )(scalars, dq, kv_part[0], kv_recv, qkv_w, cos, sin)
    da_h = da_own + yx(da_oth).astype(f32)
    tok_full = tokens.astype(f32)
    scale_one = lax.rsqrt(jnp.mean(tok_full * tok_full, axis=1, keepdims=True) + eps)
    normal_one = tok_h * scale_one
    scaled_one = da_h * gain_one_h[None, :]
    mean_one = both_halves(jnp.sum(scaled_one * normal_one, axis=1))[:, None] / D
    attn_gain_part = jnp.sum(da_h * normal_one, axis=0)
    tokens_grad_h = middle_grad + scale_one * (scaled_one - normal_one * mean_one)

    def whole_rows(own):
        return halves(y, own, yx(own))

    tokens_grad = whole_rows(tokens_grad_h.astype(bf16)).astype(f32)

    grad_gu = lax.dot_general(
        ex_x, ex_dgu, (((0,), (0,)), ((), ())), preferred_element_type=f32
    )
    grad_dt = lax.dot_general(ex_de, ex_y, (((0,), (0,)), ((), ())), preferred_element_type=f32)
    if small:
        grad_gu, grad_dt = grad_gu.astype(bf16), grad_dt.astype(bf16)
        ggs, gds = [], []
        for s in range(4):
            at = ((zi + s) % 4) * (D // 4)
            gg = lax.dynamic_slice_in_dim(grad_gu, at, D // 4, 0)
            gd = lax.dynamic_slice_in_dim(grad_dt, at, D // 4, 0)
            ggs.append(gg if s == 0 else zs(gg, s))
            gds.append(gd if s == 0 else zs(gd, s))
        expert_gate_up_grad, expert_down_grad = grads_place(
            ((zi - rc) % 4).astype(i32), ggs, gds
        )
    else:
        both_grads = jnp.concatenate([grad_gu, grad_dt], axis=1)
        both_grads = both_grads.reshape(F // EL * EL, D // F, 3 * hidden)
        both_grads = lax.psum_scatter(
            both_grads, "fsdp", scatter_dimension=0, axis_index_groups=outer, tiled=True
        )
        both_grads = lax.all_to_all(
            both_grads, "fsdp", 0, 0, axis_index_groups=inner, tiled=True
        )
        expert_gate_up_grad = jnp.stack(
            [both_grads[:, :, :hidden], both_grads[:, :, hidden : 2 * hidden]], axis=1
        )
        expert_down_grad = both_grads[:, :, 2 * hidden :].transpose(0, 2, 1)

    layer_h = middle + give_back(outs) + sh_out[0].astype(f32) + sh_out_recv.astype(f32)
    layer_out = whole_rows(layer_h.astype(bf16))

    dz_full = halves(y, dz_own, dz_oth)
    normed_full = halves(y, normed_two, normed_two_oth)

    def grad_of(a, b):
        return lax.dot_general(a, b, (((0,), (0,)), ((), ())), preferred_element_type=f32).astype(
            bf16
        )

    rest_grad = jnp.concatenate(
        [grad_of(dz_full, attended), grad_of(normed_full, sh_dgu[0]), grad_of(cotangent, sh_y[0])],
        axis=1,
    )
    rest_grad = dense_reduce(rest_grad)
    qkv_grad = dense_reduce(grad_of(normed_one, dp))
    qkv_grad = qkv_grad.reshape(rows_own, 3, heads_width).transpose(1, 0, 2)
    out_grad = rest_grad[:, :heads_width].T
    shared_gate_up_grad = jnp.stack(
        [
            rest_grad[:, heads_width : heads_width + shared_hidden],
            rest_grad[:, heads_width + shared_hidden : heads_width + 2 * shared_hidden],
        ]
    )
    shared_down_grad = rest_grad[:, heads_width + 2 * shared_hidden :].T

    def placed(part):
        first = y == 0
        return jnp.concatenate([jnp.where(first, part, 0.0), jnp.where(first, 0.0, part)])

    tail = jnp.concatenate(
        [router_part, placed(attn_gain_part)[:, None], placed(ffn_gain_part)[:, None]], axis=1
    )
    if small:
        order = back_offs // rows_own
        blocks = tail.reshape(16, rows_own * (E + 2))[order]
        tail = reduce_blocks(blocks.reshape(4, 4, rows_own * (E + 2)))
        tail = tail.reshape(rows_own, E + 2)
    else:
        tail = lax.psum_scatter(tail, ("fsdp", "ctx"), scatter_dimension=0, tiled=True)
    tail = tail + yx(tail)
    return (
        layer_out,
        tokens_grad,
        tail[:, E],
        qkv_grad,
        out_grad,
        tail[:, E + 1],
        tail[:, :E],
        expert_gate_up_grad,
        expert_down_grad,
        shared_gate_up_grad,
        shared_down_grad,
    )


def solution(mesh):
    return jax.shard_map(
        per_device,
        mesh=mesh,
        in_specs=(
            P(("fsdp", "ctx"), None),
            P("fsdp", None),
            P(("fsdp", "ctx"), None),
            P(("fsdp", "ctx")),
            P(None, ("fsdp", "ctx"), "tp"),
            P("tp", ("fsdp", "ctx")),
            P(("fsdp", "ctx")),
            P(("fsdp", "ctx"), None),
            P("ctx", None, "fsdp", "tp"),
            P("ctx", "tp", "fsdp"),
            P(None, ("fsdp", "ctx"), "tp"),
            P("tp", ("fsdp", "ctx")),
            P(("fsdp", "ctx"), None),
        ),
        out_specs=(
            P(("fsdp", "ctx"), None),
            P(("fsdp", "ctx"), None),
            P(("fsdp", "ctx")),
            P(None, ("fsdp", "ctx"), "tp"),
            P("tp", ("fsdp", "ctx")),
            P(("fsdp", "ctx")),
            P(("fsdp", "ctx"), None),
            P("ctx", None, "fsdp", "tp"),
            P("ctx", "tp", "fsdp"),
            P(None, ("fsdp", "ctx"), "tp"),
            P("tp", ("fsdp", "ctx")),
        ),
        check_vma=False,
    )
```

time: 1950 us -> 757 us (0.39)
  waiting for transfers between devices: 1340 us -> 291 us
  matrix products: 207 us -> 33.2 us
  starting transfers between devices: 21.6 us -> 169 us
  blocking collectives: 146 us -> 0 us
  Pallas kernels: 0 us -> 135 us
  local copies, waits for them, and re-layouts: 125 us -> 60.3 us
  other arithmetic: 82.3 us -> 57.1 us
    reduce_scatter x6 -> x0, waiting for transfers between devices: 800 us -> none  [the longest x1 413 us: per_device(): lax.psum_scatter(expert_gate_up_grad, 'fsdp', scatter_dimension=2, tiled=...]
    ppermute x0 -> x94, waiting for transfers between devices: none -> 291 us  [the longest x39 174 us: zs(): lax.ppermute(v, 'fsdp', [(i, i // EL * EL + (i % EL + s) % EL) for i in r...]
    all_gather x7 -> x0, waiting for transfers between devices: 179 us -> none  [the longest x1 96.4 us: expert_fetch(): lax.all_gather(expert_down, 'fsdp', axis=2, tiled=True)]
    unnamed x21 -> x0, waiting for transfers between devices: 175 us -> none
    dot_general x29 -> x7, matrix products: 205 us -> 33.2 us  [the longest x4 14 us: grad_of(): lax.dot_general(a, b, (((0,), (0,)), ((), ())), preferred_element_type=f32)]
    ppermute x0 -> x94, starting transfers between devices: none -> 169 us  [the longest x39 75.2 us: zs(): lax.ppermute(v, 'fsdp', [(i, i // EL * EL + (i % EL + s) % EL) for i in r...]
    pallas_call x0 -> x19, Pallas kernels: none -> 135 us  [the longest x14 73 us: run(): pl.pallas_call(body, out_shape=outs, in_specs=[SMEM] + [VM] * len(args),...]
    all_to_all x4 -> x0, waiting for transfers between devices: 98.4 us -> none  [the longest x1 64.8 us: per_device(): lax.all_to_all(back_rows, 'ctx', split_axis=0, concat_axis=0, tiled=True)]
  transfers between devices with their start and end apart: 23 -> 94, of which waited for: 15 -> 27; matrix products, arithmetic and copies ran while one was open for 18% -> 19% of each run, Pallas kernels for 0% -> 18%
where the time goes in v1:
time: 757 us; the launch traced here: 748 us
  waiting for transfers between devices  291 us (38%)
  starting transfers between devices  169 us (22%)
  Pallas kernels  135 us (18%)
  local copies, waits for them, and re-layouts  60.3 us (8%)
  other arithmetic  57.1 us (8%)
  matrix products  33.2 us (4%)
    ppermute x39, waiting for transfers between devices, zs(): lax.ppermute(v, 'fsdp', [(i, i // EL * EL + (i % EL + s) % EL) for i in r...  174 us
    ppermute x27, waiting for transfers between devices, cx(): return lax.ppermute(v, 'ctx', [(i, i ^ flip) for i in range(C)])  85.8 us
    ppermute x39, starting transfers between devices, zs(): lax.ppermute(v, 'fsdp', [(i, i // EL * EL + (i % EL + s) % EL) for i in r...  75.2 us
    pallas_call x14, Pallas kernels, run(): pl.pallas_call(body, out_shape=outs, in_specs=[SMEM] + [VM] * len(args),...  73 us
    ppermute x27, starting transfers between devices, cx(): return lax.ppermute(v, 'ctx', [(i, i ^ flip) for i in range(C)])  63.9 us
    pallas_call x5, Pallas kernels, ffn(): pl.pallas_call(functools.partial(ffn_body, routed), grid=(1,), out_shape=...  61.9 us
    ppermute x28, waiting for transfers between devices, yx(): return lax.ppermute(v, 'tp', [(0, 1), (1, 0)])  32.1 us
    ppermute x28, starting transfers between devices, yx(): return lax.ppermute(v, 'tp', [(0, 1), (1, 0)])  29.7 us
  transfers between devices with their start and end apart: 94, of which 27 were waited for; matrix products, arithmetic and copies ran while one was open for 19% of the time, Pallas kernels for 18%

profile of v1, /device:TPU:0, one launch (start us, length us, event | category | flops | bytes accessed | tf_op | source)
XLA Modules:
  0.0 747.6 jit_solution(3806201479395480582)
XLA Ops:
  2.5 5.1 collective-permute-start.10
  12.0 2.9 collective-permute-start.2
  17.9 11.5 %collective-permute-start = (bf16[48,1280]{1,0:T(8,128)(2,1)S(1)}, bf16[48,1280]{1,0:T(8,128)(2,1)}, u32[]{:S(2)}, u32[]{:S(2)}) collective-permute-start(bf16[48,1280]{1,0:T(8,128)(2,1)S(1)} %concatenate.34), channel_id=1, source_target_pairs={{0,8},{8,16},{16,24},{24,0},{1,9},{9,17},{17,25},{25,1},{2,10},{10... | collective-permute-start | bytes 368648 | tf_op jit(solution)/shard_map/ppermute | solution.py:444
  29.4 12.9 %collective-permute-done.9 = bf16[48,3456]{1,0:T(8,128)(2,1)S(1)} collective-permute-done((bf16[48,3456]{1,0:T(8,128)(2,1)S(1)}, bf16[48,3456]{1,0:T(8,128)(2,1)S(1)}, u32[]{:S(2)}, u32[]{:S(2)}) %collective-permute-start.9) | collective-permute-done | bytes 331808 | tf_op jit(solution)/shard_map/ppermute | solution.py:444
  55.5 38.7 %collective-permute-done.3.xs = bf16[4,48,1280]{2,1,0:T(8,128)(2,1)} collective-permute-done((bf16[4,48,1280]{2,1,0:T(8,128)(2,1)S(1)}, bf16[4,48,1280]{2,1,0:T(8,128)(2,1)}, u32[]{:S(2)}, u32[]{:S(2)}) %collective-permute-start.3) | collective-permute-done | bytes 491552 | tf_op jit(solution)/shard_map/ppermute | solution.py:441
  101.5 2.9 dense_assemble.2
  107.1 4.9 qkv.1
  114.7 17.1 %collective-permute-done.6.k2 = bf16[512,768]{1,0:T(8,128)(2,1)} collective-permute-done((bf16[512,768]{1,0:T(8,128)(2,1)}, bf16[512,768]{1,0:T(8,128)(2,1)}, u32[]{:S(2)}, u32[]{:S(2)}) %collective-permute-start.6) | collective-permute-done | bytes 786464 | tf_op jit(solution)/shard_map/ppermute | solution.py:441
  136.2 5.3 dense_assemble.3
  142.7 9.1 %attn.1 = (bf16[512,384]{1,0:T(8,128)(2,1)}, f32[512,384]{1,0:T(8,128)}, bf16[512,384]{1,0:T(8,128)(2,1)}, f32[8,512]{1,0:T(8,128)}) custom-call(s32[3]{0:T(128)} %pad_add_fusion.2.sc, bf16[512,384]{1,0:T(8,128)(2,1)} %get-tuple-element.78.q, bf16[512,768]{1,0:T(8,128)(2,1)} %get-tuple-element.79.k0, bf16[512,768]{1,0:T(8,128)(2,1)} %copy-done.73, ...), custom_call_target="tpu_custom_call" | custom-call | flops 6442450944 | bytes 8388608 | tf_op jit(solution)/shard_map/attn/pallas_call | solution.py:45
  155.4 5.0 collective-permute-done.13
  160.4 3.7 collective-permute-start.15
  167.7 3.8 collective-permute-start.26
  171.5 36.8 %collective-permute-done.29.d2 = bf16[192,1024]{1,0:T(8,128)(2,1)} collective-permute-done((bf16[192,1024]{1,0:T(8,128)(2,1)}, bf16[192,1024]{1,0:T(8,128)(2,1)}, u32[]{:S(2)}, u32[]{:S(2)}) %collective-permute-start.29) | collective-permute-done | bytes 393248 | tf_op jit(solution)/shard_map/ppermute | solution.py:444
  211.0 23.2 %collective-permute-done.30.d3 = bf16[192,1024]{1,0:T(8,128)(2,1)S(1)} collective-permute-done((bf16[192,1024]{1,0:T(8,128)(2,1)}, bf16[192,1024]{1,0:T(8,128)(2,1)S(1)}, u32[]{:S(2)}, u32[]{:S(2)}) %collective-permute-start.30) | collective-permute-done | bytes 393248 | tf_op jit(solution)/shard_map/ppermute | solution.py:444
  234.8 8.8 %collective-permute-start.18 = (bf16[512,384]{1,0:T(8,128)(2,1)}, bf16[512,384]{1,0:T(8,128)(2,1)}, u32[]{:S(2)}, u32[]{:S(2)}) collective-permute-start(bf16[512,384]{1,0:T(8,128)(2,1)} %multiply_convert_fusion.b0.xa), channel_id=1, source_target_pairs={{0,4},{2,6},{4,0},{6,2},{1,5},{3,7},{5,1},{7,3},{8,12},{10,14},{12... | collective-permute-start | bytes 1179656 | tf_op jit(solution)/shard_map/ppermute | solution.py:441
  244.3 3.7 pack.3
  249.6 16.7 %collective-permute-start.34 = (bf16[512,384]{1,0:T(8,128)(2,1)}, bf16[512,384]{1,0:T(8,128)(2,1)S(1)}, u32[]{:S(2)}, u32[]{:S(2)}) collective-permute-start(bf16[512,384]{1,0:T(8,128)(2,1)} %get-tuple-element.89), channel_id=1, source_target_pairs={{0,8},{8,16},{16,24},{24,0},{1,9},{9,17},{17,25},{25,1},{2,10},{10... | collective-permute-start | bytes 1179656 | tf_op jit(solution)/shard_map/ppermute | solution.py:444
  266.4 4.7 expert_assemble.1
  274.3 11.8 %shared_ffn.1 = (bf16[2,512,384]{2,1,0:T(8,128)(2,1)}, bf16[2,512,384]{2,1,0:T(8,128)(2,1)}, bf16[1,512,2048]{2,1,0:T(8,128)(2,1)}, bf16[1,512,1024]{2,1,0:T(8,128)(2,1)}) custom-call(s32[3]{0:T(128)} %pad_add_fusion.2.sc, bf16[512,384]{1,0:T(8,128)(2,1)} %multiply_convert_fusion.b0.xa, bf16[512,384]{1,0:T(8,128)(2,1)} %collective-permute-done.52.xb, ...), custom_call_target="tpu_custom_call" | custom-call | flops 4831838208 | bytes 16777216 | tf_op jit(solution)/shard_map/shared_ffn/pallas_call | solution.py:341
  287.1 3.4 fusion.2
  290.6 2.5 collective-permute-start.46
  293.8 3.7 pack.2
  298.9 5.2 convolution_convert_fusion
  310.9 2.6 collective-permute-done.32.xa
  314.0 12.5 %expert_ffn.4 = (bf16[2,512,384]{2,1,0:T(8,128)(2,1)}, bf16[2,512,384]{2,1,0:T(8,128)(2,1)}, f32[768,128]{1,0:T(8,128)}, bf16[4,512,2048]{2,1,0:T(8,128)(2,1)}, ...) custom-call(s32[3]{0:T(128)} %pad_add_fusion.2.sc, ...), custom_call_target="tpu_custom_call" | custom-call | flops 4831838208 | bytes 16777216 | tf_op jit(solution)/shard_map/expert_ffn/pallas_call | solution.py:341
  332.4 11.1 %collective-permute-done.33.xb = bf16[512,384]{1,0:T(8,128)(2,1)S(1)} collective-permute-done((bf16[512,384]{1,0:T(8,128)(2,1)S(1)}, bf16[512,384]{1,0:T(8,128)(2,1)S(1)}, u32[]{:S(2)}, u32[]{:S(2)}) %collective-permute-start.33) | collective-permute-done | bytes 393248 | tf_op jit(solution)/shard_map/ppermute | solution.py:438
  344.2 12.5 %expert_ffn.5 = (bf16[2,512,384]{2,1,0:T(8,128)(2,1)}, bf16[2,512,384]{2,1,0:T(8,128)(2,1)}, f32[768,128]{1,0:T(8,128)}, bf16[4,512,2048]{2,1,0:T(8,128)(2,1)}, ...) custom-call(s32[3]{0:T(128)} %pad_add_fusion.2.sc, ...), custom_call_target="tpu_custom_call", output_to_operand_aliasing={{3}: (8, {}), {4}: (9, {}), {5}: (10, {}), {6}: (11, {})} | custom-call | flops 4831838208 | bytes 16777216 | tf_op jit(solution)/shard_map/expert_ffn/pallas_call | solution.py:341
  361.2 12.5 %expert_ffn.6 = (bf16[2,512,384]{2,1,0:T(8,128)(2,1)}, bf16[2,512,384]{2,1,0:T(8,128)(2,1)}, f32[768,128]{1,0:T(8,128)}, bf16[4,512,2048]{2,1,0:T(8,128)(2,1)}, ...) custom-call(s32[3]{0:T(128)} %pad_add_fusion.2.sc, ...), custom_call_target="tpu_custom_call", output_to_operand_aliasing={{3}: (8, {}), {4}: (9, {}), {5}: (10, {}), {6}: (11, {})} | custom-call | flops 4831838208 | bytes 16777216 | tf_op jit(solution)/shard_map/expert_ffn/pallas_call | solution.py:341
  375.7 2.6 collective-permute-done.45.xb
  379.1 12.5 %expert_ffn.7 = (bf16[2,512,384]{2,1,0:T(8,128)(2,1)}, bf16[2,512,384]{2,1,0:T(8,128)(2,1)}, f32[768,128]{1,0:T(8,128)}, bf16[4,512,2048]{2,1,0:T(8,128)(2,1)}, ...) custom-call(s32[3]{0:T(128)} %pad_add_fusion.2.sc, ...), custom_call_target="tpu_custom_call", output_to_operand_aliasing={{3}: (8, {}), {4}: (9, {}), {5}: (10, {}), {6}: (11, {})} | custom-call | flops 4831838208 | bytes 16777216 | tf_op jit(solution)/shard_map/expert_ffn/pallas_call | solution.py:341
  394.0 12.3 %bitcast_convert_fusion = bf16[768,2048]{1,0:T(8,128)(2,1)} fusion(bf16[4,512,768]{2,1,0:T(8,128)(2,1)} %get-tuple-element.135, bf16[4,512,2048]{2,1,0:T(8,128)(2,1)} %get-tuple-element.136), kind=kOutput, calls=%fused_computation.1 | convolution fusion | flops 6444023808 | bytes 14680064 | tf_op jit(solution)/shard_map/dot_general | solution.py:693
  414.3 4.5 collective-permute-done.57.p1
  420.2 17.7 %collective-permute-done.59.p2 = bf16[512,384]{1,0:T(8,128)(2,1)S(1)} collective-permute-done((bf16[512,384]{1,0:T(8,128)(2,1)S(1)}, bf16[512,384]{1,0:T(8,128)(2,1)S(1)}, u32[]{:S(2)}, u32[]{:S(2)}) %collective-permute-start.59) | collective-permute-done | bytes 393248 | tf_op jit(solution)/shard_map/ppermute | solution.py:444
  439.3 3.6 unpack.3
  442.9 6.6 bitcast_convert_fusion.1
  453.1 8.1 %collective-permute-done.63 = bf16[512,384]{1,0:T(8,128)(2,1)S(1)} collective-permute-done((bf16[512,384]{1,0:T(8,128)(2,1)S(1)}, bf16[512,384]{1,0:T(8,128)(2,1)S(1)}, u32[]{:S(2)}, u32[]{:S(2)}) %collective-permute-start.63) | collective-permute-done | bytes 393248 | tf_op jit(solution)/shard_map/ppermute | solution.py:441
  472.5 2.8 collective-permute-done.66.zoth
  476.1 11.2 %attn_back.1 = (bf16[512,384]{1,0:T(8,128)(2,1)}, bf16[4,512,768]{2,1,0:T(8,128)(2,1)}) custom-call(s32[3]{0:T(128)} %pad_add_fusion.2.sc, bf16[512,384]{1,0:T(8,128)(2,1)} %get-tuple-element.78.q, bf16[512,768]{1,0:T(8,128)(2,1)} %get-tuple-element.79.k0, bf16[512,768]{1,0:T(8,128)(2,1)} %copy-done.73, bf16[512,768]{1,0:T(8,128)(2,1)} %collective-permute-done.6.k2, ...), custom_call_target="tpu_custom_call" | custom-call | flops 16106127360 | bytes 10485760 | tf_op jit(solution)/shard_map/attn_back/pallas_call | solution.py:45
  497.0 37.4 %collective-permute-done.43.p2 = bf16[512,384]{1,0:T(8,128)(2,1)} collective-permute-done((bf16[512,384]{1,0:T(8,128)(2,1)}, bf16[512,384]{1,0:T(8,128)(2,1)}, u32[]{:S(2)}, u32[]{:S(2)}) %collective-permute-start.43) | collective-permute-done | bytes 393248 | tf_op jit(solution)/shard_map/ppermute | solution.py:444
  534.4 3.6 unpack.2
  540.8 4.0 pad_maximum_fusion.full
  544.8 5.2 dense_split.3
  550.0 3.6 slice.298
  553.6 3.0 collective-permute-start.89
  561.9 18.6 %collective-permute-start.68 = (bf16[512,768]{1,0:T(8,128)(2,1)}, bf16[512,768]{1,0:T(8,128)(2,1)}, u32[]{:S(2)}, u32[]{:S(2)}) collective-permute-start(bf16[512,768]{1,0:T(8,128)(2,1)} %fusion.17), channel_id=1, source_target_pairs={{0,4},{2,6},{4,0},{6,2},{1,5},{3,7},{5,1},{7,3},{8,12},{10,14},{12... | collective-permute-start | bytes 2359304 | tf_op jit(solution)/shard_map/ppermute | solution.py:441
  581.3 9.8 %collective-permute-done.89.g2 = bf16[192,2048]{1,0:T(8,128)(2,1)} collective-permute-done((bf16[192,2048]{1,0:T(8,128)(2,1)S(1)}, bf16[192,2048]{1,0:T(8,128)(2,1)}, u32[]{:S(2)}, u32[]{:S(2)}) %collective-permute-start.89) | collective-permute-done | bytes 786464 | tf_op jit(solution)/shard_map/ppermute | solution.py:444
  592.1 7.3 grads_place.1
  599.4 5.2 copy.109
  606.6 15.2 %collective-permute-start.51 = (bf16[512,384]{1,0:T(8,128)(2,1)}, bf16[512,384]{1,0:T(8,128)(2,1)}, u32[]{:S(2)}, u32[]{:S(2)}) collective-permute-start(bf16[512,384]{1,0:T(8,128)(2,1)} %fusion.40), channel_id=1, source_target_pairs={{0,4},{2,6},{4,0},{6,2},{1,5},{3,7},{5,1},{7,3},{8,12},{10,14},{12... | collective-permute-start | bytes 1179656 | tf_op jit(solution)/shard_map/ppermute | solution.py:441
  621.8 2.7 slice_bitcast_fusion.1.keep
  624.4 5.0 proj_back.1
  630.7 3.8 convolution_convert_fusion.1.full
  634.4 2.9 dense_split.2
  643.6 5.6 convert_add_fusion
  650.3 2.4 collective-permute-done.70
  654.0 4.4 collective-permute-start.76
  659.0 2.8 fusion.14
  669.7 5.0 collective-permute-done.77
  684.1 20.6 %collective-permute-done.79 = bf16[4,48,1152]{2,1,0:T(8,128)(2,1)S(1)} collective-permute-done((bf16[4,48,1152]{2,1,0:T(8,128)(2,1)S(1)}, bf16[4,48,1152]{2,1,0:T(8,128)(2,1)S(1)}, u32[]{:S(2)}, u32[]{:S(2)}) %collective-permute-start.79) | collective-permute-done | bytes 442400 | tf_op jit(solution)/shard_map/ppermute | solution.py:441
  704.8 3.0 collective-permute-start.82
  711.5 3.5 collective-permute-start.87
  717.5 6.1 collective-permute-done.87
  723.6 20.2 %collective-permute-done.86 = bf16[48,3456]{1,0:T(8,128)(2,1)} collective-permute-done((bf16[48,3456]{1,0:T(8,128)(2,1)}, bf16[48,3456]{1,0:T(8,128)(2,1)}, u32[]{:S(2)}, u32[]{:S(2)}) %collective-permute-start.86) | collective-permute-done | bytes 331808 | tf_op jit(solution)/shard_map/ppermute | solution.py:444
  (458 shorter events, 168.2 us)
Async XLA Ops:
  7.6 34.7 %collective-permute-start.9 = (bf16[48,3456]{1,0:T(8,128)(2,1)S(1)}, bf16[48,3456]{1,0:T(8,128)(2,1)S(1)}, u32[]{:S(2)}, u32[]{:S(2)}) collective-permute-start(bf16[48,3456]{1,0:T(8,128)(2,1)S(1)} %get-tuple-element.260), channel_id=1, source_target_pairs={{0,16},{8,24},{16,0},{24,8},{1,17},{9,25},{17,1},{25,9},{2,18},{10... | collective-permute-start | bytes 995336 | tf_op jit(solution)/shard_map/ppermute | solution.py:444
  7.6 34.7 %collective-permute-start.8 = (bf16[48,3456]{1,0:T(8,128)(2,1)S(1)}, bf16[48,3456]{1,0:T(8,128)(2,1)S(1)}, u32[]{:S(2)}, u32[]{:S(2)}) collective-permute-start(bf16[48,3456]{1,0:T(8,128)(2,1)S(1)} %get-tuple-element.260), channel_id=1, source_target_pairs={{0,8},{8,16},{16,24},{24,0},{1,9},{9,17},{17,25},{25,1},{2,10},{10... | collective-permute-start | bytes 995336 | tf_op jit(solution)/shard_map/ppermute | solution.py:444
  12.0 33.8 %collective-permute-start.2 = (bf16[48,1280]{1,0:T(8,128)(2,1)S(1)}, bf16[48,1280]{1,0:T(8,128)(2,1)}, u32[]{:S(2)}, u32[]{:S(2)}) collective-permute-start(bf16[48,1280]{1,0:T(8,128)(2,1)S(1)} %concatenate.34), channel_id=1, source_target_pairs={{0,24},{8,0},{16,8},{24,16},{1,25},{9,1},{17,9},{25,17},{2,26},{10... | collective-permute-start | bytes 368648 | tf_op jit(solution)/shard_map/ppermute | solution.py:444
  14.8 31.7 %collective-permute-start.1 = (bf16[48,1280]{1,0:T(8,128)(2,1)S(1)}, bf16[48,1280]{1,0:T(8,128)(2,1)}, u32[]{:S(2)}, u32[]{:S(2)}) collective-permute-start(bf16[48,1280]{1,0:T(8,128)(2,1)S(1)} %concatenate.34), channel_id=1, source_target_pairs={{0,16},{8,24},{16,0},{24,8},{1,17},{9,25},{17,1},{25,9},{2,18},{10... | collective-permute-start | bytes 368648 | tf_op jit(solution)/shard_map/ppermute | solution.py:444
  17.9 28.7 %collective-permute-start = (bf16[48,1280]{1,0:T(8,128)(2,1)S(1)}, bf16[48,1280]{1,0:T(8,128)(2,1)}, u32[]{:S(2)}, u32[]{:S(2)}) collective-permute-start(bf16[48,1280]{1,0:T(8,128)(2,1)S(1)} %concatenate.34), channel_id=1, source_target_pairs={{0,8},{8,16},{16,24},{24,0},{1,9},{9,17},{17,25},{25,1},{2,10},{10... | collective-permute-start | bytes 368648 | tf_op jit(solution)/shard_map/ppermute | solution.py:444
  42.3 124.9 %collective-permute-start.21 = (bf16[512,384]{1,0:T(8,128)(2,1)S(1)}, bf16[512,384]{1,0:T(8,128)(2,1)}, u32[]{:S(2)}, u32[]{:S(2)}) collective-permute-start(bf16[512,384]{1,0:T(8,128)(2,1)S(1)} %get-tuple-element.247.b0.wa), channel_id=1, source_target_pairs={{0,2},{2,0},{4,6},{6,4},{1,3},{3,1},{5,7},{7,5},{8,10},{10,8},{12,... | collective-permute-start | bytes 1179656 | tf_op jit(solution)/shard_map/ppermute | solution.py:441
  43.6 51.9 %collective-permute-start.11 = (bf16[4,48,3456]{2,1,0:T(8,128)(2,1)S(1)}, bf16[4,48,3456]{2,1,0:T(8,128)(2,1)S(1)}, u32[]{:S(2)}, u32[]{:S(2)}) collective-permute-start(bf16[4,48,3456]{2,1,0:T(8,128)(2,1)S(1)} %get-tuple-element.235.st), channel_id=1, source_target_pairs={{0,4},{2,6},{4,0},{6,2},{1,5},{3,7},{5,1},{7,3},{8,12},{10,14},{12... | collective-permute-start | bytes 3981320 | tf_op jit(solution)/shard_map/ppermute | solution.py:441
  45.8 121.9 %collective-permute-start.22 = (bf16[512,384]{1,0:T(8,128)(2,1)S(1)}, bf16[512,384]{1,0:T(8,128)(2,1)}, u32[]{:S(2)}, u32[]{:S(2)}) collective-permute-start(bf16[512,384]{1,0:T(8,128)(2,1)S(1)} %get-tuple-element.247.b0.wa), channel_id=1, source_target_pairs={{0,4},{2,6},{4,0},{6,2},{1,5},{3,7},{5,1},{7,3},{8,12},{10,14},{12... | collective-permute-start | bytes 1179656 | tf_op jit(solution)/shard_map/ppermute | solution.py:441
  48.5 45.7 %collective-permute-start.3 = (bf16[4,48,1280]{2,1,0:T(8,128)(2,1)S(1)}, bf16[4,48,1280]{2,1,0:T(8,128)(2,1)}, u32[]{:S(2)}, u32[]{:S(2)}) collective-permute-start(bf16[4,48,1280]{2,1,0:T(8,128)(2,1)S(1)} %get-tuple-element.252.st), channel_id=1, source_target_pairs={{0,4},{2,6},{4,0},{6,2},{1,5},{3,7},{5,1},{7,3},{8,12},{10,14},{12... | collective-permute-start | bytes 1474568 | tf_op jit(solution)/shard_map/ppermute | solution.py:441
  97.5 37.1 %collective-permute-start.12 = (bf16[2,4,48,3456]{3,2,1,0:T(8,128)(2,1)}, bf16[2,4,48,3456]{3,2,1,0:T(8,128)(2,1)}, u32[]{:S(2)}, u32[]{:S(2)}) collective-permute-start(bf16[2,4,48,3456]{3,2,1,0:T(8,128)(2,1)} %pad_maximum_fusion.1), channel_id=1, source_target_pairs={{0,2},{2,0},{4,6},{6,4},{1,3},{3,1},{5,7},{7,5},{8,10},{10,8},{12,... | collective-permute-start | bytes 7962632 | tf_op jit(solution)/shard_map/ppermute | solution.py:441
  112.0 19.8 %collective-permute-start.6 = (bf16[512,768]{1,0:T(8,128)(2,1)}, bf16[512,768]{1,0:T(8,128)(2,1)}, u32[]{:S(2)}, u32[]{:S(2)}) collective-permute-start(bf16[512,768]{1,0:T(8,128)(2,1)} %get-tuple-element.79.k0), channel_id=1, source_target_pairs={{0,4},{2,6},{4,0},{6,2},{1,5},{3,7},{5,1},{7,3},{8,12},{10,14},{12... | collective-permute-start | bytes 2359304 | tf_op jit(solution)/shard_map/ppermute | solution.py:441
  114.6 26.9 %collective-permute-start.5 = (bf16[512,768]{1,0:T(8,128)(2,1)}, bf16[512,768]{1,0:T(8,128)(2,1)S(1)}, u32[]{:S(2)}, u32[]{:S(2)}) collective-permute-start(bf16[512,768]{1,0:T(8,128)(2,1)} %get-tuple-element.79.k0), channel_id=1, source_target_pairs={{0,2},{2,0},{4,6},{6,4},{1,3},{3,1},{5,7},{7,5},{8,10},{10,8},{12,... | collective-permute-start | bytes 2359304 | tf_op jit(solution)/shard_map/ppermute | solution.py:441
  134.7 19.1 %collective-permute-start.14 = (s32[2,512]{1,0:T(2,128)S(1)}, s32[2,512]{1,0:T(2,128)S(1)}, u32[]{:S(2)}, u32[]{:S(2)}) collective-permute-start(s32[2,512]{1,0:T(2,128)S(1)} %get-tuple-element.264), channel_id=1, source_target_pairs={{0,4},{2,6},{4,0},{6,2},{1,5},{3,7},{5,1},{7,3},{8,12},{10,14},{12... | collective-permute-start | bytes 12296 | tf_op jit(solution)/shard_map/ppermute | solution.py:441
  141.5 30.0 %collective-permute-start.28 = (bf16[192,1024]{1,0:T(8,128)(2,1)}, bf16[192,1024]{1,0:T(8,128)(2,1)}, u32[]{:S(2)}, u32[]{:S(2)}) collective-permute-start(bf16[192,1024]{1,0:T(8,128)(2,1)} %get-tuple-element.228), channel_id=1, source_target_pairs={{0,8},{8,16},{16,24},{24,0},{1,9},{9,17},{17,25},{25,1},{2,10},{10... | collective-permute-start | bytes 1179656 | tf_op jit(solution)/shard_map/ppermute | solution.py:444
  153.8 54.5 %collective-permute-start.29 = (bf16[192,1024]{1,0:T(8,128)(2,1)}, bf16[192,1024]{1,0:T(8,128)(2,1)}, u32[]{:S(2)}, u32[]{:S(2)}) collective-permute-start(bf16[192,1024]{1,0:T(8,128)(2,1)} %get-tuple-element.230), channel_id=1, source_target_pairs={{0,16},{8,24},{16,0},{24,8},{1,17},{9,25},{17,1},{25,9},{2,18},{10... | collective-permute-start | bytes 1179656 | tf_op jit(solution)/shard_map/ppermute | solution.py:444
  165.5 42.8 %collective-permute-start.16 = (f32[512]{0:T(512)S(1)}, f32[512]{0:T(512)S(1)}, u32[]{:S(2)}, u32[]{:S(2)}) collective-permute-start(f32[512]{0:T(512)S(1)} %get-tuple-element.213), channel_id=1, source_target_pairs={{0,1},{1,0},{2,3},{3,2},{4,5},{5,4},{6,7},{7,6},{8,9},{9,8},{10,11... | collective-permute-start | bytes 6152 | tf_op jit(solution)/shard_map/ppermute | solution.py:438
  167.3 80.8 %collective-permute-start.25 = (bf16[2,192,1024]{2,1,0:T(8,128)(2,1)}, bf16[2,192,1024]{2,1,0:T(8,128)(2,1)S(1)}, u32[]{:S(2)}, u32[]{:S(2)}) collective-permute-start(bf16[2,192,1024]{2,1,0:T(8,128)(2,1)} %get-tuple-element.220), channel_id=1, source_target_pairs={{0,8},{8,16},{16,24},{24,0},{1,9},{9,17},{17,25},{25,1},{2,10},{10... | collective-permute-start | bytes 2359304 | tf_op jit(solution)/shard_map/ppermute | solution.py:444
  167.7 81.9 %collective-permute-start.26 = (bf16[2,192,1024]{2,1,0:T(8,128)(2,1)}, bf16[2,192,1024]{2,1,0:T(8,128)(2,1)}, u32[]{:S(2)}, u32[]{:S(2)}) collective-permute-start(bf16[2,192,1024]{2,1,0:T(8,128)(2,1)} %get-tuple-element.222), channel_id=1, source_target_pairs={{0,16},{8,24},{16,0},{24,8},{1,17},{9,25},{17,1},{25,9},{2,18},{10... | collective-permute-start | bytes 2359304 | tf_op jit(solution)/shard_map/ppermute | solution.py:444
  171.5 94.9 %collective-permute-start.27 = (bf16[2,192,1024]{2,1,0:T(8,128)(2,1)}, bf16[2,192,1024]{2,1,0:T(8,128)(2,1)}, u32[]{:S(2)}, u32[]{:S(2)}) collective-permute-start(bf16[2,192,1024]{2,1,0:T(8,128)(2,1)} %get-tuple-element.219), channel_id=1, source_target_pairs={{0,24},{8,0},{16,8},{24,16},{1,25},{9,1},{17,9},{25,17},{2,26},{10... | collective-permute-start | bytes 2359304 | tf_op jit(solution)/shard_map/ppermute | solution.py:444
  208.3 25.9 %collective-permute-start.30 = (bf16[192,1024]{1,0:T(8,128)(2,1)}, bf16[192,1024]{1,0:T(8,128)(2,1)S(1)}, u32[]{:S(2)}, u32[]{:S(2)}) collective-permute-start(bf16[192,1024]{1,0:T(8,128)(2,1)} %get-tuple-element.227), channel_id=1, source_target_pairs={{0,24},{8,0},{16,8},{24,16},{1,25},{9,1},{17,9},{25,17},{2,26},{10... | collective-permute-start | bytes 1179656 | tf_op jit(solution)/shard_map/ppermute | solution.py:444
  208.3 26.4 %collective-permute-start.23 = (bf16[512,384]{1,0:T(8,128)(2,1)}, bf16[512,384]{1,0:T(8,128)(2,1)S(1)}, u32[]{:S(2)}, u32[]{:S(2)}) collective-permute-start(bf16[512,384]{1,0:T(8,128)(2,1)} %collective-permute-done.22.b2), channel_id=1, source_target_pairs={{0,2},{2,0},{4,6},{6,4},{1,3},{3,1},{5,7},{7,5},{8,10},{10,8},{12,... | collective-permute-start | bytes 1179656 | tf_op jit(solution)/shard_map/ppermute | solution.py:441
  234.2 38.3 %collective-permute-start.52 = (bf16[512,384]{1,0:T(8,128)(2,1)}, bf16[512,384]{1,0:T(8,128)(2,1)}, u32[]{:S(2)}, u32[]{:S(2)}) collective-permute-start(bf16[512,384]{1,0:T(8,128)(2,1)} %multiply_convert_fusion.b0.xa), channel_id=1, source_target_pairs={{0,1},{1,0},{2,3},{3,2},{4,5},{5,4},{6,7},{7,6},{8,9},{9,8},{10,11... | collective-permute-start | bytes 1179656 | tf_op jit(solution)/shard_map/ppermute | solution.py:438
  234.8 37.8 %collective-permute-start.18 = (bf16[512,384]{1,0:T(8,128)(2,1)}, bf16[512,384]{1,0:T(8,128)(2,1)}, u32[]{:S(2)}, u32[]{:S(2)}) collective-permute-start(bf16[512,384]{1,0:T(8,128)(2,1)} %multiply_convert_fusion.b0.xa), channel_id=1, source_target_pairs={{0,4},{2,6},{4,0},{6,2},{1,5},{3,7},{5,1},{7,3},{8,12},{10,14},{12... | collective-permute-start | bytes 1179656 | tf_op jit(solution)/shard_map/ppermute | solution.py:441
  248.0 50.0 %collective-permute-start.24 = (bf16[512,384]{1,0:T(8,128)(2,1)}, bf16[512,384]{1,0:T(8,128)(2,1)S(1)}, u32[]{:S(2)}, u32[]{:S(2)}) collective-permute-start(bf16[512,384]{1,0:T(8,128)(2,1)} %get-tuple-element.84.wa), channel_id=1, source_target_pairs={{0,1},{1,0},{2,3},{3,2},{4,5},{5,4},{6,7},{7,6},{8,9},{9,8},{10,11... | collective-permute-start | bytes 1179656 | tf_op jit(solution)/shard_map/ppermute | solution.py:438
  249.6 54.5 %collective-permute-start.34 = (bf16[512,384]{1,0:T(8,128)(2,1)}, bf16[512,384]{1,0:T(8,128)(2,1)S(1)}, u32[]{:S(2)}, u32[]{:S(2)}) collective-permute-start(bf16[512,384]{1,0:T(8,128)(2,1)} %get-tuple-element.89), channel_id=1, source_target_pairs={{0,8},{8,16},{16,24},{24,0},{1,9},{9,17},{17,25},{25,1},{2,10},{10... | collective-permute-start | bytes 1179656 | tf_op jit(solution)/shard_map/ppermute | solution.py:444
  266.3 39.4 %collective-permute-start.40 = (bf16[512,384]{1,0:T(8,128)(2,1)}, bf16[512,384]{1,0:T(8,128)(2,1)S(1)}, u32[]{:S(2)}, u32[]{:S(2)}) collective-permute-start(bf16[512,384]{1,0:T(8,128)(2,1)} %get-tuple-element.96), channel_id=1, source_target_pairs={{0,16},{8,24},{16,0},{24,8},{1,17},{9,25},{17,1},{25,9},{2,18},{10... | collective-permute-start | bytes 1179656 | tf_op jit(solution)/shard_map/ppermute | solution.py:444
  272.5 18.1 %collective-permute-start.17 = (bf16[512,384]{1,0:T(8,128)(2,1)}, bf16[512,384]{1,0:T(8,128)(2,1)S(1)}, u32[]{:S(2)}, u32[]{:S(2)}) collective-permute-start(bf16[512,384]{1,0:T(8,128)(2,1)} %multiply_convert_fusion.b0.xa), channel_id=1, source_target_pairs={{0,2},{2,0},{4,6},{6,4},{1,3},{3,1},{5,7},{7,5},{8,10},{10,8},{12,... | collective-permute-start | bytes 1179656 | tf_op jit(solution)/shard_map/ppermute | solution.py:441
  272.5 20.5 %collective-permute-start.19 = (bf16[512,384]{1,0:T(8,128)(2,1)}, bf16[512,384]{1,0:T(8,128)(2,1)S(1)}, u32[]{:S(2)}, u32[]{:S(2)}) collective-permute-start(bf16[512,384]{1,0:T(8,128)(2,1)} %collective-permute-done.18.b2), channel_id=1, source_target_pairs={{0,2},{2,0},{4,6},{6,4},{1,3},{3,1},{5,7},{7,5},{8,10},{10,8},{12,... | collective-permute-start | bytes 1179656 | tf_op jit(solution)/shard_map/ppermute | solution.py:441
  304.1 25.3 %collective-permute-start.35 = (bf16[512,384]{1,0:T(8,128)(2,1)S(1)}, bf16[512,384]{1,0:T(8,128)(2,1)S(1)}, u32[]{:S(2)}, u32[]{:S(2)}) collective-permute-start(bf16[512,384]{1,0:T(8,128)(2,1)S(1)} %collective-permute-done.34.wa), channel_id=1, source_target_pairs={{0,1},{1,0},{2,3},{3,2},{4,5},{5,4},{6,7},{7,6},{8,9},{9,8},{10,11... | collective-permute-start | bytes 1179656 | tf_op jit(solution)/shard_map/ppermute | solution.py:438
  305.7 52.0 %collective-permute-start.41 = (bf16[512,384]{1,0:T(8,128)(2,1)S(1)}, bf16[512,384]{1,0:T(8,128)(2,1)S(1)}, u32[]{:S(2)}, u32[]{:S(2)}) collective-permute-start(bf16[512,384]{1,0:T(8,128)(2,1)S(1)} %collective-permute-done.40.wa), channel_id=1, source_target_pairs={{0,1},{1,0},{2,3},{3,2},{4,5},{5,4},{6,7},{7,6},{8,9},{9,8},{10,11... | collective-permute-start | bytes 1179656 | tf_op jit(solution)/shard_map/ppermute | solution.py:438
  306.2 68.6 %collective-permute-start.47 = (bf16[512,384]{1,0:T(8,128)(2,1)S(1)}, bf16[512,384]{1,0:T(8,128)(2,1)S(1)}, u32[]{:S(2)}, u32[]{:S(2)}) collective-permute-start(bf16[512,384]{1,0:T(8,128)(2,1)S(1)} %collective-permute-done.46.wa), channel_id=1, source_target_pairs={{0,1},{1,0},{2,3},{3,2},{4,5},{5,4},{6,7},{7,6},{8,9},{9,8},{10,11... | collective-permute-start | bytes 1179656 | tf_op jit(solution)/shard_map/ppermute | solution.py:438
  309.8 21.2 %collective-permute-start.38 = (bf16[512,384]{1,0:T(8,128)(2,1)S(1)}, bf16[512,384]{1,0:T(8,128)(2,1)S(1)}, u32[]{:S(2)}, u32[]{:S(2)}) collective-permute-start(bf16[512,384]{1,0:T(8,128)(2,1)S(1)} %copy-done.78), channel_id=1, source_target_pairs={{0,16},{8,24},{16,0},{24,8},{1,17},{9,25},{17,1},{25,9},{2,18},{10... | collective-permute-start | bytes 1179656 | tf_op jit(solution)/shard_map/ppermute | solution.py:444
  313.5 30.0 %collective-permute-start.33 = (bf16[512,384]{1,0:T(8,128)(2,1)S(1)}, bf16[512,384]{1,0:T(8,128)(2,1)S(1)}, u32[]{:S(2)}, u32[]{:S(2)}) collective-permute-start(bf16[512,384]{1,0:T(8,128)(2,1)S(1)} %collective-permute-done.32.xa), channel_id=1, source_target_pairs={{0,1},{1,0},{2,3},{3,2},{4,5},{5,4},{6,7},{7,6},{8,9},{9,8},{10,11... | collective-permute-start | bytes 1179656 | tf_op jit(solution)/shard_map/ppermute | solution.py:438
  329.4 122.9 %collective-permute-start.64 = (bf16[512,384]{1,0:T(8,128)(2,1)S(1)}, bf16[512,384]{1,0:T(8,128)(2,1)S(1)}, u32[]{:S(2)}, u32[]{:S(2)}) collective-permute-start(bf16[512,384]{1,0:T(8,128)(2,1)S(1)} %slice_bitcast_fusion.4), channel_id=1, source_target_pairs={{0,1},{1,0},{2,3},{3,2},{4,5},{5,4},{6,7},{7,6},{8,9},{9,8},{10,11... | collective-permute-start | bytes 1179656 | tf_op jit(solution)/shard_map/ppermute | solution.py:438
  331.0 28.2 %collective-permute-start.44 = (bf16[512,384]{1,0:T(8,128)(2,1)S(1)}, bf16[512,384]{1,0:T(8,128)(2,1)S(1)}, u32[]{:S(2)}, u32[]{:S(2)}) collective-permute-start(bf16[512,384]{1,0:T(8,128)(2,1)S(1)} %copy-done.77), channel_id=1, source_target_pairs={{0,24},{8,0},{16,8},{24,16},{1,25},{9,1},{17,9},{25,17},{2,26},{10... | collective-permute-start | bytes 1179656 | tf_op jit(solution)/shard_map/ppermute | solution.py:444
  357.8 53.8 %collective-permute-start.55 = (bf16[512,384]{1,0:T(8,128)(2,1)S(1)}, bf16[512,384]{1,0:T(8,128)(2,1)}, u32[]{:S(2)}, u32[]{:S(2)}) collective-permute-start(bf16[512,384]{1,0:T(8,128)(2,1)S(1)} %slice_bitcast_fusion.8), channel_id=1, source_target_pairs={{0,1},{1,0},{2,3},{3,2},{4,5},{5,4},{6,7},{7,6},{8,9},{9,8},{10,11... | collective-permute-start | bytes 1179656 | tf_op jit(solution)/shard_map/ppermute | solution.py:438
  359.1 19.2 %collective-permute-start.45 = (bf16[512,384]{1,0:T(8,128)(2,1)S(1)}, bf16[512,384]{1,0:T(8,128)(2,1)S(1)}, u32[]{:S(2)}, u32[]{:S(2)}) collective-permute-start(bf16[512,384]{1,0:T(8,128)(2,1)S(1)} %collective-permute-done.44.xa), channel_id=1, source_target_pairs={{0,1},{1,0},{2,3},{3,2},{4,5},{5,4},{6,7},{7,6},{8,9},{9,8},{10,11... | collective-permute-start | bytes 1179656 | tf_op jit(solution)/shard_map/ppermute | solution.py:438
  360.0 47.1 %collective-permute-start.56 = (bf16[512,384]{1,0:T(8,128)(2,1)S(1)}, bf16[512,384]{1,0:T(8,128)(2,1)S(1)}, u32[]{:S(2)}, u32[]{:S(2)}) collective-permute-start(bf16[512,384]{1,0:T(8,128)(2,1)S(1)} %slice_bitcast_fusion.7), channel_id=1, source_target_pairs={{0,1},{1,0},{2,3},{3,2},{4,5},{5,4},{6,7},{7,6},{8,9},{9,8},{10,11... | collective-permute-start | bytes 1179656 | tf_op jit(solution)/shard_map/ppermute | solution.py:438
  374.8 34.5 %collective-permute-start.58 = (bf16[512,384]{1,0:T(8,128)(2,1)S(1)}, bf16[512,384]{1,0:T(8,128)(2,1)S(1)}, u32[]{:S(2)}, u32[]{:S(2)}) collective-permute-start(bf16[512,384]{1,0:T(8,128)(2,1)S(1)} %slice_bitcast_fusion.6), channel_id=1, source_target_pairs={{0,1},{1,0},{2,3},{3,2},{4,5},{5,4},{6,7},{7,6},{8,9},{9,8},{10,11... | collective-permute-start | bytes 1179656 | tf_op jit(solution)/shard_map/ppermute | solution.py:438
  409.4 28.4 %collective-permute-start.59 = (bf16[512,384]{1,0:T(8,128)(2,1)S(1)}, bf16[512,384]{1,0:T(8,128)(2,1)S(1)}, u32[]{:S(2)}, u32[]{:S(2)}) collective-permute-start(bf16[512,384]{1,0:T(8,128)(2,1)S(1)} %fusion.26), channel_id=1, source_target_pairs={{0,16},{8,24},{16,0},{24,8},{1,17},{9,25},{17,1},{25,9},{2,18},{10... | collective-permute-start | bytes 1179656 | tf_op jit(solution)/shard_map/ppermute | solution.py:444
  409.6 29.7 %collective-permute-start.61 = (bf16[512,384]{1,0:T(8,128)(2,1)S(1)}, bf16[512,384]{1,0:T(8,128)(2,1)}, u32[]{:S(2)}, u32[]{:S(2)}) collective-permute-start(bf16[512,384]{1,0:T(8,128)(2,1)S(1)} %fusion.25), channel_id=1, source_target_pairs={{0,8},{8,16},{16,24},{24,0},{1,9},{9,17},{17,25},{25,1},{2,10},{10... | collective-permute-start | bytes 1179656 | tf_op jit(solution)/shard_map/ppermute | solution.py:444
  411.6 80.9 %collective-permute-start.31 = (bf16[512,384]{1,0:T(8,128)(2,1)}, bf16[512,384]{1,0:T(8,128)(2,1)}, u32[]{:S(2)}, u32[]{:S(2)}) collective-permute-start(bf16[512,384]{1,0:T(8,128)(2,1)} %slice_bitcast_fusion.13), channel_id=1, source_target_pairs={{0,1},{1,0},{2,3},{3,2},{4,5},{5,4},{6,7},{7,6},{8,9},{9,8},{10,11... | collective-permute-start | bytes 1179656 | tf_op jit(solution)/shard_map/ppermute | solution.py:438
  418.9 43.7 %collective-permute-start.36 = (bf16[512,384]{1,0:T(8,128)(2,1)}, bf16[512,384]{1,0:T(8,128)(2,1)}, u32[]{:S(2)}, u32[]{:S(2)}) collective-permute-start(bf16[512,384]{1,0:T(8,128)(2,1)} %slice_bitcast_fusion.12), channel_id=1, source_target_pairs={{0,1},{1,0},{2,3},{3,2},{4,5},{5,4},{6,7},{7,6},{8,9},{9,8},{10,11... | collective-permute-start | bytes 1179656 | tf_op jit(solution)/shard_map/ppermute | solution.py:438
  437.9 28.6 %collective-permute-start.42 = (bf16[512,384]{1,0:T(8,128)(2,1)}, bf16[512,384]{1,0:T(8,128)(2,1)}, u32[]{:S(2)}, u32[]{:S(2)}) collective-permute-start(bf16[512,384]{1,0:T(8,128)(2,1)} %slice_bitcast_fusion.11), channel_id=1, source_target_pairs={{0,1},{1,0},{2,3},{3,2},{4,5},{5,4},{6,7},{7,6},{8,9},{9,8},{10,11... | collective-permute-start | bytes 1179656 | tf_op jit(solution)/shard_map/ppermute | solution.py:438
  464.4 32.2 %collective-permute-start.37 = (bf16[512,384]{1,0:T(8,128)(2,1)}, bf16[512,384]{1,0:T(8,128)(2,1)}, u32[]{:S(2)}, u32[]{:S(2)}) collective-permute-start(bf16[512,384]{1,0:T(8,128)(2,1)} %fusion.33), channel_id=1, source_target_pairs={{0,24},{8,0},{16,8},{24,16},{1,25},{9,1},{17,9},{25,17},{2,26},{10... | collective-permute-start | bytes 1179656 | tf_op jit(solution)/shard_map/ppermute | solution.py:444
  468.4 66.0 %collective-permute-start.43 = (bf16[512,384]{1,0:T(8,128)(2,1)}, bf16[512,384]{1,0:T(8,128)(2,1)}, u32[]{:S(2)}, u32[]{:S(2)}) collective-permute-start(bf16[512,384]{1,0:T(8,128)(2,1)} %fusion.32), channel_id=1, source_target_pairs={{0,16},{8,24},{16,0},{24,8},{1,17},{9,25},{17,1},{25,9},{2,18},{10... | collective-permute-start | bytes 1179656 | tf_op jit(solution)/shard_map/ppermute | solution.py:444
  471.2 63.2 %collective-permute-start.49 = (bf16[512,384]{1,0:T(8,128)(2,1)}, bf16[512,384]{1,0:T(8,128)(2,1)}, u32[]{:S(2)}, u32[]{:S(2)}) collective-permute-start(bf16[512,384]{1,0:T(8,128)(2,1)} %fusion.31), channel_id=1, source_target_pairs={{0,8},{8,16},{16,24},{24,0},{1,9},{9,17},{17,25},{25,1},{2,10},{10... | collective-permute-start | bytes 1179656 | tf_op jit(solution)/shard_map/ppermute | solution.py:444
  488.9 69.5 %collective-permute-start.67 = (bf16[2,512,768]{2,1,0:T(8,128)(2,1)S(1)}, bf16[2,512,768]{2,1,0:T(8,128)(2,1)S(1)}, u32[]{:S(2)}, u32[]{:S(2)}) collective-permute-start(bf16[2,512,768]{2,1,0:T(8,128)(2,1)S(1)} %slice.273), channel_id=1, source_target_pairs={{0,2},{2,0},{4,6},{6,4},{1,3},{3,1},{5,7},{7,5},{8,10},{10,8},{12,... | collective-permute-start | bytes 4718600 | tf_op jit(solution)/shard_map/ppermute | solution.py:441
  492.5 69.4 %collective-permute-start.88 = (bf16[192,2048]{1,0:T(8,128)(2,1)}, bf16[192,2048]{1,0:T(8,128)(2,1)S(1)}, u32[]{:S(2)}, u32[]{:S(2)}) collective-permute-start(bf16[192,2048]{1,0:T(8,128)(2,1)} %get-tuple-element.217), channel_id=1, source_target_pairs={{0,8},{8,16},{16,24},{24,0},{1,9},{9,17},{17,25},{25,1},{2,10},{10... | collective-permute-start | bytes 2359304 | tf_op jit(solution)/shard_map/ppermute | solution.py:444
  496.6 57.0 %collective-permute-start.91 = (bf16[192,1024]{1,0:T(8,128)(2,1)}, bf16[192,1024]{1,0:T(8,128)(2,1)S(1)}, u32[]{:S(2)}, u32[]{:S(2)}) collective-permute-start(bf16[192,1024]{1,0:T(8,128)(2,1)} %get-tuple-element.225), channel_id=1, source_target_pairs={{0,8},{8,16},{16,24},{24,0},{1,9},{9,17},{17,25},{25,1},{2,10},{10... | collective-permute-start | bytes 1179656 | tf_op jit(solution)/shard_map/ppermute | solution.py:444
  534.4 22.1 %collective-permute-start.92 = (bf16[192,1024]{1,0:T(8,128)(2,1)}, bf16[192,1024]{1,0:T(8,128)(2,1)S(1)}, u32[]{:S(2)}, u32[]{:S(2)}) collective-permute-start(bf16[192,1024]{1,0:T(8,128)(2,1)} %get-tuple-element.224), channel_id=1, source_target_pairs={{0,16},{8,24},{16,0},{24,8},{1,17},{9,25},{17,1},{25,9},{2,18},{10... | collective-permute-start | bytes 1179656 | tf_op jit(solution)/shard_map/ppermute | solution.py:444
  534.4 23.9 %collective-permute-start.93 = (bf16[192,1024]{1,0:T(8,128)(2,1)}, bf16[192,1024]{1,0:T(8,128)(2,1)}, u32[]{:S(2)}, u32[]{:S(2)}) collective-permute-start(bf16[192,1024]{1,0:T(8,128)(2,1)} %get-tuple-element.223), channel_id=1, source_target_pairs={{0,24},{8,0},{16,8},{24,16},{1,25},{9,1},{17,9},{25,17},{2,26},{10... | collective-permute-start | bytes 1179656 | tf_op jit(solution)/shard_map/ppermute | solution.py:444
  553.6 37.6 %collective-permute-start.89 = (bf16[192,2048]{1,0:T(8,128)(2,1)S(1)}, bf16[192,2048]{1,0:T(8,128)(2,1)}, u32[]{:S(2)}, u32[]{:S(2)}) collective-permute-start(bf16[192,2048]{1,0:T(8,128)(2,1)S(1)} %copy-done.43), channel_id=1, source_target_pairs={{0,16},{8,24},{16,0},{24,8},{1,17},{9,25},{17,1},{25,9},{2,18},{10... | collective-permute-start | bytes 2359304 | tf_op jit(solution)/shard_map/ppermute | solution.py:444
  556.5 35.6 %collective-permute-start.90 = (bf16[192,2048]{1,0:T(8,128)(2,1)S(1)}, bf16[192,2048]{1,0:T(8,128)(2,1)}, u32[]{:S(2)}, u32[]{:S(2)}) collective-permute-start(bf16[192,2048]{1,0:T(8,128)(2,1)S(1)} %copy-done.42), channel_id=1, source_target_pairs={{0,24},{8,0},{16,8},{24,16},{1,25},{9,1},{17,9},{25,17},{2,26},{10... | collective-permute-start | bytes 2359304 | tf_op jit(solution)/shard_map/ppermute | solution.py:444
  558.3 46.3 %collective-permute-start.50 = (bf16[2,512,384]{2,1,0:T(8,128)(2,1)}, bf16[2,512,384]{2,1,0:T(8,128)(2,1)}, u32[]{:S(2)}, u32[]{:S(2)}) collective-permute-start(bf16[2,512,384]{2,1,0:T(8,128)(2,1)} %get-tuple-element.110), channel_id=1, source_target_pairs={{0,2},{2,0},{4,6},{6,4},{1,3},{3,1},{5,7},{7,5},{8,10},{10,8},{12,... | collective-permute-start | bytes 2359304 | tf_op jit(solution)/shard_map/ppermute | solution.py:441
  558.4 85.1 %collective-permute-start.83 = (bf16[2,4,48,3456]{3,2,1,0:T(8,128)(2,1)}, bf16[2,4,48,3456]{3,2,1,0:T(8,128)(2,1)}, u32[]{:S(2)}, u32[]{:S(2)}) collective-permute-start(bf16[2,4,48,3456]{3,2,1,0:T(8,128)(2,1)} %slice.298), channel_id=1, source_target_pairs={{0,2},{2,0},{4,6},{6,4},{1,3},{3,1},{5,7},{7,5},{8,10},{10,8},{12,... | collective-permute-start | bytes 7962632 | tf_op jit(solution)/shard_map/ppermute | solution.py:441
  561.9 62.5 %collective-permute-start.68 = (bf16[512,768]{1,0:T(8,128)(2,1)}, bf16[512,768]{1,0:T(8,128)(2,1)}, u32[]{:S(2)}, u32[]{:S(2)}) collective-permute-start(bf16[512,768]{1,0:T(8,128)(2,1)} %fusion.17), channel_id=1, source_target_pairs={{0,4},{2,6},{4,0},{6,2},{1,5},{3,7},{5,1},{7,3},{8,12},{10,14},{12... | collective-permute-start | bytes 2359304 | tf_op jit(solution)/shard_map/ppermute | solution.py:441
  591.1 67.3 %collective-permute-start.53 = (bf16[512,384]{1,0:T(8,128)(2,1)}, bf16[512,384]{1,0:T(8,128)(2,1)}, u32[]{:S(2)}, u32[]{:S(2)}) collective-permute-start(bf16[512,384]{1,0:T(8,128)(2,1)} %slice_bitcast_fusion.9), channel_id=1, source_target_pairs={{0,1},{1,0},{2,3},{3,2},{4,5},{5,4},{6,7},{7,6},{8,9},{9,8},{10,11... | collective-permute-start | bytes 1179656 | tf_op jit(solution)/shard_map/ppermute | solution.py:438
  606.6 52.4 %collective-permute-start.51 = (bf16[512,384]{1,0:T(8,128)(2,1)}, bf16[512,384]{1,0:T(8,128)(2,1)}, u32[]{:S(2)}, u32[]{:S(2)}) collective-permute-start(bf16[512,384]{1,0:T(8,128)(2,1)} %fusion.40), channel_id=1, source_target_pairs={{0,4},{2,6},{4,0},{6,2},{1,5},{3,7},{5,1},{7,3},{8,12},{10,14},{12... | collective-permute-start | bytes 1179656 | tf_op jit(solution)/shard_map/ppermute | solution.py:441
  639.5 37.9 %collective-permute-start.78 = (bf16[2,4,48,1152]{3,2,1,0:T(8,128)(2,1)}, bf16[2,4,48,1152]{3,2,1,0:T(8,128)(2,1)}, u32[]{:S(2)}, u32[]{:S(2)}) collective-permute-start(bf16[2,4,48,1152]{3,2,1,0:T(8,128)(2,1)} %slice.290), channel_id=1, source_target_pairs={{0,2},{2,0},{4,6},{6,4},{1,3},{3,1},{5,7},{7,5},{8,10},{10,8},{12,... | collective-permute-start | bytes 2654216 | tf_op jit(solution)/shard_map/ppermute | solution.py:441
  666.9 42.1 %collective-permute-start.84 = (bf16[4,48,3456]{2,1,0:T(8,128)(2,1)S(1)}, bf16[4,48,3456]{2,1,0:T(8,128)(2,1)}, u32[]{:S(2)}, u32[]{:S(2)}) collective-permute-start(bf16[4,48,3456]{2,1,0:T(8,128)(2,1)S(1)} %fusion.3), channel_id=1, source_target_pairs={{0,4},{2,6},{4,0},{6,2},{1,5},{3,7},{5,1},{7,3},{8,12},{10,14},{12... | collective-permute-start | bytes 3981320 | tf_op jit(solution)/shard_map/ppermute | solution.py:441
  679.0 25.7 %collective-permute-start.79 = (bf16[4,48,1152]{2,1,0:T(8,128)(2,1)S(1)}, bf16[4,48,1152]{2,1,0:T(8,128)(2,1)S(1)}, u32[]{:S(2)}, u32[]{:S(2)}) collective-permute-start(bf16[4,48,1152]{2,1,0:T(8,128)(2,1)S(1)} %fusion.39), channel_id=1, source_target_pairs={{0,4},{2,6},{4,0},{6,2},{1,5},{3,7},{5,1},{7,3},{8,12},{10,14},{12... | collective-permute-start | bytes 1327112 | tf_op jit(solution)/shard_map/ppermute | solution.py:441
  715.1 28.8 %collective-permute-start.86 = (bf16[48,3456]{1,0:T(8,128)(2,1)}, bf16[48,3456]{1,0:T(8,128)(2,1)}, u32[]{:S(2)}, u32[]{:S(2)}) collective-permute-start(bf16[48,3456]{1,0:T(8,128)(2,1)} %get-tuple-element.233), channel_id=1, source_target_pairs={{0,16},{8,24},{16,0},{24,8},{1,17},{9,25},{17,1},{25,9},{2,18},{10... | collective-permute-start | bytes 995336 | tf_op jit(solution)/shard_map/ppermute | solution.py:444
  715.3 28.5 %collective-permute-start.85 = (bf16[48,3456]{1,0:T(8,128)(2,1)}, bf16[48,3456]{1,0:T(8,128)(2,1)}, u32[]{:S(2)}, u32[]{:S(2)}) collective-permute-start(bf16[48,3456]{1,0:T(8,128)(2,1)} %get-tuple-element.231), channel_id=1, source_target_pairs={{0,8},{8,16},{16,24},{24,0},{1,9},{9,17},{17,25},{25,1},{2,10},{10... | collective-permute-start | bytes 995336 | tf_op jit(solution)/shard_map/ppermute | solution.py:444
  (118 other events, 1462.7 us)

commit v2 on v1

v2 whole, which is shorter than its diff:
```python
import functools

import jax
import jax.numpy as jnp
from jax import lax
from jax.experimental import pallas as pl
from jax.experimental.pallas import tpu as pltpu
from jax.sharding import PartitionSpec as P

D = 768
HALF = D // 2
HD = 64
E = 16
ROWS = 512
CAP = 128
NEG = -1e30
eps = 1e-06
bf16 = jnp.bfloat16
f32 = jnp.float32
VMEM_LIMIT = 56 * 1024 * 1024


def mm(a, b):
    return lax.dot_general(a, b, (((1,), (0,)), ((), ())), preferred_element_type=f32)


def mm_t(a, b):
    return lax.dot_general(a, b, (((1,), (1,)), ((), ())), preferred_element_type=f32)


def t_mm(a, b):
    return lax.dot_general(a, b, (((0,), (0,)), ((), ())), preferred_element_type=f32)


def sds(shape, dtype):
    return jax.ShapeDtypeStruct(shape, dtype)


SMEM = pl.BlockSpec(memory_space=pltpu.SMEM)
VM = pl.BlockSpec(memory_space=pltpu.VMEM)


def call(body, outs, scratch=(), us=1.0, name=None):
    def run(scalars, *args, deps=()):
        count = 1 + len(args)

        def inner(*refs):
            body(*refs[:count], *refs[count + len(deps) :])

        return pl.pallas_call(
            inner,
            out_shape=outs,
            in_specs=[SMEM] + [VM] * len(args) + [pl.BlockSpec(memory_space=pl.ANY)] * len(deps),
            out_specs=jax.tree.map(lambda _: VM, outs),
            scratch_shapes=list(scratch),
            compiler_params=pltpu.CompilerParams(vmem_limit_bytes=VMEM_LIMIT),
            cost_estimate=pl.CostEstimate(
                flops=int(us * 1e9), bytes_accessed=0, transcendentals=0
            ),
            name=name,
        )(scalars, *args, *deps)

    return run


def after(v, *deps):
    return lax.optimization_barrier((v,) + deps)[0]


def partner(v, lane):
    return jnp.where(lane % 64 < 32, pltpu.roll(v, 96, 1), pltpu.roll(v, 32, 1))


def lane_id(rows):
    return lax.broadcasted_iota(jnp.int32, (rows, 128), 1)


def qkv_body(sc, tok, gain, w, cos, sin, a_o, q_o, kv_o):
    x = tok[...].astype(f32)
    scale = lax.rsqrt(jnp.mean(x * x, axis=1, keepdims=True) + eps)
    a = (x * scale * gain[...]).astype(bf16)
    a_o[...] = a
    n = q_o.shape[1]
    lane = lane_id(ROWS)
    for g in range(3 * n // 128):
        v = mm(a, w[:, g * 128 : (g + 1) * 128])
        lo = g * 128
        if lo < n:
            r = v * cos[...] + partner(v, lane) * sin[...]
            q_o[:, lo : lo + 128] = (r.astype(bf16).astype(f32) * (HD**-0.5)).astype(bf16)
        elif lo < 2 * n:
            r = v * cos[...] + partner(v, lane) * sin[...]
            kv_o[:, lo - n : lo - n + 128] = r.astype(bf16)
        else:
            kv_o[:, lo - n : lo - n + 128] = v.astype(bf16)


def block_bias(c, kb, segc, segq):
    off = pl.multiple_of(kb * ROWS, ROWS)
    kpos = off + lax.broadcasted_iota(jnp.int32, (ROWS, ROWS), 0)
    qpos = c * ROWS + lax.broadcasted_iota(jnp.int32, (ROWS, ROWS), 1)
    ok = (segc[pl.ds(off, ROWS), :] == segq[...]) & (kpos <= qpos)
    return jnp.where(ok, 0.0, NEG)


def attn_body(sc, q, k0, k1, k2, k3, segc, segq, wo, o_o, zown_o, zoth_o, lse_o, kvs, bias, st, ot):
    c, y = sc[0], sc[1]
    nb = c + 1
    n = q.shape[1]
    for r, ref in enumerate((k0, k1, k2, k3)):
        kvs[pl.ds(pl.multiple_of((c ^ r) * ROWS, ROWS), ROWS), :] = ref[...]

    def bias_step(kb, carry):
        bias[pl.ds(pl.multiple_of(kb * ROWS, ROWS), ROWS), :] = block_bias(c, kb, segc, segq)
        return carry

    lax.fori_loop(0, nb, bias_step, 0)
    for h in range(n // HD):
        lo = h * HD
        qh = q[:, lo : lo + HD]

        def score_step(kb, m, lo=lo, qh=qh):
            rows = pl.ds(pl.multiple_of(kb * ROWS, ROWS), ROWS)
            s = mm_t(kvs[rows, lo : lo + HD], qh) + bias[rows, :]
            st[rows, :] = s
            return jnp.maximum(m, jnp.max(s, axis=0, keepdims=True))

        m = lax.fori_loop(0, nb, score_step, jnp.full((1, ROWS), NEG, f32))

        def value_step(kb, carry, lo=lo, m=m):
            total, acc = carry
            rows = pl.ds(pl.multiple_of(kb * ROWS, ROWS), ROWS)
            p = jnp.exp(st[rows, :] - m)
            total = total + jnp.sum(p, axis=0, keepdims=True)
            return total, acc + t_mm(kvs[rows, n + lo : n + lo + HD], p.astype(bf16))

        total, acc = lax.fori_loop(
            0, nb, value_step, (jnp.zeros((1, ROWS), f32), jnp.zeros((HD, ROWS), f32))
        )
        ot[lo : lo + HD, :] = acc / total
        lse_o[h : h + 1, :] = m + jnp.log(total)
    o = ot[...].T.astype(bf16)
    o_o[...] = o
    own = pl.ds(pl.multiple_of(y * HALF, HALF), HALF)
    oth = pl.ds(pl.multiple_of((1 - y) * HALF, HALF), HALF)
    zoth_o[...] = mm_t(o, wo[oth, :]).astype(bf16)
    zown_o[...] = mm_t(o, wo[own, :])


def attn_back_body(
    sc, q, k0, k1, k2, k3, segc, segq, lse, o, zown, zoth, wo, cos, sin, dq_o, keep_o, send_o,
    kvs, bias, do_s, delta, dqt,
):
    c, y = sc[0], sc[1]
    nb = c + 1
    n = q.shape[1]
    heads = n // HD
    for r, ref in enumerate((k0, k1, k2, k3)):
        kvs[pl.ds(pl.multiple_of((c ^ r) * ROWS, ROWS), ROWS), :] = ref[...]

    def bias_step(kb, carry):
        bias[pl.ds(pl.multiple_of(kb * ROWS, ROWS), ROWS), :] = block_bias(c, kb, segc, segq)
        return carry

    lax.fori_loop(0, nb, bias_step, 0)
    own = pl.ds(pl.multiple_of(y * HALF, HALF), HALF)
    oth = pl.ds(pl.multiple_of((1 - y) * HALF, HALF), HALF)
    do = (mm(zown[...], wo[own, :]) + mm(zoth[...], wo[oth, :])).astype(bf16)
    do_s[...] = do
    pick = (
        lax.broadcasted_iota(jnp.int32, (8, n), 1) // HD
        == lax.broadcasted_iota(jnp.int32, (8, n), 0)
    ).astype(f32)
    delta[...] = lax.dot_general(
        pick,
        do.astype(f32) * o[...].astype(f32),
        (((1,), (1,)), ((), ())),
        precision=lax.Precision.HIGHEST,
        preferred_element_type=f32,
    )

    def put(kb, cols, value):
        at = kb ^ c

        @pl.when(at % 2 == 0)
        def _():
            keep_o[at // 2, :, cols] = value

        @pl.when(at % 2 == 1)
        def _():
            send_o[at // 2, :, cols] = value

    def zero_step(kb, carry):
        put(kb, slice(None), jnp.zeros((ROWS, 2 * n), bf16))
        return carry

    lax.fori_loop(nb, 4, zero_step, 0)
    for pair in range(heads // 2):
        at = pair * 128

        def step(kb, carry, at=at, pair=pair):
            rows = pl.ds(pl.multiple_of(kb * ROWS, ROWS), ROWS)
            dks, dvs, dqs = [], [], []
            for i in range(2):
                lo = at + i * HD
                h = 2 * pair + i
                kh = kvs[rows, lo : lo + HD]
                vh = kvs[rows, n + lo : n + lo + HD]
                qh = q[:, lo : lo + HD]
                dh = do_s[:, lo : lo + HD]
                p = jnp.exp(mm_t(kh, qh) + bias[rows, :] - lse[h : h + 1, :])
                ds = (p * (mm_t(vh, dh) - delta[h : h + 1, :])).astype(bf16)
                dvs.append(mm(p.astype(bf16), dh))
                dks.append(mm(ds, qh))
                dqs.append(carry[i] + t_mm(kh, ds))
            put(kb, slice(at, at + 128), jnp.concatenate(dks, axis=1).astype(bf16))
            put(kb, slice(n + at, n + at + 128), jnp.concatenate(dvs, axis=1).astype(bf16))
            return tuple(dqs)

        zero = jnp.zeros((HD, ROWS), f32)
        dqs = lax.fori_loop(0, nb, step, (zero, zero))
        dqt[at : at + HD, :] = dqs[0]
        dqt[at + HD : at + 128, :] = dqs[1]
    lane = lane_id(ROWS)
    for g in range(n // 128):
        v = dqt[g * 128 : (g + 1) * 128, :].T * (HD**-0.5)
        dq_o[:, g * 128 : (g + 1) * 128] = (v * cos[...] - partner(v, lane) * sin[...]).astype(bf16)


def proj_back_body(sc, dq, keep, near, recv, w, cos, sin, dp_o, own_o, oth_o):
    y = sc[1]
    n = dq.shape[1]
    lane = lane_id(ROWS)
    dp_o[:, :n] = dq[...]
    for g in range(2 * n // 128):
        cols = slice(g * 128, (g + 1) * 128)
        v = keep[0, :, cols].astype(f32) + near[0, :, cols].astype(f32) + recv[:, cols].astype(f32)
        if g < n // 128:
            v = v * cos[...] - partner(v, lane) * sin[...]
        dp_o[:, n + g * 128 : n + (g + 1) * 128] = v.astype(bf16)
    own = pl.ds(pl.multiple_of(y * HALF, HALF), HALF)
    oth = pl.ds(pl.multiple_of((1 - y) * HALF, HALF), HALF)
    oth_o[...] = mm_t(dp_o[...], w[oth, : 3 * n]).astype(bf16)
    own_o[...] = mm_t(dp_o[...], w[own, : 3 * n])


def slots_onehot(ids, r):
    i = lax.broadcasted_iota(jnp.int32, (4 * CAP, ROWS), 0)
    hit = (i == ids[2 * r : 2 * r + 1, :]) | (i == ids[2 * r + 1 : 2 * r + 2, :])
    return jnp.where(hit, 1.0, 0.0).astype(bf16)


def pack_body(sc, ids, b0, b1, b2, b3, p0, p1, p2, p3):
    for r, ref in enumerate((b0, b1, b2, b3)):
        rows = mm(slots_onehot(ids, r), ref[...]).astype(bf16)
        for s, out in enumerate((p0, p1, p2, p3)):
            out[r * CAP : (r + 1) * CAP, :] = rows[s * CAP : (s + 1) * CAP, :]


def unpack_body(sc, ids, p0, p1, p2, p3, keep_b, send_b, keep_o, send_o):
    for r in (1, 3, 0, 2):
        rows = jnp.concatenate(
            [p[r * CAP : (r + 1) * CAP, :] for p in (p0, p1, p2, p3)], axis=0
        )
        tok = t_mm(slots_onehot(ids, r), rows).astype(bf16)
        for at, pair in ((0, (keep_b, send_b)), (HALF, (keep_o, send_o))):
            pair[r % 2][r // 2] = tok[:, at : at + HALF]


def halves(y, a, b):
    first = y == 0
    return jnp.concatenate([jnp.where(first, a, b), jnp.where(first, b, a)], axis=1)


def ffn_body(routed, sc, xa, xb, wa, wb, weights, rt, *refs):
    if routed:
        refs = refs[len(refs) - 8 :]
        back_o, rg_o, dgu_o, y_o, x_o, de_o, acc_o, acc_b = refs
    else:
        back_o, dgu_o, y_o, acc_o, acc_b = refs[len(refs) - 5 :]
    y, e = sc[1], sc[2]
    x = halves(y, xa[...], xb[...])
    w = halves(y, wa[...], wb[...])
    hidden = weights.shape[3]
    if routed:
        lane = lane_id(ROWS)
        logits = jnp.where(lane < E, mm(x, rt[...]), NEG)
        ex = jnp.exp(logits - jnp.max(logits, axis=1, keepdims=True))
        probs = ex / jnp.sum(ex, axis=1, keepdims=True)
        gate = jnp.sum(jnp.where(lane == e, probs, 0.0), axis=1, keepdims=True)
        x_o[0] = x
        de_o[0] = (w.astype(f32) * gate).astype(bf16)
    acc_o[...] = jnp.zeros_like(acc_o)
    acc_b[...] = jnp.zeros_like(acc_b)
    tile = 256

    def columns(which, lo):
        cols = pl.ds(pl.multiple_of(lo, tile), tile)
        return jnp.concatenate(
            [weights[j, which, :, cols] for j in range(weights.shape[0])], axis=0
        )

    def step(j, dots):
        lo = pl.multiple_of(j * tile, tile)
        hi = pl.multiple_of(hidden + j * tile, tile)
        g = mm(x, columns(0, lo))
        u = mm(x, columns(1, lo))
        h = mm(w, columns(2, lo))
        sg = 1.0 / (1.0 + jnp.exp(-g))
        act = g * sg
        yv = (act * u).astype(bf16)
        if routed:
            dots = dots + jnp.sum(yv.astype(f32) * h, axis=1, keepdims=True)
            h = h * gate
        dg = (h * u * (sg + act * (1.0 - sg))).astype(bf16)
        du = (h * act).astype(bf16)
        y_o[0, :, pl.ds(lo, tile)] = yv
        dgu_o[0, :, pl.ds(lo, tile)] = dg
        dgu_o[0, :, pl.ds(hi, tile)] = du
        acc_o[...] += mm_t(yv, columns(2, lo))
        acc_b[...] += mm_t(dg, columns(0, lo)) + mm_t(du, columns(1, lo))
        return dots

    dots = lax.fori_loop(0, hidden // tile, step, jnp.zeros((ROWS, 1), f32))
    if routed:
        coef = (dots * gate) * (jnp.where(lane == e, 1.0, 0.0) - probs)
        coef = jnp.where(lane < E, coef, 0.0).astype(bf16)
        acc_b[...] += mm_t(coef, rt[...])
        rg_o[...] = t_mm(x, coef)
    for i, at in enumerate((y, 1 - y)):
        cols = pl.ds(pl.multiple_of(at * HALF, HALF), HALF)
        out = acc_o[:, cols]
        if routed:
            out = out * gate
        back_o[i, :, :HALF] = acc_b[:, cols].astype(bf16)
        back_o[i, :, HALF:] = out.astype(bf16)


def ffn(scalars, s, groups, xa, xb, wa, wb, weights, rt, prev, deps=()):
    routed = rt is not None
    hidden = weights.shape[3]
    full = lambda shape: pl.BlockSpec(shape, lambda i, n=len(shape): (0,) * n)
    part = lambda width: pl.BlockSpec((1, ROWS, width), lambda i: (s, 0, 0))
    two = (2, ROWS, D)
    outs = [sds(two, bf16)]
    out_specs = [full(two)]
    if routed:
        outs.append(sds((D, 128), f32))
        out_specs.append(full((D, 128)))
    widths = [2 * hidden, hidden] + ([D, D] if routed else [])
    base = len(outs)
    for width in widths:
        outs.append(sds((groups, ROWS, width), bf16))
        out_specs.append(part(width))
    args = [xa, xb, wa, wb, weights] + ([rt] if routed else [])
    in_specs = [SMEM] + [full(a.shape) for a in args]
    aliases = {}
    if not routed:
        args.append(scalars)
        in_specs.append(SMEM)
    for arr in deps:
        args.append(arr)
        in_specs.append(pl.BlockSpec(memory_space=pl.ANY))
    if prev is not None:
        for i, arr in enumerate(prev):
            aliases[1 + len(args)] = base + i
            args.append(arr)
            in_specs.append(pl.BlockSpec(memory_space=pl.ANY))
    return pl.pallas_call(
        functools.partial(ffn_body, routed),
        grid=(1,),
        out_shape=outs,
        in_specs=in_specs,
        out_specs=out_specs,
        scratch_shapes=[pltpu.VMEM((ROWS, D), f32), pltpu.VMEM((ROWS, D), f32)],
        input_output_aliases=aliases,
        compiler_params=pltpu.CompilerParams(vmem_limit_bytes=VMEM_LIMIT),
        cost_estimate=pl.CostEstimate(flops=int(6e9), bytes_accessed=0, transcendentals=0),
        name="expert_ffn" if routed else "shared_ffn",
    )(scalars, *args)


def grad_blocks(offs, rows, pairs):
    tile = 384
    total = sum(b.shape[1] for _, b in pairs)

    def body(sc, *refs):
        keep, send, acc = refs[-3:]
        lo = 0
        for i in range(len(pairs)):
            a, b = refs[2 * i], refs[2 * i + 1]
            turned = a[...].T
            for j in range(0, b.shape[1], tile):
                width = min(tile, b.shape[1] - j)
                acc[:, :width] = mm(turned, b[:, j : j + width])
                for k in range(16):
                    at = pl.ds(pl.multiple_of(sc[k], 16), rows)
                    out = send if (k // 4) % 2 else keep
                    out[k // 8, k % 4, :, lo : lo + width] = acc[at, :width].astype(bf16)
                lo += width

    shape = sds((2, 4, rows, total), bf16)
    args = [m for pair in pairs for m in pair]
    return call(body, [shape, shape], scratch=[pltpu.VMEM((D, tile), f32)], us=3.0, name="grad_blocks")(
        offs, *args
    )


def per_device(
    tokens,
    segments,
    experts,
    attn_gain,
    qkv_proj,
    out_proj,
    ffn_gain,
    router_proj,
    expert_gate_up,
    expert_down,
    shared_gate_up,
    shared_down,
    cotangent,
):
    F, C = lax.axis_size("fsdp"), lax.axis_size("ctx")
    f, c, y = lax.axis_index("fsdp"), lax.axis_index("ctx"), lax.axis_index("tp")
    EL = expert_gate_up.shape[0]
    small = F == EL and C == 4
    heads_width = qkv_proj.shape[2]
    hidden = expert_down.shape[1]
    shared_hidden = shared_down.shape[0]
    zi = f % EL
    i32 = jnp.int32

    def yx(v):
        return lax.ppermute(v, "tp", [(0, 1), (1, 0)])

    def cx(v, flip):
        return lax.ppermute(v, "ctx", [(i, i ^ flip) for i in range(C)])

    def zs(v, s):
        return lax.ppermute(
            v, "fsdp", [(i, i // EL * EL + (i % EL + s) % EL) for i in range(F)]
        )

    scalars = jnp.stack([c, y, EL * c + zi]).astype(i32)
    rows_own = D // (F * C)
    rc = jnp.arange(4, dtype=i32)
    if small:
        dense_offs = (
            (((f - rc)[None, :] % 4) * 4 + (c ^ rc)[:, None]).reshape(16) * rows_own
        ).astype(i32)
        back_offs = (
            (((f + rc)[None, :] % 4) * 4 + (c ^ rc)[:, None]).reshape(16) * rows_own
        ).astype(i32)

    def gathered(shard, axis=0):
        return lax.all_gather(shard, ("fsdp", "ctx"), axis=axis, tiled=True)

    def reduce_near(keep, send):
        kind = keep.dtype
        near = cx(send, 1)
        far = cx((keep[1].astype(f32) + near[1].astype(f32)).astype(kind), 2)
        return keep[0].astype(f32) + near[0].astype(f32) + far.astype(f32)

    def reduce_far(part, kind, z_after=None, sum_after=None):
        pieces = [part[s].astype(kind) for s in (1, 2, 3)]
        if z_after is not None:
            pieces = [after(piece, z_after) for piece in pieces]
        total = part[0] if sum_after is None else after(part[0], sum_after)
        for s, piece in zip((1, 2, 3), pieces):
            total = total + zs(piece, s).astype(f32)
        return total

    def grad_of(a, b):
        return lax.dot_general(a, b, (((0,), (0,)), ((), ())), preferred_element_type=f32)

    def dense_reduce(pairs):
        full = jnp.concatenate([grad_of(a, b) for a, b in pairs], axis=1)
        return lax.psum_scatter(full, ("fsdp", "ctx"), scatter_dimension=0, tiled=True)

    def half(v, which):
        return lax.dynamic_slice_in_dim(v, which * HALF, HALF, v.ndim - 1)

    qkv_shard = jnp.concatenate(
        [
            qkv_proj.transpose(1, 0, 2).reshape(rows_own, 3 * heads_width),
            router_proj,
            attn_gain[:, None],
            ffn_gain[:, None],
            jnp.zeros((rows_own, 128 - E - 2), bf16),
        ],
        axis=1,
    )
    first = gathered(jnp.concatenate([qkv_shard, out_proj.T], axis=1))
    extra = first[:, 3 * heads_width : 3 * heads_width + 128]
    out_w = first[:, 3 * heads_width + 128 :]
    gains = extra[:, E : E + 2].astype(f32)
    gain_one, gain_two = gains[:, 0], gains[:, 1]
    gain_two_h = half(gain_two, y)
    gain_one_h = half(gain_one, y)
    shared_shard = jnp.concatenate([shared_gate_up, shared_down.T[None]])
    expert_local = jnp.concatenate(
        [expert_gate_up, expert_down.transpose(0, 2, 1)[:, None]], axis=1
    )
    if small:
        expert_w = None
    else:
        inner = [[g * EL + i for i in range(EL)] for g in range(F // EL)]
        outer = [[g * EL + i for g in range(F // EL)] for i in range(EL)]
        mine = lax.all_to_all(
            expert_local, "fsdp", 0, 0, axis_index_groups=inner, tiled=True
        )
        mine = lax.all_gather(mine, "fsdp", axis=0, axis_index_groups=outer, tiled=True)
        expert_w = mine.transpose(1, 0, 2, 3).reshape(1, 3, D, hidden)

    lanes = jnp.arange(E, dtype=i32)[None, :]
    named = [(experts[:, k : k + 1] == lanes) for k in range(2)]
    both = (named[0] | named[1]).astype(bf16)
    before = (jnp.arange(ROWS)[:, None] > jnp.arange(ROWS)[None, :]).astype(bf16)
    counts = jnp.dot(before, both, preferred_element_type=f32)
    code = jnp.stack(
        [
            experts[:, k] * CAP + jnp.sum(jnp.where(named[k], counts, 0.0), axis=1).astype(i32)
            for k in range(2)
        ]
    )
    code_two = jnp.stack([code, cx(code, 2)])
    code_core = cx(code_two, 1)
    codes = jnp.concatenate([code_two[0], code_core[0], code_two[1], code_core[1]], axis=0)
    which, rank = codes // CAP, codes % CAP
    ids = jnp.where(which // EL == c, ((which - zi) % EL) * CAP + rank, -1).astype(i32)

    def dispatch(own, dep=None):
        far = cx(own, 2)
        near = cx(own, 1)
        both_far = cx(far, 1)
        packs = call(
            pack_body, [sds((4 * CAP, HALF), bf16)] * 4, name="pack"
        )(scalars, ids if dep is None else after(ids, *dep), own, near, far, both_far)
        return [packs[0]] + [zs(packs[s], s) for s in (1, 2, 3)]

    def sum_pieces(pieces, dep=None):
        total = pieces[0]
        if dep is not None:
            total = after(total, dep)
        for piece in pieces[1:]:
            total = total + piece.astype(f32)
        return total

    def over_tp(two):
        return (two[0].astype(f32) + yx(two[1]).astype(f32)).astype(bf16)

    def home(s, total):
        return total if s == 0 else zs(total, EL - s)

    def over_ctx(keep, send):
        got = cx(send, 1)
        far = (keep[1].astype(f32) + got[1].astype(f32)).astype(bf16)
        return keep[0].astype(f32) + got[0].astype(f32) + cx(far, 2).astype(f32)

    cot_h, cot_o = half(cotangent, y), half(cotangent, 1 - y)
    cot_rows = dispatch(cot_h)
    cot_pairs = [(rows, yx(rows)) for rows in cot_rows]

    positions = (c * ROWS + jnp.arange(ROWS, dtype=i32)).astype(f32)
    table = jnp.arange(128, dtype=i32)
    frequency = 10000.0 ** (-(table % 32).astype(f32) / 32)
    angles = positions[:, None] * frequency[None, :]
    cos = jnp.cos(angles)
    sin = jnp.sin(angles) * jnp.where(table % 64 < 32, -1.0, 1.0)[None, :]
    normed_one, queries, kv = call(
        qkv_body,
        [sds((ROWS, D), bf16), sds((ROWS, heads_width), bf16), sds((ROWS, 2 * heads_width), bf16)],
        us=3.0, name="qkv",
    )(
        scalars, tokens, gain_one[None, :], first, cos, sin,
        deps=[cot_pairs[0][1], *cot_rows[1:], expert_local],
    )
    kv_far = cx(kv, 2)
    kv_near = cx(kv, 1)
    kv_both = cx(kv_far, 1)
    kvs = (kv, kv_near, kv_far, kv_both)
    if small:
        expert_w = lax.all_to_all(
            after(expert_local, kv_near), "fsdp", 0, 0, tiled=True
        )
    before_attn = [cot_pairs[1][1], cot_pairs[2][1]]
    seq_ids = segments[0]
    seg_col = seq_ids[:, None]
    seg_row = lax.dynamic_slice_in_dim(seq_ids, c * ROWS, ROWS, 0)[None, :]
    attended, z_own, z_oth, lse = call(
        attn_body,
        [
            sds((ROWS, heads_width), bf16),
            sds((ROWS, HALF), f32),
            sds((ROWS, HALF), bf16),
            sds((8, ROWS), f32),
        ],
        scratch=[
            pltpu.VMEM((4 * ROWS, 2 * heads_width), bf16),
            pltpu.VMEM((4 * ROWS, ROWS), f32),
            pltpu.VMEM((4 * ROWS, ROWS), f32),
            pltpu.VMEM((heads_width, ROWS), f32),
        ],
        us=9.0, name="attn",
    )(scalars, queries, *kvs, seg_col, seg_row, out_w, deps=before_attn)
    tok_h = half(tokens, y).astype(f32)
    middle = tok_h + z_own + yx(z_oth).astype(f32)

    def whole_rows(own):
        return halves(y, own, yx(own))

    def both_halves(sums):
        return sums + yx(sums)

    square = both_halves(jnp.sum(middle * middle, axis=1))
    scale_two = lax.rsqrt(square / D + eps)[:, None]
    normal_two = middle * scale_two
    normed_two = (normal_two * gain_two_h[None, :]).astype(bf16)

    normed_two_oth = yx(normed_two)
    rows_in = dispatch(normed_two, [cot_pairs[3][1]])
    shared_w = gathered(after(shared_shard, rows_in[3]), 1)[None]
    saved, backs, sums, router_part = None, [], [], 0.0
    pairs = [(rows, yx(rows)) for rows in rows_in]
    for s in range(4):
        deps = [rows_in[1:], [pairs[2][1], pairs[3][1]], sums[:1], sums[1:2]][s]
        res = ffn(scalars, s, 4, *pairs[s], *cot_pairs[s], expert_w, extra, saved, deps)
        sums.append(over_tp(res[0]))
        backs.append(home(s, sums[s]))
        router_part = router_part + res[1][:, :E]
        saved = res[2:]
    ex_dgu, ex_y, ex_x, ex_de = [v.reshape(4 * ROWS, -1) for v in saved]

    grad_w = [
        lax.dot_general(a, b, (((0,), (0,)), ((), ())), preferred_element_type=f32)
        for a, b in ((ex_x, ex_dgu[:, :hidden]), (ex_x, ex_dgu[:, hidden:]), (ex_de, ex_y))
    ]
    if small:
        grad_w = [g.astype(bf16).reshape(4, D // 4, hidden) for g in grad_w]
        grad_w = grad_ready = jnp.stack(grad_w, axis=1)
        grad_w = lax.all_to_all(
            grad_w, "fsdp", 0, 0, tiled=True
        )
    else:
        grad_ready = saved[0]
        grad_w = jnp.stack([g.reshape(F, D // F, hidden) for g in grad_w], axis=1)
        grad_w = lax.psum_scatter(
            grad_w, "fsdp", scatter_dimension=0, axis_index_groups=outer, tiled=True
        )
        grad_w = lax.all_to_all(grad_w, "fsdp", 0, 0, axis_index_groups=inner, tiled=True)

    sh_back, sh_dgu, sh_y = ffn(
        scalars, 0, 1, normed_two, normed_two_oth, cot_h, cot_o, shared_w, None, None, [grad_ready]
    )
    sh_sum = sh_back[0].astype(f32) + yx(sh_back[1]).astype(f32)
    normed_full = halves(y, normed_two, normed_two_oth)
    shared_full = jnp.concatenate(
        [grad_of(normed_full, sh_dgu[0]), grad_of(cotangent, sh_y[0])], axis=1
    )
    shared_grad = lax.psum_scatter(
        shared_full.astype(bf16) if small else shared_full,
        ("fsdp", "ctx"), scatter_dimension=0, tiled=True,
    ).astype(f32)

    keep_b, send_b, keep_o, send_o = call(
        unpack_body, [sds((2, ROWS, HALF), bf16)] * 4, us=3.0, name="unpack"
    )(scalars, ids, *backs, deps=[sh_sum])
    back_h = over_ctx(keep_b, send_b) + sh_sum[:, :HALF]
    scaled = back_h * gain_two_h[None, :]
    mean_two = both_halves(jnp.sum(scaled * normal_two, axis=1))[:, None] / D
    ffn_gain_part = jnp.sum(back_h * normal_two, axis=0)
    middle_grad = cot_h.astype(f32) + scale_two * (scaled - normal_two * mean_two)
    dz_own = middle_grad.astype(bf16)
    dz_oth = yx(dz_own)
    dq, dkv_keep, dkv_send = call(
        attn_back_body,
        [sds((ROWS, heads_width), bf16)] + [sds((2, ROWS, 2 * heads_width), bf16)] * 2,
        scratch=[
            pltpu.VMEM((4 * ROWS, 2 * heads_width), bf16),
            pltpu.VMEM((4 * ROWS, ROWS), f32),
            pltpu.VMEM((ROWS, heads_width), bf16),
            pltpu.VMEM((8, ROWS), f32),
            pltpu.VMEM((heads_width, ROWS), f32),
        ],
        us=11.0, name="attn_back",
    )(
        scalars, queries, *kvs, seg_col, seg_row, lse, attended, dz_own, dz_oth, out_w, cos, sin,
    )
    dkv_near = cx(dkv_send, 1)
    kv_recv = cx((dkv_keep[1].astype(f32) + dkv_near[1].astype(f32)).astype(bf16), 2)
    dp, da_own, da_oth = call(
        proj_back_body,
        [sds((ROWS, 3 * heads_width), bf16), sds((ROWS, HALF), f32), sds((ROWS, HALF), bf16)],
        us=3.0, name="proj_back",
    )(scalars, dq, dkv_keep, dkv_near, kv_recv, first, cos, sin, deps=[grad_w])
    dense_pairs = [(normed_one, dp), (halves(y, dz_own, dz_oth), attended)]
    if small:
        dense_keep, dense_send = grad_blocks(back_offs, rows_own, dense_pairs)
    else:
        dense_keep = dp
    da_h = after(da_own, dense_keep) + yx(da_oth).astype(f32)
    tok_full = tokens.astype(f32)
    scale_one = lax.rsqrt(jnp.mean(tok_full * tok_full, axis=1, keepdims=True) + eps)
    normal_one = tok_h * scale_one
    scaled_one = da_h * gain_one_h[None, :]
    mean_one = both_halves(jnp.sum(scaled_one * normal_one, axis=1))[:, None] / D
    attn_gain_part = jnp.sum(da_h * normal_one, axis=0)
    tokens_grad_h = middle_grad + scale_one * (scaled_one - normal_one * mean_one)

    tokens_grad = whole_rows(tokens_grad_h.astype(bf16)).astype(f32)

    layer_h = middle + over_ctx(keep_o, send_o) + sh_sum[:, HALF:]
    layer_out = whole_rows(layer_h.astype(bf16))
    grad_w = after(grad_w, tokens_grad_h)
    expert_gate_up_grad = grad_w[:, :2].astype(f32)
    expert_down_grad = grad_w[:, 2].astype(f32).transpose(0, 2, 1)
    if small:
        dense_grad = reduce_far(reduce_near(dense_keep, dense_send), bf16, None, tokens_grad_h)
    else:
        dense_grad = dense_reduce(dense_pairs)
    qkv_grad = dense_grad[:, : 3 * heads_width].reshape(rows_own, 3, heads_width).transpose(1, 0, 2)
    out_grad = dense_grad[:, 3 * heads_width :].T
    shared_gate_up_grad = jnp.stack(
        [shared_grad[:, :shared_hidden], shared_grad[:, shared_hidden : 2 * shared_hidden]]
    )
    shared_down_grad = shared_grad[:, 2 * shared_hidden :].T

    def placed(part):
        first = y == 0
        return jnp.concatenate([jnp.where(first, part, 0.0), jnp.where(first, 0.0, part)])

    tail = jnp.concatenate(
        [router_part, placed(attn_gain_part)[:, None], placed(ffn_gain_part)[:, None]], axis=1
    )
    if small:
        order = back_offs // rows_own
        blocks = tail.reshape(16, rows_own * (E + 2))[order].reshape(2, 2, 4, rows_own * (E + 2))
        tail = reduce_far(reduce_near(blocks[:, 0], blocks[:, 1]), f32)
        tail = tail.reshape(rows_own, E + 2)
    else:
        tail = lax.psum_scatter(tail, ("fsdp", "ctx"), scatter_dimension=0, tiled=True)
    tail = tail + yx(tail)
    return (
        layer_out,
        tokens_grad,
        tail[:, E],
        qkv_grad,
        out_grad,
        tail[:, E + 1],
        tail[:, :E],
        expert_gate_up_grad,
        expert_down_grad,
        shared_gate_up_grad,
        shared_down_grad,
    )


def solution(mesh):
    return jax.shard_map(
        per_device,
        mesh=mesh,
        in_specs=(
            P(("fsdp", "ctx"), None),
            P("fsdp", None),
            P(("fsdp", "ctx"), None),
            P(("fsdp", "ctx")),
            P(None, ("fsdp", "ctx"), "tp"),
            P("tp", ("fsdp", "ctx")),
            P(("fsdp", "ctx")),
            P(("fsdp", "ctx"), None),
            P("ctx", None, "fsdp", "tp"),
            P("ctx", "tp", "fsdp"),
            P(None, ("fsdp", "ctx"), "tp"),
            P("tp", ("fsdp", "ctx")),
            P(("fsdp", "ctx"), None),
        ),
        out_specs=(
            P(("fsdp", "ctx"), None),
            P(("fsdp", "ctx"), None),
            P(("fsdp", "ctx")),
            P(None, ("fsdp", "ctx"), "tp"),
            P("tp", ("fsdp", "ctx")),
            P(("fsdp", "ctx")),
            P(("fsdp", "ctx"), None),
            P("ctx", None, "fsdp", "tp"),
            P("ctx", "tp", "fsdp"),
            P(None, ("fsdp", "ctx"), "tp"),
            P("tp", ("fsdp", "ctx")),
        ),
        check_vma=False,
    )
```

time: 757 us -> 641 us (0.85)
  starting transfers between devices: 169 us -> 95.7 us
  local copies, waits for them, and re-layouts: 60.3 us -> 36.5 us
  matrix products: 33.2 us -> 15.9 us
  Pallas kernels: 135 us -> 122 us
  between operations: 2 us -> 15 us
    ppermute x39 -> x15, waiting for transfers between devices: 174 us -> 92.9 us  [zs(): lax.ppermute(v, 'fsdp', [(i, i // EL * EL + (i % EL + s) % EL) for i in r...]
    ppermute x28 -> x23, waiting for transfers between devices: 32.1 us -> 88.6 us  [yx(): return lax.ppermute(v, 'tp', [(0, 1), (1, 0)])]
    ppermute x39 -> x15, starting transfers between devices: 75.2 us -> 19.9 us  [zs(): lax.ppermute(v, 'fsdp', [(i, i // EL * EL + (i % EL + s) % EL) for i in r...]
    ppermute x27 -> x21, waiting for transfers between devices: 85.8 us -> 51.6 us  [cx(): return lax.ppermute(v, 'ctx', [(i, i ^ flip) for i in range(C)])]
    all_gather x0 -> x2, waiting for transfers between devices: none -> 33.2 us  [gathered(): return lax.all_gather(shard, ('fsdp', 'ctx'), axis=axis, tiled=True)]
    ppermute x27 -> x21, starting transfers between devices: 63.9 us -> 39 us  [cx(): return lax.ppermute(v, 'ctx', [(i, i ^ flip) for i in range(C)])]
    all_to_all x0 -> x2, waiting for transfers between devices: none -> 24.4 us  [the longest x1 24.4 us: per_device(): grad_w = lax.all_to_all(grad_w, 'fsdp', 0, 0, tiled=True)]
    pallas_call x14 -> x8, Pallas kernels: 73 us -> 49.4 us  [run(): pl.pallas_call(inner, out_shape=outs, in_specs=[SMEM] + [VM] * len(args)...]
  transfers between devices with their start and end apart: 94 -> 64, of which waited for: 27 -> 31; matrix products, arithmetic and copies ran while one was open for 19% -> 15% of each run, Pallas kernels for 18% -> 18%
where the time goes in v2:
time: 641 us; the launch traced here: 633 us
  waiting for transfers between devices  291 us (45%)
  Pallas kernels  122 us (19%)
  starting transfers between devices  95.7 us (15%)
  other arithmetic  56.5 us (9%)
  local copies, waits for them, and re-layouts  36.5 us (6%)
  matrix products  15.9 us (2%)
  between operations  15 us (2%)
    ppermute x15, waiting for transfers between devices, zs(): lax.ppermute(v, 'fsdp', [(i, i // EL * EL + (i % EL + s) % EL) for i in r...  92.9 us
    ppermute x23, waiting for transfers between devices, yx(): return lax.ppermute(v, 'tp', [(0, 1), (1, 0)])  88.6 us
    pallas_call x5, Pallas kernels, ffn(): pl.pallas_call(functools.partial(ffn_body, routed), grid=(1,), out_shape=...  72.7 us
    ppermute x21, waiting for transfers between devices, cx(): return lax.ppermute(v, 'ctx', [(i, i ^ flip) for i in range(C)])  51.6 us
    pallas_call x8, Pallas kernels, run(): pl.pallas_call(inner, out_shape=outs, in_specs=[SMEM] + [VM] * len(args)...  49.4 us
    ppermute x21, starting transfers between devices, cx(): return lax.ppermute(v, 'ctx', [(i, i ^ flip) for i in range(C)])  39 us
    all_gather x2, waiting for transfers between devices, gathered(): return lax.all_gather(shard, ('fsdp', 'ctx'), axis=axis, tiled=True)  33.2 us
    all_to_all x1, waiting for transfers between devices, per_device(): grad_w = lax.all_to_all(grad_w, 'fsdp', 0, 0, tiled=True)  24.4 us
  transfers between devices with their start and end apart: 64, of which 31 were waited for; matrix products, arithmetic and copies ran while one was open for 15% of the time, Pallas kernels for 18%

profile of v2, /device:TPU:0, one launch (start us, length us, event | category | flops | bytes accessed | tf_op | source)
XLA Modules:
  0.0 632.7 jit_solution(3984452920746820771)
XLA Ops:
  14.1 2.9 collective-permute-start.3
  19.3 4.5 pad_maximum_fusion.refs_10_
  23.8 3.6 collective-permute-done
  30.7 3.7 pack.2
  34.5 2.3 collective-permute-start.5
  38.4 2.6 collective-permute-start.7
  42.3 33.2 %all-gather.3.cloned.1.call-done.refs_3_.refs_5_ = bf16[768,1664]{1,0:T(8,128)(2,1)} async-done(((bf16[48,1664]{1,0:T(8,128)(2,1)}), bf16[768,1664]{1,0:T(8,128)(2,1)}) %all-gather.3.cloned.1.call-update) | async-done | bytes 2555920 | tf_op jit(solution)/shard_map/all_gather | solution.py:457
  79.2 5.1 qkv.1
  84.7 2.4 collective-permute-done.9.refs_3_
  87.0 10.0 %all-to-all-start = ((bf16[4,3,192,1024]{3,2,1,0:T(8,128)(2,1)}), bf16[4,3,192,1024]{3,2,1,0:T(8,128)(2,1)}, u32[]{:S(2)}, u32[]{:S(2)}) async-start(bf16[4,3,192,1024]{3,2,1,0:T(8,128)(2,1)} %pad_maximum_fusion.refs_10_), calls=%async_computation | async-start | bytes 9437184 | tf_op jit(solution)/shard_map/all_to_all | solution.py:584
  98.6 17.9 %collective-permute-done.10.refs_4_ = bf16[512,768]{1,0:T(8,128)(2,1)} collective-permute-done((bf16[512,768]{1,0:T(8,128)(2,1)S(1)}, bf16[512,768]{1,0:T(8,128)(2,1)}, u32[]{:S(2)}, u32[]{:S(2)}) %collective-permute-start.10) | collective-permute-done | bytes 786464 | tf_op jit(solution)/shard_map/ppermute | solution.py:438
  122.5 5.9 collective-permute-done.12.refs_9_.wb
  128.4 8.0 %collective-permute-done.13.refs_10_.wb = bf16[512,384]{1,0:T(8,128)(2,1)S(1)} collective-permute-done((bf16[512,384]{1,0:T(8,128)(2,1)S(1)}, bf16[512,384]{1,0:T(8,128)(2,1)S(1)}, u32[]{:S(2)}, u32[]{:S(2)}) %collective-permute-start.13) | collective-permute-done | bytes 393248 | tf_op jit(solution)/shard_map/ppermute | solution.py:435
  137.5 9.1 %attn.1 = (bf16[512,384]{1,0:T(8,128)(2,1)}, f32[512,384]{1,0:T(8,128)}, bf16[512,384]{1,0:T(8,128)(2,1)}, f32[8,512]{1,0:T(8,128)}) custom-call(s32[3]{0:T(128)} %pad_add_fusion.2.refs_0_.sc.rt, bf16[512,384]{1,0:T(8,128)(2,1)} %get-tuple-element.75.refs_1_, bf16[512,768]{1,0:T(8,128)(2,1)} %get-tuple-element.76.refs_2_, ...), custom_call_target="tpu_custom_call" | custom-call | flops 8999999488 | tf_op jit(solution)/shard_map/attn/pallas_call | solution.py:50
  147.1 8.6 %collective-permute-done.14 = bf16[512,384]{1,0:T(8,128)(2,1)S(1)} collective-permute-done((bf16[512,384]{1,0:T(8,128)(2,1)}, bf16[512,384]{1,0:T(8,128)(2,1)S(1)}, u32[]{:S(2)}, u32[]{:S(2)}) %collective-permute-start.14) | collective-permute-done | bytes 393248 | tf_op jit(solution)/shard_map/ppermute | solution.py:435
  157.8 2.9 collective-permute-done.16
  160.9 9.9 %collective-permute-start.18 = (bf16[512,384]{1,0:T(8,128)(2,1)S(1)}, bf16[512,384]{1,0:T(8,128)(2,1)S(1)}, u32[]{:S(2)}, u32[]{:S(2)}) collective-permute-start(bf16[512,384]{1,0:T(8,128)(2,1)S(1)} %multiply_convert_fusion.refs_2_.xa), channel_id=1, source_target_pairs={{0,4},{2,6},{4,0},{6,2},{1,5},{3,7},{5,1},{7,3},{8,12},{10,14},{12... | collective-permute-start | bytes 1179656 | tf_op jit(solution)/shard_map/ppermute | solution.py:438
  173.3 5.5 collective-permute-done.18.refs_4_
  178.8 2.2 collective-permute-start.19
  183.1 3.7 pack.3
  186.9 4.8 collective-permute-start.23
  192.4 17.7 %collective-permute-done.23.refs_2_.xa = bf16[512,384]{1,0:T(8,128)(2,1)S(1)} collective-permute-done((bf16[512,384]{1,0:T(8,128)(2,1)}, bf16[512,384]{1,0:T(8,128)(2,1)S(1)}, u32[]{:S(2)}, u32[]{:S(2)}) %collective-permute-start.23) | collective-permute-done | bytes 393248 | tf_op jit(solution)/shard_map/ppermute | solution.py:441
  214.4 13.5 %collective-permute-done.21.refs_0_.xa = bf16[512,384]{1,0:T(8,128)(2,1)S(1)} collective-permute-done((bf16[512,384]{1,0:T(8,128)(2,1)}, bf16[512,384]{1,0:T(8,128)(2,1)S(1)}, u32[]{:S(2)}, u32[]{:S(2)}) %collective-permute-start.21) | collective-permute-done | bytes 393248 | tf_op jit(solution)/shard_map/ppermute | solution.py:441
  228.0 20.9 %collective-permute-done.22.refs_1_.xa = bf16[512,384]{1,0:T(8,128)(2,1)S(1)} collective-permute-done((bf16[512,384]{1,0:T(8,128)(2,1)}, bf16[512,384]{1,0:T(8,128)(2,1)S(1)}, u32[]{:S(2)}, u32[]{:S(2)}) %collective-permute-start.22) | collective-permute-done | bytes 393248 | tf_op jit(solution)/shard_map/ppermute | solution.py:441
  250.1 12.8 %expert_ffn.4 = (bf16[2,512,768]{2,1,0:T(8,128)(2,1)}, f32[768,128]{1,0:T(8,128)}, bf16[4,512,2048]{2,1,0:T(8,128)(2,1)}, bf16[4,512,1024]{2,1,0:T(8,128)(2,1)},...) custom-call(s32[3]{0:T(128)} %pad_add_fusion.2.refs_0_.sc.rt, bf16[512,384]{1,0:T(8,128)(2,1)} %get-tuple-element.80.xa, ...), custom_call_target="tpu_custom_call" | custom-call | flops 6000000000 | tf_op jit(solution)/shard_map/expert_ffn/pallas_call | solution.py:369
  263.9 13.5 %expert_ffn.5 = (bf16[2,512,768]{2,1,0:T(8,128)(2,1)}, f32[768,128]{1,0:T(8,128)}, bf16[4,512,2048]{2,1,0:T(8,128)(2,1)}, bf16[4,512,1024]{2,1,0:T(8,128)(2,1)},...) custom-call(s32[3]{0:T(128)} %pad_add_fusion.2.refs_0_.sc.rt, ...), custom_call_target="tpu_custom_call", output_to_operand_aliasing={{2}: (9, {}), {3}: (10, {}), {4}: (11, {}), {5}: (12, {})} | custom-call | flops 6000000000 | tf_op jit(solution)/shard_map/expert_ffn/pallas_call | solution.py:369
  282.6 16.7 %collective-permute-done.28 = bf16[512,768]{1,0:T(8,128)(2,1)S(1)} collective-permute-done((bf16[512,768]{1,0:T(8,128)(2,1)S(1)}, bf16[512,768]{1,0:T(8,128)(2,1)S(1)}, u32[]{:S(2)}, u32[]{:S(2)}) %collective-permute-start.28) | collective-permute-done | bytes 786464 | tf_op jit(solution)/shard_map/ppermute | solution.py:435
  299.6 16.6 %collective-permute-done.24 = bf16[512,768]{1,0:T(8,128)(2,1)S(1)} collective-permute-done((bf16[512,768]{1,0:T(8,128)(2,1)S(1)}, bf16[512,768]{1,0:T(8,128)(2,1)S(1)}, u32[]{:S(2)}, u32[]{:S(2)}) %collective-permute-start.24) | collective-permute-done | bytes 786464 | tf_op jit(solution)/shard_map/ppermute | solution.py:435
  317.2 13.2 %expert_ffn.6 = (bf16[2,512,768]{2,1,0:T(8,128)(2,1)}, f32[768,128]{1,0:T(8,128)}, bf16[4,512,2048]{2,1,0:T(8,128)(2,1)}, bf16[4,512,1024]{2,1,0:T(8,128)(2,1)},...) custom-call(s32[3]{0:T(128)} %pad_add_fusion.2.refs_0_.sc.rt, ...), custom_call_target="tpu_custom_call", output_to_operand_aliasing={{2}: (8, {}), {3}: (9, {}), {4}: (10, {}), {5}: (11, {})} | custom-call | flops 6000000000 | tf_op jit(solution)/shard_map/expert_ffn/pallas_call | solution.py:369
  330.5 22.0 %expert_ffn.7 = (bf16[2,512,768]{2,1,0:T(8,128)(2,1)}, f32[768,128]{1,0:T(8,128)}, bf16[4,512,2048]{2,1,0:T(8,128)(2,1)}, bf16[4,512,1024]{2,1,0:T(8,128)(2,1)},...) custom-call(s32[3]{0:T(128)} %pad_add_fusion.2.refs_0_.sc.rt, ...), custom_call_target="tpu_custom_call", output_to_operand_aliasing={{2}: (8, {}), {3}: (9, {}), {4}: (10, {}), {5}: (11, {})} | custom-call | flops 6000000000 | tf_op jit(solution)/shard_map/expert_ffn/pallas_call | solution.py:369
  352.4 2.2 slice_bitcast_fusion.1
  357.6 5.9 fusion.5
  363.6 3.5 fusion.8
  367.1 3.5 bitcast_convert_fusion
  370.5 2.5 pad_maximum_fusion.1.refs_0_
  373.7 11.3 %shared_ffn.1 = (bf16[2,512,768]{2,1,0:T(8,128)(2,1)}, bf16[1,512,2048]{2,1,0:T(8,128)(2,1)}, bf16[1,512,1024]{2,1,0:T(8,128)(2,1)}) custom-call(s32[3]{0:T(128)} %pad_add_fusion.2.refs_0_.sc.rt, bf16[512,384]{1,0:T(8,128)(2,1)} %copy-done.30, bf16[512,384]{1,0:T(8,128)(2,1)} %copy-done.28, bf16[512,384]{1,0:T(8,128)(2,1)} %copy-done.6, ...), custom_call_target="tpu_custom_call" | custom-call | flops 6000000000 | tf_op jit(solution)/shard_map/shared_ffn/pallas_call | solution.py:369
  392.0 12.9 %collective-permute-done.35 = bf16[512,768]{1,0:T(8,128)(2,1)S(1)} collective-permute-done((bf16[512,768]{1,0:T(8,128)(2,1)S(1)}, bf16[512,768]{1,0:T(8,128)(2,1)S(1)}, u32[]{:S(2)}, u32[]{:S(2)}) %collective-permute-start.35) | collective-permute-done | bytes 786464 | tf_op jit(solution)/shard_map/ppermute | solution.py:435
  406.1 5.5 collective-permute-done.33.refs_5_
  411.7 28.5 %collective-permute-done.31.refs_4_ = bf16[512,768]{1,0:T(8,128)(2,1)S(1)} collective-permute-done((bf16[512,768]{1,0:T(8,128)(2,1)S(1)}, bf16[512,768]{1,0:T(8,128)(2,1)S(1)}, u32[]{:S(2)}, u32[]{:S(2)}) %collective-permute-start.31) | collective-permute-done | bytes 786464 | tf_op jit(solution)/shard_map/ppermute | solution.py:441
  441.1 4.9 unpack.1
  446.5 4.9 all-to-all-start.1
  451.5 2.1 fusion.34
  458.3 7.5 %collective-permute-done.37 = bf16[512,384]{1,0:T(8,128)(2,1)} collective-permute-done((bf16[512,384]{1,0:T(8,128)(2,1)}, bf16[512,384]{1,0:T(8,128)(2,1)}, u32[]{:S(2)}, u32[]{:S(2)}) %collective-permute-start.37) | collective-permute-done | bytes 393248 | tf_op jit(solution)/shard_map/ppermute | solution.py:438
  465.8 7.7 %collective-permute-done.40 = bf16[512,384]{1,0:T(8,128)(2,1)} collective-permute-done((bf16[512,384]{1,0:T(8,128)(2,1)}, bf16[512,384]{1,0:T(8,128)(2,1)}, u32[]{:S(2)}, u32[]{:S(2)}) %collective-permute-start.40) | collective-permute-done | bytes 393248 | tf_op jit(solution)/shard_map/ppermute | solution.py:438
  473.5 3.4 multiply_reduce_fusion.1
  477.7 2.8 collective-permute-done.41
  483.8 7.4 %collective-permute-done.42.refs_11_ = bf16[512,384]{1,0:T(8,128)(2,1)} collective-permute-done((bf16[512,384]{1,0:T(8,128)(2,1)S(1)}, bf16[512,384]{1,0:T(8,128)(2,1)}, u32[]{:S(2)}, u32[]{:S(2)}) %collective-permute-start.42) | collective-permute-done | bytes 393248 | tf_op jit(solution)/shard_map/ppermute | solution.py:435
  491.2 12.0 %attn_back.1 = (bf16[512,384]{1,0:T(8,128)(2,1)}, bf16[2,512,768]{2,1,0:T(8,128)(2,1)}, bf16[2,512,768]{2,1,0:T(8,128)(2,1)}) custom-call(s32[3]{0:T(128)} %pad_add_fusion.2.refs_0_.sc.rt, bf16[512,384]{1,0:T(8,128)(2,1)} %get-tuple-element.75.refs_1_, bf16[512,768]{1,0:T(8,128)(2,1)} %get-tuple-element.76.refs_2_, ...), custom_call_target="tpu_custom_call" | custom-call | flops 11000000512 | tf_op jit(solution)/shard_map/attn_back/pallas_call | solution.py:50
  503.2 2.8 collective-permute-start.43
  510.5 2.6 pad_maximum_fusion.2
  514.9 2.4 fusion.27
  517.3 11.7 %collective-permute-start.44 = (bf16[512,768]{1,0:T(8,128)(2,1)}, bf16[512,768]{1,0:T(8,128)(2,1)}, u32[]{:S(2)}, u32[]{:S(2)}) collective-permute-start(bf16[512,768]{1,0:T(8,128)(2,1)} %fusion.27), channel_id=1, source_target_pairs={{0,4},{2,6},{4,0},{6,2},{1,5},{3,7},{5,1},{7,3},{8,12},{10,14},{12... | collective-permute-start | bytes 2359304 | tf_op jit(solution)/shard_map/ppermute | solution.py:438
  532.1 24.4 %all-to-all-done.1.refs_8_ = bf16[4,3,192,1024]{3,2,1,0:T(8,128)(2,1)} async-done(((bf16[4,3,192,1024]{3,2,1,0:T(8,128)(2,1)}), bf16[4,3,192,1024]{3,2,1,0:T(8,128)(2,1)}, u32[]{:S(2)}, u32[]{:S(2)}) %all-to-all-start.1) | async-done | bytes 4718624 | tf_op jit(solution)/shard_map/all_to_all | solution.py:642
  556.6 5.7 proj_back.1
  564.0 5.2 grad_blocks.1
  569.2 3.6 collective-permute-done.45
  582.8 2.4 collective-permute-start.51
  586.6 5.3 slice_convert_fusion
  593.4 2.0 fusion.33
  596.0 3.5 convert_bitcast_fusion
  603.2 5.5 collective-permute-done.55
  612.0 2.8 collective-permute-start.58
  614.9 3.0 collective-permute-done.56
  617.9 3.8 collective-permute-done.57
  (337 shorter events, 106.8 us)
Async XLA Ops:
  7.2 68.3 %all-gather.3.cloned.1.call-start = ((), (), s32[]{:S(2)}) async-start(), calls=%async_computation.3 | async-start | bytes 2715648 | tf_op jit(solution)/shard_map/all_gather | solution.py:457
  14.1 13.9 %collective-permute-start.3 = (bf16[512,384]{1,0:T(8,128)(2,1)S(1)}, bf16[512,384]{1,0:T(8,128)(2,1)S(1)}, u32[]{:S(2)}, u32[]{:S(2)}) collective-permute-start(bf16[512,384]{1,0:T(8,128)(2,1)S(1)} %get-tuple-element.202.refs_2_.wa), channel_id=1, source_target_pairs={{0,4},{2,6},{4,0},{6,2},{1,5},{3,7},{5,1},{7,3},{8,12},{10,14},{12... | collective-permute-start | bytes 1179656 | tf_op jit(solution)/shard_map/ppermute | solution.py:438
  17.0 12.2 %collective-permute-start.2 = (bf16[512,384]{1,0:T(8,128)(2,1)S(1)}, bf16[512,384]{1,0:T(8,128)(2,1)S(1)}, u32[]{:S(2)}, u32[]{:S(2)}) collective-permute-start(bf16[512,384]{1,0:T(8,128)(2,1)S(1)} %get-tuple-element.202.refs_2_.wa), channel_id=1, source_target_pairs={{0,2},{2,0},{4,6},{6,4},{1,3},{3,1},{5,7},{7,5},{8,10},{10,8},{12,... | collective-permute-start | bytes 1179656 | tf_op jit(solution)/shard_map/ppermute | solution.py:438
  17.4 10.0 %collective-permute-start = (s32[2,512]{1,0:T(2,128)S(1)}, s32[2,512]{1,0:T(2,128)S(1)}, u32[]{:S(2)}, u32[]{:S(2)}) collective-permute-start(s32[2,512]{1,0:T(2,128)S(1)} %get-tuple-element.215), channel_id=1, source_target_pairs={{0,4},{2,6},{4,0},{6,2},{1,5},{3,7},{5,1},{7,3},{8,12},{10,14},{12... | collective-permute-start | bytes 12296 | tf_op jit(solution)/shard_map/ppermute | solution.py:438
  27.4 1.2 collective-permute-start.1
  28.0 1.9 collective-permute-start.4
  34.5 43.6 %collective-permute-start.5 = (bf16[512,384]{1,0:T(8,128)(2,1)}, bf16[512,384]{1,0:T(8,128)(2,1)S(1)}, u32[]{:S(2)}, u32[]{:S(2)}) collective-permute-start(bf16[512,384]{1,0:T(8,128)(2,1)} %get-tuple-element.71.wa), channel_id=1, source_target_pairs={{0,1},{1,0},{2,3},{3,2},{4,5},{5,4},{6,7},{7,6},{8,9},{9,8},{10,11... | collective-permute-start | bytes 1179656 | tf_op jit(solution)/shard_map/ppermute | solution.py:435
  36.8 41.2 %collective-permute-start.6 = (bf16[512,384]{1,0:T(8,128)(2,1)}, bf16[512,384]{1,0:T(8,128)(2,1)S(1)}, u32[]{:S(2)}, u32[]{:S(2)}) collective-permute-start(bf16[512,384]{1,0:T(8,128)(2,1)} %get-tuple-element.72), channel_id=1, source_target_pairs={{0,8},{8,16},{16,24},{24,0},{1,9},{9,17},{17,25},{25,1},{2,10},{10... | collective-permute-start | bytes 1179656 | tf_op jit(solution)/shard_map/ppermute | solution.py:441
  38.4 39.7 %collective-permute-start.7 = (bf16[512,384]{1,0:T(8,128)(2,1)}, bf16[512,384]{1,0:T(8,128)(2,1)S(1)}, u32[]{:S(2)}, u32[]{:S(2)}) collective-permute-start(bf16[512,384]{1,0:T(8,128)(2,1)} %get-tuple-element.73), channel_id=1, source_target_pairs={{0,16},{8,24},{16,0},{24,8},{1,17},{9,25},{17,1},{25,9},{2,18},{10... | collective-permute-start | bytes 1179656 | tf_op jit(solution)/shard_map/ppermute | solution.py:441
  41.0 37.1 %collective-permute-start.8 = (bf16[512,384]{1,0:T(8,128)(2,1)}, bf16[512,384]{1,0:T(8,128)(2,1)S(1)}, u32[]{:S(2)}, u32[]{:S(2)}) collective-permute-start(bf16[512,384]{1,0:T(8,128)(2,1)} %get-tuple-element.74), channel_id=1, source_target_pairs={{0,24},{8,0},{16,8},{24,16},{1,25},{9,1},{17,9},{25,17},{2,26},{10... | collective-permute-start | bytes 1179656 | tf_op jit(solution)/shard_map/ppermute | solution.py:441
  84.4 2.7 collective-permute-start.9
  87.0 162.3 %all-to-all-start = ((bf16[4,3,192,1024]{3,2,1,0:T(8,128)(2,1)}), bf16[4,3,192,1024]{3,2,1,0:T(8,128)(2,1)}, u32[]{:S(2)}, u32[]{:S(2)}) async-start(bf16[4,3,192,1024]{3,2,1,0:T(8,128)(2,1)} %pad_maximum_fusion.refs_10_), calls=%async_computation | async-start | bytes 9437184 | tf_op jit(solution)/shard_map/all_to_all | solution.py:584
  97.0 276.0 %all-gather.5.cloned.1.call-start = ((), (), s32[]{:S(2)}) async-start(), calls=%async_computation.4 | async-start | bytes 5013504 | tf_op jit(solution)/shard_map/all_gather | solution.py:457
  97.0 19.5 %collective-permute-start.10 = (bf16[512,768]{1,0:T(8,128)(2,1)S(1)}, bf16[512,768]{1,0:T(8,128)(2,1)}, u32[]{:S(2)}, u32[]{:S(2)}) collective-permute-start(bf16[512,768]{1,0:T(8,128)(2,1)S(1)} %copy-done.55), channel_id=1, source_target_pairs={{0,4},{2,6},{4,0},{6,2},{1,5},{3,7},{5,1},{7,3},{8,12},{10,14},{12... | collective-permute-start | bytes 2359304 | tf_op jit(solution)/shard_map/ppermute | solution.py:438
  116.5 20.0 %collective-permute-start.11 = (bf16[512,768]{1,0:T(8,128)(2,1)}, bf16[512,768]{1,0:T(8,128)(2,1)S(1)}, u32[]{:S(2)}, u32[]{:S(2)}) collective-permute-start(bf16[512,768]{1,0:T(8,128)(2,1)} %collective-permute-done.10.refs_4_), channel_id=1, source_target_pairs={{0,2},{2,0},{4,6},{6,4},{1,3},{3,1},{5,7},{7,5},{8,10},{10,8},{12,... | collective-permute-start | bytes 2359304 | tf_op jit(solution)/shard_map/ppermute | solution.py:438
  116.5 11.9 %collective-permute-start.12 = (bf16[512,384]{1,0:T(8,128)(2,1)S(1)}, bf16[512,384]{1,0:T(8,128)(2,1)S(1)}, u32[]{:S(2)}, u32[]{:S(2)}) collective-permute-start(bf16[512,384]{1,0:T(8,128)(2,1)S(1)} %copy-done.41), channel_id=1, source_target_pairs={{0,1},{1,0},{2,3},{3,2},{4,5},{5,4},{6,7},{7,6},{8,9},{9,8},{10,11... | collective-permute-start | bytes 1179656 | tf_op jit(solution)/shard_map/ppermute | solution.py:435
  117.0 19.4 %collective-permute-start.13 = (bf16[512,384]{1,0:T(8,128)(2,1)S(1)}, bf16[512,384]{1,0:T(8,128)(2,1)S(1)}, u32[]{:S(2)}, u32[]{:S(2)}) collective-permute-start(bf16[512,384]{1,0:T(8,128)(2,1)S(1)} %copy-done.39), channel_id=1, source_target_pairs={{0,1},{1,0},{2,3},{3,2},{4,5},{5,4},{6,7},{7,6},{8,9},{9,8},{10,11... | collective-permute-start | bytes 1179656 | tf_op jit(solution)/shard_map/ppermute | solution.py:435
  146.5 9.1 %collective-permute-start.14 = (bf16[512,384]{1,0:T(8,128)(2,1)}, bf16[512,384]{1,0:T(8,128)(2,1)S(1)}, u32[]{:S(2)}, u32[]{:S(2)}) collective-permute-start(bf16[512,384]{1,0:T(8,128)(2,1)} %get-tuple-element.78), channel_id=1, source_target_pairs={{0,1},{1,0},{2,3},{3,2},{4,5},{5,4},{6,7},{7,6},{8,9},{9,8},{10,11... | collective-permute-start | bytes 1179656 | tf_op jit(solution)/shard_map/ppermute | solution.py:435
  157.1 3.6 collective-permute-start.16
  160.9 17.9 %collective-permute-start.18 = (bf16[512,384]{1,0:T(8,128)(2,1)S(1)}, bf16[512,384]{1,0:T(8,128)(2,1)S(1)}, u32[]{:S(2)}, u32[]{:S(2)}) collective-permute-start(bf16[512,384]{1,0:T(8,128)(2,1)S(1)} %multiply_convert_fusion.refs_2_.xa), channel_id=1, source_target_pairs={{0,4},{2,6},{4,0},{6,2},{1,5},{3,7},{5,1},{7,3},{8,12},{10,14},{12... | collective-permute-start | bytes 1179656 | tf_op jit(solution)/shard_map/ppermute | solution.py:438
  170.8 10.6 %collective-permute-start.15 = (bf16[512,384]{1,0:T(8,128)(2,1)S(1)}, bf16[512,384]{1,0:T(8,128)(2,1)S(1)}, u32[]{:S(2)}, u32[]{:S(2)}) collective-permute-start(bf16[512,384]{1,0:T(8,128)(2,1)S(1)} %copy-done.37), channel_id=1, source_target_pairs={{0,1},{1,0},{2,3},{3,2},{4,5},{5,4},{6,7},{7,6},{8,9},{9,8},{10,11... | collective-permute-start | bytes 1179656 | tf_op jit(solution)/shard_map/ppermute | solution.py:435
  171.3 10.1 %collective-permute-start.17 = (bf16[512,384]{1,0:T(8,128)(2,1)S(1)}, bf16[512,384]{1,0:T(8,128)(2,1)S(1)}, u32[]{:S(2)}, u32[]{:S(2)}) collective-permute-start(bf16[512,384]{1,0:T(8,128)(2,1)S(1)} %multiply_convert_fusion.refs_2_.xa), channel_id=1, source_target_pairs={{0,2},{2,0},{4,6},{6,4},{1,3},{3,1},{5,7},{7,5},{8,10},{10,8},{12,... | collective-permute-start | bytes 1179656 | tf_op jit(solution)/shard_map/ppermute | solution.py:438
  178.8 3.5 collective-permute-start.19
  186.9 23.2 %collective-permute-start.23 = (bf16[512,384]{1,0:T(8,128)(2,1)}, bf16[512,384]{1,0:T(8,128)(2,1)S(1)}, u32[]{:S(2)}, u32[]{:S(2)}) collective-permute-start(bf16[512,384]{1,0:T(8,128)(2,1)} %get-tuple-element.84), channel_id=1, source_target_pairs={{0,24},{8,0},{16,8},{24,16},{1,25},{9,1},{17,9},{25,17},{2,26},{10... | collective-permute-start | bytes 1179656 | tf_op jit(solution)/shard_map/ppermute | solution.py:441
  210.1 17.9 %collective-permute-start.21 = (bf16[512,384]{1,0:T(8,128)(2,1)}, bf16[512,384]{1,0:T(8,128)(2,1)S(1)}, u32[]{:S(2)}, u32[]{:S(2)}) collective-permute-start(bf16[512,384]{1,0:T(8,128)(2,1)} %get-tuple-element.82), channel_id=1, source_target_pairs={{0,8},{8,16},{16,24},{24,0},{1,9},{9,17},{17,25},{25,1},{2,10},{10... | collective-permute-start | bytes 1179656 | tf_op jit(solution)/shard_map/ppermute | solution.py:441
  210.8 38.0 %collective-permute-start.22 = (bf16[512,384]{1,0:T(8,128)(2,1)}, bf16[512,384]{1,0:T(8,128)(2,1)S(1)}, u32[]{:S(2)}, u32[]{:S(2)}) collective-permute-start(bf16[512,384]{1,0:T(8,128)(2,1)} %get-tuple-element.83), channel_id=1, source_target_pairs={{0,16},{8,24},{16,0},{24,8},{1,17},{9,25},{17,1},{25,9},{2,18},{10... | collective-permute-start | bytes 1179656 | tf_op jit(solution)/shard_map/ppermute | solution.py:441
  210.8 38.6 %collective-permute-start.20 = (bf16[512,384]{1,0:T(8,128)(2,1)}, bf16[512,384]{1,0:T(8,128)(2,1)S(1)}, u32[]{:S(2)}, u32[]{:S(2)}) collective-permute-start(bf16[512,384]{1,0:T(8,128)(2,1)} %get-tuple-element.80.xa), channel_id=1, source_target_pairs={{0,1},{1,0},{2,3},{3,2},{4,5},{5,4},{6,7},{7,6},{8,9},{9,8},{10,11... | collective-permute-start | bytes 1179656 | tf_op jit(solution)/shard_map/ppermute | solution.py:435
  212.9 50.0 %collective-permute-start.27 = (bf16[512,384]{1,0:T(8,128)(2,1)S(1)}, bf16[512,384]{1,0:T(8,128)(2,1)S(1)}, u32[]{:S(2)}, u32[]{:S(2)}) collective-permute-start(bf16[512,384]{1,0:T(8,128)(2,1)S(1)} %collective-permute-done.23.refs_2_.xa), channel_id=1, source_target_pairs={{0,1},{1,0},{2,3},{3,2},{4,5},{5,4},{6,7},{7,6},{8,9},{9,8},{10,11... | collective-permute-start | bytes 1179656 | tf_op jit(solution)/shard_map/ppermute | solution.py:435
  228.0 34.9 %collective-permute-start.25 = (bf16[512,384]{1,0:T(8,128)(2,1)S(1)}, bf16[512,384]{1,0:T(8,128)(2,1)S(1)}, u32[]{:S(2)}, u32[]{:S(2)}) collective-permute-start(bf16[512,384]{1,0:T(8,128)(2,1)S(1)} %collective-permute-done.21.refs_0_.xa), channel_id=1, source_target_pairs={{0,1},{1,0},{2,3},{3,2},{4,5},{5,4},{6,7},{7,6},{8,9},{9,8},{10,11... | collective-permute-start | bytes 1179656 | tf_op jit(solution)/shard_map/ppermute | solution.py:435
  248.8 14.1 %collective-permute-start.26 = (bf16[512,384]{1,0:T(8,128)(2,1)S(1)}, bf16[512,384]{1,0:T(8,128)(2,1)S(1)}, u32[]{:S(2)}, u32[]{:S(2)}) collective-permute-start(bf16[512,384]{1,0:T(8,128)(2,1)S(1)} %collective-permute-done.22.refs_1_.xa), channel_id=1, source_target_pairs={{0,1},{1,0},{2,3},{3,2},{4,5},{5,4},{6,7},{7,6},{8,9},{9,8},{10,11... | collective-permute-start | bytes 1179656 | tf_op jit(solution)/shard_map/ppermute | solution.py:435
  278.8 20.5 %collective-permute-start.28 = (bf16[512,768]{1,0:T(8,128)(2,1)S(1)}, bf16[512,768]{1,0:T(8,128)(2,1)S(1)}, u32[]{:S(2)}, u32[]{:S(2)}) collective-permute-start(bf16[512,768]{1,0:T(8,128)(2,1)S(1)} %slice_bitcast_fusion.3), channel_id=1, source_target_pairs={{0,1},{1,0},{2,3},{3,2},{4,5},{5,4},{6,7},{7,6},{8,9},{9,8},{10,11... | collective-permute-start | bytes 2359304 | tf_op jit(solution)/shard_map/ppermute | solution.py:435
  280.5 35.6 %collective-permute-start.24 = (bf16[512,768]{1,0:T(8,128)(2,1)S(1)}, bf16[512,768]{1,0:T(8,128)(2,1)S(1)}, u32[]{:S(2)}, u32[]{:S(2)}) collective-permute-start(bf16[512,768]{1,0:T(8,128)(2,1)S(1)} %slice_bitcast_fusion.4), channel_id=1, source_target_pairs={{0,1},{1,0},{2,3},{3,2},{4,5},{5,4},{6,7},{7,6},{8,9},{9,8},{10,11... | collective-permute-start | bytes 2359304 | tf_op jit(solution)/shard_map/ppermute | solution.py:435
  281.0 92.0 %collective-permute-start.34 = (bf16[512,384]{1,0:T(8,128)(2,1)S(1)}, bf16[512,384]{1,0:T(8,128)(2,1)S(1)}, u32[]{:S(2)}, u32[]{:S(2)}) collective-permute-start(bf16[512,384]{1,0:T(8,128)(2,1)S(1)} %copy-done.31), channel_id=1, source_target_pairs={{0,1},{1,0},{2,3},{3,2},{4,5},{5,4},{6,7},{7,6},{8,9},{9,8},{10,11... | collective-permute-start | bytes 1179656 | tf_op jit(solution)/shard_map/ppermute | solution.py:435
  299.5 106.6 %collective-permute-start.29 = (bf16[512,768]{1,0:T(8,128)(2,1)S(1)}, bf16[512,768]{1,0:T(8,128)(2,1)}, u32[]{:S(2)}, u32[]{:S(2)}) collective-permute-start(bf16[512,768]{1,0:T(8,128)(2,1)S(1)} %fusion.13.refs_0_), channel_id=1, source_target_pairs={{0,24},{8,0},{16,8},{24,16},{1,25},{9,1},{17,9},{25,17},{2,26},{10... | collective-permute-start | bytes 2359304 | tf_op jit(solution)/shard_map/ppermute | solution.py:441
  354.7 33.3 %collective-permute-start.32 = (bf16[512,768]{1,0:T(8,128)(2,1)}, bf16[512,768]{1,0:T(8,128)(2,1)}, u32[]{:S(2)}, u32[]{:S(2)}) collective-permute-start(bf16[512,768]{1,0:T(8,128)(2,1)} %slice_bitcast_fusion.1), channel_id=1, source_target_pairs={{0,1},{1,0},{2,3},{3,2},{4,5},{5,4},{6,7},{7,6},{8,9},{9,8},{10,11... | collective-permute-start | bytes 2359304 | tf_op jit(solution)/shard_map/ppermute | solution.py:435
  357.3 33.3 %collective-permute-start.30 = (bf16[512,768]{1,0:T(8,128)(2,1)}, bf16[512,768]{1,0:T(8,128)(2,1)}, u32[]{:S(2)}, u32[]{:S(2)}) collective-permute-start(bf16[512,768]{1,0:T(8,128)(2,1)} %slice_bitcast_fusion.2), channel_id=1, source_target_pairs={{0,1},{1,0},{2,3},{3,2},{4,5},{5,4},{6,7},{7,6},{8,9},{9,8},{10,11... | collective-permute-start | bytes 2359304 | tf_op jit(solution)/shard_map/ppermute | solution.py:435
  386.3 18.5 %collective-permute-start.35 = (bf16[512,768]{1,0:T(8,128)(2,1)S(1)}, bf16[512,768]{1,0:T(8,128)(2,1)S(1)}, u32[]{:S(2)}, u32[]{:S(2)}) collective-permute-start(bf16[512,768]{1,0:T(8,128)(2,1)S(1)} %slice_bitcast_fusion), channel_id=1, source_target_pairs={{0,1},{1,0},{2,3},{3,2},{4,5},{5,4},{6,7},{7,6},{8,9},{9,8},{10,11... | collective-permute-start | bytes 2359304 | tf_op jit(solution)/shard_map/ppermute | solution.py:435
  389.3 22.4 %collective-permute-start.33 = (bf16[512,768]{1,0:T(8,128)(2,1)S(1)}, bf16[512,768]{1,0:T(8,128)(2,1)S(1)}, u32[]{:S(2)}, u32[]{:S(2)}) collective-permute-start(bf16[512,768]{1,0:T(8,128)(2,1)S(1)} %fusion.11), channel_id=1, source_target_pairs={{0,8},{8,16},{16,24},{24,0},{1,9},{9,17},{17,25},{25,1},{2,10},{10... | collective-permute-start | bytes 2359304 | tf_op jit(solution)/shard_map/ppermute | solution.py:441
  391.9 48.3 %collective-permute-start.31 = (bf16[512,768]{1,0:T(8,128)(2,1)S(1)}, bf16[512,768]{1,0:T(8,128)(2,1)S(1)}, u32[]{:S(2)}, u32[]{:S(2)}) collective-permute-start(bf16[512,768]{1,0:T(8,128)(2,1)S(1)} %fusion.12), channel_id=1, source_target_pairs={{0,16},{8,24},{16,0},{24,8},{1,17},{9,25},{17,1},{25,9},{2,18},{10... | collective-permute-start | bytes 2359304 | tf_op jit(solution)/shard_map/ppermute | solution.py:441
  445.9 5.5 collective-permute-start.36
  446.0 9.3 %collective-permute-start.39 = (bf16[2,512,384]{2,1,0:T(8,128)(2,1)}, bf16[2,512,384]{2,1,0:T(8,128)(2,1)}, u32[]{:S(2)}, u32[]{:S(2)}) collective-permute-start(bf16[2,512,384]{2,1,0:T(8,128)(2,1)} %get-tuple-element.110), channel_id=1, source_target_pairs={{0,2},{2,0},{4,6},{6,4},{1,3},{3,1},{5,7},{7,5},{8,10},{10,8},{12,... | collective-permute-start | bytes 2359304 | tf_op jit(solution)/shard_map/ppermute | solution.py:438
  446.5 110.1 %all-to-all-start.1 = ((bf16[4,3,192,1024]{3,2,1,0:T(8,128)(2,1)}), bf16[4,3,192,1024]{3,2,1,0:T(8,128)(2,1)}, u32[]{:S(2)}, u32[]{:S(2)}) async-start(bf16[4,3,192,1024]{3,2,1,0:T(8,128)(2,1)} %pad_maximum_fusion.1.refs_0_), calls=%async_computation.1 | async-start | bytes 9437184 | tf_op jit(solution)/shard_map/all_to_all | solution.py:642
  451.4 171.8 %reduce-scatter.2.cloned.1.call-start = ((), (), s32[]{:S(2)}) async-start(), calls=%async_computation.5 | async-start | bytes 5013504 | tf_op jit(solution)/shard_map/reduce_scatter | solution.py:661
  453.6 12.3 %collective-permute-start.37 = (bf16[512,384]{1,0:T(8,128)(2,1)}, bf16[512,384]{1,0:T(8,128)(2,1)}, u32[]{:S(2)}, u32[]{:S(2)}) collective-permute-start(bf16[512,384]{1,0:T(8,128)(2,1)} %fusion.34), channel_id=1, source_target_pairs={{0,4},{2,6},{4,0},{6,2},{1,5},{3,7},{5,1},{7,3},{8,12},{10,14},{12... | collective-permute-start | bytes 1179656 | tf_op jit(solution)/shard_map/ppermute | solution.py:438
  457.1 16.4 %collective-permute-start.40 = (bf16[512,384]{1,0:T(8,128)(2,1)}, bf16[512,384]{1,0:T(8,128)(2,1)}, u32[]{:S(2)}, u32[]{:S(2)}) collective-permute-start(bf16[512,384]{1,0:T(8,128)(2,1)} %fusion.35), channel_id=1, source_target_pairs={{0,4},{2,6},{4,0},{6,2},{1,5},{3,7},{5,1},{7,3},{8,12},{10,14},{12... | collective-permute-start | bytes 1179656 | tf_op jit(solution)/shard_map/ppermute | solution.py:438
  476.9 3.6 collective-permute-start.41
  481.4 9.8 %collective-permute-start.42 = (bf16[512,384]{1,0:T(8,128)(2,1)S(1)}, bf16[512,384]{1,0:T(8,128)(2,1)}, u32[]{:S(2)}, u32[]{:S(2)}) collective-permute-start(bf16[512,384]{1,0:T(8,128)(2,1)S(1)} %fusion.64.refs_10_), channel_id=1, source_target_pairs={{0,1},{1,0},{2,3},{3,2},{4,5},{5,4},{6,7},{7,6},{8,9},{9,8},{10,11... | collective-permute-start | bytes 1179656 | tf_op jit(solution)/shard_map/ppermute | solution.py:435
  503.2 11.7 %collective-permute-start.43 = (bf16[2,512,768]{2,1,0:T(8,128)(2,1)}, bf16[2,512,768]{2,1,0:T(8,128)(2,1)}, u32[]{:S(2)}, u32[]{:S(2)}) collective-permute-start(bf16[2,512,768]{2,1,0:T(8,128)(2,1)} %get-tuple-element.115), channel_id=1, source_target_pairs={{0,2},{2,0},{4,6},{6,4},{1,3},{3,1},{5,7},{7,5},{8,10},{10,8},{12,... | collective-permute-start | bytes 4718600 | tf_op jit(solution)/shard_map/ppermute | solution.py:438
  514.2 15.8 %collective-permute-start.38 = (bf16[512,384]{1,0:T(8,128)(2,1)S(1)}, bf16[512,384]{1,0:T(8,128)(2,1)S(1)}, u32[]{:S(2)}, u32[]{:S(2)}) collective-permute-start(bf16[512,384]{1,0:T(8,128)(2,1)S(1)} %copy-done.11), channel_id=1, source_target_pairs={{0,1},{1,0},{2,3},{3,2},{4,5},{5,4},{6,7},{7,6},{8,9},{9,8},{10,11... | collective-permute-start | bytes 1179656 | tf_op jit(solution)/shard_map/ppermute | solution.py:435
  517.3 39.2 %collective-permute-start.44 = (bf16[512,768]{1,0:T(8,128)(2,1)}, bf16[512,768]{1,0:T(8,128)(2,1)}, u32[]{:S(2)}, u32[]{:S(2)}) collective-permute-start(bf16[512,768]{1,0:T(8,128)(2,1)} %fusion.27), channel_id=1, source_target_pairs={{0,4},{2,6},{4,0},{6,2},{1,5},{3,7},{5,1},{7,3},{8,12},{10,14},{12... | collective-permute-start | bytes 2359304 | tf_op jit(solution)/shard_map/ppermute | solution.py:438
  562.3 10.5 %collective-permute-start.45 = (bf16[512,384]{1,0:T(8,128)(2,1)}, bf16[512,384]{1,0:T(8,128)(2,1)S(1)}, u32[]{:S(2)}, u32[]{:S(2)}) collective-permute-start(bf16[512,384]{1,0:T(8,128)(2,1)} %get-tuple-element.121), channel_id=1, source_target_pairs={{0,1},{1,0},{2,3},{3,2},{4,5},{5,4},{6,7},{7,6},{8,9},{9,8},{10,11... | collective-permute-start | bytes 1179656 | tf_op jit(solution)/shard_map/ppermute | solution.py:435
  569.2 24.2 %collective-permute-start.54 = (bf16[2,4,48,1536]{3,2,1,0:T(8,128)(2,1)}, bf16[2,4,48,1536]{3,2,1,0:T(8,128)(2,1)}, u32[]{:S(2)}, u32[]{:S(2)}) collective-permute-start(bf16[2,4,48,1536]{3,2,1,0:T(8,128)(2,1)} %get-tuple-element.126), channel_id=1, source_target_pairs={{0,2},{2,0},{4,6},{6,4},{1,3},{3,1},{5,7},{7,5},{8,10},{10,8},{12,... | collective-permute-start | bytes 3538952 | tf_op jit(solution)/shard_map/ppermute | solution.py:438
  573.8 3.7 collective-permute-start.46
  576.0 2.3 collective-permute-start.48
  578.3 4.4 collective-permute-start.49
  581.8 19.1 %collective-permute-start.47 = (bf16[512,384]{1,0:T(8,128)(2,1)S(1)}, bf16[512,384]{1,0:T(8,128)(2,1)}, u32[]{:S(2)}, u32[]{:S(2)}) collective-permute-start(bf16[512,384]{1,0:T(8,128)(2,1)S(1)} %fusion.24), channel_id=1, source_target_pairs={{0,1},{1,0},{2,3},{3,2},{4,5},{5,4},{6,7},{7,6},{8,9},{9,8},{10,11... | collective-permute-start | bytes 1179656 | tf_op jit(solution)/shard_map/ppermute | solution.py:435
  582.7 9.2 %collective-permute-start.50 = (f32[864]{0:T(1024)S(1)}, f32[864]{0:T(1024)S(1)}, u32[]{:S(2)}, u32[]{:S(2)}) collective-permute-start(f32[864]{0:T(1024)S(1)} %get-tuple-element.183), channel_id=1, source_target_pairs={{0,8},{8,16},{16,24},{24,0},{1,9},{9,17},{17,25},{25,1},{2,10},{10... | collective-permute-start | bytes 10376 | tf_op jit(solution)/shard_map/ppermute | solution.py:441
  582.8 9.2 %collective-permute-start.51 = (f32[864]{0:T(1024)S(1)}, f32[864]{0:T(1024)S(1)}, u32[]{:S(2)}, u32[]{:S(2)}) collective-permute-start(f32[864]{0:T(1024)S(1)} %get-tuple-element.185), channel_id=1, source_target_pairs={{0,16},{8,24},{16,0},{24,8},{1,17},{9,25},{17,1},{25,9},{2,18},{10... | collective-permute-start | bytes 10376 | tf_op jit(solution)/shard_map/ppermute | solution.py:441
  585.1 6.8 %collective-permute-start.52 = (f32[864]{0:T(1024)S(1)}, f32[864]{0:T(1024)S(1)}, u32[]{:S(2)}, u32[]{:S(2)}) collective-permute-start(f32[864]{0:T(1024)S(1)} %get-tuple-element.184), channel_id=1, source_target_pairs={{0,24},{8,0},{16,8},{24,16},{1,25},{9,1},{17,9},{25,17},{2,26},{10... | collective-permute-start | bytes 10376 | tf_op jit(solution)/shard_map/ppermute | solution.py:441
  592.1 7.4 %collective-permute-start.53 = (f32[48,18]{1,0:T(8,128)S(1)}, f32[48,18]{1,0:T(8,128)S(1)}, u32[]{:S(2)}, u32[]{:S(2)}) collective-permute-start(f32[48,18]{1,0:T(8,128)S(1)} %reshape.288), channel_id=1, source_target_pairs={{0,1},{1,0},{2,3},{3,2},{4,5},{5,4},{6,7},{7,6},{8,9},{9,8},{10,11... | collective-permute-start | bytes 10376 | tf_op jit(solution)/shard_map/ppermute | solution.py:435
  595.4 13.2 %collective-permute-start.55 = (bf16[4,48,1536]{2,1,0:T(8,128)(2,1)}, bf16[4,48,1536]{2,1,0:T(8,128)(2,1)S(1)}, u32[]{:S(2)}, u32[]{:S(2)}) collective-permute-start(bf16[4,48,1536]{2,1,0:T(8,128)(2,1)} %fusion.33), channel_id=1, source_target_pairs={{0,4},{2,6},{4,0},{6,2},{1,5},{3,7},{5,1},{7,3},{8,12},{10,14},{12... | collective-permute-start | bytes 1769480 | tf_op jit(solution)/shard_map/ppermute | solution.py:438
  610.0 7.8 %collective-permute-start.56 = (bf16[48,1536]{1,0:T(8,128)(2,1)S(1)}, bf16[48,1536]{1,0:T(8,128)(2,1)S(1)}, u32[]{:S(2)}, u32[]{:S(2)}) collective-permute-start(bf16[48,1536]{1,0:T(8,128)(2,1)S(1)} %get-tuple-element.206), channel_id=1, source_target_pairs={{0,8},{8,16},{16,24},{24,0},{1,9},{9,17},{17,25},{25,1},{2,10},{10... | collective-permute-start | bytes 442376 | tf_op jit(solution)/shard_map/ppermute | solution.py:441
  610.8 10.8 %collective-permute-start.57 = (bf16[48,1536]{1,0:T(8,128)(2,1)S(1)}, bf16[48,1536]{1,0:T(8,128)(2,1)S(1)}, u32[]{:S(2)}, u32[]{:S(2)}) collective-permute-start(bf16[48,1536]{1,0:T(8,128)(2,1)S(1)} %get-tuple-element.208), channel_id=1, source_target_pairs={{0,16},{8,24},{16,0},{24,8},{1,17},{9,25},{17,1},{25,9},{2,18},{10... | collective-permute-start | bytes 442376 | tf_op jit(solution)/shard_map/ppermute | solution.py:441
  612.0 9.7 %collective-permute-start.58 = (bf16[48,1536]{1,0:T(8,128)(2,1)S(1)}, bf16[48,1536]{1,0:T(8,128)(2,1)S(1)}, u32[]{:S(2)}, u32[]{:S(2)}) collective-permute-start(bf16[48,1536]{1,0:T(8,128)(2,1)S(1)} %get-tuple-element.207), channel_id=1, source_target_pairs={{0,24},{8,0},{16,8},{24,16},{1,25},{9,1},{17,9},{25,17},{2,26},{10... | collective-permute-start | bytes 442376 | tf_op jit(solution)/shard_map/ppermute | solution.py:441
  (72 other events, 701.5 us)
Sparse Core Ops, SparseCore 0:
  12.2 63.1 all-gather.2
  210.2 65.8 all-gather.4
  513.3 86.0 reduce-scatter.1

commit v3 on v2

--- a/solution.py
+++ b/solution.py
@@ -55,7 +55,7 @@
             scratch_shapes=list(scratch),
             compiler_params=pltpu.CompilerParams(vmem_limit_bytes=VMEM_LIMIT),
             cost_estimate=pl.CostEstimate(
-                flops=int(us * 1e9), bytes_accessed=0, transcendentals=0
+                flops=int(us * 1.1e9), bytes_accessed=0, transcendentals=0
             ),
             name=name,
         )(scalars, *args, *deps)
@@ -375,7 +375,7 @@
         scratch_shapes=[pltpu.VMEM((ROWS, D), f32), pltpu.VMEM((ROWS, D), f32)],
         input_output_aliases=aliases,
         compiler_params=pltpu.CompilerParams(vmem_limit_bytes=VMEM_LIMIT),
-        cost_estimate=pl.CostEstimate(flops=int(6e9), bytes_accessed=0, transcendentals=0),
+        cost_estimate=pl.CostEstimate(flops=int(16e9) if routed else 0, bytes_accessed=0, transcendentals=0),
         name="expert_ffn" if routed else "shared_ffn",
     )(scalars, *args)
 
@@ -571,7 +571,7 @@
     normed_one, queries, kv = call(
         qkv_body,
         [sds((ROWS, D), bf16), sds((ROWS, heads_width), bf16), sds((ROWS, 2 * heads_width), bf16)],
-        us=3.0, name="qkv",
+        us=5.0, name="qkv",
     )(
         scalars, tokens, gain_one[None, :], first, cos, sin,
         deps=[cot_pairs[0][1], *cot_rows[1:], expert_local],
@@ -584,7 +584,7 @@
         expert_w = lax.all_to_all(
             after(expert_local, kv_near), "fsdp", 0, 0, tiled=True
         )
-    before_attn = [cot_pairs[1][1], cot_pairs[2][1]]
+    before_attn = []
     seq_ids = segments[0]
     seg_col = seq_ids[:, None]
     seg_row = lax.dynamic_slice_in_dim(seq_ids, c * ROWS, ROWS, 0)[None, :]
@@ -602,7 +602,7 @@
             pltpu.VMEM((4 * ROWS, ROWS), f32),
             pltpu.VMEM((heads_width, ROWS), f32),
         ],
-        us=9.0, name="attn",
+        us=17.0, name="attn",
     )(scalars, queries, *kvs, seg_col, seg_row, out_w, deps=before_attn)
     tok_h = half(tokens, y).astype(f32)
     middle = tok_h + z_own + yx(z_oth).astype(f32)
@@ -619,18 +619,20 @@
     normed_two = (normal_two * gain_two_h[None, :]).astype(bf16)
 
     normed_two_oth = yx(normed_two)
-    rows_in = dispatch(normed_two, [cot_pairs[3][1]])
+    rows_in = dispatch(normed_two, [normed_two_oth])
     shared_w = gathered(after(shared_shard, rows_in[3]), 1)[None]
-    saved, backs, sums, router_part = None, [], [], 0.0
-    pairs = [(rows, yx(rows)) for rows in rows_in]
-    for s in range(4):
-        deps = [rows_in[1:], [pairs[2][1], pairs[3][1]], sums[:1], sums[1:2]][s]
+    saved, backs, sums, router_part = None, [None] * 4, [], 0.0
+    tied = [rows_in[0]] + [after(rows, *[pair[1] for pair in cot_pairs]) for rows in rows_in[1:]]
+    pairs = [(rows, yx(rows)) for rows in tied]
+    for i, s in enumerate((2, 1, 3, 0)):
+        deps = [rows_in[1:], [pairs[3][1], pairs[0][1]], sums[:1], sums[1:2]][i]
         res = ffn(scalars, s, 4, *pairs[s], *cot_pairs[s], expert_w, extra, saved, deps)
         sums.append(over_tp(res[0]))
-        backs.append(home(s, sums[s]))
+        backs[s] = home(s, sums[i])
         router_part = router_part + res[1][:, :E]
         saved = res[2:]
     ex_dgu, ex_y, ex_x, ex_de = [v.reshape(4 * ROWS, -1) for v in saved]
+    ex_x = after(ex_x, backs[2])
 
     grad_w = [
         lax.dot_general(a, b, (((0,), (0,)), ((), ())), preferred_element_type=f32)
@@ -651,20 +653,22 @@
         grad_w = lax.all_to_all(grad_w, "fsdp", 0, 0, axis_index_groups=inner, tiled=True)
 
     sh_back, sh_dgu, sh_y = ffn(
-        scalars, 0, 1, normed_two, normed_two_oth, cot_h, cot_o, shared_w, None, None, [grad_ready]
+        scalars, 0, 1, normed_two, normed_two_oth, cot_h, cot_o, shared_w, None, None,
+        [grad_ready, backs[1], backs[3]],
     )
     sh_sum = sh_back[0].astype(f32) + yx(sh_back[1]).astype(f32)
     normed_full = halves(y, normed_two, normed_two_oth)
     shared_full = jnp.concatenate(
         [grad_of(normed_full, sh_dgu[0]), grad_of(cotangent, sh_y[0])], axis=1
     )
+    shared_full = shared_full.astype(bf16) if small else shared_full
     shared_grad = lax.psum_scatter(
-        shared_full.astype(bf16) if small else shared_full,
+        shared_full,
         ("fsdp", "ctx"), scatter_dimension=0, tiled=True,
     ).astype(f32)
 
     keep_b, send_b, keep_o, send_o = call(
-        unpack_body, [sds((2, ROWS, HALF), bf16)] * 4, us=3.0, name="unpack"
+        unpack_body, [sds((2, ROWS, HALF), bf16)] * 4, us=0.0, name="unpack"
     )(scalars, ids, *backs, deps=[sh_sum])
     back_h = over_ctx(keep_b, send_b) + sh_sum[:, :HALF]
     scaled = back_h * gain_two_h[None, :]
@@ -683,40 +687,42 @@
             pltpu.VMEM((8, ROWS), f32),
             pltpu.VMEM((heads_width, ROWS), f32),
         ],
-        us=11.0, name="attn_back",
+        us=0.0, name="attn_back",
     )(
         scalars, queries, *kvs, seg_col, seg_row, lse, attended, dz_own, dz_oth, out_w, cos, sin,
-    )
+        deps=[shared_full],
+    )
+    layer_h = middle + over_ctx(keep_o, after(send_o, dz_oth)) + sh_sum[:, HALF:]
     dkv_near = cx(dkv_send, 1)
     kv_recv = cx((dkv_keep[1].astype(f32) + dkv_near[1].astype(f32)).astype(bf16), 2)
     dp, da_own, da_oth = call(
         proj_back_body,
         [sds((ROWS, 3 * heads_width), bf16), sds((ROWS, HALF), f32), sds((ROWS, HALF), bf16)],
-        us=3.0, name="proj_back",
-    )(scalars, dq, dkv_keep, dkv_near, kv_recv, first, cos, sin, deps=[grad_w])
+        us=5.0, name="proj_back",
+    )(scalars, dq, dkv_keep, dkv_near, kv_recv, first, cos, sin, deps=[grad_w, layer_h])
     dense_pairs = [(normed_one, dp), (halves(y, dz_own, dz_oth), attended)]
     if small:
         dense_keep, dense_send = grad_blocks(back_offs, rows_own, dense_pairs)
+        dense_part = reduce_near(dense_keep, dense_send)
     else:
-        dense_keep = dp
+        dense_keep = dense_part = dp
     da_h = after(da_own, dense_keep) + yx(da_oth).astype(f32)
     tok_full = tokens.astype(f32)
     scale_one = lax.rsqrt(jnp.mean(tok_full * tok_full, axis=1, keepdims=True) + eps)
     normal_one = tok_h * scale_one
     scaled_one = da_h * gain_one_h[None, :]
     mean_one = both_halves(jnp.sum(scaled_one * normal_one, axis=1))[:, None] / D
-    attn_gain_part = jnp.sum(da_h * normal_one, axis=0)
+    attn_gain_part = jnp.sum(after(da_h, mean_one) * normal_one, axis=0)
     tokens_grad_h = middle_grad + scale_one * (scaled_one - normal_one * mean_one)
 
     tokens_grad = whole_rows(tokens_grad_h.astype(bf16)).astype(f32)
 
-    layer_h = middle + over_ctx(keep_o, send_o) + sh_sum[:, HALF:]
-    layer_out = whole_rows(layer_h.astype(bf16))
-    grad_w = after(grad_w, tokens_grad_h)
+    layer_out = whole_rows(after(layer_h, mean_one).astype(bf16))
+    grad_w = after(grad_w, tokens_grad_h, dense_part)
     expert_gate_up_grad = grad_w[:, :2].astype(f32)
     expert_down_grad = grad_w[:, 2].astype(f32).transpose(0, 2, 1)
     if small:
-        dense_grad = reduce_far(reduce_near(dense_keep, dense_send), bf16, None, tokens_grad_h)
+        dense_grad = reduce_far(dense_part, bf16, None, tokens_grad_h)
     else:
         dense_grad = dense_reduce(dense_pairs)
     qkv_grad = dense_grad[:, : 3 * heads_width].reshape(rows_own, 3, heads_width).transpose(1, 0, 2)

time: 641 us -> 584 us (0.911)
  waiting for transfers between devices: 291 us -> 211 us
  starting transfers between devices: 95.7 us -> 117 us
  Pallas kernels: 122 us -> 114 us
    ppermute x15, waiting for transfers between devices: 92.9 us -> 51.5 us  [zs(): lax.ppermute(v, 'fsdp', [(i, i // EL * EL + (i % EL + s) % EL) for i in r...]
    ppermute x23, waiting for transfers between devices: 88.6 us -> 66.2 us  [yx(): return lax.ppermute(v, 'tp', [(0, 1), (1, 0)])]
    ppermute x15, starting transfers between devices: 19.9 us -> 33.7 us  [zs(): lax.ppermute(v, 'fsdp', [(i, i // EL * EL + (i % EL + s) % EL) for i in r...]
    all_to_all x1, waiting for transfers between devices: 24.4 us -> 12.4 us  [per_device(): grad_w = lax.all_to_all(grad_w, 'fsdp', 0, 0, tiled=True)]
    pallas_call x5, Pallas kernels: 72.7 us -> 64.2 us  [ffn(): pl.pallas_call(functools.partial(ffn_body, routed), grid=(1,), out_shape=...]
  transfers between devices with their start and end apart: 64 -> 64, of which waited for: 31 -> 32; matrix products, arithmetic and copies ran while one was open for 15% -> 18% of each run, Pallas kernels for 18% -> 19%
where the time goes in v3:
time: 584 us; the launch traced here: 576 us
  waiting for transfers between devices  211 us (36%)
  starting transfers between devices  117 us (20%)
  Pallas kernels  114 us (20%)
  other arithmetic  61.8 us (11%)
  local copies, waits for them, and re-layouts  39.9 us (7%)
  matrix products  16.9 us (3%)
  between operations  14.9 us (3%)
    ppermute x23, waiting for transfers between devices, yx(): return lax.ppermute(v, 'tp', [(0, 1), (1, 0)])  66.2 us
    pallas_call x5, Pallas kernels, ffn(): pl.pallas_call(functools.partial(ffn_body, routed), grid=(1,), out_shape=...  64.2 us
    ppermute x15, waiting for transfers between devices, zs(): lax.ppermute(v, 'fsdp', [(i, i // EL * EL + (i % EL + s) % EL) for i in r...  51.5 us
    pallas_call x8, Pallas kernels, run(): pl.pallas_call(inner, out_shape=outs, in_specs=[SMEM] + [VM] * len(args)...  50 us
    ppermute x21, waiting for transfers between devices, cx(): return lax.ppermute(v, 'ctx', [(i, i ^ flip) for i in range(C)])  47.5 us
    ppermute x21, starting transfers between devices, cx(): return lax.ppermute(v, 'ctx', [(i, i ^ flip) for i in range(C)])  40.9 us
    ppermute x15, starting transfers between devices, zs(): lax.ppermute(v, 'fsdp', [(i, i // EL * EL + (i % EL + s) % EL) for i in r...  33.7 us
    all_gather x2, waiting for transfers between devices, gathered(): return lax.all_gather(shard, ('fsdp', 'ctx'), axis=axis, tiled=True)  33.2 us
  transfers between devices with their start and end apart: 64, of which 32 were waited for; matrix products, arithmetic and copies ran while one was open for 18% of the time, Pallas kernels for 19%

profile of v3, /device:TPU:0, one launch (start us, length us, event | category | flops | bytes accessed | tf_op | source)
XLA Modules:
  0.0 575.6 jit_solution(17669397884617798992)
XLA Ops:
  14.1 2.9 collective-permute-start.3
  19.3 4.5 pad_maximum_fusion.refs_10_
  23.8 3.6 collective-permute-done
  30.7 3.7 pack.2
  34.4 2.3 collective-permute-start.5
  38.3 2.6 collective-permute-start.7
  42.3 33.2 %all-gather.3.cloned.1.call-done.refs_3_.refs_5_ = bf16[768,1664]{1,0:T(8,128)(2,1)} async-done(((bf16[48,1664]{1,0:T(8,128)(2,1)}), bf16[768,1664]{1,0:T(8,128)(2,1)}) %all-gather.3.cloned.1.call-update) | async-done | bytes 2555920 | tf_op jit(solution)/shard_map/all_gather | solution.py:457
  79.2 5.1 qkv.1
  84.5 2.2 collective-permute-done.9.refs_3_
  87.6 10.0 %all-to-all-start = ((bf16[4,3,192,1024]{3,2,1,0:T(8,128)(2,1)}), bf16[4,3,192,1024]{3,2,1,0:T(8,128)(2,1)}, u32[]{:S(2)}, u32[]{:S(2)}) async-start(bf16[4,3,192,1024]{3,2,1,0:T(8,128)(2,1)} %pad_maximum_fusion.refs_10_), calls=%async_computation | async-start | bytes 9437184 | tf_op jit(solution)/shard_map/all_to_all | solution.py:584
  99.2 17.8 %collective-permute-done.10.refs_4_ = bf16[512,768]{1,0:T(8,128)(2,1)S(1)} collective-permute-done((bf16[512,768]{1,0:T(8,128)(2,1)S(1)}, bf16[512,768]{1,0:T(8,128)(2,1)S(1)}, u32[]{:S(2)}, u32[]{:S(2)}) %collective-permute-start.10) | collective-permute-done | bytes 786464 | tf_op jit(solution)/shard_map/ppermute | solution.py:438
  121.8 9.1 %attn.1 = (bf16[512,384]{1,0:T(8,128)(2,1)}, f32[512,384]{1,0:T(8,128)}, bf16[512,384]{1,0:T(8,128)(2,1)}, f32[8,512]{1,0:T(8,128)}) custom-call(s32[3]{0:T(128)} %pad_add_fusion.2.refs_0_.sc.rt, bf16[512,384]{1,0:T(8,128)(2,1)} %get-tuple-element.82.refs_1_, bf16[512,768]{1,0:T(8,128)(2,1)} %get-tuple-element.83.refs_2_, bf16[512,768]{1,0:T(8,128)(2,1)} %copy-done.24, ...), custom_call_target="tpu_custom_call" | custom-call | flops 18699999232 | tf_op jit(solution)/shard_map/attn/pallas_call | solution.py:50
  131.4 7.9 %collective-permute-done.12 = bf16[512,384]{1,0:T(8,128)(2,1)S(1)} collective-permute-done((bf16[512,384]{1,0:T(8,128)(2,1)}, bf16[512,384]{1,0:T(8,128)(2,1)S(1)}, u32[]{:S(2)}, u32[]{:S(2)}) %collective-permute-start.12) | collective-permute-done | bytes 393248 | tf_op jit(solution)/shard_map/ppermute | solution.py:435
  141.5 2.9 collective-permute-done.13
  144.6 9.9 %collective-permute-start.16 = (bf16[512,384]{1,0:T(8,128)(2,1)S(1)}, bf16[512,384]{1,0:T(8,128)(2,1)S(1)}, u32[]{:S(2)}, u32[]{:S(2)}) collective-permute-start(bf16[512,384]{1,0:T(8,128)(2,1)S(1)} %multiply_convert_fusion.refs_2_.xa), channel_id=1, source_target_pairs={{0,4},{2,6},{4,0},{6,2},{1,5},{3,7},{5,1},{7,3},{8,12},{10,14},{12... | collective-permute-start | bytes 1179656 | tf_op jit(solution)/shard_map/ppermute | solution.py:438
  155.0 2.7 collective-permute-start.15
  157.7 4.1 collective-permute-done.16.refs_4_
  161.8 2.9 collective-permute-start.17
  168.8 3.7 pack.3
  172.6 2.6 collective-permute-start.26
  175.2 2.6 collective-permute-start.24
  179.5 5.6 collective-permute-done.21.wb
  185.1 7.5 %collective-permute-done.22.wb = bf16[512,384]{1,0:T(8,128)(2,1)S(1)} collective-permute-done((bf16[512,384]{1,0:T(8,128)(2,1)S(1)}, bf16[512,384]{1,0:T(8,128)(2,1)S(1)}, u32[]{:S(2)}, u32[]{:S(2)}) %collective-permute-start.22) | collective-permute-done | bytes 393248 | tf_op jit(solution)/shard_map/ppermute | solution.py:435
  192.6 36.2 %collective-permute-done.26.xa.refs_1_ = bf16[512,384]{1,0:T(8,128)(2,1)} collective-permute-done((bf16[512,384]{1,0:T(8,128)(2,1)}, bf16[512,384]{1,0:T(8,128)(2,1)}, u32[]{:S(2)}, u32[]{:S(2)}) %collective-permute-start.26) | collective-permute-done | bytes 393248 | tf_op jit(solution)/shard_map/ppermute | solution.py:441
  235.3 5.8 %collective-permute-done.27.xb = bf16[512,384]{1,0:T(8,128)(2,1)S(1)} collective-permute-done((bf16[512,384]{1,0:T(8,128)(2,1)}, bf16[512,384]{1,0:T(8,128)(2,1)S(1)}, u32[]{:S(2)}, u32[]{:S(2)}) %collective-permute-start.27) | collective-permute-done | bytes 393248 | tf_op jit(solution)/shard_map/ppermute | solution.py:435
  241.8 13.5 %expert_ffn.4 = (bf16[2,512,768]{2,1,0:T(8,128)(2,1)}, f32[768,128]{1,0:T(8,128)}, bf16[4,512,2048]{2,1,0:T(8,128)(2,1)}, bf16[4,512,1024]{2,1,0:T(8,128)(2,1)},...) custom-call(s32[3]{0:T(128)} %pad_add_fusion.2.refs_0_.sc.rt, ...), custom_call_target="tpu_custom_call" | custom-call | flops 16000000000 | tf_op jit(solution)/shard_map/expert_ffn/pallas_call | solution.py:369
  257.9 8.5 %collective-permute-done.23.xb = bf16[512,384]{1,0:T(8,128)(2,1)} collective-permute-done((bf16[512,384]{1,0:T(8,128)(2,1)}, bf16[512,384]{1,0:T(8,128)(2,1)}, u32[]{:S(2)}, u32[]{:S(2)}) %collective-permute-start.23) | collective-permute-done | bytes 393248 | tf_op jit(solution)/shard_map/ppermute | solution.py:435
  266.4 13.4 %expert_ffn.5 = (bf16[2,512,768]{2,1,0:T(8,128)(2,1)}, f32[768,128]{1,0:T(8,128)}, bf16[4,512,2048]{2,1,0:T(8,128)(2,1)}, bf16[4,512,1024]{2,1,0:T(8,128)(2,1)},...) custom-call(s32[3]{0:T(128)} %pad_add_fusion.2.refs_0_.sc.rt, ...), custom_call_target="tpu_custom_call", output_to_operand_aliasing={{2}: (9, {}), {3}: (10, {}), {4}: (11, {}), {5}: (12, {})} | custom-call | flops 16000000000 | tf_op jit(solution)/shard_map/expert_ffn/pallas_call | solution.py:369
  283.5 13.2 %expert_ffn.6 = (bf16[2,512,768]{2,1,0:T(8,128)(2,1)}, f32[768,128]{1,0:T(8,128)}, bf16[4,512,2048]{2,1,0:T(8,128)(2,1)}, bf16[4,512,1024]{2,1,0:T(8,128)(2,1)},...) custom-call(s32[3]{0:T(128)} %pad_add_fusion.2.refs_0_.sc.rt, ...), custom_call_target="tpu_custom_call", output_to_operand_aliasing={{2}: (8, {}), {3}: (9, {}), {4}: (10, {}), {5}: (11, {})} | custom-call | flops 16000000000 | tf_op jit(solution)/shard_map/expert_ffn/pallas_call | solution.py:369
  299.2 2.5 collective-permute-start.31
  301.6 12.8 %expert_ffn.7 = (bf16[2,512,768]{2,1,0:T(8,128)(2,1)}, f32[768,128]{1,0:T(8,128)}, bf16[4,512,2048]{2,1,0:T(8,128)(2,1)}, bf16[4,512,1024]{2,1,0:T(8,128)(2,1)},...) custom-call(s32[3]{0:T(128)} %pad_add_fusion.2.refs_0_.sc.rt, ...), custom_call_target="tpu_custom_call", output_to_operand_aliasing={{2}: (8, {}), {3}: (9, {}), {4}: (10, {}), {5}: (11, {})} | custom-call | flops 16000000000 | tf_op jit(solution)/shard_map/expert_ffn/pallas_call | solution.py:369
  317.5 6.7 %bitcast_convert_fusion = bf16[768,1024]{1,0:T(8,128)(2,1)S(1)} fusion(bf16[4,512,768]{2,1,0:T(8,128)(2,1)} %get-tuple-element.115, bf16[4,512,1024]{2,1,0:T(8,128)(2,1)} %get-tuple-element.116), kind=kOutput, calls=%fused_computation.10 | convolution fusion | flops 3222011904 | bytes 8912896 | tf_op jit(solution)/shard_map/dot_general | solution.py:638
  325.0 3.5 fusion.5
  328.5 3.5 fusion.8
  332.0 2.5 pad_maximum_fusion.1.refs_0_
  334.5 12.9 %collective-permute-done.31.refs_1_.refs_3_ = bf16[512,768]{1,0:T(8,128)(2,1)S(1)} collective-permute-done((bf16[512,768]{1,0:T(8,128)(2,1)S(1)}, bf16[512,768]{1,0:T(8,128)(2,1)S(1)}, u32[]{:S(2)}, u32[]{:S(2)}) %collective-permute-start.31) | collective-permute-done | bytes 786464 | tf_op jit(solution)/shard_map/ppermute | solution.py:441
  348.5 11.3 %shared_ffn.1 = (bf16[2,512,768]{2,1,0:T(8,128)(2,1)}, bf16[1,512,2048]{2,1,0:T(8,128)(2,1)}, bf16[1,512,1024]{2,1,0:T(8,128)(2,1)}) custom-call(s32[3]{0:T(128)} %pad_add_fusion.2.refs_0_.sc.rt, bf16[512,384]{1,0:T(8,128)(2,1)} %copy-done.11, bf16[512,384]{1,0:T(8,128)(2,1)} %copy-done.9, bf16[512,384]{1,0:T(8,128)(2,1)} %copy-done.5, ...), custom_call_target="tpu_custom_call" | custom-call | tf_op jit(solution)/shard_map/shared_ffn/pallas_call | solution.py:369
  363.0 8.5 %all-to-all-start.1 = ((bf16[4,3,192,1024]{3,2,1,0:T(8,128)(2,1)}), bf16[4,3,192,1024]{3,2,1,0:T(8,128)(2,1)}, u32[]{:S(2)}, u32[]{:S(2)}) async-start(bf16[4,3,192,1024]{3,2,1,0:T(8,128)(2,1)} %pad_maximum_fusion.1.refs_0_), calls=%async_computation.1 | async-start | bytes 9437184 | tf_op jit(solution)/shard_map/all_to_all | solution.py:644
  371.8 2.4 fusion.12.refs_2_
  374.1 2.3 collective-permute-done.35
  376.4 2.4 convert_add_fusion.refs_6_
  378.8 5.0 unpack.1
  391.7 7.3 %collective-permute-done.37 = bf16[512,384]{1,0:T(8,128)(2,1)S(1)} collective-permute-done((bf16[512,384]{1,0:T(8,128)(2,1)S(1)}, bf16[512,384]{1,0:T(8,128)(2,1)S(1)}, u32[]{:S(2)}, u32[]{:S(2)}) %collective-permute-start.37) | collective-permute-done | bytes 393248 | tf_op jit(solution)/shard_map/ppermute | solution.py:438
  406.9 2.7 pad_maximum_fusion.2.refs_15_
  409.5 5.6 collective-permute-done.39.refs_11_
  415.1 12.0 %attn_back.1 = (bf16[512,384]{1,0:T(8,128)(2,1)}, bf16[2,512,768]{2,1,0:T(8,128)(2,1)}, bf16[2,512,768]{2,1,0:T(8,128)(2,1)}) custom-call(s32[3]{0:T(128)} %pad_add_fusion.2.refs_0_.sc.rt, bf16[512,384]{1,0:T(8,128)(2,1)} %get-tuple-element.82.refs_1_, bf16[512,768]{1,0:T(8,128)(2,1)} %get-tuple-element.83.refs_2_, bf16[512,768]{1,0:T(8,128)(2,1)} %copy-done.24, ...), custom_call_target="tpu_custom_call" | custom-call | tf_op jit(solution)/shard_map/attn_back/pallas_call | solution.py:50
  427.1 2.7 collective-permute-start.42
  439.6 11.8 %collective-permute-start.41 = (bf16[512,384]{1,0:T(8,128)(2,1)S(1)}, bf16[512,384]{1,0:T(8,128)(2,1)S(1)}, u32[]{:S(2)}, u32[]{:S(2)}) collective-permute-start(bf16[512,384]{1,0:T(8,128)(2,1)S(1)} %fusion.34), channel_id=1, source_target_pairs={{0,4},{2,6},{4,0},{6,2},{1,5},{3,7},{5,1},{7,3},{8,12},{10,14},{12... | collective-permute-start | bytes 1179656 | tf_op jit(solution)/shard_map/ppermute | solution.py:438
  451.4 2.5 fusion.27
  456.6 4.8 collective-permute-done.41
  461.4 2.2 slice_add_fusion.refs_9_
  463.6 12.4 %all-to-all-done.1.refs_8_ = bf16[4,3,192,1024]{3,2,1,0:T(8,128)(2,1)} async-done(((bf16[4,3,192,1024]{3,2,1,0:T(8,128)(2,1)}), bf16[4,3,192,1024]{3,2,1,0:T(8,128)(2,1)}, u32[]{:S(2)}, u32[]{:S(2)}) %all-to-all-start.1) | async-done | bytes 4718624 | tf_op jit(solution)/shard_map/all_to_all | solution.py:644
  475.9 2.2 collective-permute-done.43.refs_4_
  478.2 5.8 %proj_back.1 = (bf16[512,1152]{1,0:T(8,128)(2,1)}, f32[512,384]{1,0:T(8,128)}, bf16[512,384]{1,0:T(8,128)(2,1)}) custom-call(s32[3]{0:T(128)} %pad_add_fusion.2.refs_0_.sc.rt, bf16[512,384]{1,0:T(8,128)(2,1)} %get-tuple-element.127.refs_1_, bf16[2,512,768]{2,1,0:T(8,128)(2,1)} %get-tuple-element.128.refs_2_, ...), custom_call_target="tpu_custom_call" | custom-call | flops 5500000256 | tf_op jit(solution)/shard_map/proj_back/pallas_call | solution.py:50
  485.8 5.7 grad_blocks.1
  491.6 3.6 collective-permute-done.44
  496.7 2.4 collective-permute-done.45
  505.8 2.2 collective-permute-done.49
  508.0 11.2 %collective-permute-start.50 = (f32[864]{0:T(1024)S(1)}, f32[864]{0:T(1024)S(1)}, u32[]{:S(2)}, u32[]{:S(2)}) collective-permute-start(f32[864]{0:T(1024)S(1)} %get-tuple-element.195), channel_id=1, source_target_pairs={{0,8},{8,16},{16,24},{24,0},{1,9},{9,17},{17,25},{25,1},{2,10},{10... | collective-permute-start | bytes 10376 | tf_op jit(solution)/shard_map/ppermute | solution.py:441
  526.2 2.4 fusion.24
  534.9 11.6 %collective-permute-done.46 = bf16[512,384]{1,0:T(8,128)(2,1)S(1)} collective-permute-done((bf16[512,384]{1,0:T(8,128)(2,1)S(1)}, bf16[512,384]{1,0:T(8,128)(2,1)S(1)}, u32[]{:S(2)}, u32[]{:S(2)}) %collective-permute-start.46) | collective-permute-done | bytes 393248 | tf_op jit(solution)/shard_map/ppermute | solution.py:435
  551.9 2.5 collective-permute-start.57
  555.7 5.3 slice_convert_fusion
  561.1 3.5 convert_bitcast_fusion
  (337 shorter events, 122.3 us)
Async XLA Ops:
  7.2 68.2 %all-gather.3.cloned.1.call-start = ((), (), s32[]{:S(2)}) async-start(), calls=%async_computation.3 | async-start | bytes 2715648 | tf_op jit(solution)/shard_map/all_gather | solution.py:457
  14.1 13.9 %collective-permute-start.3 = (bf16[512,384]{1,0:T(8,128)(2,1)S(1)}, bf16[512,384]{1,0:T(8,128)(2,1)S(1)}, u32[]{:S(2)}, u32[]{:S(2)}) collective-permute-start(bf16[512,384]{1,0:T(8,128)(2,1)S(1)} %get-tuple-element.215.refs_2_.wa), channel_id=1, source_target_pairs={{0,4},{2,6},{4,0},{6,2},{1,5},{3,7},{5,1},{7,3},{8,12},{10,14},{12... | collective-permute-start | bytes 1179656 | tf_op jit(solution)/shard_map/ppermute | solution.py:438
  17.0 12.2 %collective-permute-start.2 = (bf16[512,384]{1,0:T(8,128)(2,1)S(1)}, bf16[512,384]{1,0:T(8,128)(2,1)S(1)}, u32[]{:S(2)}, u32[]{:S(2)}) collective-permute-start(bf16[512,384]{1,0:T(8,128)(2,1)S(1)} %get-tuple-element.215.refs_2_.wa), channel_id=1, source_target_pairs={{0,2},{2,0},{4,6},{6,4},{1,3},{3,1},{5,7},{7,5},{8,10},{10,8},{12,... | collective-permute-start | bytes 1179656 | tf_op jit(solution)/shard_map/ppermute | solution.py:438
  17.4 10.0 %collective-permute-start = (s32[2,512]{1,0:T(2,128)S(1)}, s32[2,512]{1,0:T(2,128)S(1)}, u32[]{:S(2)}, u32[]{:S(2)}) collective-permute-start(s32[2,512]{1,0:T(2,128)S(1)} %get-tuple-element.228), channel_id=1, source_target_pairs={{0,4},{2,6},{4,0},{6,2},{1,5},{3,7},{5,1},{7,3},{8,12},{10,14},{12... | collective-permute-start | bytes 12296 | tf_op jit(solution)/shard_map/ppermute | solution.py:438
  27.4 1.2 collective-permute-start.1
  28.0 1.9 collective-permute-start.4
  34.4 43.5 %collective-permute-start.5 = (bf16[512,384]{1,0:T(8,128)(2,1)}, bf16[512,384]{1,0:T(8,128)(2,1)S(1)}, u32[]{:S(2)}, u32[]{:S(2)}) collective-permute-start(bf16[512,384]{1,0:T(8,128)(2,1)} %get-tuple-element.78.wa), channel_id=1, source_target_pairs={{0,1},{1,0},{2,3},{3,2},{4,5},{5,4},{6,7},{7,6},{8,9},{9,8},{10,11... | collective-permute-start | bytes 1179656 | tf_op jit(solution)/shard_map/ppermute | solution.py:435
  36.7 41.2 %collective-permute-start.6 = (bf16[512,384]{1,0:T(8,128)(2,1)}, bf16[512,384]{1,0:T(8,128)(2,1)S(1)}, u32[]{:S(2)}, u32[]{:S(2)}) collective-permute-start(bf16[512,384]{1,0:T(8,128)(2,1)} %get-tuple-element.79), channel_id=1, source_target_pairs={{0,8},{8,16},{16,24},{24,0},{1,9},{9,17},{17,25},{25,1},{2,10},{10... | collective-permute-start | bytes 1179656 | tf_op jit(solution)/shard_map/ppermute | solution.py:441
  38.3 39.7 %collective-permute-start.7 = (bf16[512,384]{1,0:T(8,128)(2,1)}, bf16[512,384]{1,0:T(8,128)(2,1)S(1)}, u32[]{:S(2)}, u32[]{:S(2)}) collective-permute-start(bf16[512,384]{1,0:T(8,128)(2,1)} %get-tuple-element.80), channel_id=1, source_target_pairs={{0,16},{8,24},{16,0},{24,8},{1,17},{9,25},{17,1},{25,9},{2,18},{10... | collective-permute-start | bytes 1179656 | tf_op jit(solution)/shard_map/ppermute | solution.py:441
  40.9 37.1 %collective-permute-start.8 = (bf16[512,384]{1,0:T(8,128)(2,1)}, bf16[512,384]{1,0:T(8,128)(2,1)S(1)}, u32[]{:S(2)}, u32[]{:S(2)}) collective-permute-start(bf16[512,384]{1,0:T(8,128)(2,1)} %get-tuple-element.81), channel_id=1, source_target_pairs={{0,24},{8,0},{16,8},{24,16},{1,25},{9,1},{17,9},{25,17},{2,26},{10... | collective-permute-start | bytes 1179656 | tf_op jit(solution)/shard_map/ppermute | solution.py:441
  84.2 2.5 collective-permute-start.9
  87.6 153.4 %all-to-all-start = ((bf16[4,3,192,1024]{3,2,1,0:T(8,128)(2,1)}), bf16[4,3,192,1024]{3,2,1,0:T(8,128)(2,1)}, u32[]{:S(2)}, u32[]{:S(2)}) async-start(bf16[4,3,192,1024]{3,2,1,0:T(8,128)(2,1)} %pad_maximum_fusion.refs_10_), calls=%async_computation | async-start | bytes 9437184 | tf_op jit(solution)/shard_map/all_to_all | solution.py:584
  97.6 249.7 %all-gather.5.cloned.1.call-start = ((), (), s32[]{:S(2)}) async-start(), calls=%async_computation.4 | async-start | bytes 5013504 | tf_op jit(solution)/shard_map/all_gather | solution.py:457
  97.6 19.4 %collective-permute-start.10 = (bf16[512,768]{1,0:T(8,128)(2,1)S(1)}, bf16[512,768]{1,0:T(8,128)(2,1)S(1)}, u32[]{:S(2)}, u32[]{:S(2)}) collective-permute-start(bf16[512,768]{1,0:T(8,128)(2,1)S(1)} %copy-done.23), channel_id=1, source_target_pairs={{0,4},{2,6},{4,0},{6,2},{1,5},{3,7},{5,1},{7,3},{8,12},{10,14},{12... | collective-permute-start | bytes 2359304 | tf_op jit(solution)/shard_map/ppermute | solution.py:438
  117.0 3.9 collective-permute-start.11
  130.8 8.4 %collective-permute-start.12 = (bf16[512,384]{1,0:T(8,128)(2,1)}, bf16[512,384]{1,0:T(8,128)(2,1)S(1)}, u32[]{:S(2)}, u32[]{:S(2)}) collective-permute-start(bf16[512,384]{1,0:T(8,128)(2,1)} %get-tuple-element.85), channel_id=1, source_target_pairs={{0,1},{1,0},{2,3},{3,2},{4,5},{5,4},{6,7},{7,6},{8,9},{9,8},{10,11... | collective-permute-start | bytes 1179656 | tf_op jit(solution)/shard_map/ppermute | solution.py:435
  140.7 3.6 collective-permute-start.13
  144.6 17.2 %collective-permute-start.16 = (bf16[512,384]{1,0:T(8,128)(2,1)S(1)}, bf16[512,384]{1,0:T(8,128)(2,1)S(1)}, u32[]{:S(2)}, u32[]{:S(2)}) collective-permute-start(bf16[512,384]{1,0:T(8,128)(2,1)S(1)} %multiply_convert_fusion.refs_2_.xa), channel_id=1, source_target_pairs={{0,4},{2,6},{4,0},{6,2},{1,5},{3,7},{5,1},{7,3},{8,12},{10,14},{12... | collective-permute-start | bytes 1179656 | tf_op jit(solution)/shard_map/ppermute | solution.py:438
  154.5 12.2 %collective-permute-start.14 = (bf16[512,384]{1,0:T(8,128)(2,1)S(1)}, bf16[512,384]{1,0:T(8,128)(2,1)S(1)}, u32[]{:S(2)}, u32[]{:S(2)}) collective-permute-start(bf16[512,384]{1,0:T(8,128)(2,1)S(1)} %multiply_convert_fusion.refs_2_.xa), channel_id=1, source_target_pairs={{0,1},{1,0},{2,3},{3,2},{4,5},{5,4},{6,7},{7,6},{8,9},{9,8},{10,11... | collective-permute-start | bytes 1179656 | tf_op jit(solution)/shard_map/ppermute | solution.py:435
  155.0 12.3 %collective-permute-start.15 = (bf16[512,384]{1,0:T(8,128)(2,1)S(1)}, bf16[512,384]{1,0:T(8,128)(2,1)S(1)}, u32[]{:S(2)}, u32[]{:S(2)}) collective-permute-start(bf16[512,384]{1,0:T(8,128)(2,1)S(1)} %multiply_convert_fusion.refs_2_.xa), channel_id=1, source_target_pairs={{0,2},{2,0},{4,6},{6,4},{1,3},{3,1},{5,7},{7,5},{8,10},{10,8},{12,... | collective-permute-start | bytes 1179656 | tf_op jit(solution)/shard_map/ppermute | solution.py:438
  161.8 5.5 collective-permute-start.17
  164.7 13.1 %collective-permute-start.20 = (bf16[512,384]{1,0:T(8,128)(2,1)S(1)}, bf16[512,384]{1,0:T(8,128)(2,1)S(1)}, u32[]{:S(2)}, u32[]{:S(2)}) collective-permute-start(bf16[512,384]{1,0:T(8,128)(2,1)S(1)} %copy-done.53), channel_id=1, source_target_pairs={{0,1},{1,0},{2,3},{3,2},{4,5},{5,4},{6,7},{7,6},{8,9},{9,8},{10,11... | collective-permute-start | bytes 1179656 | tf_op jit(solution)/shard_map/ppermute | solution.py:435
  165.2 19.9 %collective-permute-start.21 = (bf16[512,384]{1,0:T(8,128)(2,1)S(1)}, bf16[512,384]{1,0:T(8,128)(2,1)S(1)}, u32[]{:S(2)}, u32[]{:S(2)}) collective-permute-start(bf16[512,384]{1,0:T(8,128)(2,1)S(1)} %copy-done.55), channel_id=1, source_target_pairs={{0,1},{1,0},{2,3},{3,2},{4,5},{5,4},{6,7},{7,6},{8,9},{9,8},{10,11... | collective-permute-start | bytes 1179656 | tf_op jit(solution)/shard_map/ppermute | solution.py:435
  166.7 25.9 %collective-permute-start.22 = (bf16[512,384]{1,0:T(8,128)(2,1)S(1)}, bf16[512,384]{1,0:T(8,128)(2,1)S(1)}, u32[]{:S(2)}, u32[]{:S(2)}) collective-permute-start(bf16[512,384]{1,0:T(8,128)(2,1)S(1)} %copy-done.51), channel_id=1, source_target_pairs={{0,1},{1,0},{2,3},{3,2},{4,5},{5,4},{6,7},{7,6},{8,9},{9,8},{10,11... | collective-permute-start | bytes 1179656 | tf_op jit(solution)/shard_map/ppermute | solution.py:435
  172.6 56.2 %collective-permute-start.26 = (bf16[512,384]{1,0:T(8,128)(2,1)}, bf16[512,384]{1,0:T(8,128)(2,1)}, u32[]{:S(2)}, u32[]{:S(2)}) collective-permute-start(bf16[512,384]{1,0:T(8,128)(2,1)} %get-tuple-element.93), channel_id=1, source_target_pairs={{0,16},{8,24},{16,0},{24,8},{1,17},{9,25},{17,1},{25,9},{2,18},{10... | collective-permute-start | bytes 1179656 | tf_op jit(solution)/shard_map/ppermute | solution.py:441
  175.2 58.0 %collective-permute-start.24 = (bf16[512,384]{1,0:T(8,128)(2,1)}, bf16[512,384]{1,0:T(8,128)(2,1)S(1)}, u32[]{:S(2)}, u32[]{:S(2)}) collective-permute-start(bf16[512,384]{1,0:T(8,128)(2,1)} %get-tuple-element.91), channel_id=1, source_target_pairs={{0,24},{8,0},{16,8},{24,16},{1,25},{9,1},{17,9},{25,17},{2,26},{10... | collective-permute-start | bytes 1179656 | tf_op jit(solution)/shard_map/ppermute | solution.py:441
  177.8 55.9 %collective-permute-start.19 = (bf16[512,384]{1,0:T(8,128)(2,1)}, bf16[512,384]{1,0:T(8,128)(2,1)}, u32[]{:S(2)}, u32[]{:S(2)}) collective-permute-start(bf16[512,384]{1,0:T(8,128)(2,1)} %get-tuple-element.89), channel_id=1, source_target_pairs={{0,8},{8,16},{16,24},{24,0},{1,9},{9,17},{17,25},{25,1},{2,10},{10... | collective-permute-start | bytes 1179656 | tf_op jit(solution)/shard_map/ppermute | solution.py:441
  228.8 12.3 %collective-permute-start.27 = (bf16[512,384]{1,0:T(8,128)(2,1)}, bf16[512,384]{1,0:T(8,128)(2,1)S(1)}, u32[]{:S(2)}, u32[]{:S(2)}) collective-permute-start(bf16[512,384]{1,0:T(8,128)(2,1)} %collective-permute-done.26.xa.refs_1_), channel_id=1, source_target_pairs={{0,1},{1,0},{2,3},{3,2},{4,5},{5,4},{6,7},{7,6},{8,9},{9,8},{10,11... | collective-permute-start | bytes 1179656 | tf_op jit(solution)/shard_map/ppermute | solution.py:435
  231.7 25.3 %collective-permute-start.18 = (bf16[512,384]{1,0:T(8,128)(2,1)}, bf16[512,384]{1,0:T(8,128)(2,1)S(1)}, u32[]{:S(2)}, u32[]{:S(2)}) collective-permute-start(bf16[512,384]{1,0:T(8,128)(2,1)} %get-tuple-element.87.xa), channel_id=1, source_target_pairs={{0,1},{1,0},{2,3},{3,2},{4,5},{5,4},{6,7},{7,6},{8,9},{9,8},{10,11... | collective-permute-start | bytes 1179656 | tf_op jit(solution)/shard_map/ppermute | solution.py:435
  233.2 24.7 %collective-permute-start.25 = (bf16[512,384]{1,0:T(8,128)(2,1)S(1)}, bf16[512,384]{1,0:T(8,128)(2,1)S(1)}, u32[]{:S(2)}, u32[]{:S(2)}) collective-permute-start(bf16[512,384]{1,0:T(8,128)(2,1)S(1)} %collective-permute-done.24.refs_2_.xa), channel_id=1, source_target_pairs={{0,1},{1,0},{2,3},{3,2},{4,5},{5,4},{6,7},{7,6},{8,9},{9,8},{10,11... | collective-permute-start | bytes 1179656 | tf_op jit(solution)/shard_map/ppermute | solution.py:435
  233.7 32.7 %collective-permute-start.23 = (bf16[512,384]{1,0:T(8,128)(2,1)}, bf16[512,384]{1,0:T(8,128)(2,1)}, u32[]{:S(2)}, u32[]{:S(2)}) collective-permute-start(bf16[512,384]{1,0:T(8,128)(2,1)} %collective-permute-done.19.refs_0_.xa), channel_id=1, source_target_pairs={{0,1},{1,0},{2,3},{3,2},{4,5},{5,4},{6,7},{7,6},{8,9},{9,8},{10,11... | collective-permute-start | bytes 1179656 | tf_op jit(solution)/shard_map/ppermute | solution.py:435
  256.5 25.9 %collective-permute-start.29 = (bf16[512,768]{1,0:T(8,128)(2,1)S(1)}, bf16[512,768]{1,0:T(8,128)(2,1)S(1)}, u32[]{:S(2)}, u32[]{:S(2)}) collective-permute-start(bf16[512,768]{1,0:T(8,128)(2,1)S(1)} %slice_bitcast_fusion.3), channel_id=1, source_target_pairs={{0,1},{1,0},{2,3},{3,2},{4,5},{5,4},{6,7},{7,6},{8,9},{9,8},{10,11... | collective-permute-start | bytes 2359304 | tf_op jit(solution)/shard_map/ppermute | solution.py:435
  281.2 17.8 %collective-permute-start.28 = (bf16[512,768]{1,0:T(8,128)(2,1)S(1)}, bf16[512,768]{1,0:T(8,128)(2,1)S(1)}, u32[]{:S(2)}, u32[]{:S(2)}) collective-permute-start(bf16[512,768]{1,0:T(8,128)(2,1)S(1)} %slice_bitcast_fusion.4), channel_id=1, source_target_pairs={{0,1},{1,0},{2,3},{3,2},{4,5},{5,4},{6,7},{7,6},{8,9},{9,8},{10,11... | collective-permute-start | bytes 2359304 | tf_op jit(solution)/shard_map/ppermute | solution.py:435
  282.6 42.3 %collective-permute-start.32 = (bf16[512,768]{1,0:T(8,128)(2,1)S(1)}, bf16[512,768]{1,0:T(8,128)(2,1)S(1)}, u32[]{:S(2)}, u32[]{:S(2)}) collective-permute-start(bf16[512,768]{1,0:T(8,128)(2,1)S(1)} %fusion.13.refs_0_), channel_id=1, source_target_pairs={{0,16},{8,24},{16,0},{24,8},{1,17},{9,25},{17,1},{25,9},{2,18},{10... | collective-permute-start | bytes 2359304 | tf_op jit(solution)/shard_map/ppermute | solution.py:441
  298.1 26.2 %collective-permute-start.33 = (bf16[512,768]{1,0:T(8,128)(2,1)S(1)}, bf16[512,768]{1,0:T(8,128)(2,1)S(1)}, u32[]{:S(2)}, u32[]{:S(2)}) collective-permute-start(bf16[512,768]{1,0:T(8,128)(2,1)S(1)} %slice_bitcast_fusion.1), channel_id=1, source_target_pairs={{0,1},{1,0},{2,3},{3,2},{4,5},{5,4},{6,7},{7,6},{8,9},{9,8},{10,11... | collective-permute-start | bytes 2359304 | tf_op jit(solution)/shard_map/ppermute | solution.py:435
  299.2 48.2 %collective-permute-start.31 = (bf16[512,768]{1,0:T(8,128)(2,1)S(1)}, bf16[512,768]{1,0:T(8,128)(2,1)S(1)}, u32[]{:S(2)}, u32[]{:S(2)}) collective-permute-start(bf16[512,768]{1,0:T(8,128)(2,1)S(1)} %fusion.14.refs_0_), channel_id=1, source_target_pairs={{0,24},{8,0},{16,8},{24,16},{1,25},{9,1},{17,9},{25,17},{2,26},{10... | collective-permute-start | bytes 2359304 | tf_op jit(solution)/shard_map/ppermute | solution.py:441
  316.5 55.3 %collective-permute-start.30 = (bf16[512,768]{1,0:T(8,128)(2,1)}, bf16[512,768]{1,0:T(8,128)(2,1)}, u32[]{:S(2)}, u32[]{:S(2)}) collective-permute-start(bf16[512,768]{1,0:T(8,128)(2,1)} %slice_bitcast_fusion.2), channel_id=1, source_target_pairs={{0,1},{1,0},{2,3},{3,2},{4,5},{5,4},{6,7},{7,6},{8,9},{9,8},{10,11... | collective-permute-start | bytes 2359304 | tf_op jit(solution)/shard_map/ppermute | solution.py:435
  324.5 22.8 %collective-permute-start.34 = (bf16[512,768]{1,0:T(8,128)(2,1)S(1)}, bf16[512,768]{1,0:T(8,128)(2,1)S(1)}, u32[]{:S(2)}, u32[]{:S(2)}) collective-permute-start(bf16[512,768]{1,0:T(8,128)(2,1)S(1)} %fusion.11), channel_id=1, source_target_pairs={{0,8},{8,16},{16,24},{24,0},{1,9},{9,17},{17,25},{25,1},{2,10},{10... | collective-permute-start | bytes 2359304 | tf_op jit(solution)/shard_map/ppermute | solution.py:441
  360.9 15.5 %collective-permute-start.35 = (bf16[512,768]{1,0:T(8,128)(2,1)S(1)}, bf16[512,768]{1,0:T(8,128)(2,1)}, u32[]{:S(2)}, u32[]{:S(2)}) collective-permute-start(bf16[512,768]{1,0:T(8,128)(2,1)S(1)} %slice_bitcast_fusion), channel_id=1, source_target_pairs={{0,1},{1,0},{2,3},{3,2},{4,5},{5,4},{6,7},{7,6},{8,9},{9,8},{10,11... | collective-permute-start | bytes 2359304 | tf_op jit(solution)/shard_map/ppermute | solution.py:435
  363.0 112.9 %all-to-all-start.1 = ((bf16[4,3,192,1024]{3,2,1,0:T(8,128)(2,1)}), bf16[4,3,192,1024]{3,2,1,0:T(8,128)(2,1)}, u32[]{:S(2)}, u32[]{:S(2)}) async-start(bf16[4,3,192,1024]{3,2,1,0:T(8,128)(2,1)} %pad_maximum_fusion.1.refs_0_), calls=%async_computation.1 | async-start | bytes 9437184 | tf_op jit(solution)/shard_map/all_to_all | solution.py:644
  371.5 194.6 %reduce-scatter.2.cloned.1.call-start = ((), (), s32[]{:S(2)}) async-start(), calls=%async_computation.5 | async-start | bytes 5013504 | tf_op jit(solution)/shard_map/reduce_scatter | solution.py:665
  383.8 2.5 collective-permute-start.36
  387.8 11.2 %collective-permute-start.37 = (bf16[512,384]{1,0:T(8,128)(2,1)S(1)}, bf16[512,384]{1,0:T(8,128)(2,1)S(1)}, u32[]{:S(2)}, u32[]{:S(2)}) collective-permute-start(bf16[512,384]{1,0:T(8,128)(2,1)S(1)} %fusion.33), channel_id=1, source_target_pairs={{0,4},{2,6},{4,0},{6,2},{1,5},{3,7},{5,1},{7,3},{8,12},{10,14},{12... | collective-permute-start | bytes 1179656 | tf_op jit(solution)/shard_map/ppermute | solution.py:438
  399.9 3.6 collective-permute-start.38
  405.1 10.0 %collective-permute-start.39 = (bf16[512,384]{1,0:T(8,128)(2,1)}, bf16[512,384]{1,0:T(8,128)(2,1)}, u32[]{:S(2)}, u32[]{:S(2)}) collective-permute-start(bf16[512,384]{1,0:T(8,128)(2,1)} %fusion.63.refs_10_), channel_id=1, source_target_pairs={{0,1},{1,0},{2,3},{3,2},{4,5},{5,4},{6,7},{7,6},{8,9},{9,8},{10,11... | collective-permute-start | bytes 1179656 | tf_op jit(solution)/shard_map/ppermute | solution.py:435
  427.1 24.3 %collective-permute-start.42 = (bf16[2,512,768]{2,1,0:T(8,128)(2,1)}, bf16[2,512,768]{2,1,0:T(8,128)(2,1)}, u32[]{:S(2)}, u32[]{:S(2)}) collective-permute-start(bf16[2,512,768]{2,1,0:T(8,128)(2,1)} %get-tuple-element.129), channel_id=1, source_target_pairs={{0,2},{2,0},{4,6},{6,4},{1,3},{3,1},{5,7},{7,5},{8,10},{10,8},{12,... | collective-permute-start | bytes 4718600 | tf_op jit(solution)/shard_map/ppermute | solution.py:438
  431.9 6.5 %collective-permute-start.40 = (bf16[2,512,384]{2,1,0:T(8,128)(2,1)}, bf16[2,512,384]{2,1,0:T(8,128)(2,1)}, u32[]{:S(2)}, u32[]{:S(2)}) collective-permute-start(bf16[2,512,384]{2,1,0:T(8,128)(2,1)} %get-tuple-element.122), channel_id=1, source_target_pairs={{0,2},{2,0},{4,6},{6,4},{1,3},{3,1},{5,7},{7,5},{8,10},{10,8},{12,... | collective-permute-start | bytes 2359304 | tf_op jit(solution)/shard_map/ppermute | solution.py:438
  439.6 21.7 %collective-permute-start.41 = (bf16[512,384]{1,0:T(8,128)(2,1)S(1)}, bf16[512,384]{1,0:T(8,128)(2,1)S(1)}, u32[]{:S(2)}, u32[]{:S(2)}) collective-permute-start(bf16[512,384]{1,0:T(8,128)(2,1)S(1)} %fusion.34), channel_id=1, source_target_pairs={{0,4},{2,6},{4,0},{6,2},{1,5},{3,7},{5,1},{7,3},{8,12},{10,14},{12... | collective-permute-start | bytes 1179656 | tf_op jit(solution)/shard_map/ppermute | solution.py:438
  453.9 24.2 %collective-permute-start.43 = (bf16[512,768]{1,0:T(8,128)(2,1)}, bf16[512,768]{1,0:T(8,128)(2,1)}, u32[]{:S(2)}, u32[]{:S(2)}) collective-permute-start(bf16[512,768]{1,0:T(8,128)(2,1)} %fusion.27), channel_id=1, source_target_pairs={{0,4},{2,6},{4,0},{6,2},{1,5},{3,7},{5,1},{7,3},{8,12},{10,14},{12... | collective-permute-start | bytes 2359304 | tf_op jit(solution)/shard_map/ppermute | solution.py:438
  483.9 11.2 %collective-permute-start.44 = (bf16[512,384]{1,0:T(8,128)(2,1)}, bf16[512,384]{1,0:T(8,128)(2,1)S(1)}, u32[]{:S(2)}, u32[]{:S(2)}) collective-permute-start(bf16[512,384]{1,0:T(8,128)(2,1)} %get-tuple-element.135), channel_id=1, source_target_pairs={{0,1},{1,0},{2,3},{3,2},{4,5},{5,4},{6,7},{7,6},{8,9},{9,8},{10,11... | collective-permute-start | bytes 1179656 | tf_op jit(solution)/shard_map/ppermute | solution.py:435
  495.4 3.7 collective-permute-start.45
  503.0 1.3 collective-permute-start.48
  503.1 29.1 %collective-permute-start.54 = (bf16[2,4,48,1536]{3,2,1,0:T(8,128)(2,1)}, bf16[2,4,48,1536]{3,2,1,0:T(8,128)(2,1)}, u32[]{:S(2)}, u32[]{:S(2)}) collective-permute-start(bf16[2,4,48,1536]{3,2,1,0:T(8,128)(2,1)} %get-tuple-element.142), channel_id=1, source_target_pairs={{0,2},{2,0},{4,6},{6,4},{1,3},{3,1},{5,7},{7,5},{8,10},{10,8},{12,... | collective-permute-start | bytes 3538952 | tf_op jit(solution)/shard_map/ppermute | solution.py:438
  504.3 3.7 collective-permute-start.49
  508.0 14.4 %collective-permute-start.50 = (f32[864]{0:T(1024)S(1)}, f32[864]{0:T(1024)S(1)}, u32[]{:S(2)}, u32[]{:S(2)}) collective-permute-start(f32[864]{0:T(1024)S(1)} %get-tuple-element.195), channel_id=1, source_target_pairs={{0,8},{8,16},{16,24},{24,0},{1,9},{9,17},{17,25},{25,1},{2,10},{10... | collective-permute-start | bytes 10376 | tf_op jit(solution)/shard_map/ppermute | solution.py:441
  519.2 4.6 collective-permute-start.51
  521.3 3.7 collective-permute-start.52
  525.7 5.1 collective-permute-start.53
  528.6 19.0 %collective-permute-start.47 = (bf16[512,384]{1,0:T(8,128)(2,1)}, bf16[512,384]{1,0:T(8,128)(2,1)S(1)}, u32[]{:S(2)}, u32[]{:S(2)}) collective-permute-start(bf16[512,384]{1,0:T(8,128)(2,1)} %fusion.24), channel_id=1, source_target_pairs={{0,1},{1,0},{2,3},{3,2},{4,5},{5,4},{6,7},{7,6},{8,9},{9,8},{10,11... | collective-permute-start | bytes 1179656 | tf_op jit(solution)/shard_map/ppermute | solution.py:435
  530.1 16.4 %collective-permute-start.46 = (bf16[512,384]{1,0:T(8,128)(2,1)S(1)}, bf16[512,384]{1,0:T(8,128)(2,1)S(1)}, u32[]{:S(2)}, u32[]{:S(2)}) collective-permute-start(bf16[512,384]{1,0:T(8,128)(2,1)S(1)} %convert_element_type.316), channel_id=1, source_target_pairs={{0,1},{1,0},{2,3},{3,2},{4,5},{5,4},{6,7},{7,6},{8,9},{9,8},{10,11... | collective-permute-start | bytes 1179656 | tf_op jit(solution)/shard_map/ppermute | solution.py:435
  533.3 16.6 %collective-permute-start.55 = (bf16[4,48,1536]{2,1,0:T(8,128)(2,1)S(1)}, bf16[4,48,1536]{2,1,0:T(8,128)(2,1)S(1)}, u32[]{:S(2)}, u32[]{:S(2)}) collective-permute-start(bf16[4,48,1536]{2,1,0:T(8,128)(2,1)S(1)} %fusion.32), channel_id=1, source_target_pairs={{0,4},{2,6},{4,0},{6,2},{1,5},{3,7},{5,1},{7,3},{8,12},{10,14},{12... | collective-permute-start | bytes 1769480 | tf_op jit(solution)/shard_map/ppermute | solution.py:438
  551.9 12.7 %collective-permute-start.56 = (bf16[48,1536]{1,0:T(8,128)(2,1)S(1)}, bf16[48,1536]{1,0:T(8,128)(2,1)S(1)}, u32[]{:S(2)}, u32[]{:S(2)}) collective-permute-start(bf16[48,1536]{1,0:T(8,128)(2,1)S(1)} %get-tuple-element.219), channel_id=1, source_target_pairs={{0,8},{8,16},{16,24},{24,0},{1,9},{9,17},{17,25},{25,1},{2,10},{10... | collective-permute-start | bytes 442376 | tf_op jit(solution)/shard_map/ppermute | solution.py:441
  551.9 12.7 %collective-permute-start.57 = (bf16[48,1536]{1,0:T(8,128)(2,1)S(1)}, bf16[48,1536]{1,0:T(8,128)(2,1)S(1)}, u32[]{:S(2)}, u32[]{:S(2)}) collective-permute-start(bf16[48,1536]{1,0:T(8,128)(2,1)S(1)} %get-tuple-element.221), channel_id=1, source_target_pairs={{0,16},{8,24},{16,0},{24,8},{1,17},{9,25},{17,1},{25,9},{2,18},{10... | collective-permute-start | bytes 442376 | tf_op jit(solution)/shard_map/ppermute | solution.py:441
  554.5 10.1 %collective-permute-start.58 = (bf16[48,1536]{1,0:T(8,128)(2,1)S(1)}, bf16[48,1536]{1,0:T(8,128)(2,1)S(1)}, u32[]{:S(2)}, u32[]{:S(2)}) collective-permute-start(bf16[48,1536]{1,0:T(8,128)(2,1)S(1)} %get-tuple-element.220), channel_id=1, source_target_pairs={{0,24},{8,0},{16,8},{24,16},{1,25},{9,1},{17,9},{25,17},{2,26},{10... | collective-permute-start | bytes 442376 | tf_op jit(solution)/shard_map/ppermute | solution.py:441
  (71 other events, 844.1 us)
Sparse Core Ops, SparseCore 0:
  12.2 63.1 all-gather.2
  235.4 74.1 all-gather.4
  438.5 94.7 reduce-scatter.1

commit v4 on v3

--- a/solution.py
+++ b/solution.py
@@ -712,17 +712,17 @@
     normal_one = tok_h * scale_one
     scaled_one = da_h * gain_one_h[None, :]
     mean_one = both_halves(jnp.sum(scaled_one * normal_one, axis=1))[:, None] / D
-    attn_gain_part = jnp.sum(after(da_h, mean_one) * normal_one, axis=0)
+    attn_gain_part = jnp.sum(da_h * normal_one, axis=0)
     tokens_grad_h = middle_grad + scale_one * (scaled_one - normal_one * mean_one)
 
     tokens_grad = whole_rows(tokens_grad_h.astype(bf16)).astype(f32)
 
-    layer_out = whole_rows(after(layer_h, mean_one).astype(bf16))
-    grad_w = after(grad_w, tokens_grad_h, dense_part)
+    layer_out = whole_rows(after(layer_h, tokens_grad_h).astype(bf16))
+    grad_w = after(grad_w, tokens_grad_h)
     expert_gate_up_grad = grad_w[:, :2].astype(f32)
     expert_down_grad = grad_w[:, 2].astype(f32).transpose(0, 2, 1)
     if small:
-        dense_grad = reduce_far(dense_part, bf16, None, tokens_grad_h)
+        dense_grad = reduce_far(dense_part, bf16)
     else:
         dense_grad = dense_reduce(dense_pairs)
     qkv_grad = dense_grad[:, : 3 * heads_width].reshape(rows_own, 3, heads_width).transpose(1, 0, 2)
@@ -739,13 +739,10 @@
     tail = jnp.concatenate(
         [router_part, placed(attn_gain_part)[:, None], placed(ffn_gain_part)[:, None]], axis=1
     )
-    if small:
-        order = back_offs // rows_own
-        blocks = tail.reshape(16, rows_own * (E + 2))[order].reshape(2, 2, 4, rows_own * (E + 2))
-        tail = reduce_far(reduce_near(blocks[:, 0], blocks[:, 1]), f32)
-        tail = tail.reshape(rows_own, E + 2)
-    else:
-        tail = lax.psum_scatter(tail, ("fsdp", "ctx"), scatter_dimension=0, tiled=True)
+    tail = after(tail, dense_part).reshape(F * C, rows_own * (E + 2))
+    tail = jnp.sum(lax.all_to_all(tail, ("fsdp", "ctx"), 0, 0, tiled=True), axis=0)
+    tail = after(tail, dense_grad, expert_gate_up_grad, expert_down_grad)
+    tail = tail.reshape(rows_own, E + 2)
     tail = tail + yx(tail)
     return (
         layer_out,

time: 584 us -> 574 us (0.983)
  other arithmetic: 61.8 us -> 52.3 us
    all_to_all x0 -> x1, waiting for transfers between devices: none -> 5.85 us  [per_device(): lax.all_to_all(tail, ('fsdp', 'ctx'), 0, 0, tiled=True)]
    ppermute x15 -> x12, waiting for transfers between devices: 51.5 us -> 49.2 us  [zs(): lax.ppermute(v, 'fsdp', [(i, i // EL * EL + (i % EL + s) % EL) for i in r...]
    ppermute x15 -> x12, starting transfers between devices: 33.7 us -> 31.7 us  [zs(): lax.ppermute(v, 'fsdp', [(i, i // EL * EL + (i % EL + s) % EL) for i in r...]
    ppermute x21 -> x19, starting transfers between devices: 40.9 us -> 39 us  [cx(): return lax.ppermute(v, 'ctx', [(i, i ^ flip) for i in range(C)])]
    unnamed x145 -> x131, local copies, waits for them, and re-layouts: 11.7 us -> 10.2 us
    ppermute x21 -> x19, waiting for transfers between devices: 47.5 us -> 48 us  [cx(): return lax.ppermute(v, 'ctx', [(i, i ^ flip) for i in range(C)])]
  transfers between devices with their start and end apart: 64 -> 60, of which waited for: 32 -> 30; matrix products, arithmetic and copies ran while one was open for 18% -> 16% of each run, Pallas kernels for 19% -> 19%
where the time goes in v4:
time: 574 us; the launch traced here: 565 us
  waiting for transfers between devices  212 us (37%)
  starting transfers between devices  117 us (20%)
  Pallas kernels  114 us (20%)
  other arithmetic  52.3 us (9%)
  local copies, waits for them, and re-layouts  37.7 us (7%)
  matrix products  16.9 us (3%)
  between operations  14.9 us (3%)
    pallas_call x5, Pallas kernels, ffn(): pl.pallas_call(functools.partial(ffn_body, routed), grid=(1,), out_shape=...  64.1 us
    ppermute x23, waiting for transfers between devices, yx(): return lax.ppermute(v, 'tp', [(0, 1), (1, 0)])  61.9 us
    pallas_call x8, Pallas kernels, run(): pl.pallas_call(inner, out_shape=outs, in_specs=[SMEM] + [VM] * len(args)...  50.1 us
    ppermute x12, waiting for transfers between devices, zs(): lax.ppermute(v, 'fsdp', [(i, i // EL * EL + (i % EL + s) % EL) for i in r...  49.2 us
    ppermute x19, waiting for transfers between devices, cx(): return lax.ppermute(v, 'ctx', [(i, i ^ flip) for i in range(C)])  48 us
    ppermute x19, starting transfers between devices, cx(): return lax.ppermute(v, 'ctx', [(i, i ^ flip) for i in range(C)])  39 us
    all_gather x2, waiting for transfers between devices, gathered(): return lax.all_gather(shard, ('fsdp', 'ctx'), axis=axis, tiled=True)  33.3 us
    ppermute x12, starting transfers between devices, zs(): lax.ppermute(v, 'fsdp', [(i, i // EL * EL + (i % EL + s) % EL) for i in r...  31.7 us
  transfers between devices with their start and end apart: 60, of which 30 were waited for; matrix products, arithmetic and copies ran while one was open for 16% of the time, Pallas kernels for 19%

profile of v4, /device:TPU:0, one launch (start us, length us, event | category | flops | bytes accessed | tf_op | source)
XLA Modules:
  0.0 564.9 jit_solution(9896851325555425918)
XLA Ops:
  14.1 2.9 collective-permute-start.3
  19.9 4.0 pad_maximum_fusion.refs_10_
  23.9 3.6 collective-permute-done
  30.9 3.7 pack.2
  34.6 2.4 collective-permute-start.5
  38.6 2.6 collective-permute-start.7
  42.5 33.3 %all-gather.3.cloned.1.call-done.refs_3_.refs_5_ = bf16[768,1664]{1,0:T(8,128)(2,1)} async-done(((bf16[48,1664]{1,0:T(8,128)(2,1)}), bf16[768,1664]{1,0:T(8,128)(2,1)}) %all-gather.3.cloned.1.call-update) | async-done | bytes 2555920 | tf_op jit(solution)/shard_map/all_gather | solution.py:457
  79.5 5.1 qkv.1
  84.9 2.2 collective-permute-done.9.refs_3_
  88.0 10.0 %all-to-all-start = ((bf16[4,3,192,1024]{3,2,1,0:T(8,128)(2,1)}), bf16[4,3,192,1024]{3,2,1,0:T(8,128)(2,1)}, u32[]{:S(2)}, u32[]{:S(2)}) async-start(bf16[4,3,192,1024]{3,2,1,0:T(8,128)(2,1)} %pad_maximum_fusion.refs_10_), calls=%async_computation | async-start | bytes 9437184 | tf_op jit(solution)/shard_map/all_to_all | solution.py:584
  99.6 17.8 %collective-permute-done.10.refs_4_ = bf16[512,768]{1,0:T(8,128)(2,1)S(1)} collective-permute-done((bf16[512,768]{1,0:T(8,128)(2,1)S(1)}, bf16[512,768]{1,0:T(8,128)(2,1)S(1)}, u32[]{:S(2)}, u32[]{:S(2)}) %collective-permute-start.10) | collective-permute-done | bytes 786464 | tf_op jit(solution)/shard_map/ppermute | solution.py:438
  122.2 9.1 %attn.1 = (bf16[512,384]{1,0:T(8,128)(2,1)}, f32[512,384]{1,0:T(8,128)}, bf16[512,384]{1,0:T(8,128)(2,1)}, f32[8,512]{1,0:T(8,128)}) custom-call(s32[3]{0:T(128)} %pad_add_fusion.2.refs_0_.sc.rt, bf16[512,384]{1,0:T(8,128)(2,1)} %get-tuple-element.82.refs_1_, bf16[512,768]{1,0:T(8,128)(2,1)} %get-tuple-element.83.refs_2_, bf16[512,768]{1,0:T(8,128)(2,1)} %copy-done.22, ...), custom_call_target="tpu_custom_call" | custom-call | flops 18699999232 | tf_op jit(solution)/shard_map/attn/pallas_call | solution.py:50
  131.7 7.9 %collective-permute-done.12 = bf16[512,384]{1,0:T(8,128)(2,1)S(1)} collective-permute-done((bf16[512,384]{1,0:T(8,128)(2,1)}, bf16[512,384]{1,0:T(8,128)(2,1)S(1)}, u32[]{:S(2)}, u32[]{:S(2)}) %collective-permute-start.12) | collective-permute-done | bytes 393248 | tf_op jit(solution)/shard_map/ppermute | solution.py:435
  141.9 2.9 collective-permute-done.13
  145.0 9.9 %collective-permute-start.16 = (bf16[512,384]{1,0:T(8,128)(2,1)S(1)}, bf16[512,384]{1,0:T(8,128)(2,1)S(1)}, u32[]{:S(2)}, u32[]{:S(2)}) collective-permute-start(bf16[512,384]{1,0:T(8,128)(2,1)S(1)} %multiply_convert_fusion.refs_2_.xa), channel_id=1, source_target_pairs={{0,4},{2,6},{4,0},{6,2},{1,5},{3,7},{5,1},{7,3},{8,12},{10,14},{12... | collective-permute-start | bytes 1179656 | tf_op jit(solution)/shard_map/ppermute | solution.py:438
  155.4 2.7 collective-permute-start.15
  158.1 4.1 collective-permute-done.16.refs_4_
  162.2 2.9 collective-permute-start.17
  169.2 3.8 pack.3
  173.0 2.5 collective-permute-start.26
  175.5 2.7 collective-permute-start.24
  179.9 5.5 collective-permute-done.21.wb
  185.4 7.5 %collective-permute-done.22.wb = bf16[512,384]{1,0:T(8,128)(2,1)S(1)} collective-permute-done((bf16[512,384]{1,0:T(8,128)(2,1)S(1)}, bf16[512,384]{1,0:T(8,128)(2,1)S(1)}, u32[]{:S(2)}, u32[]{:S(2)}) %collective-permute-start.22) | collective-permute-done | bytes 393248 | tf_op jit(solution)/shard_map/ppermute | solution.py:435
  193.0 36.2 %collective-permute-done.26.xa.refs_1_ = bf16[512,384]{1,0:T(8,128)(2,1)} collective-permute-done((bf16[512,384]{1,0:T(8,128)(2,1)}, bf16[512,384]{1,0:T(8,128)(2,1)}, u32[]{:S(2)}, u32[]{:S(2)}) %collective-permute-start.26) | collective-permute-done | bytes 393248 | tf_op jit(solution)/shard_map/ppermute | solution.py:441
  235.7 5.9 %collective-permute-done.27.xb = bf16[512,384]{1,0:T(8,128)(2,1)} collective-permute-done((bf16[512,384]{1,0:T(8,128)(2,1)}, bf16[512,384]{1,0:T(8,128)(2,1)}, u32[]{:S(2)}, u32[]{:S(2)}) %collective-permute-start.27) | collective-permute-done | bytes 393248 | tf_op jit(solution)/shard_map/ppermute | solution.py:435
  241.6 13.4 %expert_ffn.4 = (bf16[2,512,768]{2,1,0:T(8,128)(2,1)}, f32[768,128]{1,0:T(8,128)}, bf16[4,512,2048]{2,1,0:T(8,128)(2,1)}, bf16[4,512,1024]{2,1,0:T(8,128)(2,1)},...) custom-call(s32[3]{0:T(128)} %pad_add_fusion.2.refs_0_.sc.rt, ...), custom_call_target="tpu_custom_call" | custom-call | flops 16000000000 | tf_op jit(solution)/shard_map/expert_ffn/pallas_call | solution.py:369
  258.3 8.5 %collective-permute-done.23.xb = bf16[512,384]{1,0:T(8,128)(2,1)} collective-permute-done((bf16[512,384]{1,0:T(8,128)(2,1)S(1)}, bf16[512,384]{1,0:T(8,128)(2,1)}, u32[]{:S(2)}, u32[]{:S(2)}) %collective-permute-start.23) | collective-permute-done | bytes 393248 | tf_op jit(solution)/shard_map/ppermute | solution.py:435
  266.8 13.4 %expert_ffn.5 = (bf16[2,512,768]{2,1,0:T(8,128)(2,1)}, f32[768,128]{1,0:T(8,128)}, bf16[4,512,2048]{2,1,0:T(8,128)(2,1)}, bf16[4,512,1024]{2,1,0:T(8,128)(2,1)},...) custom-call(s32[3]{0:T(128)} %pad_add_fusion.2.refs_0_.sc.rt, ...), custom_call_target="tpu_custom_call", output_to_operand_aliasing={{2}: (9, {}), {3}: (10, {}), {4}: (11, {}), {5}: (12, {})} | custom-call | flops 16000000000 | tf_op jit(solution)/shard_map/expert_ffn/pallas_call | solution.py:369
  283.9 13.2 %expert_ffn.6 = (bf16[2,512,768]{2,1,0:T(8,128)(2,1)}, f32[768,128]{1,0:T(8,128)}, bf16[4,512,2048]{2,1,0:T(8,128)(2,1)}, bf16[4,512,1024]{2,1,0:T(8,128)(2,1)},...) custom-call(s32[3]{0:T(128)} %pad_add_fusion.2.refs_0_.sc.rt, ...), custom_call_target="tpu_custom_call", output_to_operand_aliasing={{2}: (8, {}), {3}: (9, {}), {4}: (10, {}), {5}: (11, {})} | custom-call | flops 16000000000 | tf_op jit(solution)/shard_map/expert_ffn/pallas_call | solution.py:369
  299.6 2.5 collective-permute-start.31
  302.1 12.8 %expert_ffn.7 = (bf16[2,512,768]{2,1,0:T(8,128)(2,1)}, f32[768,128]{1,0:T(8,128)}, bf16[4,512,2048]{2,1,0:T(8,128)(2,1)}, bf16[4,512,1024]{2,1,0:T(8,128)(2,1)},...) custom-call(s32[3]{0:T(128)} %pad_add_fusion.2.refs_0_.sc.rt, ...), custom_call_target="tpu_custom_call", output_to_operand_aliasing={{2}: (8, {}), {3}: (9, {}), {4}: (10, {}), {5}: (11, {})} | custom-call | flops 16000000000 | tf_op jit(solution)/shard_map/expert_ffn/pallas_call | solution.py:369
  317.8 6.7 %bitcast_convert_fusion = bf16[768,1024]{1,0:T(8,128)(2,1)S(1)} fusion(bf16[4,512,768]{2,1,0:T(8,128)(2,1)} %get-tuple-element.115, bf16[4,512,1024]{2,1,0:T(8,128)(2,1)} %get-tuple-element.116), kind=kOutput, calls=%fused_computation.9 | convolution fusion | flops 3222011904 | bytes 8912896 | tf_op jit(solution)/shard_map/dot_general | solution.py:638
  325.4 3.5 fusion.5
  328.9 3.5 fusion.8
  332.4 2.5 pad_maximum_fusion.1.refs_0_
  334.9 13.0 %collective-permute-done.31.refs_1_.refs_3_ = bf16[512,768]{1,0:T(8,128)(2,1)S(1)} collective-permute-done((bf16[512,768]{1,0:T(8,128)(2,1)S(1)}, bf16[512,768]{1,0:T(8,128)(2,1)S(1)}, u32[]{:S(2)}, u32[]{:S(2)}) %collective-permute-start.31) | collective-permute-done | bytes 786464 | tf_op jit(solution)/shard_map/ppermute | solution.py:441
  349.0 11.3 %shared_ffn.1 = (bf16[2,512,768]{2,1,0:T(8,128)(2,1)}, bf16[1,512,2048]{2,1,0:T(8,128)(2,1)}, bf16[1,512,1024]{2,1,0:T(8,128)(2,1)}) custom-call(s32[3]{0:T(128)} %pad_add_fusion.2.refs_0_.sc.rt, bf16[512,384]{1,0:T(8,128)(2,1)} %copy-done.12, bf16[512,384]{1,0:T(8,128)(2,1)} %copy-done.10, bf16[512,384]{1,0:T(8,128)(2,1)} %copy-done.2, ...), custom_call_target="tpu_custom_call" | custom-call | tf_op jit(solution)/shard_map/shared_ffn/pallas_call | solution.py:369
  363.3 8.5 %all-to-all-start.1 = ((bf16[4,3,192,1024]{3,2,1,0:T(8,128)(2,1)}), bf16[4,3,192,1024]{3,2,1,0:T(8,128)(2,1)}, u32[]{:S(2)}, u32[]{:S(2)}) async-start(bf16[4,3,192,1024]{3,2,1,0:T(8,128)(2,1)} %pad_maximum_fusion.1.refs_0_), calls=%async_computation.1 | async-start | bytes 9437184 | tf_op jit(solution)/shard_map/all_to_all | solution.py:644
  372.1 2.4 fusion.12.refs_2_
  374.4 2.3 collective-permute-done.35
  376.7 2.4 convert_add_fusion.refs_6_
  379.1 5.0 unpack.1
  384.1 2.5 collective-permute-done.36
  392.1 7.2 %collective-permute-done.37 = bf16[512,384]{1,0:T(8,128)(2,1)S(1)} collective-permute-done((bf16[512,384]{1,0:T(8,128)(2,1)S(1)}, bf16[512,384]{1,0:T(8,128)(2,1)S(1)}, u32[]{:S(2)}, u32[]{:S(2)}) %collective-permute-start.37) | collective-permute-done | bytes 393248 | tf_op jit(solution)/shard_map/ppermute | solution.py:438
  407.1 2.6 pad_maximum_fusion.2.refs_15_
  409.7 5.8 %collective-permute-done.39.refs_11_ = bf16[512,384]{1,0:T(8,128)(2,1)} collective-permute-done((bf16[512,384]{1,0:T(8,128)(2,1)}, bf16[512,384]{1,0:T(8,128)(2,1)}, u32[]{:S(2)}, u32[]{:S(2)}) %collective-permute-start.39) | collective-permute-done | bytes 393248 | tf_op jit(solution)/shard_map/ppermute | solution.py:435
  415.6 11.9 %attn_back.1 = (bf16[512,384]{1,0:T(8,128)(2,1)}, bf16[2,512,768]{2,1,0:T(8,128)(2,1)}, bf16[2,512,768]{2,1,0:T(8,128)(2,1)}) custom-call(s32[3]{0:T(128)} %pad_add_fusion.2.refs_0_.sc.rt, bf16[512,384]{1,0:T(8,128)(2,1)} %get-tuple-element.82.refs_1_, bf16[512,768]{1,0:T(8,128)(2,1)} %get-tuple-element.83.refs_2_, bf16[512,768]{1,0:T(8,128)(2,1)} %copy-done.22, ...), custom_call_target="tpu_custom_call" | custom-call | tf_op jit(solution)/shard_map/attn_back/pallas_call | solution.py:50
  427.5 2.9 collective-permute-start.42
  438.7 11.6 %collective-permute-start.41 = (bf16[512,384]{1,0:T(8,128)(2,1)S(1)}, bf16[512,384]{1,0:T(8,128)(2,1)S(1)}, u32[]{:S(2)}, u32[]{:S(2)}) collective-permute-start(bf16[512,384]{1,0:T(8,128)(2,1)S(1)} %fusion.34), channel_id=1, source_target_pairs={{0,4},{2,6},{4,0},{6,2},{1,5},{3,7},{5,1},{7,3},{8,12},{10,14},{12... | collective-permute-start | bytes 1179656 | tf_op jit(solution)/shard_map/ppermute | solution.py:438
  450.3 2.5 fusion.27
  455.6 4.7 collective-permute-done.41
  460.3 2.2 slice_add_fusion.refs_9_
  462.5 13.7 %all-to-all-done.1.refs_8_ = bf16[4,3,192,1024]{3,2,1,0:T(8,128)(2,1)} async-done(((bf16[4,3,192,1024]{3,2,1,0:T(8,128)(2,1)}), bf16[4,3,192,1024]{3,2,1,0:T(8,128)(2,1)}, u32[]{:S(2)}, u32[]{:S(2)}) %all-to-all-start.1) | async-done | bytes 4718624 | tf_op jit(solution)/shard_map/all_to_all | solution.py:644
  477.1 5.8 %proj_back.1 = (bf16[512,1152]{1,0:T(8,128)(2,1)}, f32[512,384]{1,0:T(8,128)}, bf16[512,384]{1,0:T(8,128)(2,1)}) custom-call(s32[3]{0:T(128)} %pad_add_fusion.2.refs_0_.sc.rt, bf16[512,384]{1,0:T(8,128)(2,1)} %get-tuple-element.127.refs_1_, bf16[2,512,768]{2,1,0:T(8,128)(2,1)} %get-tuple-element.128.refs_2_, ...), custom_call_target="tpu_custom_call" | custom-call | flops 5500000256 | tf_op jit(solution)/shard_map/proj_back/pallas_call | solution.py:50
  484.8 5.8 %grad_blocks.1 = (bf16[2,4,48,1536]{3,2,1,0:T(8,128)(2,1)}, bf16[2,4,48,1536]{3,2,1,0:T(8,128)(2,1)}) custom-call(s32[16]{0:T(128)} %mul.197.refs_0_, bf16[512,768]{1,0:T(8,128)(2,1)} %get-tuple-element.131.refs_1_, bf16[512,1152]{1,0:T(8,128)(2,1)} %get-tuple-element.132.refs_2_, bf16[512,768]{1,0:T(8,128)(2,1)} %pad_maximum_fusion.3.refs_3_, ...), custom_call_target="tpu_custom_call" | custom-call | flops 3300000000 | tf_op jit(solution)/shard_map/grad_blocks/pallas_call | solution.py:50
  490.7 3.3 collective-permute-done.44
  495.5 2.5 collective-permute-done.45
  500.8 5.3 slice_convert_fusion
  508.0 3.5 convert_bitcast_fusion
  511.6 4.9 collective-permute-done.46
  516.6 4.2 collective-permute-done.49
  521.0 13.1 %collective-permute-start.50 = (bf16[48,1536]{1,0:T(8,128)(2,1)S(1)}, bf16[48,1536]{1,0:T(8,128)(2,1)S(1)}, u32[]{:S(2)}, u32[]{:S(2)}) collective-permute-start(bf16[48,1536]{1,0:T(8,128)(2,1)S(1)} %get-tuple-element.204), channel_id=1, source_target_pairs={{0,8},{8,16},{16,24},{24,0},{1,9},{9,17},{17,25},{25,1},{2,10},{10... | collective-permute-start | bytes 442376 | tf_op jit(solution)/shard_map/ppermute | solution.py:441
  539.6 3.5 all-to-all-start.2
  544.0 5.8 %all-to-all-done.2 = f32[16,1,864]{2,1,0:T(1,128)S(1)} async-done(((f32[16,1,864]{2,1,0:T(1,128)}), f32[16,1,864]{2,1,0:T(1,128)S(1)}, u32[]{:S(2)}, u32[]{:S(2)}) %all-to-all-start.2) | async-done | bytes 55328 | tf_op jit(solution)/shard_map/all_to_all | solution.py:743
  (304 shorter events, 108.6 us)
Async XLA Ops:
  7.2 68.6 %all-gather.3.cloned.1.call-start = ((), (), s32[]{:S(2)}) async-start(), calls=%async_computation.4 | async-start | bytes 2715648 | tf_op jit(solution)/shard_map/all_gather | solution.py:457
  14.1 14.0 %collective-permute-start.3 = (bf16[512,384]{1,0:T(8,128)(2,1)S(1)}, bf16[512,384]{1,0:T(8,128)(2,1)}, u32[]{:S(2)}, u32[]{:S(2)}) collective-permute-start(bf16[512,384]{1,0:T(8,128)(2,1)S(1)} %get-tuple-element.200.refs_2_.wa), channel_id=1, source_target_pairs={{0,4},{2,6},{4,0},{6,2},{1,5},{3,7},{5,1},{7,3},{8,12},{10,14},{12... | collective-permute-start | bytes 1179656 | tf_op jit(solution)/shard_map/ppermute | solution.py:438
  17.1 12.2 %collective-permute-start.2 = (bf16[512,384]{1,0:T(8,128)(2,1)S(1)}, bf16[512,384]{1,0:T(8,128)(2,1)}, u32[]{:S(2)}, u32[]{:S(2)}) collective-permute-start(bf16[512,384]{1,0:T(8,128)(2,1)S(1)} %get-tuple-element.200.refs_2_.wa), channel_id=1, source_target_pairs={{0,2},{2,0},{4,6},{6,4},{1,3},{3,1},{5,7},{7,5},{8,10},{10,8},{12,... | collective-permute-start | bytes 1179656 | tf_op jit(solution)/shard_map/ppermute | solution.py:438
  18.0 9.4 %collective-permute-start = (s32[2,512]{1,0:T(2,128)}, s32[2,512]{1,0:T(2,128)S(1)}, u32[]{:S(2)}, u32[]{:S(2)}) collective-permute-start(s32[2,512]{1,0:T(2,128)} %get-tuple-element.213), channel_id=1, source_target_pairs={{0,4},{2,6},{4,0},{6,2},{1,5},{3,7},{5,1},{7,3},{8,12},{10,14},{12... | collective-permute-start | bytes 12296 | tf_op jit(solution)/shard_map/ppermute | solution.py:438
  27.5 1.2 collective-permute-start.1
  28.1 2.1 collective-permute-start.4
  34.6 43.7 %collective-permute-start.5 = (bf16[512,384]{1,0:T(8,128)(2,1)}, bf16[512,384]{1,0:T(8,128)(2,1)S(1)}, u32[]{:S(2)}, u32[]{:S(2)}) collective-permute-start(bf16[512,384]{1,0:T(8,128)(2,1)} %get-tuple-element.78.wa), channel_id=1, source_target_pairs={{0,1},{1,0},{2,3},{3,2},{4,5},{5,4},{6,7},{7,6},{8,9},{9,8},{10,11... | collective-permute-start | bytes 1179656 | tf_op jit(solution)/shard_map/ppermute | solution.py:435
  37.0 41.4 %collective-permute-start.6 = (bf16[512,384]{1,0:T(8,128)(2,1)}, bf16[512,384]{1,0:T(8,128)(2,1)S(1)}, u32[]{:S(2)}, u32[]{:S(2)}) collective-permute-start(bf16[512,384]{1,0:T(8,128)(2,1)} %get-tuple-element.79), channel_id=1, source_target_pairs={{0,8},{8,16},{16,24},{24,0},{1,9},{9,17},{17,25},{25,1},{2,10},{10... | collective-permute-start | bytes 1179656 | tf_op jit(solution)/shard_map/ppermute | solution.py:441
  38.6 39.8 %collective-permute-start.7 = (bf16[512,384]{1,0:T(8,128)(2,1)}, bf16[512,384]{1,0:T(8,128)(2,1)S(1)}, u32[]{:S(2)}, u32[]{:S(2)}) collective-permute-start(bf16[512,384]{1,0:T(8,128)(2,1)} %get-tuple-element.80), channel_id=1, source_target_pairs={{0,16},{8,24},{16,0},{24,8},{1,17},{9,25},{17,1},{25,9},{2,18},{10... | collective-permute-start | bytes 1179656 | tf_op jit(solution)/shard_map/ppermute | solution.py:441
  41.2 37.2 %collective-permute-start.8 = (bf16[512,384]{1,0:T(8,128)(2,1)}, bf16[512,384]{1,0:T(8,128)(2,1)S(1)}, u32[]{:S(2)}, u32[]{:S(2)}) collective-permute-start(bf16[512,384]{1,0:T(8,128)(2,1)} %get-tuple-element.81), channel_id=1, source_target_pairs={{0,24},{8,0},{16,8},{24,16},{1,25},{9,1},{17,9},{25,17},{2,26},{10... | collective-permute-start | bytes 1179656 | tf_op jit(solution)/shard_map/ppermute | solution.py:441
  84.6 2.5 collective-permute-start.9
  88.0 153.6 %all-to-all-start = ((bf16[4,3,192,1024]{3,2,1,0:T(8,128)(2,1)}), bf16[4,3,192,1024]{3,2,1,0:T(8,128)(2,1)}, u32[]{:S(2)}, u32[]{:S(2)}) async-start(bf16[4,3,192,1024]{3,2,1,0:T(8,128)(2,1)} %pad_maximum_fusion.refs_10_), calls=%async_computation | async-start | bytes 9437184 | tf_op jit(solution)/shard_map/all_to_all | solution.py:584
  98.0 249.9 %all-gather.5.cloned.1.call-start = ((), (), s32[]{:S(2)}) async-start(), calls=%async_computation.5 | async-start | bytes 5013504 | tf_op jit(solution)/shard_map/all_gather | solution.py:457
  98.0 19.4 %collective-permute-start.10 = (bf16[512,768]{1,0:T(8,128)(2,1)S(1)}, bf16[512,768]{1,0:T(8,128)(2,1)S(1)}, u32[]{:S(2)}, u32[]{:S(2)}) collective-permute-start(bf16[512,768]{1,0:T(8,128)(2,1)S(1)} %copy-done.21), channel_id=1, source_target_pairs={{0,4},{2,6},{4,0},{6,2},{1,5},{3,7},{5,1},{7,3},{8,12},{10,14},{12... | collective-permute-start | bytes 2359304 | tf_op jit(solution)/shard_map/ppermute | solution.py:438
  117.4 3.9 collective-permute-start.11
  131.2 8.4 %collective-permute-start.12 = (bf16[512,384]{1,0:T(8,128)(2,1)}, bf16[512,384]{1,0:T(8,128)(2,1)S(1)}, u32[]{:S(2)}, u32[]{:S(2)}) collective-permute-start(bf16[512,384]{1,0:T(8,128)(2,1)} %get-tuple-element.85), channel_id=1, source_target_pairs={{0,1},{1,0},{2,3},{3,2},{4,5},{5,4},{6,7},{7,6},{8,9},{9,8},{10,11... | collective-permute-start | bytes 1179656 | tf_op jit(solution)/shard_map/ppermute | solution.py:435
  141.1 3.6 collective-permute-start.13
  145.0 84.7 %copy-start.34 = (bf16[2,48,1024]{2,1,0:T(8,128)(2,1)S(1)}, bf16[2,48,1024]{2,1,0:T(8,128)(2,1)}, u32[]{:S(2)}) copy-start(bf16[2,48,1024]{2,1,0:T(8,128)(2,1)} %param.23) | copy-start | bytes 589828
  145.0 84.7 %copy-start.35 = (bf16[1024,48]{0,1:T(8,128)(2,1)S(1)}, bf16[1024,48]{0,1:T(8,128)(2,1)}, u32[]{:S(2)}) copy-start(bf16[1024,48]{0,1:T(8,128)(2,1)} %param.24) | copy-start | bytes 294916
  145.0 17.2 %collective-permute-start.16 = (bf16[512,384]{1,0:T(8,128)(2,1)S(1)}, bf16[512,384]{1,0:T(8,128)(2,1)S(1)}, u32[]{:S(2)}, u32[]{:S(2)}) collective-permute-start(bf16[512,384]{1,0:T(8,128)(2,1)S(1)} %multiply_convert_fusion.refs_2_.xa), channel_id=1, source_target_pairs={{0,4},{2,6},{4,0},{6,2},{1,5},{3,7},{5,1},{7,3},{8,12},{10,14},{12... | collective-permute-start | bytes 1179656 | tf_op jit(solution)/shard_map/ppermute | solution.py:438
  154.8 12.2 %collective-permute-start.14 = (bf16[512,384]{1,0:T(8,128)(2,1)S(1)}, bf16[512,384]{1,0:T(8,128)(2,1)S(1)}, u32[]{:S(2)}, u32[]{:S(2)}) collective-permute-start(bf16[512,384]{1,0:T(8,128)(2,1)S(1)} %multiply_convert_fusion.refs_2_.xa), channel_id=1, source_target_pairs={{0,1},{1,0},{2,3},{3,2},{4,5},{5,4},{6,7},{7,6},{8,9},{9,8},{10,11... | collective-permute-start | bytes 1179656 | tf_op jit(solution)/shard_map/ppermute | solution.py:435
  155.4 12.3 %collective-permute-start.15 = (bf16[512,384]{1,0:T(8,128)(2,1)S(1)}, bf16[512,384]{1,0:T(8,128)(2,1)S(1)}, u32[]{:S(2)}, u32[]{:S(2)}) collective-permute-start(bf16[512,384]{1,0:T(8,128)(2,1)S(1)} %multiply_convert_fusion.refs_2_.xa), channel_id=1, source_target_pairs={{0,2},{2,0},{4,6},{6,4},{1,3},{3,1},{5,7},{7,5},{8,10},{10,8},{12,... | collective-permute-start | bytes 1179656 | tf_op jit(solution)/shard_map/ppermute | solution.py:438
  162.2 5.5 collective-permute-start.17
  165.0 13.2 %collective-permute-start.20 = (bf16[512,384]{1,0:T(8,128)(2,1)S(1)}, bf16[512,384]{1,0:T(8,128)(2,1)S(1)}, u32[]{:S(2)}, u32[]{:S(2)}) collective-permute-start(bf16[512,384]{1,0:T(8,128)(2,1)S(1)} %copy-done.48), channel_id=1, source_target_pairs={{0,1},{1,0},{2,3},{3,2},{4,5},{5,4},{6,7},{7,6},{8,9},{9,8},{10,11... | collective-permute-start | bytes 1179656 | tf_op jit(solution)/shard_map/ppermute | solution.py:435
  165.6 19.8 %collective-permute-start.21 = (bf16[512,384]{1,0:T(8,128)(2,1)S(1)}, bf16[512,384]{1,0:T(8,128)(2,1)S(1)}, u32[]{:S(2)}, u32[]{:S(2)}) collective-permute-start(bf16[512,384]{1,0:T(8,128)(2,1)S(1)} %copy-done.50), channel_id=1, source_target_pairs={{0,1},{1,0},{2,3},{3,2},{4,5},{5,4},{6,7},{7,6},{8,9},{9,8},{10,11... | collective-permute-start | bytes 1179656 | tf_op jit(solution)/shard_map/ppermute | solution.py:435
  167.1 25.9 %collective-permute-start.22 = (bf16[512,384]{1,0:T(8,128)(2,1)S(1)}, bf16[512,384]{1,0:T(8,128)(2,1)S(1)}, u32[]{:S(2)}, u32[]{:S(2)}) collective-permute-start(bf16[512,384]{1,0:T(8,128)(2,1)S(1)} %copy-done.46), channel_id=1, source_target_pairs={{0,1},{1,0},{2,3},{3,2},{4,5},{5,4},{6,7},{7,6},{8,9},{9,8},{10,11... | collective-permute-start | bytes 1179656 | tf_op jit(solution)/shard_map/ppermute | solution.py:435
  173.0 56.2 %collective-permute-start.26 = (bf16[512,384]{1,0:T(8,128)(2,1)}, bf16[512,384]{1,0:T(8,128)(2,1)}, u32[]{:S(2)}, u32[]{:S(2)}) collective-permute-start(bf16[512,384]{1,0:T(8,128)(2,1)} %get-tuple-element.93), channel_id=1, source_target_pairs={{0,16},{8,24},{16,0},{24,8},{1,17},{9,25},{17,1},{25,9},{2,18},{10... | collective-permute-start | bytes 1179656 | tf_op jit(solution)/shard_map/ppermute | solution.py:441
  175.5 58.1 %collective-permute-start.24 = (bf16[512,384]{1,0:T(8,128)(2,1)}, bf16[512,384]{1,0:T(8,128)(2,1)S(1)}, u32[]{:S(2)}, u32[]{:S(2)}) collective-permute-start(bf16[512,384]{1,0:T(8,128)(2,1)} %get-tuple-element.91), channel_id=1, source_target_pairs={{0,24},{8,0},{16,8},{24,16},{1,25},{9,1},{17,9},{25,17},{2,26},{10... | collective-permute-start | bytes 1179656 | tf_op jit(solution)/shard_map/ppermute | solution.py:441
  178.2 76.8 %copy-start.53 = (bf16[512,384]{1,0:T(8,128)(2,1)}, bf16[512,384]{1,0:T(8,128)(2,1)S(1)}, u32[]{:S(2)}) copy-start(bf16[512,384]{1,0:T(8,128)(2,1)S(1)} %collective-permute-done.20.wb) | copy-start | bytes 1179652
  178.2 55.9 %collective-permute-start.19 = (bf16[512,384]{1,0:T(8,128)(2,1)}, bf16[512,384]{1,0:T(8,128)(2,1)S(1)}, u32[]{:S(2)}, u32[]{:S(2)}) collective-permute-start(bf16[512,384]{1,0:T(8,128)(2,1)} %get-tuple-element.89), channel_id=1, source_target_pairs={{0,8},{8,16},{16,24},{24,0},{1,9},{9,17},{17,25},{25,1},{2,10},{10... | collective-permute-start | bytes 1179656 | tf_op jit(solution)/shard_map/ppermute | solution.py:441
  193.0 62.0 %copy-start.51 = (bf16[512,384]{1,0:T(8,128)(2,1)}, bf16[512,384]{1,0:T(8,128)(2,1)S(1)}, u32[]{:S(2)}) copy-start(bf16[512,384]{1,0:T(8,128)(2,1)S(1)} %collective-permute-done.22.wb) | copy-start | bytes 1179652
  229.2 12.4 %collective-permute-start.27 = (bf16[512,384]{1,0:T(8,128)(2,1)}, bf16[512,384]{1,0:T(8,128)(2,1)}, u32[]{:S(2)}, u32[]{:S(2)}) collective-permute-start(bf16[512,384]{1,0:T(8,128)(2,1)} %collective-permute-done.26.xa.refs_1_), channel_id=1, source_target_pairs={{0,1},{1,0},{2,3},{3,2},{4,5},{5,4},{6,7},{7,6},{8,9},{9,8},{10,11... | collective-permute-start | bytes 1179656 | tf_op jit(solution)/shard_map/ppermute | solution.py:435
  232.1 24.6 %collective-permute-start.18 = (bf16[512,384]{1,0:T(8,128)(2,1)}, bf16[512,384]{1,0:T(8,128)(2,1)S(1)}, u32[]{:S(2)}, u32[]{:S(2)}) collective-permute-start(bf16[512,384]{1,0:T(8,128)(2,1)} %get-tuple-element.87.xa), channel_id=1, source_target_pairs={{0,1},{1,0},{2,3},{3,2},{4,5},{5,4},{6,7},{7,6},{8,9},{9,8},{10,11... | collective-permute-start | bytes 1179656 | tf_op jit(solution)/shard_map/ppermute | solution.py:435
  233.6 24.7 %collective-permute-start.25 = (bf16[512,384]{1,0:T(8,128)(2,1)S(1)}, bf16[512,384]{1,0:T(8,128)(2,1)S(1)}, u32[]{:S(2)}, u32[]{:S(2)}) collective-permute-start(bf16[512,384]{1,0:T(8,128)(2,1)S(1)} %collective-permute-done.24.refs_2_.xa), channel_id=1, source_target_pairs={{0,1},{1,0},{2,3},{3,2},{4,5},{5,4},{6,7},{7,6},{8,9},{9,8},{10,11... | collective-permute-start | bytes 1179656 | tf_op jit(solution)/shard_map/ppermute | solution.py:435
  234.1 32.7 %collective-permute-start.23 = (bf16[512,384]{1,0:T(8,128)(2,1)S(1)}, bf16[512,384]{1,0:T(8,128)(2,1)}, u32[]{:S(2)}, u32[]{:S(2)}) collective-permute-start(bf16[512,384]{1,0:T(8,128)(2,1)S(1)} %collective-permute-done.19.refs_0_.xa), channel_id=1, source_target_pairs={{0,1},{1,0},{2,3},{3,2},{4,5},{5,4},{6,7},{7,6},{8,9},{9,8},{10,11... | collective-permute-start | bytes 1179656 | tf_op jit(solution)/shard_map/ppermute | solution.py:435
  256.2 26.6 %collective-permute-start.29 = (bf16[512,768]{1,0:T(8,128)(2,1)S(1)}, bf16[512,768]{1,0:T(8,128)(2,1)S(1)}, u32[]{:S(2)}, u32[]{:S(2)}) collective-permute-start(bf16[512,768]{1,0:T(8,128)(2,1)S(1)} %slice_bitcast_fusion.3), channel_id=1, source_target_pairs={{0,1},{1,0},{2,3},{3,2},{4,5},{5,4},{6,7},{7,6},{8,9},{9,8},{10,11... | collective-permute-start | bytes 2359304 | tf_op jit(solution)/shard_map/ppermute | solution.py:435
  281.6 17.8 %collective-permute-start.28 = (bf16[512,768]{1,0:T(8,128)(2,1)S(1)}, bf16[512,768]{1,0:T(8,128)(2,1)S(1)}, u32[]{:S(2)}, u32[]{:S(2)}) collective-permute-start(bf16[512,768]{1,0:T(8,128)(2,1)S(1)} %slice_bitcast_fusion.4), channel_id=1, source_target_pairs={{0,1},{1,0},{2,3},{3,2},{4,5},{5,4},{6,7},{7,6},{8,9},{9,8},{10,11... | collective-permute-start | bytes 2359304 | tf_op jit(solution)/shard_map/ppermute | solution.py:435
  283.0 42.3 %collective-permute-start.32 = (bf16[512,768]{1,0:T(8,128)(2,1)S(1)}, bf16[512,768]{1,0:T(8,128)(2,1)S(1)}, u32[]{:S(2)}, u32[]{:S(2)}) collective-permute-start(bf16[512,768]{1,0:T(8,128)(2,1)S(1)} %fusion.13.refs_0_), channel_id=1, source_target_pairs={{0,16},{8,24},{16,0},{24,8},{1,17},{9,25},{17,1},{25,9},{2,18},{10... | collective-permute-start | bytes 2359304 | tf_op jit(solution)/shard_map/ppermute | solution.py:441
  298.5 26.1 %collective-permute-start.33 = (bf16[512,768]{1,0:T(8,128)(2,1)S(1)}, bf16[512,768]{1,0:T(8,128)(2,1)S(1)}, u32[]{:S(2)}, u32[]{:S(2)}) collective-permute-start(bf16[512,768]{1,0:T(8,128)(2,1)S(1)} %slice_bitcast_fusion.1), channel_id=1, source_target_pairs={{0,1},{1,0},{2,3},{3,2},{4,5},{5,4},{6,7},{7,6},{8,9},{9,8},{10,11... | collective-permute-start | bytes 2359304 | tf_op jit(solution)/shard_map/ppermute | solution.py:435
  299.6 48.3 %collective-permute-start.31 = (bf16[512,768]{1,0:T(8,128)(2,1)S(1)}, bf16[512,768]{1,0:T(8,128)(2,1)S(1)}, u32[]{:S(2)}, u32[]{:S(2)}) collective-permute-start(bf16[512,768]{1,0:T(8,128)(2,1)S(1)} %fusion.14.refs_0_), channel_id=1, source_target_pairs={{0,24},{8,0},{16,8},{24,16},{1,25},{9,1},{17,9},{25,17},{2,26},{10... | collective-permute-start | bytes 2359304 | tf_op jit(solution)/shard_map/ppermute | solution.py:441
  316.9 55.1 %collective-permute-start.30 = (bf16[512,768]{1,0:T(8,128)(2,1)}, bf16[512,768]{1,0:T(8,128)(2,1)}, u32[]{:S(2)}, u32[]{:S(2)}) collective-permute-start(bf16[512,768]{1,0:T(8,128)(2,1)} %slice_bitcast_fusion.2), channel_id=1, source_target_pairs={{0,1},{1,0},{2,3},{3,2},{4,5},{5,4},{6,7},{7,6},{8,9},{9,8},{10,11... | collective-permute-start | bytes 2359304 | tf_op jit(solution)/shard_map/ppermute | solution.py:435
  324.8 23.0 %collective-permute-start.34 = (bf16[512,768]{1,0:T(8,128)(2,1)S(1)}, bf16[512,768]{1,0:T(8,128)(2,1)S(1)}, u32[]{:S(2)}, u32[]{:S(2)}) collective-permute-start(bf16[512,768]{1,0:T(8,128)(2,1)S(1)} %fusion.11), channel_id=1, source_target_pairs={{0,8},{8,16},{16,24},{24,0},{1,9},{9,17},{17,25},{25,1},{2,10},{10... | collective-permute-start | bytes 2359304 | tf_op jit(solution)/shard_map/ppermute | solution.py:441
  361.5 15.2 %collective-permute-start.35 = (bf16[512,768]{1,0:T(8,128)(2,1)S(1)}, bf16[512,768]{1,0:T(8,128)(2,1)}, u32[]{:S(2)}, u32[]{:S(2)}) collective-permute-start(bf16[512,768]{1,0:T(8,128)(2,1)S(1)} %slice_bitcast_fusion), channel_id=1, source_target_pairs={{0,1},{1,0},{2,3},{3,2},{4,5},{5,4},{6,7},{7,6},{8,9},{9,8},{10,11... | collective-permute-start | bytes 2359304 | tf_op jit(solution)/shard_map/ppermute | solution.py:435
  363.3 112.9 %all-to-all-start.1 = ((bf16[4,3,192,1024]{3,2,1,0:T(8,128)(2,1)}), bf16[4,3,192,1024]{3,2,1,0:T(8,128)(2,1)}, u32[]{:S(2)}, u32[]{:S(2)}) async-start(bf16[4,3,192,1024]{3,2,1,0:T(8,128)(2,1)} %pad_maximum_fusion.1.refs_0_), calls=%async_computation.1 | async-start | bytes 9437184 | tf_op jit(solution)/shard_map/all_to_all | solution.py:644
  371.8 183.6 %reduce-scatter.2.cloned.1.call-start = ((), (), s32[]{:S(2)}) async-start(), calls=%async_computation.6 | async-start | bytes 5013504 | tf_op jit(solution)/shard_map/reduce_scatter | solution.py:665
  384.1 2.5 collective-permute-start.36
  388.1 11.3 %collective-permute-start.37 = (bf16[512,384]{1,0:T(8,128)(2,1)S(1)}, bf16[512,384]{1,0:T(8,128)(2,1)S(1)}, u32[]{:S(2)}, u32[]{:S(2)}) collective-permute-start(bf16[512,384]{1,0:T(8,128)(2,1)S(1)} %fusion.33), channel_id=1, source_target_pairs={{0,4},{2,6},{4,0},{6,2},{1,5},{3,7},{5,1},{7,3},{8,12},{10,14},{12... | collective-permute-start | bytes 1179656 | tf_op jit(solution)/shard_map/ppermute | solution.py:438
  400.3 3.6 collective-permute-start.38
  405.4 10.1 %collective-permute-start.39 = (bf16[512,384]{1,0:T(8,128)(2,1)}, bf16[512,384]{1,0:T(8,128)(2,1)}, u32[]{:S(2)}, u32[]{:S(2)}) collective-permute-start(bf16[512,384]{1,0:T(8,128)(2,1)} %fusion.60.refs_10_), channel_id=1, source_target_pairs={{0,1},{1,0},{2,3},{3,2},{4,5},{5,4},{6,7},{7,6},{8,9},{9,8},{10,11... | collective-permute-start | bytes 1179656 | tf_op jit(solution)/shard_map/ppermute | solution.py:435
  427.5 22.9 %collective-permute-start.42 = (bf16[2,512,768]{2,1,0:T(8,128)(2,1)}, bf16[2,512,768]{2,1,0:T(8,128)(2,1)}, u32[]{:S(2)}, u32[]{:S(2)}) collective-permute-start(bf16[2,512,768]{2,1,0:T(8,128)(2,1)} %get-tuple-element.129), channel_id=1, source_target_pairs={{0,2},{2,0},{4,6},{6,4},{1,3},{3,1},{5,7},{7,5},{8,10},{10,8},{12,... | collective-permute-start | bytes 4718600 | tf_op jit(solution)/shard_map/ppermute | solution.py:438
  430.3 7.2 %collective-permute-start.40 = (bf16[2,512,384]{2,1,0:T(8,128)(2,1)}, bf16[2,512,384]{2,1,0:T(8,128)(2,1)}, u32[]{:S(2)}, u32[]{:S(2)}) collective-permute-start(bf16[2,512,384]{2,1,0:T(8,128)(2,1)} %get-tuple-element.122), channel_id=1, source_target_pairs={{0,2},{2,0},{4,6},{6,4},{1,3},{3,1},{5,7},{7,5},{8,10},{10,8},{12,... | collective-permute-start | bytes 2359304 | tf_op jit(solution)/shard_map/ppermute | solution.py:438
  438.7 21.6 %collective-permute-start.41 = (bf16[512,384]{1,0:T(8,128)(2,1)S(1)}, bf16[512,384]{1,0:T(8,128)(2,1)S(1)}, u32[]{:S(2)}, u32[]{:S(2)}) collective-permute-start(bf16[512,384]{1,0:T(8,128)(2,1)S(1)} %fusion.34), channel_id=1, source_target_pairs={{0,4},{2,6},{4,0},{6,2},{1,5},{3,7},{5,1},{7,3},{8,12},{10,14},{12... | collective-permute-start | bytes 1179656 | tf_op jit(solution)/shard_map/ppermute | solution.py:438
  452.8 24.2 %collective-permute-start.43 = (bf16[512,768]{1,0:T(8,128)(2,1)}, bf16[512,768]{1,0:T(8,128)(2,1)}, u32[]{:S(2)}, u32[]{:S(2)}) collective-permute-start(bf16[512,768]{1,0:T(8,128)(2,1)} %fusion.27), channel_id=1, source_target_pairs={{0,4},{2,6},{4,0},{6,2},{1,5},{3,7},{5,1},{7,3},{8,12},{10,14},{12... | collective-permute-start | bytes 2359304 | tf_op jit(solution)/shard_map/ppermute | solution.py:438
  482.9 11.2 %collective-permute-start.44 = (bf16[512,384]{1,0:T(8,128)(2,1)}, bf16[512,384]{1,0:T(8,128)(2,1)S(1)}, u32[]{:S(2)}, u32[]{:S(2)}) collective-permute-start(bf16[512,384]{1,0:T(8,128)(2,1)} %get-tuple-element.135), channel_id=1, source_target_pairs={{0,1},{1,0},{2,3},{3,2},{4,5},{5,4},{6,7},{7,6},{8,9},{9,8},{10,11... | collective-permute-start | bytes 1179656 | tf_op jit(solution)/shard_map/ppermute | solution.py:435
  490.7 15.5 %collective-permute-start.48 = (bf16[2,4,48,1536]{3,2,1,0:T(8,128)(2,1)}, bf16[2,4,48,1536]{3,2,1,0:T(8,128)(2,1)S(1)}, u32[]{:S(2)}, u32[]{:S(2)}) collective-permute-start(bf16[2,4,48,1536]{3,2,1,0:T(8,128)(2,1)} %get-tuple-element.141), channel_id=1, source_target_pairs={{0,2},{2,0},{4,6},{6,4},{1,3},{3,1},{5,7},{7,5},{8,10},{10,8},{12,... | collective-permute-start | bytes 3538952 | tf_op jit(solution)/shard_map/ppermute | solution.py:438
  494.4 3.6 collective-permute-start.45
  498.6 13.0 %collective-permute-start.47 = (bf16[512,384]{1,0:T(8,128)(2,1)S(1)}, bf16[512,384]{1,0:T(8,128)(2,1)S(1)}, u32[]{:S(2)}, u32[]{:S(2)}) collective-permute-start(bf16[512,384]{1,0:T(8,128)(2,1)S(1)} %fusion.24), channel_id=1, source_target_pairs={{0,1},{1,0},{2,3},{3,2},{4,5},{5,4},{6,7},{7,6},{8,9},{9,8},{10,11... | collective-permute-start | bytes 1179656 | tf_op jit(solution)/shard_map/ppermute | solution.py:435
  499.7 16.8 %collective-permute-start.46 = (bf16[512,384]{1,0:T(8,128)(2,1)S(1)}, bf16[512,384]{1,0:T(8,128)(2,1)S(1)}, u32[]{:S(2)}, u32[]{:S(2)}) collective-permute-start(bf16[512,384]{1,0:T(8,128)(2,1)S(1)} %convert_element_type.316), channel_id=1, source_target_pairs={{0,1},{1,0},{2,3},{3,2},{4,5},{5,4},{6,7},{7,6},{8,9},{9,8},{10,11... | collective-permute-start | bytes 1179656 | tf_op jit(solution)/shard_map/ppermute | solution.py:435
  506.3 14.5 %collective-permute-start.49 = (bf16[4,48,1536]{2,1,0:T(8,128)(2,1)S(1)}, bf16[4,48,1536]{2,1,0:T(8,128)(2,1)S(1)}, u32[]{:S(2)}, u32[]{:S(2)}) collective-permute-start(bf16[4,48,1536]{2,1,0:T(8,128)(2,1)S(1)} %fusion.32), channel_id=1, source_target_pairs={{0,4},{2,6},{4,0},{6,2},{1,5},{3,7},{5,1},{7,3},{8,12},{10,14},{12... | collective-permute-start | bytes 1769480 | tf_op jit(solution)/shard_map/ppermute | solution.py:438
  521.0 28.9 %collective-permute-start.50 = (bf16[48,1536]{1,0:T(8,128)(2,1)S(1)}, bf16[48,1536]{1,0:T(8,128)(2,1)S(1)}, u32[]{:S(2)}, u32[]{:S(2)}) collective-permute-start(bf16[48,1536]{1,0:T(8,128)(2,1)S(1)} %get-tuple-element.204), channel_id=1, source_target_pairs={{0,8},{8,16},{16,24},{24,0},{1,9},{9,17},{17,25},{25,1},{2,10},{10... | collective-permute-start | bytes 442376 | tf_op jit(solution)/shard_map/ppermute | solution.py:441
  534.2 15.8 %collective-permute-start.51 = (bf16[48,1536]{1,0:T(8,128)(2,1)S(1)}, bf16[48,1536]{1,0:T(8,128)(2,1)S(1)}, u32[]{:S(2)}, u32[]{:S(2)}) collective-permute-start(bf16[48,1536]{1,0:T(8,128)(2,1)S(1)} %get-tuple-element.206), channel_id=1, source_target_pairs={{0,16},{8,24},{16,0},{24,8},{1,17},{9,25},{17,1},{25,9},{2,18},{10... | collective-permute-start | bytes 442376 | tf_op jit(solution)/shard_map/ppermute | solution.py:441
  535.9 14.0 %collective-permute-start.52 = (bf16[48,1536]{1,0:T(8,128)(2,1)S(1)}, bf16[48,1536]{1,0:T(8,128)(2,1)S(1)}, u32[]{:S(2)}, u32[]{:S(2)}) collective-permute-start(bf16[48,1536]{1,0:T(8,128)(2,1)S(1)} %get-tuple-element.205), channel_id=1, source_target_pairs={{0,24},{8,0},{16,8},{24,16},{1,25},{9,1},{17,9},{25,17},{2,26},{10... | collective-permute-start | bytes 442376 | tf_op jit(solution)/shard_map/ppermute | solution.py:441
  539.6 10.3 %all-to-all-start.2 = ((f32[16,1,864]{2,1,0:T(1,128)}), f32[16,1,864]{2,1,0:T(1,128)S(1)}, u32[]{:S(2)}, u32[]{:S(2)}) async-start(f32[16,1,864]{2,1,0:T(1,128)} %all_to_all.16), calls=%async_computation.2 | async-start | bytes 114688 | tf_op jit(solution)/shard_map/all_to_all | solution.py:743
  550.1 3.9 collective-permute-start.53
  (60 other events, 463.0 us)
Sparse Core Ops, SparseCore 0:
  12.3 63.4 all-gather.2
  235.8 74.0 all-gather.4
  437.6 97.8 reduce-scatter.1

commit v5 on v4

--- a/solution.py
+++ b/solution.py
@@ -582,7 +582,7 @@
     kvs = (kv, kv_near, kv_far, kv_both)
     if small:
         expert_w = lax.all_to_all(
-            after(expert_local, kv_near), "fsdp", 0, 0, tiled=True
+            after(expert_local, *cot_rows[1:]), "fsdp", 0, 0, tiled=True
         )
     before_attn = []
     seq_ids = segments[0]
@@ -692,14 +692,13 @@
         scalars, queries, *kvs, seg_col, seg_row, lse, attended, dz_own, dz_oth, out_w, cos, sin,
         deps=[shared_full],
     )
-    layer_h = middle + over_ctx(keep_o, after(send_o, dz_oth)) + sh_sum[:, HALF:]
     dkv_near = cx(dkv_send, 1)
     kv_recv = cx((dkv_keep[1].astype(f32) + dkv_near[1].astype(f32)).astype(bf16), 2)
     dp, da_own, da_oth = call(
         proj_back_body,
         [sds((ROWS, 3 * heads_width), bf16), sds((ROWS, HALF), f32), sds((ROWS, HALF), bf16)],
         us=5.0, name="proj_back",
-    )(scalars, dq, dkv_keep, dkv_near, kv_recv, first, cos, sin, deps=[grad_w, layer_h])
+    )(scalars, dq, dkv_keep, dkv_near, kv_recv, first, cos, sin, deps=[grad_w])
     dense_pairs = [(normed_one, dp), (halves(y, dz_own, dz_oth), attended)]
     if small:
         dense_keep, dense_send = grad_blocks(back_offs, rows_own, dense_pairs)
@@ -717,8 +716,9 @@
 
     tokens_grad = whole_rows(tokens_grad_h.astype(bf16)).astype(f32)
 
+    layer_h = middle + over_ctx(keep_o, after(send_o, kv_recv)) + sh_sum[:, HALF:]
     layer_out = whole_rows(after(layer_h, tokens_grad_h).astype(bf16))
-    grad_w = after(grad_w, tokens_grad_h)
+    grad_w = after(grad_w, tokens_grad_h, dense_part)
     expert_gate_up_grad = grad_w[:, :2].astype(f32)
     expert_down_grad = grad_w[:, 2].astype(f32).transpose(0, 2, 1)
     if small:

time: 574 us -> 561 us (0.977)
  starting transfers between devices: 117 us -> 109 us
    all_gather x2, waiting for transfers between devices: 33.3 us -> 0.02 us  [gathered(): return lax.all_gather(shard, ('fsdp', 'ctx'), axis=axis, tiled=True)]
    ppermute x12, waiting for transfers between devices: 49.2 us -> 72.3 us  [zs(): lax.ppermute(v, 'fsdp', [(i, i // EL * EL + (i % EL + s) % EL) for i in r...]
    ppermute x19, waiting for transfers between devices: 48 us -> 59.4 us  [cx(): return lax.ppermute(v, 'ctx', [(i, i ^ flip) for i in range(C)])]
    ppermute x12, starting transfers between devices: 31.7 us -> 22.1 us  [zs(): lax.ppermute(v, 'fsdp', [(i, i // EL * EL + (i % EL + s) % EL) for i in r...]
    all_to_all x1, waiting for transfers between devices: 5.85 us -> 0.01 us  [per_device(): lax.all_to_all(tail, ('fsdp', 'ctx'), 0, 0, tiled=True)]
  transfers between devices with their start and end apart: 60 -> 60, of which waited for: 30 -> 27; matrix products, arithmetic and copies ran while one was open for 16% -> 16% of each run, Pallas kernels for 19% -> 21%
where the time goes in v5:
time: 561 us; the launch traced here: 552 us
  waiting for transfers between devices  208 us (37%)
  Pallas kernels  114 us (20%)
  starting transfers between devices  109 us (19%)
  other arithmetic  51 us (9%)
  local copies, waits for them, and re-layouts  38.4 us (7%)
  matrix products  16.9 us (3%)
  between operations  14.9 us (3%)
    ppermute x12, waiting for transfers between devices, zs(): lax.ppermute(v, 'fsdp', [(i, i // EL * EL + (i % EL + s) % EL) for i in r...  72.3 us
    ppermute x23, waiting for transfers between devices, yx(): return lax.ppermute(v, 'tp', [(0, 1), (1, 0)])  66.4 us
    pallas_call x5, Pallas kernels, ffn(): pl.pallas_call(functools.partial(ffn_body, routed), grid=(1,), out_shape=...  64.1 us
    ppermute x19, waiting for transfers between devices, cx(): return lax.ppermute(v, 'ctx', [(i, i ^ flip) for i in range(C)])  59.4 us
    pallas_call x8, Pallas kernels, run(): pl.pallas_call(inner, out_shape=outs, in_specs=[SMEM] + [VM] * len(args)...  49.5 us
    ppermute x19, starting transfers between devices, cx(): return lax.ppermute(v, 'ctx', [(i, i ^ flip) for i in range(C)])  36.3 us
    ppermute x23, starting transfers between devices, yx(): return lax.ppermute(v, 'tp', [(0, 1), (1, 0)])  25.8 us
    ppermute x12, starting transfers between devices, zs(): lax.ppermute(v, 'fsdp', [(i, i // EL * EL + (i % EL + s) % EL) for i in r...  22.1 us
  transfers between devices with their start and end apart: 60, of which 27 were waited for; matrix products, arithmetic and copies ran while one was open for 16% of the time, Pallas kernels for 21%

profile of v5, /device:TPU:0, one launch (start us, length us, event | category | flops | bytes accessed | tf_op | source)
XLA Modules:
  0.0 552.0 jit_solution(6673242486718656350)
XLA Ops:
  14.1 2.9 collective-permute-start.3
  17.4 4.5 pad_maximum_fusion.refs_10_
  21.9 5.4 collective-permute-done
  30.7 3.7 pack.2
  34.4 2.4 collective-permute-start.6
  36.8 2.6 collective-permute-start.7
  44.1 8.5 %collective-permute-done.6.refs_7_.wa = bf16[512,384]{1,0:T(8,128)(2,1)S(1)} collective-permute-done((bf16[512,384]{1,0:T(8,128)(2,1)}, bf16[512,384]{1,0:T(8,128)(2,1)S(1)}, u32[]{:S(2)}, u32[]{:S(2)}) %collective-permute-start.6) | collective-permute-done | bytes 393248 | tf_op jit(solution)/shard_map/ppermute | solution.py:441
  52.6 23.2 %collective-permute-done.7.refs_8_.wa = bf16[512,384]{1,0:T(8,128)(2,1)S(1)} collective-permute-done((bf16[512,384]{1,0:T(8,128)(2,1)}, bf16[512,384]{1,0:T(8,128)(2,1)S(1)}, u32[]{:S(2)}, u32[]{:S(2)}) %collective-permute-start.7) | collective-permute-done | bytes 393248 | tf_op jit(solution)/shard_map/ppermute | solution.py:441
  76.7 11.2 %all-to-all-start = ((bf16[4,3,192,1024]{3,2,1,0:T(8,128)(2,1)}), bf16[4,3,192,1024]{3,2,1,0:T(8,128)(2,1)}, u32[]{:S(2)}, u32[]{:S(2)}) async-start(bf16[4,3,192,1024]{3,2,1,0:T(8,128)(2,1)} %pad_maximum_fusion.refs_10_), calls=%async_computation | async-start | bytes 9437184 | tf_op jit(solution)/shard_map/all_to_all | solution.py:584
  91.2 5.1 qkv.1
  97.9 17.3 %collective-permute-done.10.refs_4_ = bf16[512,768]{1,0:T(8,128)(2,1)S(1)} collective-permute-done((bf16[512,768]{1,0:T(8,128)(2,1)}, bf16[512,768]{1,0:T(8,128)(2,1)S(1)}, u32[]{:S(2)}, u32[]{:S(2)}) %collective-permute-start.10) | collective-permute-done | bytes 786464 | tf_op jit(solution)/shard_map/ppermute | solution.py:438
  117.1 2.0 slice.230.refs_8_.refs_12_
  120.3 9.1 %attn.1 = (bf16[512,384]{1,0:T(8,128)(2,1)}, f32[512,384]{1,0:T(8,128)}, bf16[512,384]{1,0:T(8,128)(2,1)}, f32[8,512]{1,0:T(8,128)}) custom-call(s32[3]{0:T(128)} %pad_add_fusion.2.refs_0_.sc.rt, bf16[512,384]{1,0:T(8,128)(2,1)} %get-tuple-element.82.refs_1_, bf16[512,768]{1,0:T(8,128)(2,1)} %get-tuple-element.83.refs_2_, bf16[512,768]{1,0:T(8,128)(2,1)} %copy-done.21, ...), custom_call_target="tpu_custom_call" | custom-call | flops 18699999232 | tf_op jit(solution)/shard_map/attn/pallas_call | solution.py:50
  130.9 6.9 %collective-permute-done.12 = bf16[512,384]{1,0:T(8,128)(2,1)S(1)} collective-permute-done((bf16[512,384]{1,0:T(8,128)(2,1)}, bf16[512,384]{1,0:T(8,128)(2,1)S(1)}, u32[]{:S(2)}, u32[]{:S(2)}) %collective-permute-start.12) | collective-permute-done | bytes 393248 | tf_op jit(solution)/shard_map/ppermute | solution.py:435
  143.1 9.9 %collective-permute-start.16 = (bf16[512,384]{1,0:T(8,128)(2,1)S(1)}, bf16[512,384]{1,0:T(8,128)(2,1)S(1)}, u32[]{:S(2)}, u32[]{:S(2)}) collective-permute-start(bf16[512,384]{1,0:T(8,128)(2,1)S(1)} %multiply_convert_fusion.refs_2_.xa), channel_id=1, source_target_pairs={{0,4},{2,6},{4,0},{6,2},{1,5},{3,7},{5,1},{7,3},{8,12},{10,14},{12... | collective-permute-start | bytes 1179656 | tf_op jit(solution)/shard_map/ppermute | solution.py:438
  156.4 4.7 collective-permute-done.16.refs_4_
  161.1 2.0 collective-permute-start.17
  168.3 3.7 pack.3
  172.0 2.7 collective-permute-start.26
  174.8 3.1 collective-permute-start.24
  178.6 4.9 collective-permute-done.21.wb
  183.5 7.5 %collective-permute-done.22.wb = bf16[512,384]{1,0:T(8,128)(2,1)S(1)} collective-permute-done((bf16[512,384]{1,0:T(8,128)(2,1)S(1)}, bf16[512,384]{1,0:T(8,128)(2,1)S(1)}, u32[]{:S(2)}, u32[]{:S(2)}) %collective-permute-start.22) | collective-permute-done | bytes 393248 | tf_op jit(solution)/shard_map/ppermute | solution.py:435
  191.0 27.8 %collective-permute-done.26.xa.refs_1_ = bf16[512,384]{1,0:T(8,128)(2,1)} collective-permute-done((bf16[512,384]{1,0:T(8,128)(2,1)}, bf16[512,384]{1,0:T(8,128)(2,1)}, u32[]{:S(2)}, u32[]{:S(2)}) %collective-permute-start.26) | collective-permute-done | bytes 393248 | tf_op jit(solution)/shard_map/ppermute | solution.py:441
  225.2 5.8 %collective-permute-done.27.xb = bf16[512,384]{1,0:T(8,128)(2,1)S(1)} collective-permute-done((bf16[512,384]{1,0:T(8,128)(2,1)}, bf16[512,384]{1,0:T(8,128)(2,1)S(1)}, u32[]{:S(2)}, u32[]{:S(2)}) %collective-permute-start.27) | collective-permute-done | bytes 393248 | tf_op jit(solution)/shard_map/ppermute | solution.py:435
  231.8 13.5 %expert_ffn.4 = (bf16[2,512,768]{2,1,0:T(8,128)(2,1)}, f32[768,128]{1,0:T(8,128)}, bf16[4,512,2048]{2,1,0:T(8,128)(2,1)}, bf16[4,512,1024]{2,1,0:T(8,128)(2,1)},...) custom-call(s32[3]{0:T(128)} %pad_add_fusion.2.refs_0_.sc.rt, ...), custom_call_target="tpu_custom_call" | custom-call | flops 16000000000 | tf_op jit(solution)/shard_map/expert_ffn/pallas_call | solution.py:369
  248.1 8.3 %collective-permute-done.23.xb = bf16[512,384]{1,0:T(8,128)(2,1)} collective-permute-done((bf16[512,384]{1,0:T(8,128)(2,1)}, bf16[512,384]{1,0:T(8,128)(2,1)}, u32[]{:S(2)}, u32[]{:S(2)}) %collective-permute-start.23) | collective-permute-done | bytes 393248 | tf_op jit(solution)/shard_map/ppermute | solution.py:435
  256.4 13.4 %expert_ffn.5 = (bf16[2,512,768]{2,1,0:T(8,128)(2,1)}, f32[768,128]{1,0:T(8,128)}, bf16[4,512,2048]{2,1,0:T(8,128)(2,1)}, bf16[4,512,1024]{2,1,0:T(8,128)(2,1)},...) custom-call(s32[3]{0:T(128)} %pad_add_fusion.2.refs_0_.sc.rt, ...), custom_call_target="tpu_custom_call", output_to_operand_aliasing={{2}: (9, {}), {3}: (10, {}), {4}: (11, {}), {5}: (12, {})} | custom-call | flops 16000000000 | tf_op jit(solution)/shard_map/expert_ffn/pallas_call | solution.py:369
  273.8 13.2 %expert_ffn.6 = (bf16[2,512,768]{2,1,0:T(8,128)(2,1)}, f32[768,128]{1,0:T(8,128)}, bf16[4,512,2048]{2,1,0:T(8,128)(2,1)}, bf16[4,512,1024]{2,1,0:T(8,128)(2,1)},...) custom-call(s32[3]{0:T(128)} %pad_add_fusion.2.refs_0_.sc.rt, ...), custom_call_target="tpu_custom_call", output_to_operand_aliasing={{2}: (8, {}), {3}: (9, {}), {4}: (10, {}), {5}: (11, {})} | custom-call | flops 16000000000 | tf_op jit(solution)/shard_map/expert_ffn/pallas_call | solution.py:369
  289.8 2.7 collective-permute-start.31
  292.5 12.8 %expert_ffn.7 = (bf16[2,512,768]{2,1,0:T(8,128)(2,1)}, f32[768,128]{1,0:T(8,128)}, bf16[4,512,2048]{2,1,0:T(8,128)(2,1)}, bf16[4,512,1024]{2,1,0:T(8,128)(2,1)},...) custom-call(s32[3]{0:T(128)} %pad_add_fusion.2.refs_0_.sc.rt, ...), custom_call_target="tpu_custom_call", output_to_operand_aliasing={{2}: (8, {}), {3}: (9, {}), {4}: (10, {}), {5}: (11, {})} | custom-call | flops 16000000000 | tf_op jit(solution)/shard_map/expert_ffn/pallas_call | solution.py:369
  305.4 2.0 slice_bitcast_fusion.2
  308.3 6.7 %bitcast_convert_fusion = bf16[768,1024]{1,0:T(8,128)(2,1)S(1)} fusion(bf16[4,512,768]{2,1,0:T(8,128)(2,1)} %get-tuple-element.115, bf16[4,512,1024]{2,1,0:T(8,128)(2,1)} %get-tuple-element.116), kind=kOutput, calls=%fused_computation.9 | convolution fusion | flops 3222011904 | bytes 8912896 | tf_op jit(solution)/shard_map/dot_general | solution.py:638
  315.7 3.5 fusion.5
  319.2 3.5 fusion.8
  322.7 2.5 pad_maximum_fusion.1.refs_0_
  325.2 12.8 %collective-permute-done.31.refs_1_.refs_3_ = bf16[512,768]{1,0:T(8,128)(2,1)S(1)} collective-permute-done((bf16[512,768]{1,0:T(8,128)(2,1)S(1)}, bf16[512,768]{1,0:T(8,128)(2,1)S(1)}, u32[]{:S(2)}, u32[]{:S(2)}) %collective-permute-start.31) | collective-permute-done | bytes 786464 | tf_op jit(solution)/shard_map/ppermute | solution.py:441
  339.2 11.3 %shared_ffn.1 = (bf16[2,512,768]{2,1,0:T(8,128)(2,1)}, bf16[1,512,2048]{2,1,0:T(8,128)(2,1)}, bf16[1,512,1024]{2,1,0:T(8,128)(2,1)}) custom-call(s32[3]{0:T(128)} %pad_add_fusion.2.refs_0_.sc.rt, bf16[512,384]{1,0:T(8,128)(2,1)} %copy-done.10, bf16[512,384]{1,0:T(8,128)(2,1)} %copy-done.8, bf16[512,384]{1,0:T(8,128)(2,1)} %copy-done.1, ...), custom_call_target="tpu_custom_call" | custom-call | tf_op jit(solution)/shard_map/shared_ffn/pallas_call | solution.py:369
  352.2 9.5 %all-to-all-start.1 = ((bf16[4,3,192,1024]{3,2,1,0:T(8,128)(2,1)}), bf16[4,3,192,1024]{3,2,1,0:T(8,128)(2,1)}, u32[]{:S(2)}, u32[]{:S(2)}) async-start(bf16[4,3,192,1024]{3,2,1,0:T(8,128)(2,1)} %pad_maximum_fusion.1.refs_0_), calls=%async_computation.1 | async-start | bytes 9437184 | tf_op jit(solution)/shard_map/all_to_all | solution.py:644
  362.0 2.4 fusion.12.refs_2_
  364.4 2.2 collective-permute-done.35
  366.6 2.4 convert_add_fusion.refs_6_
  369.1 5.0 unpack.1
  374.1 2.5 collective-permute-done.36
  382.0 7.3 %collective-permute-done.37 = bf16[512,384]{1,0:T(8,128)(2,1)S(1)} collective-permute-done((bf16[512,384]{1,0:T(8,128)(2,1)S(1)}, bf16[512,384]{1,0:T(8,128)(2,1)S(1)}, u32[]{:S(2)}, u32[]{:S(2)}) %collective-permute-start.37) | collective-permute-done | bytes 393248 | tf_op jit(solution)/shard_map/ppermute | solution.py:438
  391.5 2.2 collective-permute-done.38
  395.6 2.7 pad_maximum_fusion.2.refs_15_
  398.3 7.1 %collective-permute-done.39.refs_11_ = bf16[512,384]{1,0:T(8,128)(2,1)} collective-permute-done((bf16[512,384]{1,0:T(8,128)(2,1)}, bf16[512,384]{1,0:T(8,128)(2,1)}, u32[]{:S(2)}, u32[]{:S(2)}) %collective-permute-start.39) | collective-permute-done | bytes 393248 | tf_op jit(solution)/shard_map/ppermute | solution.py:435
  405.3 11.9 %attn_back.1 = (bf16[512,384]{1,0:T(8,128)(2,1)}, bf16[2,512,768]{2,1,0:T(8,128)(2,1)}, bf16[2,512,768]{2,1,0:T(8,128)(2,1)}) custom-call(s32[3]{0:T(128)} %pad_add_fusion.2.refs_0_.sc.rt, bf16[512,384]{1,0:T(8,128)(2,1)} %get-tuple-element.82.refs_1_, bf16[512,768]{1,0:T(8,128)(2,1)} %get-tuple-element.83.refs_2_, bf16[512,768]{1,0:T(8,128)(2,1)} %copy-done.21, ...), custom_call_target="tpu_custom_call" | custom-call | tf_op jit(solution)/shard_map/attn_back/pallas_call | solution.py:50
  417.2 2.7 collective-permute-start.40
  423.4 2.5 fusion.27
  425.9 11.7 %collective-permute-start.41 = (bf16[512,768]{1,0:T(8,128)(2,1)}, bf16[512,768]{1,0:T(8,128)(2,1)}, u32[]{:S(2)}, u32[]{:S(2)}) collective-permute-start(bf16[512,768]{1,0:T(8,128)(2,1)} %fusion.27), channel_id=1, source_target_pairs={{0,4},{2,6},{4,0},{6,2},{1,5},{3,7},{5,1},{7,3},{8,12},{10,14},{12... | collective-permute-start | bytes 2359304 | tf_op jit(solution)/shard_map/ppermute | solution.py:438
  441.5 2.1 broadcast_select_fusion.5
  443.5 12.4 %collective-permute-done.41.refs_4_ = bf16[512,768]{1,0:T(8,128)(2,1)} collective-permute-done((bf16[512,768]{1,0:T(8,128)(2,1)}, bf16[512,768]{1,0:T(8,128)(2,1)}, u32[]{:S(2)}, u32[]{:S(2)}) %collective-permute-start.41) | collective-permute-done | bytes 786464 | tf_op jit(solution)/shard_map/ppermute | solution.py:438
  455.9 10.3 %all-to-all-done.1.refs_8_ = bf16[4,3,192,1024]{3,2,1,0:T(8,128)(2,1)} async-done(((bf16[4,3,192,1024]{3,2,1,0:T(8,128)(2,1)}), bf16[4,3,192,1024]{3,2,1,0:T(8,128)(2,1)}, u32[]{:S(2)}, u32[]{:S(2)}) %all-to-all-start.1) | async-done | bytes 4718624 | tf_op jit(solution)/shard_map/all_to_all | solution.py:644
  466.2 5.8 %proj_back.1 = (bf16[512,1152]{1,0:T(8,128)(2,1)}, f32[512,384]{1,0:T(8,128)}, bf16[512,384]{1,0:T(8,128)(2,1)}) custom-call(s32[3]{0:T(128)} %pad_add_fusion.2.refs_0_.sc.rt, bf16[512,384]{1,0:T(8,128)(2,1)} %get-tuple-element.129.refs_1_, bf16[2,512,768]{2,1,0:T(8,128)(2,1)} %get-tuple-element.126.refs_2_, ...), custom_call_target="tpu_custom_call" | custom-call | flops 5500000256 | tf_op jit(solution)/shard_map/proj_back/pallas_call | solution.py:50
  473.6 5.2 grad_blocks.1
  478.9 2.9 collective-permute-done.44
  485.9 9.0 %collective-permute-done.43 = bf16[512,384]{1,0:T(8,128)(2,1)S(1)} collective-permute-done((bf16[512,384]{1,0:T(8,128)(2,1)S(1)}, bf16[512,384]{1,0:T(8,128)(2,1)S(1)}, u32[]{:S(2)}, u32[]{:S(2)}) %collective-permute-start.43) | collective-permute-done | bytes 393248 | tf_op jit(solution)/shard_map/ppermute | solution.py:438
  499.2 15.7 %collective-permute-done.46 = bf16[512,384]{1,0:T(8,128)(2,1)S(1)} collective-permute-done((bf16[512,384]{1,0:T(8,128)(2,1)S(1)}, bf16[512,384]{1,0:T(8,128)(2,1)S(1)}, u32[]{:S(2)}, u32[]{:S(2)}) %collective-permute-start.46) | collective-permute-done | bytes 393248 | tf_op jit(solution)/shard_map/ppermute | solution.py:435
  517.6 2.2 collective-permute-start.50
  519.8 2.4 collective-permute-start.51
  524.7 3.5 all-to-all-start.2
  528.2 5.3 slice_convert_fusion
  533.5 3.5 convert_bitcast_fusion
  (310 shorter events, 101.4 us)
Async XLA Ops:
  7.2 80.8 %all-gather.3.cloned.1.call-start = ((), (), s32[]{:S(2)}) async-start(), calls=%async_computation.4 | async-start | bytes 2715648 | tf_op jit(solution)/shard_map/all_gather | solution.py:457
  14.1 13.9 %collective-permute-start.3 = (bf16[512,384]{1,0:T(8,128)(2,1)S(1)}, bf16[512,384]{1,0:T(8,128)(2,1)S(1)}, u32[]{:S(2)}, u32[]{:S(2)}) collective-permute-start(bf16[512,384]{1,0:T(8,128)(2,1)S(1)} %get-tuple-element.202.refs_2_.wa), channel_id=1, source_target_pairs={{0,4},{2,6},{4,0},{6,2},{1,5},{3,7},{5,1},{7,3},{8,12},{10,14},{12... | collective-permute-start | bytes 1179656 | tf_op jit(solution)/shard_map/ppermute | solution.py:438
  17.0 12.2 %collective-permute-start.2 = (bf16[512,384]{1,0:T(8,128)(2,1)S(1)}, bf16[512,384]{1,0:T(8,128)(2,1)S(1)}, u32[]{:S(2)}, u32[]{:S(2)}) collective-permute-start(bf16[512,384]{1,0:T(8,128)(2,1)S(1)} %get-tuple-element.202.refs_2_.wa), channel_id=1, source_target_pairs={{0,2},{2,0},{4,6},{6,4},{1,3},{3,1},{5,7},{7,5},{8,10},{10,8},{12,... | collective-permute-start | bytes 1179656 | tf_op jit(solution)/shard_map/ppermute | solution.py:438
  17.3 10.0 %collective-permute-start = (s32[2,512]{1,0:T(2,128)S(1)}, s32[2,512]{1,0:T(2,128)S(1)}, u32[]{:S(2)}, u32[]{:S(2)}) collective-permute-start(s32[2,512]{1,0:T(2,128)S(1)} %get-tuple-element.215), channel_id=1, source_target_pairs={{0,4},{2,6},{4,0},{6,2},{1,5},{3,7},{5,1},{7,3},{8,12},{10,14},{12... | collective-permute-start | bytes 12296 | tf_op jit(solution)/shard_map/ppermute | solution.py:438
  27.3 1.2 collective-permute-start.1
  28.0 1.9 collective-permute-start.4
  34.4 18.2 %collective-permute-start.6 = (bf16[512,384]{1,0:T(8,128)(2,1)}, bf16[512,384]{1,0:T(8,128)(2,1)S(1)}, u32[]{:S(2)}, u32[]{:S(2)}) collective-permute-start(bf16[512,384]{1,0:T(8,128)(2,1)} %get-tuple-element.79), channel_id=1, source_target_pairs={{0,8},{8,16},{16,24},{24,0},{1,9},{9,17},{17,25},{25,1},{2,10},{10... | collective-permute-start | bytes 1179656 | tf_op jit(solution)/shard_map/ppermute | solution.py:441
  36.8 39.0 %collective-permute-start.7 = (bf16[512,384]{1,0:T(8,128)(2,1)}, bf16[512,384]{1,0:T(8,128)(2,1)S(1)}, u32[]{:S(2)}, u32[]{:S(2)}) collective-permute-start(bf16[512,384]{1,0:T(8,128)(2,1)} %get-tuple-element.80), channel_id=1, source_target_pairs={{0,16},{8,24},{16,0},{24,8},{1,17},{9,25},{17,1},{25,9},{2,18},{10... | collective-permute-start | bytes 1179656 | tf_op jit(solution)/shard_map/ppermute | solution.py:441
  39.4 36.5 %collective-permute-start.8 = (bf16[512,384]{1,0:T(8,128)(2,1)}, bf16[512,384]{1,0:T(8,128)(2,1)S(1)}, u32[]{:S(2)}, u32[]{:S(2)}) collective-permute-start(bf16[512,384]{1,0:T(8,128)(2,1)} %get-tuple-element.81), channel_id=1, source_target_pairs={{0,24},{8,0},{16,8},{24,16},{1,25},{9,1},{17,9},{25,17},{2,26},{10... | collective-permute-start | bytes 1179656 | tf_op jit(solution)/shard_map/ppermute | solution.py:441
  42.6 47.9 %collective-permute-start.5 = (bf16[512,384]{1,0:T(8,128)(2,1)}, bf16[512,384]{1,0:T(8,128)(2,1)S(1)}, u32[]{:S(2)}, u32[]{:S(2)}) collective-permute-start(bf16[512,384]{1,0:T(8,128)(2,1)} %get-tuple-element.78.wa), channel_id=1, source_target_pairs={{0,1},{1,0},{2,3},{3,2},{4,5},{5,4},{6,7},{7,6},{8,9},{9,8},{10,11... | collective-permute-start | bytes 1179656 | tf_op jit(solution)/shard_map/ppermute | solution.py:435
  76.7 148.5 %all-to-all-start = ((bf16[4,3,192,1024]{3,2,1,0:T(8,128)(2,1)}), bf16[4,3,192,1024]{3,2,1,0:T(8,128)(2,1)}, u32[]{:S(2)}, u32[]{:S(2)}) async-start(bf16[4,3,192,1024]{3,2,1,0:T(8,128)(2,1)} %pad_maximum_fusion.refs_10_), calls=%async_computation | async-start | bytes 9437184 | tf_op jit(solution)/shard_map/all_to_all | solution.py:584
  87.9 250.1 %all-gather.5.cloned.1.call-start = ((), (), s32[]{:S(2)}) async-start(), calls=%async_computation.5 | async-start | bytes 5013504 | tf_op jit(solution)/shard_map/all_gather | solution.py:457
  96.3 18.8 %collective-permute-start.10 = (bf16[512,768]{1,0:T(8,128)(2,1)}, bf16[512,768]{1,0:T(8,128)(2,1)S(1)}, u32[]{:S(2)}, u32[]{:S(2)}) collective-permute-start(bf16[512,768]{1,0:T(8,128)(2,1)} %get-tuple-element.83.refs_2_), channel_id=1, source_target_pairs={{0,4},{2,6},{4,0},{6,2},{1,5},{3,7},{5,1},{7,3},{8,12},{10,14},{12... | collective-permute-start | bytes 2359304 | tf_op jit(solution)/shard_map/ppermute | solution.py:438
  97.8 21.2 %collective-permute-start.9 = (bf16[512,768]{1,0:T(8,128)(2,1)}, bf16[512,768]{1,0:T(8,128)(2,1)S(1)}, u32[]{:S(2)}, u32[]{:S(2)}) collective-permute-start(bf16[512,768]{1,0:T(8,128)(2,1)} %get-tuple-element.83.refs_2_), channel_id=1, source_target_pairs={{0,2},{2,0},{4,6},{6,4},{1,3},{3,1},{5,7},{7,5},{8,10},{10,8},{12,... | collective-permute-start | bytes 2359304 | tf_op jit(solution)/shard_map/ppermute | solution.py:438
  115.2 3.9 collective-permute-start.11
  129.3 8.4 %collective-permute-start.12 = (bf16[512,384]{1,0:T(8,128)(2,1)}, bf16[512,384]{1,0:T(8,128)(2,1)S(1)}, u32[]{:S(2)}, u32[]{:S(2)}) collective-permute-start(bf16[512,384]{1,0:T(8,128)(2,1)} %get-tuple-element.85), channel_id=1, source_target_pairs={{0,1},{1,0},{2,3},{3,2},{4,5},{5,4},{6,7},{7,6},{8,9},{9,8},{10,11... | collective-permute-start | bytes 1179656 | tf_op jit(solution)/shard_map/ppermute | solution.py:435
  139.3 3.6 collective-permute-start.13
  143.1 77.2 %copy-start.37 = (bf16[2,48,1024]{2,1,0:T(8,128)(2,1)S(1)}, bf16[2,48,1024]{2,1,0:T(8,128)(2,1)}, u32[]{:S(2)}) copy-start(bf16[2,48,1024]{2,1,0:T(8,128)(2,1)} %param.23) | copy-start | bytes 589828
  143.1 77.2 %copy-start.38 = (bf16[1024,48]{0,1:T(8,128)(2,1)S(1)}, bf16[1024,48]{0,1:T(8,128)(2,1)}, u32[]{:S(2)}) copy-start(bf16[1024,48]{0,1:T(8,128)(2,1)} %param.24) | copy-start | bytes 294916
  143.1 18.0 %collective-permute-start.16 = (bf16[512,384]{1,0:T(8,128)(2,1)S(1)}, bf16[512,384]{1,0:T(8,128)(2,1)S(1)}, u32[]{:S(2)}, u32[]{:S(2)}) collective-permute-start(bf16[512,384]{1,0:T(8,128)(2,1)S(1)} %multiply_convert_fusion.refs_2_.xa), channel_id=1, source_target_pairs={{0,4},{2,6},{4,0},{6,2},{1,5},{3,7},{5,1},{7,3},{8,12},{10,14},{12... | collective-permute-start | bytes 1179656 | tf_op jit(solution)/shard_map/ppermute | solution.py:438
  153.0 12.1 %collective-permute-start.14 = (bf16[512,384]{1,0:T(8,128)(2,1)S(1)}, bf16[512,384]{1,0:T(8,128)(2,1)S(1)}, u32[]{:S(2)}, u32[]{:S(2)}) collective-permute-start(bf16[512,384]{1,0:T(8,128)(2,1)S(1)} %multiply_convert_fusion.refs_2_.xa), channel_id=1, source_target_pairs={{0,1},{1,0},{2,3},{3,2},{4,5},{5,4},{6,7},{7,6},{8,9},{9,8},{10,11... | collective-permute-start | bytes 1179656 | tf_op jit(solution)/shard_map/ppermute | solution.py:435
  154.5 12.2 %collective-permute-start.15 = (bf16[512,384]{1,0:T(8,128)(2,1)S(1)}, bf16[512,384]{1,0:T(8,128)(2,1)S(1)}, u32[]{:S(2)}, u32[]{:S(2)}) collective-permute-start(bf16[512,384]{1,0:T(8,128)(2,1)S(1)} %multiply_convert_fusion.refs_2_.xa), channel_id=1, source_target_pairs={{0,2},{2,0},{4,6},{6,4},{1,3},{3,1},{5,7},{7,5},{8,10},{10,8},{12,... | collective-permute-start | bytes 1179656 | tf_op jit(solution)/shard_map/ppermute | solution.py:438
  161.1 5.6 %collective-permute-start.17 = (bf16[512,384]{1,0:T(8,128)(2,1)S(1)}, bf16[512,384]{1,0:T(8,128)(2,1)S(1)}, u32[]{:S(2)}, u32[]{:S(2)}) collective-permute-start(bf16[512,384]{1,0:T(8,128)(2,1)S(1)} %collective-permute-done.16.refs_4_), channel_id=1, source_target_pairs={{0,2},{2,0},{4,6},{6,4},{1,3},{3,1},{5,7},{7,5},{8,10},{10,8},{12,... | collective-permute-start | bytes 1179656 | tf_op jit(solution)/shard_map/ppermute | solution.py:438
  163.1 14.8 %collective-permute-start.20 = (bf16[512,384]{1,0:T(8,128)(2,1)S(1)}, bf16[512,384]{1,0:T(8,128)(2,1)S(1)}, u32[]{:S(2)}, u32[]{:S(2)}) collective-permute-start(bf16[512,384]{1,0:T(8,128)(2,1)S(1)} %copy-done.50), channel_id=1, source_target_pairs={{0,1},{1,0},{2,3},{3,2},{4,5},{5,4},{6,7},{7,6},{8,9},{9,8},{10,11... | collective-permute-start | bytes 1179656 | tf_op jit(solution)/shard_map/ppermute | solution.py:435
  164.6 18.9 %collective-permute-start.21 = (bf16[512,384]{1,0:T(8,128)(2,1)S(1)}, bf16[512,384]{1,0:T(8,128)(2,1)S(1)}, u32[]{:S(2)}, u32[]{:S(2)}) collective-permute-start(bf16[512,384]{1,0:T(8,128)(2,1)S(1)} %copy-done.52), channel_id=1, source_target_pairs={{0,1},{1,0},{2,3},{3,2},{4,5},{5,4},{6,7},{7,6},{8,9},{9,8},{10,11... | collective-permute-start | bytes 1179656 | tf_op jit(solution)/shard_map/ppermute | solution.py:435
  165.1 25.9 %collective-permute-start.22 = (bf16[512,384]{1,0:T(8,128)(2,1)S(1)}, bf16[512,384]{1,0:T(8,128)(2,1)S(1)}, u32[]{:S(2)}, u32[]{:S(2)}) collective-permute-start(bf16[512,384]{1,0:T(8,128)(2,1)S(1)} %copy-done.48), channel_id=1, source_target_pairs={{0,1},{1,0},{2,3},{3,2},{4,5},{5,4},{6,7},{7,6},{8,9},{9,8},{10,11... | collective-permute-start | bytes 1179656 | tf_op jit(solution)/shard_map/ppermute | solution.py:435
  172.0 46.8 %collective-permute-start.26 = (bf16[512,384]{1,0:T(8,128)(2,1)}, bf16[512,384]{1,0:T(8,128)(2,1)}, u32[]{:S(2)}, u32[]{:S(2)}) collective-permute-start(bf16[512,384]{1,0:T(8,128)(2,1)} %get-tuple-element.93), channel_id=1, source_target_pairs={{0,16},{8,24},{16,0},{24,8},{1,17},{9,25},{17,1},{25,9},{2,18},{10... | collective-permute-start | bytes 1179656 | tf_op jit(solution)/shard_map/ppermute | solution.py:441
  174.8 48.4 %collective-permute-start.24 = (bf16[512,384]{1,0:T(8,128)(2,1)}, bf16[512,384]{1,0:T(8,128)(2,1)S(1)}, u32[]{:S(2)}, u32[]{:S(2)}) collective-permute-start(bf16[512,384]{1,0:T(8,128)(2,1)} %get-tuple-element.91), channel_id=1, source_target_pairs={{0,24},{8,0},{16,8},{24,16},{1,25},{9,1},{17,9},{25,17},{2,26},{10... | collective-permute-start | bytes 1179656 | tf_op jit(solution)/shard_map/ppermute | solution.py:441
  177.9 67.4 %copy-start.55 = (bf16[512,384]{1,0:T(8,128)(2,1)}, bf16[512,384]{1,0:T(8,128)(2,1)S(1)}, u32[]{:S(2)}) copy-start(bf16[512,384]{1,0:T(8,128)(2,1)S(1)} %collective-permute-done.20.wb) | copy-start | bytes 1179652
  177.9 46.8 %collective-permute-start.19 = (bf16[512,384]{1,0:T(8,128)(2,1)}, bf16[512,384]{1,0:T(8,128)(2,1)}, u32[]{:S(2)}, u32[]{:S(2)}) collective-permute-start(bf16[512,384]{1,0:T(8,128)(2,1)} %get-tuple-element.89), channel_id=1, source_target_pairs={{0,8},{8,16},{16,24},{24,0},{1,9},{9,17},{17,25},{25,1},{2,10},{10... | collective-permute-start | bytes 1179656 | tf_op jit(solution)/shard_map/ppermute | solution.py:441
  191.0 54.3 %copy-start.53 = (bf16[512,384]{1,0:T(8,128)(2,1)}, bf16[512,384]{1,0:T(8,128)(2,1)S(1)}, u32[]{:S(2)}) copy-start(bf16[512,384]{1,0:T(8,128)(2,1)S(1)} %collective-permute-done.22.wb) | copy-start | bytes 1179652
  218.8 12.3 %collective-permute-start.27 = (bf16[512,384]{1,0:T(8,128)(2,1)}, bf16[512,384]{1,0:T(8,128)(2,1)S(1)}, u32[]{:S(2)}, u32[]{:S(2)}) collective-permute-start(bf16[512,384]{1,0:T(8,128)(2,1)} %collective-permute-done.26.xa.refs_1_), channel_id=1, source_target_pairs={{0,1},{1,0},{2,3},{3,2},{4,5},{5,4},{6,7},{7,6},{8,9},{9,8},{10,11... | collective-permute-start | bytes 1179656 | tf_op jit(solution)/shard_map/ppermute | solution.py:435
  222.7 25.4 %collective-permute-start.18 = (bf16[512,384]{1,0:T(8,128)(2,1)}, bf16[512,384]{1,0:T(8,128)(2,1)S(1)}, u32[]{:S(2)}, u32[]{:S(2)}) collective-permute-start(bf16[512,384]{1,0:T(8,128)(2,1)} %get-tuple-element.87.xa), channel_id=1, source_target_pairs={{0,1},{1,0},{2,3},{3,2},{4,5},{5,4},{6,7},{7,6},{8,9},{9,8},{10,11... | collective-permute-start | bytes 1179656 | tf_op jit(solution)/shard_map/ppermute | solution.py:435
  223.2 24.9 %collective-permute-start.25 = (bf16[512,384]{1,0:T(8,128)(2,1)S(1)}, bf16[512,384]{1,0:T(8,128)(2,1)S(1)}, u32[]{:S(2)}, u32[]{:S(2)}) collective-permute-start(bf16[512,384]{1,0:T(8,128)(2,1)S(1)} %collective-permute-done.24.refs_2_.xa), channel_id=1, source_target_pairs={{0,1},{1,0},{2,3},{3,2},{4,5},{5,4},{6,7},{7,6},{8,9},{9,8},{10,11... | collective-permute-start | bytes 1179656 | tf_op jit(solution)/shard_map/ppermute | solution.py:435
  224.7 31.7 %collective-permute-start.23 = (bf16[512,384]{1,0:T(8,128)(2,1)}, bf16[512,384]{1,0:T(8,128)(2,1)}, u32[]{:S(2)}, u32[]{:S(2)}) collective-permute-start(bf16[512,384]{1,0:T(8,128)(2,1)} %collective-permute-done.19.refs_0_.xa), channel_id=1, source_target_pairs={{0,1},{1,0},{2,3},{3,2},{4,5},{5,4},{6,7},{7,6},{8,9},{9,8},{10,11... | collective-permute-start | bytes 1179656 | tf_op jit(solution)/shard_map/ppermute | solution.py:435
  246.5 26.2 %collective-permute-start.29 = (bf16[512,768]{1,0:T(8,128)(2,1)S(1)}, bf16[512,768]{1,0:T(8,128)(2,1)S(1)}, u32[]{:S(2)}, u32[]{:S(2)}) collective-permute-start(bf16[512,768]{1,0:T(8,128)(2,1)S(1)} %slice_bitcast_fusion.3), channel_id=1, source_target_pairs={{0,1},{1,0},{2,3},{3,2},{4,5},{5,4},{6,7},{7,6},{8,9},{9,8},{10,11... | collective-permute-start | bytes 2359304 | tf_op jit(solution)/shard_map/ppermute | solution.py:435
  271.1 18.5 %collective-permute-start.28 = (bf16[512,768]{1,0:T(8,128)(2,1)S(1)}, bf16[512,768]{1,0:T(8,128)(2,1)S(1)}, u32[]{:S(2)}, u32[]{:S(2)}) collective-permute-start(bf16[512,768]{1,0:T(8,128)(2,1)S(1)} %slice_bitcast_fusion.4), channel_id=1, source_target_pairs={{0,1},{1,0},{2,3},{3,2},{4,5},{5,4},{6,7},{7,6},{8,9},{9,8},{10,11... | collective-permute-start | bytes 2359304 | tf_op jit(solution)/shard_map/ppermute | solution.py:435
  272.9 42.8 %collective-permute-start.32 = (bf16[512,768]{1,0:T(8,128)(2,1)S(1)}, bf16[512,768]{1,0:T(8,128)(2,1)S(1)}, u32[]{:S(2)}, u32[]{:S(2)}) collective-permute-start(bf16[512,768]{1,0:T(8,128)(2,1)S(1)} %fusion.13.refs_0_), channel_id=1, source_target_pairs={{0,16},{8,24},{16,0},{24,8},{1,17},{9,25},{17,1},{25,9},{2,18},{10... | collective-permute-start | bytes 2359304 | tf_op jit(solution)/shard_map/ppermute | solution.py:441
  288.3 26.7 %collective-permute-start.33 = (bf16[512,768]{1,0:T(8,128)(2,1)S(1)}, bf16[512,768]{1,0:T(8,128)(2,1)S(1)}, u32[]{:S(2)}, u32[]{:S(2)}) collective-permute-start(bf16[512,768]{1,0:T(8,128)(2,1)S(1)} %slice_bitcast_fusion.1), channel_id=1, source_target_pairs={{0,1},{1,0},{2,3},{3,2},{4,5},{5,4},{6,7},{7,6},{8,9},{9,8},{10,11... | collective-permute-start | bytes 2359304 | tf_op jit(solution)/shard_map/ppermute | solution.py:435
  289.8 48.2 %collective-permute-start.31 = (bf16[512,768]{1,0:T(8,128)(2,1)S(1)}, bf16[512,768]{1,0:T(8,128)(2,1)S(1)}, u32[]{:S(2)}, u32[]{:S(2)}) collective-permute-start(bf16[512,768]{1,0:T(8,128)(2,1)S(1)} %fusion.14.refs_0_), channel_id=1, source_target_pairs={{0,24},{8,0},{16,8},{24,16},{1,25},{9,1},{17,9},{25,17},{2,26},{10... | collective-permute-start | bytes 2359304 | tf_op jit(solution)/shard_map/ppermute | solution.py:441
  307.4 54.6 %collective-permute-start.30 = (bf16[512,768]{1,0:T(8,128)(2,1)}, bf16[512,768]{1,0:T(8,128)(2,1)}, u32[]{:S(2)}, u32[]{:S(2)}) collective-permute-start(bf16[512,768]{1,0:T(8,128)(2,1)} %slice_bitcast_fusion.2), channel_id=1, source_target_pairs={{0,1},{1,0},{2,3},{3,2},{4,5},{5,4},{6,7},{7,6},{8,9},{9,8},{10,11... | collective-permute-start | bytes 2359304 | tf_op jit(solution)/shard_map/ppermute | solution.py:435
  315.3 22.7 %collective-permute-start.34 = (bf16[512,768]{1,0:T(8,128)(2,1)S(1)}, bf16[512,768]{1,0:T(8,128)(2,1)S(1)}, u32[]{:S(2)}, u32[]{:S(2)}) collective-permute-start(bf16[512,768]{1,0:T(8,128)(2,1)S(1)} %fusion.11), channel_id=1, source_target_pairs={{0,8},{8,16},{16,24},{24,0},{1,9},{9,17},{17,25},{25,1},{2,10},{10... | collective-permute-start | bytes 2359304 | tf_op jit(solution)/shard_map/ppermute | solution.py:441
  351.6 15.0 %collective-permute-start.35 = (bf16[512,768]{1,0:T(8,128)(2,1)S(1)}, bf16[512,768]{1,0:T(8,128)(2,1)}, u32[]{:S(2)}, u32[]{:S(2)}) collective-permute-start(bf16[512,768]{1,0:T(8,128)(2,1)S(1)} %slice_bitcast_fusion), channel_id=1, source_target_pairs={{0,1},{1,0},{2,3},{3,2},{4,5},{5,4},{6,7},{7,6},{8,9},{9,8},{10,11... | collective-permute-start | bytes 2359304 | tf_op jit(solution)/shard_map/ppermute | solution.py:435
  352.2 114.0 %all-to-all-start.1 = ((bf16[4,3,192,1024]{3,2,1,0:T(8,128)(2,1)}), bf16[4,3,192,1024]{3,2,1,0:T(8,128)(2,1)}, u32[]{:S(2)}, u32[]{:S(2)}) async-start(bf16[4,3,192,1024]{3,2,1,0:T(8,128)(2,1)} %pad_maximum_fusion.1.refs_0_), calls=%async_computation.1 | async-start | bytes 9437184 | tf_op jit(solution)/shard_map/all_to_all | solution.py:644
  361.8 180.7 %reduce-scatter.2.cloned.1.call-start = ((), (), s32[]{:S(2)}) async-start(), calls=%async_computation.6 | async-start | bytes 5013504 | tf_op jit(solution)/shard_map/reduce_scatter | solution.py:665
  374.1 2.5 collective-permute-start.36
  378.0 11.2 %collective-permute-start.37 = (bf16[512,384]{1,0:T(8,128)(2,1)S(1)}, bf16[512,384]{1,0:T(8,128)(2,1)S(1)}, u32[]{:S(2)}, u32[]{:S(2)}) collective-permute-start(bf16[512,384]{1,0:T(8,128)(2,1)S(1)} %fusion.33), channel_id=1, source_target_pairs={{0,4},{2,6},{4,0},{6,2},{1,5},{3,7},{5,1},{7,3},{8,12},{10,14},{12... | collective-permute-start | bytes 1179656 | tf_op jit(solution)/shard_map/ppermute | solution.py:438
  390.2 3.6 collective-permute-start.38
  395.3 10.0 %collective-permute-start.39 = (bf16[512,384]{1,0:T(8,128)(2,1)}, bf16[512,384]{1,0:T(8,128)(2,1)}, u32[]{:S(2)}, u32[]{:S(2)}) collective-permute-start(bf16[512,384]{1,0:T(8,128)(2,1)} %fusion.60.refs_10_), channel_id=1, source_target_pairs={{0,1},{1,0},{2,3},{3,2},{4,5},{5,4},{6,7},{7,6},{8,9},{9,8},{10,11... | collective-permute-start | bytes 1179656 | tf_op jit(solution)/shard_map/ppermute | solution.py:435
  417.2 6.1 %collective-permute-start.40 = (bf16[2,512,768]{2,1,0:T(8,128)(2,1)}, bf16[2,512,768]{2,1,0:T(8,128)(2,1)}, u32[]{:S(2)}, u32[]{:S(2)}) collective-permute-start(bf16[2,512,768]{2,1,0:T(8,128)(2,1)} %get-tuple-element.127), channel_id=1, source_target_pairs={{0,2},{2,0},{4,6},{6,4},{1,3},{3,1},{5,7},{7,5},{8,10},{10,8},{12,... | collective-permute-start | bytes 4718600 | tf_op jit(solution)/shard_map/ppermute | solution.py:438
  425.9 30.0 %collective-permute-start.41 = (bf16[512,768]{1,0:T(8,128)(2,1)}, bf16[512,768]{1,0:T(8,128)(2,1)}, u32[]{:S(2)}, u32[]{:S(2)}) collective-permute-start(bf16[512,768]{1,0:T(8,128)(2,1)} %fusion.27), channel_id=1, source_target_pairs={{0,4},{2,6},{4,0},{6,2},{1,5},{3,7},{5,1},{7,3},{8,12},{10,14},{12... | collective-permute-start | bytes 2359304 | tf_op jit(solution)/shard_map/ppermute | solution.py:438
  455.9 27.2 %collective-permute-start.42 = (bf16[2,512,384]{2,1,0:T(8,128)(2,1)}, bf16[2,512,384]{2,1,0:T(8,128)(2,1)}, u32[]{:S(2)}, u32[]{:S(2)}) collective-permute-start(bf16[2,512,384]{2,1,0:T(8,128)(2,1)} %get-tuple-element.128), channel_id=1, source_target_pairs={{0,2},{2,0},{4,6},{6,4},{1,3},{3,1},{5,7},{7,5},{8,10},{10,8},{12,... | collective-permute-start | bytes 2359304 | tf_op jit(solution)/shard_map/ppermute | solution.py:438
  472.0 9.9 %collective-permute-start.44 = (bf16[512,384]{1,0:T(8,128)(2,1)}, bf16[512,384]{1,0:T(8,128)(2,1)S(1)}, u32[]{:S(2)}, u32[]{:S(2)}) collective-permute-start(bf16[512,384]{1,0:T(8,128)(2,1)} %get-tuple-element.135), channel_id=1, source_target_pairs={{0,1},{1,0},{2,3},{3,2},{4,5},{5,4},{6,7},{7,6},{8,9},{9,8},{10,11... | collective-permute-start | bytes 1179656 | tf_op jit(solution)/shard_map/ppermute | solution.py:435
  478.8 19.8 %collective-permute-start.48 = (bf16[2,4,48,1536]{3,2,1,0:T(8,128)(2,1)}, bf16[2,4,48,1536]{3,2,1,0:T(8,128)(2,1)S(1)}, u32[]{:S(2)}, u32[]{:S(2)}) collective-permute-start(bf16[2,4,48,1536]{3,2,1,0:T(8,128)(2,1)} %get-tuple-element.141), channel_id=1, source_target_pairs={{0,2},{2,0},{4,6},{6,4},{1,3},{3,1},{5,7},{7,5},{8,10},{10,8},{12,... | collective-permute-start | bytes 3538952 | tf_op jit(solution)/shard_map/ppermute | solution.py:438
  482.3 3.6 collective-permute-start.45
  484.2 10.7 %collective-permute-start.43 = (bf16[512,384]{1,0:T(8,128)(2,1)S(1)}, bf16[512,384]{1,0:T(8,128)(2,1)S(1)}, u32[]{:S(2)}, u32[]{:S(2)}) collective-permute-start(bf16[512,384]{1,0:T(8,128)(2,1)S(1)} %fusion.34), channel_id=1, source_target_pairs={{0,4},{2,6},{4,0},{6,2},{1,5},{3,7},{5,1},{7,3},{8,12},{10,14},{12... | collective-permute-start | bytes 1179656 | tf_op jit(solution)/shard_map/ppermute | solution.py:438
  496.6 19.4 %collective-permute-start.47 = (bf16[512,384]{1,0:T(8,128)(2,1)S(1)}, bf16[512,384]{1,0:T(8,128)(2,1)S(1)}, u32[]{:S(2)}, u32[]{:S(2)}) collective-permute-start(bf16[512,384]{1,0:T(8,128)(2,1)S(1)} %get-tuple-element.195), channel_id=1, source_target_pairs={{0,1},{1,0},{2,3},{3,2},{4,5},{5,4},{6,7},{7,6},{8,9},{9,8},{10,11... | collective-permute-start | bytes 1179656 | tf_op jit(solution)/shard_map/ppermute | solution.py:435
  498.1 16.8 %collective-permute-start.46 = (bf16[512,384]{1,0:T(8,128)(2,1)S(1)}, bf16[512,384]{1,0:T(8,128)(2,1)S(1)}, u32[]{:S(2)}, u32[]{:S(2)}) collective-permute-start(bf16[512,384]{1,0:T(8,128)(2,1)S(1)} %get-tuple-element.136), channel_id=1, source_target_pairs={{0,1},{1,0},{2,3},{3,2},{4,5},{5,4},{6,7},{7,6},{8,9},{9,8},{10,11... | collective-permute-start | bytes 1179656 | tf_op jit(solution)/shard_map/ppermute | solution.py:435
  498.8 18.5 %collective-permute-start.49 = (bf16[4,48,1536]{2,1,0:T(8,128)(2,1)S(1)}, bf16[4,48,1536]{2,1,0:T(8,128)(2,1)S(1)}, u32[]{:S(2)}, u32[]{:S(2)}) collective-permute-start(bf16[4,48,1536]{2,1,0:T(8,128)(2,1)S(1)} %fusion.32), channel_id=1, source_target_pairs={{0,4},{2,6},{4,0},{6,2},{1,5},{3,7},{5,1},{7,3},{8,12},{10,14},{12... | collective-permute-start | bytes 1769480 | tf_op jit(solution)/shard_map/ppermute | solution.py:438
  517.6 19.5 %collective-permute-start.50 = (bf16[48,1536]{1,0:T(8,128)(2,1)S(1)}, bf16[48,1536]{1,0:T(8,128)(2,1)S(1)}, u32[]{:S(2)}, u32[]{:S(2)}) collective-permute-start(bf16[48,1536]{1,0:T(8,128)(2,1)S(1)} %get-tuple-element.206), channel_id=1, source_target_pairs={{0,8},{8,16},{16,24},{24,0},{1,9},{9,17},{17,25},{25,1},{2,10},{10... | collective-permute-start | bytes 442376 | tf_op jit(solution)/shard_map/ppermute | solution.py:441
  519.8 17.3 %collective-permute-start.51 = (bf16[48,1536]{1,0:T(8,128)(2,1)S(1)}, bf16[48,1536]{1,0:T(8,128)(2,1)S(1)}, u32[]{:S(2)}, u32[]{:S(2)}) collective-permute-start(bf16[48,1536]{1,0:T(8,128)(2,1)S(1)} %get-tuple-element.208), channel_id=1, source_target_pairs={{0,16},{8,24},{16,0},{24,8},{1,17},{9,25},{17,1},{25,9},{2,18},{10... | collective-permute-start | bytes 442376 | tf_op jit(solution)/shard_map/ppermute | solution.py:441
  522.2 14.9 %collective-permute-start.52 = (bf16[48,1536]{1,0:T(8,128)(2,1)S(1)}, bf16[48,1536]{1,0:T(8,128)(2,1)S(1)}, u32[]{:S(2)}, u32[]{:S(2)}) collective-permute-start(bf16[48,1536]{1,0:T(8,128)(2,1)S(1)} %get-tuple-element.207), channel_id=1, source_target_pairs={{0,24},{8,0},{16,8},{24,16},{1,25},{9,1},{17,9},{25,17},{2,26},{10... | collective-permute-start | bytes 442376 | tf_op jit(solution)/shard_map/ppermute | solution.py:441
  524.7 12.3 %all-to-all-start.2 = ((f32[16,1,864]{2,1,0:T(1,128)}), f32[16,1,864]{2,1,0:T(1,128)S(1)}, u32[]{:S(2)}, u32[]{:S(2)}) async-start(f32[16,1,864]{2,1,0:T(1,128)} %all_to_all.16), calls=%async_computation.2 | async-start | bytes 114688 | tf_op jit(solution)/shard_map/all_to_all | solution.py:743
  537.2 3.9 collective-permute-start.53
  (64 other events, 511.4 us)
Sparse Core Ops, SparseCore 0:
  12.2 61.9 all-gather.2
  225.4 74.5 all-gather.4
  423.3 98.0 reduce-scatter.1

commit v6 on v5

--- a/solution.py
+++ b/solution.py
@@ -292,7 +292,7 @@
         de_o[0] = (w.astype(f32) * gate).astype(bf16)
     acc_o[...] = jnp.zeros_like(acc_o)
     acc_b[...] = jnp.zeros_like(acc_b)
-    tile = 256
+    tile = 512
 
     def columns(which, lo):
         cols = pl.ds(pl.multiple_of(lo, tile), tile)

time: 561 us -> 560 us (level)
  transfers between devices with their start and end apart: 60 -> 60, of which waited for: 27 -> 29; matrix products, arithmetic and copies ran while one was open for 16% -> 16% of each run, Pallas kernels for 21% -> 20%
where the time goes in v6:
time: 560 us; the launch traced here: 551 us
  waiting for transfers between devices  210 us (38%)
  Pallas kernels  110 us (20%)
  starting transfers between devices  109 us (19%)
  other arithmetic  51 us (9%)
  local copies, waits for them, and re-layouts  38.5 us (7%)
  matrix products  16.9 us (3%)
  between operations  14.9 us (3%)
    ppermute x12, waiting for transfers between devices, zs(): lax.ppermute(v, 'fsdp', [(i, i // EL * EL + (i % EL + s) % EL) for i in r...  72.2 us
    ppermute x23, waiting for transfers between devices, yx(): return lax.ppermute(v, 'tp', [(0, 1), (1, 0)])  66.9 us
    pallas_call x5, Pallas kernels, ffn(): pl.pallas_call(functools.partial(ffn_body, routed), grid=(1,), out_shape=...  60.8 us
    ppermute x19, waiting for transfers between devices, cx(): return lax.ppermute(v, 'ctx', [(i, i ^ flip) for i in range(C)])  59.5 us
    pallas_call x8, Pallas kernels, run(): pl.pallas_call(inner, out_shape=outs, in_specs=[SMEM] + [VM] * len(args)...  49.5 us
    ppermute x19, starting transfers between devices, cx(): return lax.ppermute(v, 'ctx', [(i, i ^ flip) for i in range(C)])  36.1 us
    ppermute x23, starting transfers between devices, yx(): return lax.ppermute(v, 'tp', [(0, 1), (1, 0)])  25.8 us
    ppermute x12, starting transfers between devices, zs(): lax.ppermute(v, 'fsdp', [(i, i // EL * EL + (i % EL + s) % EL) for i in r...  22.1 us
  transfers between devices with their start and end apart: 60, of which 29 were waited for; matrix products, arithmetic and copies ran while one was open for 16% of the time, Pallas kernels for 20%

profile of v6, /device:TPU:0, one launch (start us, length us, event | category | flops | bytes accessed | tf_op | source)
XLA Modules:
  0.0 551.0 jit_solution(6738672413230519902)
XLA Ops:
  12.1 1.9 constant_dynamic-slice_fusion
  14.1 2.9 collective-permute-start.3
  17.4 4.5 pad_maximum_fusion.refs_10_
  21.9 5.4 collective-permute-done
  30.7 3.7 pack.2
  34.4 2.4 collective-permute-start.6
  36.8 2.6 collective-permute-start.7
  44.1 8.5 %collective-permute-done.6.refs_7_.wa = bf16[512,384]{1,0:T(8,128)(2,1)S(1)} collective-permute-done((bf16[512,384]{1,0:T(8,128)(2,1)}, bf16[512,384]{1,0:T(8,128)(2,1)S(1)}, u32[]{:S(2)}, u32[]{:S(2)}) %collective-permute-start.6) | collective-permute-done | bytes 393248 | tf_op jit(solution)/shard_map/ppermute | solution.py:441
  52.6 23.2 %collective-permute-done.7.refs_8_.wa = bf16[512,384]{1,0:T(8,128)(2,1)S(1)} collective-permute-done((bf16[512,384]{1,0:T(8,128)(2,1)}, bf16[512,384]{1,0:T(8,128)(2,1)S(1)}, u32[]{:S(2)}, u32[]{:S(2)}) %collective-permute-start.7) | collective-permute-done | bytes 393248 | tf_op jit(solution)/shard_map/ppermute | solution.py:441
  76.7 11.2 %all-to-all-start = ((bf16[4,3,192,1024]{3,2,1,0:T(8,128)(2,1)}), bf16[4,3,192,1024]{3,2,1,0:T(8,128)(2,1)}, u32[]{:S(2)}, u32[]{:S(2)}) async-start(bf16[4,3,192,1024]{3,2,1,0:T(8,128)(2,1)} %pad_maximum_fusion.refs_10_), calls=%async_computation | async-start | bytes 9437184 | tf_op jit(solution)/shard_map/all_to_all | solution.py:584
  91.2 5.1 qkv.1
  97.9 17.3 %collective-permute-done.10.refs_4_ = bf16[512,768]{1,0:T(8,128)(2,1)S(1)} collective-permute-done((bf16[512,768]{1,0:T(8,128)(2,1)}, bf16[512,768]{1,0:T(8,128)(2,1)S(1)}, u32[]{:S(2)}, u32[]{:S(2)}) %collective-permute-start.10) | collective-permute-done | bytes 786464 | tf_op jit(solution)/shard_map/ppermute | solution.py:438
  117.1 2.0 slice.230.refs_8_.refs_12_
  120.3 9.1 %attn.1 = (bf16[512,384]{1,0:T(8,128)(2,1)}, f32[512,384]{1,0:T(8,128)}, bf16[512,384]{1,0:T(8,128)(2,1)}, f32[8,512]{1,0:T(8,128)}) custom-call(s32[3]{0:T(128)} %pad_add_fusion.2.refs_0_.sc.rt, bf16[512,384]{1,0:T(8,128)(2,1)} %get-tuple-element.82.refs_1_, bf16[512,768]{1,0:T(8,128)(2,1)} %get-tuple-element.83.refs_2_, bf16[512,768]{1,0:T(8,128)(2,1)} %copy-done.21, ...), custom_call_target="tpu_custom_call" | custom-call | flops 18699999232 | tf_op jit(solution)/shard_map/attn/pallas_call | solution.py:50
  130.9 6.9 %collective-permute-done.12 = bf16[512,384]{1,0:T(8,128)(2,1)S(1)} collective-permute-done((bf16[512,384]{1,0:T(8,128)(2,1)}, bf16[512,384]{1,0:T(8,128)(2,1)S(1)}, u32[]{:S(2)}, u32[]{:S(2)}) %collective-permute-start.12) | collective-permute-done | bytes 393248 | tf_op jit(solution)/shard_map/ppermute | solution.py:435
  143.1 9.9 %collective-permute-start.16 = (bf16[512,384]{1,0:T(8,128)(2,1)S(1)}, bf16[512,384]{1,0:T(8,128)(2,1)S(1)}, u32[]{:S(2)}, u32[]{:S(2)}) collective-permute-start(bf16[512,384]{1,0:T(8,128)(2,1)S(1)} %multiply_convert_fusion.refs_2_.xa), channel_id=1, source_target_pairs={{0,4},{2,6},{4,0},{6,2},{1,5},{3,7},{5,1},{7,3},{8,12},{10,14},{12... | collective-permute-start | bytes 1179656 | tf_op jit(solution)/shard_map/ppermute | solution.py:438
  156.4 4.7 collective-permute-done.16.refs_4_
  161.1 2.0 collective-permute-start.17
  168.3 3.7 pack.3
  172.0 2.7 collective-permute-start.26
  174.8 3.1 collective-permute-start.24
  178.6 4.9 collective-permute-done.21.wb
  183.5 7.5 %collective-permute-done.22.wb = bf16[512,384]{1,0:T(8,128)(2,1)S(1)} collective-permute-done((bf16[512,384]{1,0:T(8,128)(2,1)S(1)}, bf16[512,384]{1,0:T(8,128)(2,1)S(1)}, u32[]{:S(2)}, u32[]{:S(2)}) %collective-permute-start.22) | collective-permute-done | bytes 393248 | tf_op jit(solution)/shard_map/ppermute | solution.py:435
  191.0 27.8 %collective-permute-done.26.xa.refs_1_ = bf16[512,384]{1,0:T(8,128)(2,1)} collective-permute-done((bf16[512,384]{1,0:T(8,128)(2,1)}, bf16[512,384]{1,0:T(8,128)(2,1)}, u32[]{:S(2)}, u32[]{:S(2)}) %collective-permute-start.26) | collective-permute-done | bytes 393248 | tf_op jit(solution)/shard_map/ppermute | solution.py:441
  225.2 5.8 %collective-permute-done.27.xb = bf16[512,384]{1,0:T(8,128)(2,1)S(1)} collective-permute-done((bf16[512,384]{1,0:T(8,128)(2,1)}, bf16[512,384]{1,0:T(8,128)(2,1)S(1)}, u32[]{:S(2)}, u32[]{:S(2)}) %collective-permute-start.27) | collective-permute-done | bytes 393248 | tf_op jit(solution)/shard_map/ppermute | solution.py:435
  231.8 12.8 %expert_ffn.4 = (bf16[2,512,768]{2,1,0:T(8,128)(2,1)}, f32[768,128]{1,0:T(8,128)}, bf16[4,512,2048]{2,1,0:T(8,128)(2,1)}, bf16[4,512,1024]{2,1,0:T(8,128)(2,1)},...) custom-call(s32[3]{0:T(128)} %pad_add_fusion.2.refs_0_.sc.rt, ...), custom_call_target="tpu_custom_call" | custom-call | flops 16000000000 | tf_op jit(solution)/shard_map/expert_ffn/pallas_call | solution.py:369
  247.9 8.5 %collective-permute-done.23.xb = bf16[512,384]{1,0:T(8,128)(2,1)} collective-permute-done((bf16[512,384]{1,0:T(8,128)(2,1)}, bf16[512,384]{1,0:T(8,128)(2,1)}, u32[]{:S(2)}, u32[]{:S(2)}) %collective-permute-start.23) | collective-permute-done | bytes 393248 | tf_op jit(solution)/shard_map/ppermute | solution.py:435
  256.4 12.7 %expert_ffn.5 = (bf16[2,512,768]{2,1,0:T(8,128)(2,1)}, f32[768,128]{1,0:T(8,128)}, bf16[4,512,2048]{2,1,0:T(8,128)(2,1)}, bf16[4,512,1024]{2,1,0:T(8,128)(2,1)},...) custom-call(s32[3]{0:T(128)} %pad_add_fusion.2.refs_0_.sc.rt, ...), custom_call_target="tpu_custom_call", output_to_operand_aliasing={{2}: (9, {}), {3}: (10, {}), {4}: (11, {}), {5}: (12, {})} | custom-call | flops 16000000000 | tf_op jit(solution)/shard_map/expert_ffn/pallas_call | solution.py:369
  274.2 13.0 %expert_ffn.6 = (bf16[2,512,768]{2,1,0:T(8,128)(2,1)}, f32[768,128]{1,0:T(8,128)}, bf16[4,512,2048]{2,1,0:T(8,128)(2,1)}, bf16[4,512,1024]{2,1,0:T(8,128)(2,1)},...) custom-call(s32[3]{0:T(128)} %pad_add_fusion.2.refs_0_.sc.rt, ...), custom_call_target="tpu_custom_call", output_to_operand_aliasing={{2}: (8, {}), {3}: (9, {}), {4}: (10, {}), {5}: (11, {})} | custom-call | flops 16000000000 | tf_op jit(solution)/shard_map/expert_ffn/pallas_call | solution.py:369
  290.3 2.4 collective-permute-start.31
  292.6 12.1 %expert_ffn.7 = (bf16[2,512,768]{2,1,0:T(8,128)(2,1)}, f32[768,128]{1,0:T(8,128)}, bf16[4,512,2048]{2,1,0:T(8,128)(2,1)}, bf16[4,512,1024]{2,1,0:T(8,128)(2,1)},...) custom-call(s32[3]{0:T(128)} %pad_add_fusion.2.refs_0_.sc.rt, ...), custom_call_target="tpu_custom_call", output_to_operand_aliasing={{2}: (8, {}), {3}: (9, {}), {4}: (10, {}), {5}: (11, {})} | custom-call | flops 16000000000 | tf_op jit(solution)/shard_map/expert_ffn/pallas_call | solution.py:369
  304.8 2.0 slice_bitcast_fusion.2
  307.3 6.7 %bitcast_convert_fusion = bf16[768,1024]{1,0:T(8,128)(2,1)S(1)} fusion(bf16[4,512,768]{2,1,0:T(8,128)(2,1)} %get-tuple-element.115, bf16[4,512,1024]{2,1,0:T(8,128)(2,1)} %get-tuple-element.116), kind=kOutput, calls=%fused_computation.9 | convolution fusion | flops 3222011904 | bytes 8912896 | tf_op jit(solution)/shard_map/dot_general | solution.py:638
  315.1 3.5 fusion.5
  318.6 3.5 fusion.8
  322.1 2.5 pad_maximum_fusion.1.refs_0_
  324.6 12.7 %collective-permute-done.31.refs_1_.refs_3_ = bf16[512,768]{1,0:T(8,128)(2,1)S(1)} collective-permute-done((bf16[512,768]{1,0:T(8,128)(2,1)S(1)}, bf16[512,768]{1,0:T(8,128)(2,1)S(1)}, u32[]{:S(2)}, u32[]{:S(2)}) %collective-permute-start.31) | collective-permute-done | bytes 786464 | tf_op jit(solution)/shard_map/ppermute | solution.py:441
  338.5 10.2 %shared_ffn.1 = (bf16[2,512,768]{2,1,0:T(8,128)(2,1)}, bf16[1,512,2048]{2,1,0:T(8,128)(2,1)}, bf16[1,512,1024]{2,1,0:T(8,128)(2,1)}) custom-call(s32[3]{0:T(128)} %pad_add_fusion.2.refs_0_.sc.rt, bf16[512,384]{1,0:T(8,128)(2,1)} %copy-done.10, bf16[512,384]{1,0:T(8,128)(2,1)} %copy-done.8, bf16[512,384]{1,0:T(8,128)(2,1)} %copy-done.1, ...), custom_call_target="tpu_custom_call" | custom-call | tf_op jit(solution)/shard_map/shared_ffn/pallas_call | solution.py:369
  350.5 10.2 %all-to-all-start.1 = ((bf16[4,3,192,1024]{3,2,1,0:T(8,128)(2,1)}), bf16[4,3,192,1024]{3,2,1,0:T(8,128)(2,1)}, u32[]{:S(2)}, u32[]{:S(2)}) async-start(bf16[4,3,192,1024]{3,2,1,0:T(8,128)(2,1)} %pad_maximum_fusion.1.refs_0_), calls=%async_computation.1 | async-start | bytes 9437184 | tf_op jit(solution)/shard_map/all_to_all | solution.py:644
  361.0 2.4 fusion.12.refs_2_
  364.3 2.4 convert_add_fusion.refs_6_
  366.7 5.0 unpack.1
  371.8 2.5 collective-permute-done.36
  379.6 7.3 %collective-permute-done.37 = bf16[512,384]{1,0:T(8,128)(2,1)S(1)} collective-permute-done((bf16[512,384]{1,0:T(8,128)(2,1)S(1)}, bf16[512,384]{1,0:T(8,128)(2,1)S(1)}, u32[]{:S(2)}, u32[]{:S(2)}) %collective-permute-start.37) | collective-permute-done | bytes 393248 | tf_op jit(solution)/shard_map/ppermute | solution.py:438
  389.2 2.2 collective-permute-done.38
  393.3 2.7 pad_maximum_fusion.2.refs_15_
  396.0 7.1 %collective-permute-done.39.refs_11_ = bf16[512,384]{1,0:T(8,128)(2,1)} collective-permute-done((bf16[512,384]{1,0:T(8,128)(2,1)}, bf16[512,384]{1,0:T(8,128)(2,1)}, u32[]{:S(2)}, u32[]{:S(2)}) %collective-permute-start.39) | collective-permute-done | bytes 393248 | tf_op jit(solution)/shard_map/ppermute | solution.py:435
  403.0 11.9 %attn_back.1 = (bf16[512,384]{1,0:T(8,128)(2,1)}, bf16[2,512,768]{2,1,0:T(8,128)(2,1)}, bf16[2,512,768]{2,1,0:T(8,128)(2,1)}) custom-call(s32[3]{0:T(128)} %pad_add_fusion.2.refs_0_.sc.rt, bf16[512,384]{1,0:T(8,128)(2,1)} %get-tuple-element.82.refs_1_, bf16[512,768]{1,0:T(8,128)(2,1)} %get-tuple-element.83.refs_2_, bf16[512,768]{1,0:T(8,128)(2,1)} %copy-done.21, ...), custom_call_target="tpu_custom_call" | custom-call | tf_op jit(solution)/shard_map/attn_back/pallas_call | solution.py:50
  414.9 2.7 collective-permute-start.40
  421.0 2.5 fusion.27
  423.6 11.7 %collective-permute-start.41 = (bf16[512,768]{1,0:T(8,128)(2,1)}, bf16[512,768]{1,0:T(8,128)(2,1)}, u32[]{:S(2)}, u32[]{:S(2)}) collective-permute-start(bf16[512,768]{1,0:T(8,128)(2,1)} %fusion.27), channel_id=1, source_target_pairs={{0,4},{2,6},{4,0},{6,2},{1,5},{3,7},{5,1},{7,3},{8,12},{10,14},{12... | collective-permute-start | bytes 2359304 | tf_op jit(solution)/shard_map/ppermute | solution.py:438
  439.1 2.1 broadcast_select_fusion.5
  441.2 12.4 %collective-permute-done.41.refs_4_ = bf16[512,768]{1,0:T(8,128)(2,1)} collective-permute-done((bf16[512,768]{1,0:T(8,128)(2,1)}, bf16[512,768]{1,0:T(8,128)(2,1)}, u32[]{:S(2)}, u32[]{:S(2)}) %collective-permute-start.41) | collective-permute-done | bytes 786464 | tf_op jit(solution)/shard_map/ppermute | solution.py:438
  453.6 11.5 %all-to-all-done.1.refs_8_ = bf16[4,3,192,1024]{3,2,1,0:T(8,128)(2,1)} async-done(((bf16[4,3,192,1024]{3,2,1,0:T(8,128)(2,1)}), bf16[4,3,192,1024]{3,2,1,0:T(8,128)(2,1)}, u32[]{:S(2)}, u32[]{:S(2)}) %all-to-all-start.1) | async-done | bytes 4718624 | tf_op jit(solution)/shard_map/all_to_all | solution.py:644
  465.1 5.8 %proj_back.1 = (bf16[512,1152]{1,0:T(8,128)(2,1)}, f32[512,384]{1,0:T(8,128)}, bf16[512,384]{1,0:T(8,128)(2,1)}) custom-call(s32[3]{0:T(128)} %pad_add_fusion.2.refs_0_.sc.rt, bf16[512,384]{1,0:T(8,128)(2,1)} %get-tuple-element.129.refs_1_, bf16[2,512,768]{2,1,0:T(8,128)(2,1)} %get-tuple-element.126.refs_2_, ...), custom_call_target="tpu_custom_call" | custom-call | flops 5500000256 | tf_op jit(solution)/shard_map/proj_back/pallas_call | solution.py:50
  472.5 5.2 grad_blocks.1
  477.8 2.9 collective-permute-done.44
  484.8 9.1 %collective-permute-done.43 = bf16[512,384]{1,0:T(8,128)(2,1)S(1)} collective-permute-done((bf16[512,384]{1,0:T(8,128)(2,1)S(1)}, bf16[512,384]{1,0:T(8,128)(2,1)S(1)}, u32[]{:S(2)}, u32[]{:S(2)}) %collective-permute-start.43) | collective-permute-done | bytes 393248 | tf_op jit(solution)/shard_map/ppermute | solution.py:438
  498.1 15.8 %collective-permute-done.46 = bf16[512,384]{1,0:T(8,128)(2,1)S(1)} collective-permute-done((bf16[512,384]{1,0:T(8,128)(2,1)S(1)}, bf16[512,384]{1,0:T(8,128)(2,1)S(1)}, u32[]{:S(2)}, u32[]{:S(2)}) %collective-permute-start.46) | collective-permute-done | bytes 393248 | tf_op jit(solution)/shard_map/ppermute | solution.py:435
  516.6 2.2 collective-permute-start.50
  518.7 2.4 collective-permute-start.51
  523.7 3.5 all-to-all-start.2
  527.2 5.3 slice_convert_fusion
  532.5 3.5 convert_bitcast_fusion
  (310 shorter events, 102.4 us)
Async XLA Ops:
  7.2 80.8 %all-gather.3.cloned.1.call-start = ((), (), s32[]{:S(2)}) async-start(), calls=%async_computation.4 | async-start | bytes 2715648 | tf_op jit(solution)/shard_map/all_gather | solution.py:457
  14.1 13.9 %collective-permute-start.3 = (bf16[512,384]{1,0:T(8,128)(2,1)S(1)}, bf16[512,384]{1,0:T(8,128)(2,1)S(1)}, u32[]{:S(2)}, u32[]{:S(2)}) collective-permute-start(bf16[512,384]{1,0:T(8,128)(2,1)S(1)} %get-tuple-element.202.refs_2_.wa), channel_id=1, source_target_pairs={{0,4},{2,6},{4,0},{6,2},{1,5},{3,7},{5,1},{7,3},{8,12},{10,14},{12... | collective-permute-start | bytes 1179656 | tf_op jit(solution)/shard_map/ppermute | solution.py:438
  17.0 12.2 %collective-permute-start.2 = (bf16[512,384]{1,0:T(8,128)(2,1)S(1)}, bf16[512,384]{1,0:T(8,128)(2,1)S(1)}, u32[]{:S(2)}, u32[]{:S(2)}) collective-permute-start(bf16[512,384]{1,0:T(8,128)(2,1)S(1)} %get-tuple-element.202.refs_2_.wa), channel_id=1, source_target_pairs={{0,2},{2,0},{4,6},{6,4},{1,3},{3,1},{5,7},{7,5},{8,10},{10,8},{12,... | collective-permute-start | bytes 1179656 | tf_op jit(solution)/shard_map/ppermute | solution.py:438
  17.3 10.0 %collective-permute-start = (s32[2,512]{1,0:T(2,128)S(1)}, s32[2,512]{1,0:T(2,128)S(1)}, u32[]{:S(2)}, u32[]{:S(2)}) collective-permute-start(s32[2,512]{1,0:T(2,128)S(1)} %get-tuple-element.215), channel_id=1, source_target_pairs={{0,4},{2,6},{4,0},{6,2},{1,5},{3,7},{5,1},{7,3},{8,12},{10,14},{12... | collective-permute-start | bytes 12296 | tf_op jit(solution)/shard_map/ppermute | solution.py:438
  27.3 1.2 collective-permute-start.1
  28.0 1.9 collective-permute-start.4
  34.4 18.2 %collective-permute-start.6 = (bf16[512,384]{1,0:T(8,128)(2,1)}, bf16[512,384]{1,0:T(8,128)(2,1)S(1)}, u32[]{:S(2)}, u32[]{:S(2)}) collective-permute-start(bf16[512,384]{1,0:T(8,128)(2,1)} %get-tuple-element.79), channel_id=1, source_target_pairs={{0,8},{8,16},{16,24},{24,0},{1,9},{9,17},{17,25},{25,1},{2,10},{10... | collective-permute-start | bytes 1179656 | tf_op jit(solution)/shard_map/ppermute | solution.py:441
  36.8 39.0 %collective-permute-start.7 = (bf16[512,384]{1,0:T(8,128)(2,1)}, bf16[512,384]{1,0:T(8,128)(2,1)S(1)}, u32[]{:S(2)}, u32[]{:S(2)}) collective-permute-start(bf16[512,384]{1,0:T(8,128)(2,1)} %get-tuple-element.80), channel_id=1, source_target_pairs={{0,16},{8,24},{16,0},{24,8},{1,17},{9,25},{17,1},{25,9},{2,18},{10... | collective-permute-start | bytes 1179656 | tf_op jit(solution)/shard_map/ppermute | solution.py:441
  39.4 36.5 %collective-permute-start.8 = (bf16[512,384]{1,0:T(8,128)(2,1)}, bf16[512,384]{1,0:T(8,128)(2,1)S(1)}, u32[]{:S(2)}, u32[]{:S(2)}) collective-permute-start(bf16[512,384]{1,0:T(8,128)(2,1)} %get-tuple-element.81), channel_id=1, source_target_pairs={{0,24},{8,0},{16,8},{24,16},{1,25},{9,1},{17,9},{25,17},{2,26},{10... | collective-permute-start | bytes 1179656 | tf_op jit(solution)/shard_map/ppermute | solution.py:441
  42.6 47.9 %collective-permute-start.5 = (bf16[512,384]{1,0:T(8,128)(2,1)}, bf16[512,384]{1,0:T(8,128)(2,1)S(1)}, u32[]{:S(2)}, u32[]{:S(2)}) collective-permute-start(bf16[512,384]{1,0:T(8,128)(2,1)} %get-tuple-element.78.wa), channel_id=1, source_target_pairs={{0,1},{1,0},{2,3},{3,2},{4,5},{5,4},{6,7},{7,6},{8,9},{9,8},{10,11... | collective-permute-start | bytes 1179656 | tf_op jit(solution)/shard_map/ppermute | solution.py:435
  76.7 148.5 %all-to-all-start = ((bf16[4,3,192,1024]{3,2,1,0:T(8,128)(2,1)}), bf16[4,3,192,1024]{3,2,1,0:T(8,128)(2,1)}, u32[]{:S(2)}, u32[]{:S(2)}) async-start(bf16[4,3,192,1024]{3,2,1,0:T(8,128)(2,1)} %pad_maximum_fusion.refs_10_), calls=%async_computation | async-start | bytes 9437184 | tf_op jit(solution)/shard_map/all_to_all | solution.py:584
  87.9 249.4 %all-gather.5.cloned.1.call-start = ((), (), s32[]{:S(2)}) async-start(), calls=%async_computation.5 | async-start | bytes 5013504 | tf_op jit(solution)/shard_map/all_gather | solution.py:457
  96.3 18.8 %collective-permute-start.10 = (bf16[512,768]{1,0:T(8,128)(2,1)}, bf16[512,768]{1,0:T(8,128)(2,1)S(1)}, u32[]{:S(2)}, u32[]{:S(2)}) collective-permute-start(bf16[512,768]{1,0:T(8,128)(2,1)} %get-tuple-element.83.refs_2_), channel_id=1, source_target_pairs={{0,4},{2,6},{4,0},{6,2},{1,5},{3,7},{5,1},{7,3},{8,12},{10,14},{12... | collective-permute-start | bytes 2359304 | tf_op jit(solution)/shard_map/ppermute | solution.py:438
  97.8 21.2 %collective-permute-start.9 = (bf16[512,768]{1,0:T(8,128)(2,1)}, bf16[512,768]{1,0:T(8,128)(2,1)S(1)}, u32[]{:S(2)}, u32[]{:S(2)}) collective-permute-start(bf16[512,768]{1,0:T(8,128)(2,1)} %get-tuple-element.83.refs_2_), channel_id=1, source_target_pairs={{0,2},{2,0},{4,6},{6,4},{1,3},{3,1},{5,7},{7,5},{8,10},{10,8},{12,... | collective-permute-start | bytes 2359304 | tf_op jit(solution)/shard_map/ppermute | solution.py:438
  115.2 3.9 collective-permute-start.11
  129.3 8.4 %collective-permute-start.12 = (bf16[512,384]{1,0:T(8,128)(2,1)}, bf16[512,384]{1,0:T(8,128)(2,1)S(1)}, u32[]{:S(2)}, u32[]{:S(2)}) collective-permute-start(bf16[512,384]{1,0:T(8,128)(2,1)} %get-tuple-element.85), channel_id=1, source_target_pairs={{0,1},{1,0},{2,3},{3,2},{4,5},{5,4},{6,7},{7,6},{8,9},{9,8},{10,11... | collective-permute-start | bytes 1179656 | tf_op jit(solution)/shard_map/ppermute | solution.py:435
  139.3 3.6 collective-permute-start.13
  143.1 77.2 %copy-start.37 = (bf16[2,48,1024]{2,1,0:T(8,128)(2,1)S(1)}, bf16[2,48,1024]{2,1,0:T(8,128)(2,1)}, u32[]{:S(2)}) copy-start(bf16[2,48,1024]{2,1,0:T(8,128)(2,1)} %param.23) | copy-start | bytes 589828
  143.1 77.2 %copy-start.38 = (bf16[1024,48]{0,1:T(8,128)(2,1)S(1)}, bf16[1024,48]{0,1:T(8,128)(2,1)}, u32[]{:S(2)}) copy-start(bf16[1024,48]{0,1:T(8,128)(2,1)} %param.24) | copy-start | bytes 294916
  143.1 18.0 %collective-permute-start.16 = (bf16[512,384]{1,0:T(8,128)(2,1)S(1)}, bf16[512,384]{1,0:T(8,128)(2,1)S(1)}, u32[]{:S(2)}, u32[]{:S(2)}) collective-permute-start(bf16[512,384]{1,0:T(8,128)(2,1)S(1)} %multiply_convert_fusion.refs_2_.xa), channel_id=1, source_target_pairs={{0,4},{2,6},{4,0},{6,2},{1,5},{3,7},{5,1},{7,3},{8,12},{10,14},{12... | collective-permute-start | bytes 1179656 | tf_op jit(solution)/shard_map/ppermute | solution.py:438
  153.0 12.1 %collective-permute-start.14 = (bf16[512,384]{1,0:T(8,128)(2,1)S(1)}, bf16[512,384]{1,0:T(8,128)(2,1)S(1)}, u32[]{:S(2)}, u32[]{:S(2)}) collective-permute-start(bf16[512,384]{1,0:T(8,128)(2,1)S(1)} %multiply_convert_fusion.refs_2_.xa), channel_id=1, source_target_pairs={{0,1},{1,0},{2,3},{3,2},{4,5},{5,4},{6,7},{7,6},{8,9},{9,8},{10,11... | collective-permute-start | bytes 1179656 | tf_op jit(solution)/shard_map/ppermute | solution.py:435
  154.5 12.2 %collective-permute-start.15 = (bf16[512,384]{1,0:T(8,128)(2,1)S(1)}, bf16[512,384]{1,0:T(8,128)(2,1)S(1)}, u32[]{:S(2)}, u32[]{:S(2)}) collective-permute-start(bf16[512,384]{1,0:T(8,128)(2,1)S(1)} %multiply_convert_fusion.refs_2_.xa), channel_id=1, source_target_pairs={{0,2},{2,0},{4,6},{6,4},{1,3},{3,1},{5,7},{7,5},{8,10},{10,8},{12,... | collective-permute-start | bytes 1179656 | tf_op jit(solution)/shard_map/ppermute | solution.py:438
  161.1 5.6 %collective-permute-start.17 = (bf16[512,384]{1,0:T(8,128)(2,1)S(1)}, bf16[512,384]{1,0:T(8,128)(2,1)S(1)}, u32[]{:S(2)}, u32[]{:S(2)}) collective-permute-start(bf16[512,384]{1,0:T(8,128)(2,1)S(1)} %collective-permute-done.16.refs_4_), channel_id=1, source_target_pairs={{0,2},{2,0},{4,6},{6,4},{1,3},{3,1},{5,7},{7,5},{8,10},{10,8},{12,... | collective-permute-start | bytes 1179656 | tf_op jit(solution)/shard_map/ppermute | solution.py:438
  163.1 14.8 %collective-permute-start.20 = (bf16[512,384]{1,0:T(8,128)(2,1)S(1)}, bf16[512,384]{1,0:T(8,128)(2,1)S(1)}, u32[]{:S(2)}, u32[]{:S(2)}) collective-permute-start(bf16[512,384]{1,0:T(8,128)(2,1)S(1)} %copy-done.50), channel_id=1, source_target_pairs={{0,1},{1,0},{2,3},{3,2},{4,5},{5,4},{6,7},{7,6},{8,9},{9,8},{10,11... | collective-permute-start | bytes 1179656 | tf_op jit(solution)/shard_map/ppermute | solution.py:435
  164.6 18.9 %collective-permute-start.21 = (bf16[512,384]{1,0:T(8,128)(2,1)S(1)}, bf16[512,384]{1,0:T(8,128)(2,1)S(1)}, u32[]{:S(2)}, u32[]{:S(2)}) collective-permute-start(bf16[512,384]{1,0:T(8,128)(2,1)S(1)} %copy-done.52), channel_id=1, source_target_pairs={{0,1},{1,0},{2,3},{3,2},{4,5},{5,4},{6,7},{7,6},{8,9},{9,8},{10,11... | collective-permute-start | bytes 1179656 | tf_op jit(solution)/shard_map/ppermute | solution.py:435
  165.1 25.9 %collective-permute-start.22 = (bf16[512,384]{1,0:T(8,128)(2,1)S(1)}, bf16[512,384]{1,0:T(8,128)(2,1)S(1)}, u32[]{:S(2)}, u32[]{:S(2)}) collective-permute-start(bf16[512,384]{1,0:T(8,128)(2,1)S(1)} %copy-done.48), channel_id=1, source_target_pairs={{0,1},{1,0},{2,3},{3,2},{4,5},{5,4},{6,7},{7,6},{8,9},{9,8},{10,11... | collective-permute-start | bytes 1179656 | tf_op jit(solution)/shard_map/ppermute | solution.py:435
  172.0 46.8 %collective-permute-start.26 = (bf16[512,384]{1,0:T(8,128)(2,1)}, bf16[512,384]{1,0:T(8,128)(2,1)}, u32[]{:S(2)}, u32[]{:S(2)}) collective-permute-start(bf16[512,384]{1,0:T(8,128)(2,1)} %get-tuple-element.93), channel_id=1, source_target_pairs={{0,16},{8,24},{16,0},{24,8},{1,17},{9,25},{17,1},{25,9},{2,18},{10... | collective-permute-start | bytes 1179656 | tf_op jit(solution)/shard_map/ppermute | solution.py:441
  174.8 48.4 %collective-permute-start.24 = (bf16[512,384]{1,0:T(8,128)(2,1)}, bf16[512,384]{1,0:T(8,128)(2,1)S(1)}, u32[]{:S(2)}, u32[]{:S(2)}) collective-permute-start(bf16[512,384]{1,0:T(8,128)(2,1)} %get-tuple-element.91), channel_id=1, source_target_pairs={{0,24},{8,0},{16,8},{24,16},{1,25},{9,1},{17,9},{25,17},{2,26},{10... | collective-permute-start | bytes 1179656 | tf_op jit(solution)/shard_map/ppermute | solution.py:441
  177.9 66.7 %copy-start.55 = (bf16[512,384]{1,0:T(8,128)(2,1)}, bf16[512,384]{1,0:T(8,128)(2,1)S(1)}, u32[]{:S(2)}) copy-start(bf16[512,384]{1,0:T(8,128)(2,1)S(1)} %collective-permute-done.20.wb) | copy-start | bytes 1179652
  177.9 46.8 %collective-permute-start.19 = (bf16[512,384]{1,0:T(8,128)(2,1)}, bf16[512,384]{1,0:T(8,128)(2,1)}, u32[]{:S(2)}, u32[]{:S(2)}) collective-permute-start(bf16[512,384]{1,0:T(8,128)(2,1)} %get-tuple-element.89), channel_id=1, source_target_pairs={{0,8},{8,16},{16,24},{24,0},{1,9},{9,17},{17,25},{25,1},{2,10},{10... | collective-permute-start | bytes 1179656 | tf_op jit(solution)/shard_map/ppermute | solution.py:441
  191.0 53.6 %copy-start.53 = (bf16[512,384]{1,0:T(8,128)(2,1)}, bf16[512,384]{1,0:T(8,128)(2,1)S(1)}, u32[]{:S(2)}) copy-start(bf16[512,384]{1,0:T(8,128)(2,1)S(1)} %collective-permute-done.22.wb) | copy-start | bytes 1179652
  218.8 12.3 %collective-permute-start.27 = (bf16[512,384]{1,0:T(8,128)(2,1)}, bf16[512,384]{1,0:T(8,128)(2,1)S(1)}, u32[]{:S(2)}, u32[]{:S(2)}) collective-permute-start(bf16[512,384]{1,0:T(8,128)(2,1)} %collective-permute-done.26.xa.refs_1_), channel_id=1, source_target_pairs={{0,1},{1,0},{2,3},{3,2},{4,5},{5,4},{6,7},{7,6},{8,9},{9,8},{10,11... | collective-permute-start | bytes 1179656 | tf_op jit(solution)/shard_map/ppermute | solution.py:435
  222.7 24.7 %collective-permute-start.18 = (bf16[512,384]{1,0:T(8,128)(2,1)}, bf16[512,384]{1,0:T(8,128)(2,1)S(1)}, u32[]{:S(2)}, u32[]{:S(2)}) collective-permute-start(bf16[512,384]{1,0:T(8,128)(2,1)} %get-tuple-element.87.xa), channel_id=1, source_target_pairs={{0,1},{1,0},{2,3},{3,2},{4,5},{5,4},{6,7},{7,6},{8,9},{9,8},{10,11... | collective-permute-start | bytes 1179656 | tf_op jit(solution)/shard_map/ppermute | solution.py:435
  223.2 24.7 %collective-permute-start.25 = (bf16[512,384]{1,0:T(8,128)(2,1)S(1)}, bf16[512,384]{1,0:T(8,128)(2,1)S(1)}, u32[]{:S(2)}, u32[]{:S(2)}) collective-permute-start(bf16[512,384]{1,0:T(8,128)(2,1)S(1)} %collective-permute-done.24.refs_2_.xa), channel_id=1, source_target_pairs={{0,1},{1,0},{2,3},{3,2},{4,5},{5,4},{6,7},{7,6},{8,9},{9,8},{10,11... | collective-permute-start | bytes 1179656 | tf_op jit(solution)/shard_map/ppermute | solution.py:435
  224.7 31.7 %collective-permute-start.23 = (bf16[512,384]{1,0:T(8,128)(2,1)}, bf16[512,384]{1,0:T(8,128)(2,1)}, u32[]{:S(2)}, u32[]{:S(2)}) collective-permute-start(bf16[512,384]{1,0:T(8,128)(2,1)} %collective-permute-done.19.refs_0_.xa), channel_id=1, source_target_pairs={{0,1},{1,0},{2,3},{3,2},{4,5},{5,4},{6,7},{7,6},{8,9},{9,8},{10,11... | collective-permute-start | bytes 1179656 | tf_op jit(solution)/shard_map/ppermute | solution.py:435
  245.8 27.2 %collective-permute-start.29 = (bf16[512,768]{1,0:T(8,128)(2,1)S(1)}, bf16[512,768]{1,0:T(8,128)(2,1)S(1)}, u32[]{:S(2)}, u32[]{:S(2)}) collective-permute-start(bf16[512,768]{1,0:T(8,128)(2,1)S(1)} %slice_bitcast_fusion.3), channel_id=1, source_target_pairs={{0,1},{1,0},{2,3},{3,2},{4,5},{5,4},{6,7},{7,6},{8,9},{9,8},{10,11... | collective-permute-start | bytes 2359304 | tf_op jit(solution)/shard_map/ppermute | solution.py:435
  270.5 19.5 %collective-permute-start.28 = (bf16[512,768]{1,0:T(8,128)(2,1)S(1)}, bf16[512,768]{1,0:T(8,128)(2,1)S(1)}, u32[]{:S(2)}, u32[]{:S(2)}) collective-permute-start(bf16[512,768]{1,0:T(8,128)(2,1)S(1)} %slice_bitcast_fusion.4), channel_id=1, source_target_pairs={{0,1},{1,0},{2,3},{3,2},{4,5},{5,4},{6,7},{7,6},{8,9},{9,8},{10,11... | collective-permute-start | bytes 2359304 | tf_op jit(solution)/shard_map/ppermute | solution.py:435
  273.3 41.8 %collective-permute-start.32 = (bf16[512,768]{1,0:T(8,128)(2,1)S(1)}, bf16[512,768]{1,0:T(8,128)(2,1)S(1)}, u32[]{:S(2)}, u32[]{:S(2)}) collective-permute-start(bf16[512,768]{1,0:T(8,128)(2,1)S(1)} %fusion.13.refs_0_), channel_id=1, source_target_pairs={{0,16},{8,24},{16,0},{24,8},{1,17},{9,25},{17,1},{25,9},{2,18},{10... | collective-permute-start | bytes 2359304 | tf_op jit(solution)/shard_map/ppermute | solution.py:441
  288.4 25.6 %collective-permute-start.33 = (bf16[512,768]{1,0:T(8,128)(2,1)S(1)}, bf16[512,768]{1,0:T(8,128)(2,1)S(1)}, u32[]{:S(2)}, u32[]{:S(2)}) collective-permute-start(bf16[512,768]{1,0:T(8,128)(2,1)S(1)} %slice_bitcast_fusion.1), channel_id=1, source_target_pairs={{0,1},{1,0},{2,3},{3,2},{4,5},{5,4},{6,7},{7,6},{8,9},{9,8},{10,11... | collective-permute-start | bytes 2359304 | tf_op jit(solution)/shard_map/ppermute | solution.py:435
  290.3 47.1 %collective-permute-start.31 = (bf16[512,768]{1,0:T(8,128)(2,1)S(1)}, bf16[512,768]{1,0:T(8,128)(2,1)S(1)}, u32[]{:S(2)}, u32[]{:S(2)}) collective-permute-start(bf16[512,768]{1,0:T(8,128)(2,1)S(1)} %fusion.14.refs_0_), channel_id=1, source_target_pairs={{0,24},{8,0},{16,8},{24,16},{1,25},{9,1},{17,9},{25,17},{2,26},{10... | collective-permute-start | bytes 2359304 | tf_op jit(solution)/shard_map/ppermute | solution.py:441
  306.8 54.1 %collective-permute-start.30 = (bf16[512,768]{1,0:T(8,128)(2,1)}, bf16[512,768]{1,0:T(8,128)(2,1)}, u32[]{:S(2)}, u32[]{:S(2)}) collective-permute-start(bf16[512,768]{1,0:T(8,128)(2,1)} %slice_bitcast_fusion.2), channel_id=1, source_target_pairs={{0,1},{1,0},{2,3},{3,2},{4,5},{5,4},{6,7},{7,6},{8,9},{9,8},{10,11... | collective-permute-start | bytes 2359304 | tf_op jit(solution)/shard_map/ppermute | solution.py:435
  314.3 23.0 %collective-permute-start.34 = (bf16[512,768]{1,0:T(8,128)(2,1)S(1)}, bf16[512,768]{1,0:T(8,128)(2,1)S(1)}, u32[]{:S(2)}, u32[]{:S(2)}) collective-permute-start(bf16[512,768]{1,0:T(8,128)(2,1)S(1)} %fusion.11), channel_id=1, source_target_pairs={{0,8},{8,16},{16,24},{24,0},{1,9},{9,17},{17,25},{25,1},{2,10},{10... | collective-permute-start | bytes 2359304 | tf_op jit(solution)/shard_map/ppermute | solution.py:441
  349.9 14.4 %collective-permute-start.35 = (bf16[512,768]{1,0:T(8,128)(2,1)S(1)}, bf16[512,768]{1,0:T(8,128)(2,1)}, u32[]{:S(2)}, u32[]{:S(2)}) collective-permute-start(bf16[512,768]{1,0:T(8,128)(2,1)S(1)} %slice_bitcast_fusion), channel_id=1, source_target_pairs={{0,1},{1,0},{2,3},{3,2},{4,5},{5,4},{6,7},{7,6},{8,9},{9,8},{10,11... | collective-permute-start | bytes 2359304 | tf_op jit(solution)/shard_map/ppermute | solution.py:435
  350.5 114.6 %all-to-all-start.1 = ((bf16[4,3,192,1024]{3,2,1,0:T(8,128)(2,1)}), bf16[4,3,192,1024]{3,2,1,0:T(8,128)(2,1)}, u32[]{:S(2)}, u32[]{:S(2)}) async-start(bf16[4,3,192,1024]{3,2,1,0:T(8,128)(2,1)} %pad_maximum_fusion.1.refs_0_), calls=%async_computation.1 | async-start | bytes 9437184 | tf_op jit(solution)/shard_map/all_to_all | solution.py:644
  360.7 180.8 %reduce-scatter.2.cloned.1.call-start = ((), (), s32[]{:S(2)}) async-start(), calls=%async_computation.6 | async-start | bytes 5013504 | tf_op jit(solution)/shard_map/reduce_scatter | solution.py:665
  371.8 2.5 collective-permute-start.36
  375.7 11.2 %collective-permute-start.37 = (bf16[512,384]{1,0:T(8,128)(2,1)S(1)}, bf16[512,384]{1,0:T(8,128)(2,1)S(1)}, u32[]{:S(2)}, u32[]{:S(2)}) collective-permute-start(bf16[512,384]{1,0:T(8,128)(2,1)S(1)} %fusion.33), channel_id=1, source_target_pairs={{0,4},{2,6},{4,0},{6,2},{1,5},{3,7},{5,1},{7,3},{8,12},{10,14},{12... | collective-permute-start | bytes 1179656 | tf_op jit(solution)/shard_map/ppermute | solution.py:438
  387.9 3.6 collective-permute-start.38
  393.0 10.0 %collective-permute-start.39 = (bf16[512,384]{1,0:T(8,128)(2,1)}, bf16[512,384]{1,0:T(8,128)(2,1)}, u32[]{:S(2)}, u32[]{:S(2)}) collective-permute-start(bf16[512,384]{1,0:T(8,128)(2,1)} %fusion.60.refs_10_), channel_id=1, source_target_pairs={{0,1},{1,0},{2,3},{3,2},{4,5},{5,4},{6,7},{7,6},{8,9},{9,8},{10,11... | collective-permute-start | bytes 1179656 | tf_op jit(solution)/shard_map/ppermute | solution.py:435
  414.9 6.1 %collective-permute-start.40 = (bf16[2,512,768]{2,1,0:T(8,128)(2,1)}, bf16[2,512,768]{2,1,0:T(8,128)(2,1)}, u32[]{:S(2)}, u32[]{:S(2)}) collective-permute-start(bf16[2,512,768]{2,1,0:T(8,128)(2,1)} %get-tuple-element.127), channel_id=1, source_target_pairs={{0,2},{2,0},{4,6},{6,4},{1,3},{3,1},{5,7},{7,5},{8,10},{10,8},{12,... | collective-permute-start | bytes 4718600 | tf_op jit(solution)/shard_map/ppermute | solution.py:438
  423.6 30.0 %collective-permute-start.41 = (bf16[512,768]{1,0:T(8,128)(2,1)}, bf16[512,768]{1,0:T(8,128)(2,1)}, u32[]{:S(2)}, u32[]{:S(2)}) collective-permute-start(bf16[512,768]{1,0:T(8,128)(2,1)} %fusion.27), channel_id=1, source_target_pairs={{0,4},{2,6},{4,0},{6,2},{1,5},{3,7},{5,1},{7,3},{8,12},{10,14},{12... | collective-permute-start | bytes 2359304 | tf_op jit(solution)/shard_map/ppermute | solution.py:438
  453.6 28.4 %collective-permute-start.42 = (bf16[2,512,384]{2,1,0:T(8,128)(2,1)}, bf16[2,512,384]{2,1,0:T(8,128)(2,1)}, u32[]{:S(2)}, u32[]{:S(2)}) collective-permute-start(bf16[2,512,384]{2,1,0:T(8,128)(2,1)} %get-tuple-element.128), channel_id=1, source_target_pairs={{0,2},{2,0},{4,6},{6,4},{1,3},{3,1},{5,7},{7,5},{8,10},{10,8},{12,... | collective-permute-start | bytes 2359304 | tf_op jit(solution)/shard_map/ppermute | solution.py:438
  470.9 9.9 %collective-permute-start.44 = (bf16[512,384]{1,0:T(8,128)(2,1)}, bf16[512,384]{1,0:T(8,128)(2,1)S(1)}, u32[]{:S(2)}, u32[]{:S(2)}) collective-permute-start(bf16[512,384]{1,0:T(8,128)(2,1)} %get-tuple-element.135), channel_id=1, source_target_pairs={{0,1},{1,0},{2,3},{3,2},{4,5},{5,4},{6,7},{7,6},{8,9},{9,8},{10,11... | collective-permute-start | bytes 1179656 | tf_op jit(solution)/shard_map/ppermute | solution.py:435
  477.8 19.8 %collective-permute-start.48 = (bf16[2,4,48,1536]{3,2,1,0:T(8,128)(2,1)}, bf16[2,4,48,1536]{3,2,1,0:T(8,128)(2,1)S(1)}, u32[]{:S(2)}, u32[]{:S(2)}) collective-permute-start(bf16[2,4,48,1536]{3,2,1,0:T(8,128)(2,1)} %get-tuple-element.141), channel_id=1, source_target_pairs={{0,2},{2,0},{4,6},{6,4},{1,3},{3,1},{5,7},{7,5},{8,10},{10,8},{12,... | collective-permute-start | bytes 3538952 | tf_op jit(solution)/shard_map/ppermute | solution.py:438
  481.1 3.6 collective-permute-start.45
  483.1 10.8 %collective-permute-start.43 = (bf16[512,384]{1,0:T(8,128)(2,1)S(1)}, bf16[512,384]{1,0:T(8,128)(2,1)S(1)}, u32[]{:S(2)}, u32[]{:S(2)}) collective-permute-start(bf16[512,384]{1,0:T(8,128)(2,1)S(1)} %fusion.34), channel_id=1, source_target_pairs={{0,4},{2,6},{4,0},{6,2},{1,5},{3,7},{5,1},{7,3},{8,12},{10,14},{12... | collective-permute-start | bytes 1179656 | tf_op jit(solution)/shard_map/ppermute | solution.py:438
  495.5 19.4 %collective-permute-start.47 = (bf16[512,384]{1,0:T(8,128)(2,1)S(1)}, bf16[512,384]{1,0:T(8,128)(2,1)S(1)}, u32[]{:S(2)}, u32[]{:S(2)}) collective-permute-start(bf16[512,384]{1,0:T(8,128)(2,1)S(1)} %get-tuple-element.195), channel_id=1, source_target_pairs={{0,1},{1,0},{2,3},{3,2},{4,5},{5,4},{6,7},{7,6},{8,9},{9,8},{10,11... | collective-permute-start | bytes 1179656 | tf_op jit(solution)/shard_map/ppermute | solution.py:435
  497.1 16.8 %collective-permute-start.46 = (bf16[512,384]{1,0:T(8,128)(2,1)S(1)}, bf16[512,384]{1,0:T(8,128)(2,1)S(1)}, u32[]{:S(2)}, u32[]{:S(2)}) collective-permute-start(bf16[512,384]{1,0:T(8,128)(2,1)S(1)} %get-tuple-element.136), channel_id=1, source_target_pairs={{0,1},{1,0},{2,3},{3,2},{4,5},{5,4},{6,7},{7,6},{8,9},{9,8},{10,11... | collective-permute-start | bytes 1179656 | tf_op jit(solution)/shard_map/ppermute | solution.py:435
  497.8 18.5 %collective-permute-start.49 = (bf16[4,48,1536]{2,1,0:T(8,128)(2,1)S(1)}, bf16[4,48,1536]{2,1,0:T(8,128)(2,1)S(1)}, u32[]{:S(2)}, u32[]{:S(2)}) collective-permute-start(bf16[4,48,1536]{2,1,0:T(8,128)(2,1)S(1)} %fusion.32), channel_id=1, source_target_pairs={{0,4},{2,6},{4,0},{6,2},{1,5},{3,7},{5,1},{7,3},{8,12},{10,14},{12... | collective-permute-start | bytes 1769480 | tf_op jit(solution)/shard_map/ppermute | solution.py:438
  516.6 19.5 %collective-permute-start.50 = (bf16[48,1536]{1,0:T(8,128)(2,1)S(1)}, bf16[48,1536]{1,0:T(8,128)(2,1)S(1)}, u32[]{:S(2)}, u32[]{:S(2)}) collective-permute-start(bf16[48,1536]{1,0:T(8,128)(2,1)S(1)} %get-tuple-element.206), channel_id=1, source_target_pairs={{0,8},{8,16},{16,24},{24,0},{1,9},{9,17},{17,25},{25,1},{2,10},{10... | collective-permute-start | bytes 442376 | tf_op jit(solution)/shard_map/ppermute | solution.py:441
  518.7 17.3 %collective-permute-start.51 = (bf16[48,1536]{1,0:T(8,128)(2,1)S(1)}, bf16[48,1536]{1,0:T(8,128)(2,1)S(1)}, u32[]{:S(2)}, u32[]{:S(2)}) collective-permute-start(bf16[48,1536]{1,0:T(8,128)(2,1)S(1)} %get-tuple-element.208), channel_id=1, source_target_pairs={{0,16},{8,24},{16,0},{24,8},{1,17},{9,25},{17,1},{25,9},{2,18},{10... | collective-permute-start | bytes 442376 | tf_op jit(solution)/shard_map/ppermute | solution.py:441
  521.1 14.9 %collective-permute-start.52 = (bf16[48,1536]{1,0:T(8,128)(2,1)S(1)}, bf16[48,1536]{1,0:T(8,128)(2,1)S(1)}, u32[]{:S(2)}, u32[]{:S(2)}) collective-permute-start(bf16[48,1536]{1,0:T(8,128)(2,1)S(1)} %get-tuple-element.207), channel_id=1, source_target_pairs={{0,24},{8,0},{16,8},{24,16},{1,25},{9,1},{17,9},{25,17},{2,26},{10... | collective-permute-start | bytes 442376 | tf_op jit(solution)/shard_map/ppermute | solution.py:441
  523.7 12.3 %all-to-all-start.2 = ((f32[16,1,864]{2,1,0:T(1,128)}), f32[16,1,864]{2,1,0:T(1,128)S(1)}, u32[]{:S(2)}, u32[]{:S(2)}) async-start(f32[16,1,864]{2,1,0:T(1,128)} %all_to_all.16), calls=%async_computation.2 | async-start | bytes 114688 | tf_op jit(solution)/shard_map/all_to_all | solution.py:743
  536.3 3.9 collective-permute-start.53
  (64 other events, 513.1 us)
Sparse Core Ops, SparseCore 0:
  12.2 61.9 all-gather.2
  225.4 74.5 all-gather.4
  420.9 99.2 reduce-scatter.1
